TPU v7x, 32 devices: a whole 2x2x4 slice. The times are simulated.
32 devices in a mesh: grp: 2 (over x), row: 8 (over z, y), col: 2 (over core).
Axes of the slice: x: 2, y: 2, z: 4, core: 2. Of those that a mesh axis runs over, the one named last changes fastest.
Arguments:
- pair: bfloat16 [352, 176, 128], P(('grp', 'row'), 'col'), parts along dimension 0, may hold values from -6 to 6
- cotangent: bfloat16 [352, 176, 128], P(('grp', 'row'), 'col'), parts along dimension 0, may hold values from -6 to 6
- chain_lengths: int32 [16], P('grp'), parts along dimension 0, may hold values from 1 to 22, 132 in all
- input_norm_gain: float32 [128], replicated, may hold values from 0.1 to 1.9
- input_norm_bias: float32 [128], replicated, may hold values from -3 to 3
- w_in: bfloat16 [128, 640], replicated, may hold values from -0.5 to 0.5
- output_norm_gain: float32 [128], replicated, may hold values from 0.1 to 1.9
- output_norm_bias: float32 [128], replicated, may hold values from -3 to 3
- w_out: bfloat16 [128, 128], replicated, may hold values from -0.5 to 0.5
Outputs:
- update: bfloat16 [352, 176, 128], P(('grp', 'row'), 'col'), parts along dimension 0
- pair_gradient: bfloat16 [352, 176, 128], P(('grp', 'row'), 'col'), parts along dimension 0
- grad_w_in: float32 [256, 640], P('grp'), parts along dimension 0
- grad_w_out: float32 [256, 128], P('grp'), parts along dimension 0
There are 2 independent parts, one for each index of `grp`. A program takes and returns all parts, laid end to end along the dimension named above; an argument that names none is the same for every part. Nothing has to cross between parts.
Inputs may be any that keep to these rules, and one draw needn't show every extreme that they name: Chain slot c holds positions c * 22 to c * 22 + chain_lengths[c] - 1; the entries sum to 132 and one of them equals 22.
All inputs are finite; a program needn't handle non-finite values.
Results may differ from a plain program's by a relative error of at most 0.017.
Values may be sent and summed in bfloat16 or wider, within the bound.
No kernel may reach another device: no remote copies, remote signals or barrier semaphores. Data moves between devices by JAX's collectives and lax.ppermute only.
A program may use at most 192 MiB of HBM per device.

v0:
```python
import jax
import jax.numpy as jnp
from jax import lax
from jax.sharding import PartitionSpec as P

eps = 1e-05


def layer_norm_forward(values, norm_gain, shift_bias):
    average_value = jnp.mean(values, axis=-1, keepdims=True)
    centered_input = values - average_value
    inverse_deviation = lax.rsqrt(
        jnp.mean(centered_input * centered_input, axis=-1, keepdims=True) + eps
    )
    standardized_input = centered_input * inverse_deviation
    return (standardized_input * norm_gain + shift_bias, standardized_input, inverse_deviation)


def layer_norm_backward(output_gradient, standardized_input, inverse_deviation, norm_gain):
    scaled_output = output_gradient * norm_gain
    first_operand = jnp.mean(scaled_output, axis=-1, keepdims=True)
    second_operand = jnp.mean(scaled_output * standardized_input, axis=-1, keepdims=True)
    return inverse_deviation * (scaled_output - first_operand - standardized_input * second_operand)


def present_rows(positions, chain_lengths, slot_size):
    chain_ids = positions // slot_size
    offsets = positions - chain_ids * slot_size
    slots = jnp.arange(chain_lengths.shape[0], dtype=jnp.int32)
    lengths = jnp.sum(
        jnp.where(chain_ids[:, None] == slots[None, :], chain_lengths[None, :], 0), axis=1
    )
    return (offsets < lengths).astype(jnp.float32)


def shards(
    pair,
    cotangent,
    chain_lengths,
    input_norm_gain,
    input_norm_bias,
    w_in,
    output_norm_gain,
    output_norm_bias,
    w_out,
):
    rows_here = pair.shape[0]
    half = pair.shape[1]
    channels = pair.shape[2]
    hidden = w_out.shape[0]
    width = w_in.shape[1]
    row_count = lax.axis_size("row")
    residues = rows_here * row_count
    slot_size = residues // chain_lengths.shape[0]
    row_ids = lax.axis_index("row") * rows_here + jnp.arange(rows_here, dtype=jnp.int32)
    col_ids = lax.axis_index("col") * half + jnp.arange(half, dtype=jnp.int32)
    pair_mask = (
        present_rows(row_ids, chain_lengths, slot_size)[:, None, None]
        * present_rows(col_ids, chain_lengths, slot_size)[None, :, None]
    )
    normalized_float32, standardized_pair, input_inverse_deviation = layer_norm_forward(
        pair.astype(jnp.float32), input_norm_gain, input_norm_bias
    )
    normed = normalized_float32.astype(jnp.bfloat16)
    normed_flat = normed.reshape(rows_here * half, channels)
    proj = jnp.dot(normed_flat, w_in, preferred_element_type=jnp.float32).reshape(
        rows_here, half, width
    )
    sig_left = jax.nn.sigmoid(proj[..., 0:hidden])
    val_left = proj[..., hidden : 2 * hidden]
    sig_right = jax.nn.sigmoid(proj[..., 2 * hidden : 3 * hidden])
    val_right = proj[..., 3 * hidden : 4 * hidden]
    gate = jax.nn.sigmoid(proj[..., 4 * hidden :])
    left_proj = (pair_mask * sig_left * val_left).astype(jnp.bfloat16)
    right_proj = (pair_mask * sig_right * val_right).astype(jnp.bfloat16)
    partial_tri = jnp.einsum(
        "ikh,jkh->ijh",
        left_proj,
        lax.all_gather(right_proj, "row", axis=0, tiled=True),
        preferred_element_type=jnp.float32,
    )
    triangle_product = lax.psum_scatter(
        partial_tri.astype(jnp.bfloat16), "col", scatter_dimension=1, tiled=True
    ).astype(jnp.float32)
    triangle_output, standardized_triangle, triangle_inverse_deviation = layer_norm_forward(
        triangle_product, output_norm_gain, output_norm_bias
    )
    tri_norm = triangle_output.astype(jnp.bfloat16)
    tri_flat = tri_norm.reshape(rows_here * half, hidden)
    projected = jnp.dot(tri_flat, w_out, preferred_element_type=jnp.float32).reshape(
        rows_here, half, channels
    )
    update = (gate * projected).astype(jnp.bfloat16)
    grad_up = cotangent.astype(jnp.float32)
    grad_proj_out = (grad_up * gate).astype(jnp.bfloat16)
    grad_gate = grad_up * projected * gate * (1.0 - gate)
    grad_flat = grad_proj_out.reshape(rows_here * half, channels)
    local_w_out = lax.dot_general(
        tri_flat, grad_flat, (((0,), (0,)), ((), ())), preferred_element_type=jnp.float32
    )
    triangle_norm_gradient = lax.dot_general(
        grad_flat, w_out, (((1,), (1,)), ((), ())), preferred_element_type=jnp.float32
    ).reshape(rows_here, half, hidden)
    triangle_gradient = layer_norm_backward(
        triangle_norm_gradient, standardized_triangle, triangle_inverse_deviation, output_norm_gain
    ).astype(jnp.bfloat16)
    grad_tri_rows = lax.all_gather(triangle_gradient, "col", axis=1, tiled=True)
    columns = grad_tri_rows
    grad_left = jnp.einsum(
        "ijh,jkh->ikh",
        columns,
        lax.all_gather(right_proj, "row", axis=0, tiled=True),
        preferred_element_type=jnp.float32,
    )
    columns = grad_tri_rows
    grad_right = lax.psum_scatter(
        jnp.einsum("ijh,ikh->jkh", columns, left_proj, preferred_element_type=jnp.float32).astype(
            jnp.bfloat16
        ),
        "row",
        scatter_dimension=0,
        tiled=True,
    ).astype(jnp.float32)
    grad_proj = jnp.concatenate(
        [
            grad_left * pair_mask * val_left * sig_left * (1.0 - sig_left),
            grad_left * pair_mask * sig_left,
            grad_right * pair_mask * val_right * sig_right * (1.0 - sig_right),
            grad_right * pair_mask * sig_right,
            grad_gate,
        ],
        axis=-1,
    ).astype(jnp.bfloat16)
    proj_flat = grad_proj.reshape(rows_here * half, width)
    local_w_in = lax.dot_general(
        normed_flat, proj_flat, (((0,), (0,)), ((), ())), preferred_element_type=jnp.float32
    )
    normalized_gradient = lax.dot_general(
        proj_flat, w_in, (((1,), (1,)), ((), ())), preferred_element_type=jnp.float32
    ).reshape(rows_here, half, channels)
    pair_gradient = layer_norm_backward(
        normalized_gradient, standardized_pair, input_inverse_deviation, input_norm_gain
    ).astype(jnp.bfloat16)
    grad_w_in, grad_w_out = (
        lax.psum(local_w_in.astype(jnp.bfloat16), ("row", "col")).astype(jnp.float32),
        lax.psum(local_w_out.astype(jnp.bfloat16), ("row", "col")).astype(jnp.float32),
    )
    return (update, pair_gradient, grad_w_in, grad_w_out)


def solution(mesh):
    placed = (
        P(("grp", "row"), "col", None),
        P(("grp", "row"), "col", None),
        P("grp"),
        P(),
        P(),
        P(),
        P(),
        P(),
        P(),
    )
    return jax.shard_map(
        shards,
        mesh=mesh,
        in_specs=placed,
        out_specs=(
            P(("grp", "row"), "col", None),
            P(("grp", "row"), "col", None),
            P("grp", None),
            P("grp", None),
        ),
        check_vma=False,
    )
```

profile of v0, /device:TPU:0, one launch (start us, length us, event | category | flops | bytes accessed | tf_op | source)
XLA Modules:
  0.0 333.8 jit_solution(9856985314081938905)
XLA Ops:
  7.2 0.0 copy-start
  7.2 0.0 all-gather.2.cloned.1.call-start
  7.3 0.7 select_reduce_fusion.1
  8.0 0.7 select_reduce_fusion
  8.8 1.3 convert_reduce_fusion.1
  10.1 1.8 fusion.26
  11.9 0.1 broadcast_multiply_fusion
  12.0 0.0 copy-done
  12.0 2.4 fusion.46
  14.4 0.0 copy-start.1
  14.4 1.8 multiply_convert_fusion.5
  16.3 0.5 copy-done.1
  16.8 0.0 all-gather.2.cloned.1.call-update
  16.8 0.0 reduce-scatter.3.cloned.1.call-start
  16.8 0.4 copy.33
  17.3 72.9 %all-gather.2.cloned.1.call-done = bf16[176,88,128]{2,1,0:T(8,128)(2,1)} async-done(((bf16[22,88,128]{2,1,0:T(8,128)(2,1)}), bf16[176,88,128]{2,1,0:T(8,128)(2,1)}) %all-gather.2.cloned.1.call-update) | async-done | bytes 3964944 | tf_op jit(solution)/shard_map/all_gather | solution.py:79
  90.1 8.0 %copy.32 = bf16[176,88,128]{1,0,2:T(8,128)(2,1)} copy(bf16[176,88,128]{2,1,0:T(8,128)(2,1)} %all-gather.2.cloned.1.call-done) | data formatting | bytes 7929856 | tf_op jit(solution)/shard_map/all_gather | solution.py:79
  98.2 5.7 %fusion = bf16[22,176,128]{1,0,2:T(8,128)(2,1)S(1)} fusion(bf16[176,88,128]{1,0,2:T(8,128)(2,1)} %copy.32, bf16[22,88,128]{1,0,2:T(8,128)(2,1)S(1)} %copy.33), kind=kOutput, calls=%fused_computation.2 | convolution fusion | flops 87724032 | bytes 5451776 | tf_op jit(solution)/shard_map/ikh,jkh->ijh/dot_general | solution.py:76
  103.9 0.0 copy-start.14
  103.9 2.2 copy.34
  106.1 0.0 reduce-scatter.3.cloned.1.call-update
  106.1 0.0 reduce-scatter.5.cloned.1.call-start
  106.2 7.1 %reduce-scatter.3.cloned.1.call-done = bf16[22,88,128]{2,0,1:T(8,128)(2,1)} async-done(((bf16[22,176,128]{2,0,1:T(8,128)(2,1)}), bf16[22,88,128]{2,0,1:T(8,128)(2,1)}) %reduce-scatter.3.cloned.1.call-update) | async-done | bytes 495632 | tf_op jit(solution)/shard_map/reduce_scatter | solution.py:82
  113.2 1.5 convert_reduce_fusion
  114.7 1.8 fusion.19
  116.5 0.0 copy-done.12
  116.6 0.0 copy-done.14
  116.6 0.0 copy-start.3
  116.6 3.0 fusion.62
  119.5 0.0 copy-done.3
  119.6 1.2 fusion.18
  120.8 2.6 all_gather.8
  123.5 2.1 copy.37
  125.6 4.3 %fusion.64 = bf16[128,88,176]{2,1,0:T(8,128)(2,1)} fusion(bf16[22,88,128]{1,0,2:T(8,128)(2,1)S(1)} %copy.33, bf16[22,176,128]{1,0,2:T(8,128)(2,1)S(1)} %copy.37), kind=kOutput, calls=%fused_computation.99 | convolution fusion | flops 87228416 | bytes 5451776 | tf_op jit(solution)/shard_map/ijh,ikh->jkh/dot_general | solution.py:117
  129.9 9.2 %copy.41 = bf16[128,88,176]{0,1,2:T(8,128)(2,1)} copy(bf16[128,88,176]{2,1,0:T(8,128)(2,1)} %fusion.64) | data formatting | bytes 7929856 | tf_op jit(solution)/shard_map/ijh,ikh->jkh/dot_general | solution.py:117
  139.1 0.0 reduce-scatter.5.cloned.1.call-update
  139.1 0.0 all-reduce.2.cloned.1.call-start
  139.2 1.0 copy-done.8
  140.1 0.0 copy-done.13
  140.1 2.2 fusion.12
  142.3 63.7 %psum.15 = bf16[128,128]{1,0:T(8,128)(2,1)S(1)} all-reduce(bf16[128,128]{1,0:T(8,128)(2,1)S(1)} %fusion.12), channel_id=1, replica_groups=mesh['grp'=2,'row'=8,'col'=2] {'row','col'}, use_global_device_ids=true, to_apply=%region_13.14 | all-reduce | flops 16384 | bytes 65536 | tf_op jit(solution)/shard_map/psum | solution.py:146
  206.0 0.6 convert_element_type.98
  206.7 4.2 %fusion.63 = f32[128,88,22]{1,2,0:T(8,128)S(1)} fusion(bf16[176,88,128]{1,0,2:T(8,128)(2,1)} %copy.32, bf16[22,176,128]{1,0,2:T(8,128)(2,1)S(1)} %copy.37), kind=kOutput, calls=%fused_computation.98 | convolution fusion | flops 87228416 | bytes 5947392 | tf_op jit(solution)/shard_map/ijh,jkh->ikh/dot_general | solution.py:109
  210.9 0.5 copy.38
  211.4 0.0 copy-start.4
  211.4 2.0 fusion.40
  213.3 1.7 fusion.41
  215.0 0.0 copy-start.5
  215.0 1.4 copy-done.5
  216.5 0.0 copy-done.4
  216.5 2.7 multiply_convert_fusion.4
  219.1 5.2 %reduce-scatter.5.cloned.1.call-done = bf16[22,88,128]{2,1,0:T(8,128)(2,1)} async-done(((bf16[176,88,128]{2,1,0:T(8,128)(2,1)}), bf16[22,88,128]{2,1,0:T(8,128)(2,1)}) %reduce-scatter.5.cloned.1.call-update) | async-done | bytes 495632 | tf_op jit(solution)/shard_map/reduce_scatter | solution.py:116
  224.3 2.9 fusion.42
  227.3 0.0 copy-done.7
  227.3 2.4 fusion.43
  229.7 2.4 fusion.44
  232.1 0.0 copy-done.11
  232.1 0.0 copy-start.6
  232.1 3.8 %fusion.11 = bf16[128,640]{1,0:T(8,128)(2,1)} fusion(bf16[22,88,640]{2,1,0:T(8,128)(2,1)} %fusion.44, bf16[22,88,128]{2,1,0:T(8,128)(2,1)S(1)} %copy-done.2, f32[128]{0:T(128)S(1)} %copy-done.10, f32[128]{0:T(128)S(1)} %copy-done.11, f32[22,88]{1,0:T(8,128)S(1)} %add_rsqrt_fusion.1, f32[22,88]{1,0:T(8,128)S(1)} %broadcast_multiply_fusion.6), kind=kOutput, calls=%fused_computation.22 | convolution fusion | flops 318763008 | bytes 3154048 | tf_op jit(solution)/shard_map/dot_general | solution.py:135
  236.0 2.3 fusion.61
  238.2 0.0 all-reduce.2.cloned.1.call-update
  238.3 2.9 fusion.25
  241.2 84.4 %all-reduce.2.cloned.1.call-done = bf16[128,640]{1,0:T(8,128)(2,1)} async-done(((bf16[128,640]{1,0:T(8,128)(2,1)}), bf16[128,640]{1,0:T(8,128)(2,1)}) %all-reduce.2.cloned.1.call-update) | async-done | bytes 163856 | tf_op jit(solution)/shard_map/psum | solution.py:145
  325.6 1.7 convert_element_type.96
  (23 shorter events, 0.1 us)
Async XLA Ops:
  7.2 4.8 %copy-start = (bf16[128,640]{1,0:T(8,128)(2,1)S(1)}, bf16[128,640]{1,0:T(8,128)(2,1)}, u32[]{:S(2)}) copy-start(bf16[128,640]{1,0:T(8,128)(2,1)} %param.14) | copy-start | bytes 491524
  7.2 83.0 %all-gather.2.cloned.1.call-start = ((), (), s32[]{:S(2)}) async-start(), calls=%async_computation.2 | async-start | bytes 4460544 | tf_op jit(solution)/shard_map/all_gather | solution.py:79
  14.4 2.3 copy-start.1
  16.8 96.4 %reduce-scatter.3.cloned.1.call-start = ((), (), s32[]{:S(2)}) async-start(), calls=%async_computation.3 | async-start | bytes 1622016 | tf_op jit(solution)/shard_map/reduce_scatter | solution.py:82
  103.9 12.7 %copy-start.12 = (bf16[128,128]{1,0:T(8,128)(2,1)S(1)}, bf16[128,128]{1,0:T(8,128)(2,1)}, u32[]{:S(2)}) copy-start(bf16[128,128]{1,0:T(8,128)(2,1)} %param.17) | copy-start | bytes 98308
  103.9 12.7 %copy-start.14 = (f32[128]{0:T(128)S(1)}, f32[128]{0:T(128)}, u32[]{:S(2)}) copy-start(f32[128]{0:T(128)} %param.15) | copy-start | bytes 1540
  106.1 118.2 %reduce-scatter.5.cloned.1.call-start = ((), (), s32[]{:S(2)}) async-start(), calls=%async_computation.4 | async-start | bytes 4460544 | tf_op jit(solution)/shard_map/reduce_scatter | solution.py:116
  116.6 3.0 copy-start.3
  139.1 1.0 copy-start.8
  139.1 1.0 copy-start.13
  139.1 186.4 %all-reduce.2.cloned.1.call-start = ((), (), s32[]{:S(2)}) async-start(), calls=%async_computation.5 | async-start | bytes 327680 | tf_op jit(solution)/shard_map/psum | solution.py:145
  211.4 5.1 %copy-start.4 = (bf16[22,88,128]{2,0,1:T(8,128)(2,1)S(1)}, bf16[22,88,128]{2,0,1:T(8,128)(2,1)}, u32[]{:S(2)}) copy-start(bf16[22,88,128]{2,0,1:T(8,128)(2,1)} %reduce-scatter.3.cloned.1.call-done) | copy-start | bytes 1486852
  215.0 1.4 copy-start.5
  219.1 10.6 %copy-start.9 = (bf16[22,88,128]{2,1,0:T(8,128)(2,1)S(1)}, bf16[22,88,128]{2,1,0:T(8,128)(2,1)}, u32[]{:S(2)}) copy-start(bf16[22,88,128]{2,1,0:T(8,128)(2,1)} %param.10) | copy-start | bytes 1486852
  224.3 3.0 copy-start.7
  227.3 4.8 %copy-start.2 = (bf16[22,88,128]{2,1,0:T(8,128)(2,1)S(1)}, bf16[22,88,128]{2,1,0:T(8,128)(2,1)}, u32[]{:S(2)}) copy-start(bf16[22,88,128]{2,1,0:T(8,128)(2,1)} %param.9) | copy-start | bytes 1486852
  227.3 4.8 %copy-start.10 = (f32[128]{0:T(128)S(1)}, f32[128]{0:T(128)}, u32[]{:S(2)}) copy-start(f32[128]{0:T(128)} %param.13) | copy-start | bytes 1540
  227.3 4.8 %copy-start.11 = (f32[128]{0:T(128)S(1)}, f32[128]{0:T(128)}, u32[]{:S(2)}) copy-start(f32[128]{0:T(128)} %param.12) | copy-start | bytes 1540
  232.1 3.8 %copy-start.6 = (bf16[22,88,640]{2,1,0:T(8,128)(2,1)S(1)}, bf16[22,88,640]{2,1,0:T(8,128)(2,1)}, u32[]{:S(2)}) copy-start(bf16[22,88,640]{2,1,0:T(8,128)(2,1)} %fusion.44) | copy-start | bytes 7434244
Sparse Core Ops, SparseCore 0:
  16.9 73.1 all-gather.1
  106.3 6.9 reduce-scatter.2
  139.2 85.0 reduce-scatter.4
  238.4 87.1 all-reduce.1
where the time goes:
time: 335 us; the launch traced here: 334 us
  waiting for transfers between devices  170 us (51%)
  blocking collectives  66.4 us (20%)
  matrix products  30.6 us (9%)
  other arithmetic  27.7 us (8%)
  local copies, waits for them, and re-layouts  25.4 us (8%)
  between operations  14 us (4%)
    psum x1, waiting for transfers between devices, shards(): lax.psum(local_w_in.astype(jnp.bfloat16), ('row', 'col'))  84.4 us
    all_gather x1, waiting for transfers between devices, shards(): lax.all_gather(right_proj, 'row', axis=0, tiled=True)  72.9 us
    psum x1, blocking collectives, shards(): lax.psum(local_w_out.astype(jnp.bfloat16), ('row', 'col'))  63.7 us
    dot_general x1, local copies, waits for them, and re-layouts, shards(): jnp.einsum('ijh,ikh->jkh', columns, left_proj, preferred_element_type=jnp...  9.17 us
    unnamed x4, other arithmetic  9 us
    all_gather x1, local copies, waits for them, and re-layouts, shards(): lax.all_gather(right_proj, 'row', axis=0, tiled=True)  8.02 us
    reduce_scatter x1, waiting for transfers between devices, shards(): lax.psum_scatter(partial_tri.astype(jnp.bfloat16), 'col', scatter_dimensi...  7.06 us
  transfers between devices with their start and end apart: 4, of which 4 were waited for; matrix products, arithmetic and copies ran while one was open for 5% of the time, Pallas kernels for 0%

commit v1 on v0

v1 whole, which is shorter than its diff:
```python
import jax
import jax.numpy as jnp
from jax import lax
from jax.sharding import PartitionSpec as P

eps = 1e-05


def layer_norm_forward(values, norm_gain, shift_bias):
    average_value = jnp.mean(values, axis=-1, keepdims=True)
    centered_input = values - average_value
    inverse_deviation = lax.rsqrt(
        jnp.mean(centered_input * centered_input, axis=-1, keepdims=True) + eps
    )
    standardized_input = centered_input * inverse_deviation
    return (standardized_input * norm_gain + shift_bias, standardized_input, inverse_deviation)


def layer_norm_backward(output_gradient, standardized_input, inverse_deviation, norm_gain):
    scaled_output = output_gradient * norm_gain
    first_operand = jnp.mean(scaled_output, axis=-1, keepdims=True)
    second_operand = jnp.mean(scaled_output * standardized_input, axis=-1, keepdims=True)
    return inverse_deviation * (scaled_output - first_operand - standardized_input * second_operand)


def present_rows(positions, chain_lengths, slot_size):
    chain_ids = positions // slot_size
    offsets = positions - chain_ids * slot_size
    slots = jnp.arange(chain_lengths.shape[0], dtype=jnp.int32)
    lengths = jnp.sum(
        jnp.where(chain_ids[:, None] == slots[None, :], chain_lengths[None, :], 0), axis=1
    )
    return (offsets < lengths).astype(jnp.float32)


def ring_order(row_count):
    if row_count == 8:
        return [0, 2, 4, 6, 7, 5, 3, 1]
    return list(range(row_count))


def swap_col(x):
    return lax.ppermute(x, "col", [(0, 1), (1, 0)])


def sum_all(x, row_count):
    def add(a, b):
        return (a.astype(jnp.float32) + b.astype(jnp.float32)).astype(jnp.bfloat16)

    x = add(x, swap_col(x))
    step = 1
    while step < row_count:
        x = add(x, lax.ppermute(x, "row", [(r, r ^ step) for r in range(row_count)]))
        step *= 2
    return x


def ring_gather(block, order, place):
    n = len(order)
    forward = [(order[p], order[(p + 1) % n]) for p in range(n)]
    backward = [(order[p], order[(p - 1) % n]) for p in range(n)]
    rows = block.shape[0]
    whole = jnp.zeros((n * rows,) + block.shape[1:], block.dtype)
    ring = jnp.asarray(order, jnp.int32)

    def put(whole, part, position, offset):
        start = ring[position % n] * rows + offset
        return lax.dynamic_update_slice_in_dim(whole, part, start, 0)

    whole = put(whole, block, place, 0)
    ahead = behind = block
    cut = rows // 2
    for step in range(1, n // 2):
        ahead = lax.ppermute(ahead, "row", forward)
        behind = lax.ppermute(behind, "row", backward)
        whole = put(whole, ahead, place - step, 0)
        whole = put(whole, behind, place + step, 0)
    ahead = lax.ppermute(ahead[:cut], "row", forward)
    behind = lax.ppermute(behind[cut:], "row", backward)
    whole = put(whole, ahead, place + n // 2, 0)
    whole = put(whole, behind, place + n // 2, cut)
    return whole


def ring_scatter(part_of, order, place, rows):
    n = len(order)
    forward = [(order[p], order[(p + 1) % n]) for p in range(n)]
    backward = [(order[p], order[(p - 1) % n]) for p in range(n)]
    cut = rows // 2
    far = part_of(place + n // 2).astype(jnp.bfloat16)
    up = lax.ppermute(far[:cut], "row", forward).astype(jnp.float32)
    down = lax.ppermute(far[cut:], "row", backward).astype(jnp.float32)
    for step in range(n // 2 - 1, 0, -1):
        up_part = part_of(place + step)
        down_part = part_of(place - step)
        if up.shape[0] != rows:
            up = jnp.concatenate([up_part[:cut] + up, up_part[cut:]], axis=0)
            down = jnp.concatenate([down_part[:cut], down_part[cut:] + down], axis=0)
        else:
            up, down = up_part + up, down_part + down
        up = lax.ppermute(up.astype(jnp.bfloat16), "row", forward).astype(jnp.float32)
        down = lax.ppermute(down.astype(jnp.bfloat16), "row", backward).astype(jnp.float32)
    return part_of(place) + up + down


def shards(
    pair,
    cotangent,
    chain_lengths,
    input_norm_gain,
    input_norm_bias,
    w_in,
    output_norm_gain,
    output_norm_bias,
    w_out,
):
    rows_here = pair.shape[0]
    half = pair.shape[1]
    channels = pair.shape[2]
    hidden = w_out.shape[0]
    row_count = lax.axis_size("row")
    residues = rows_here * row_count
    slot_size = residues // chain_lengths.shape[0]
    order = ring_order(row_count)
    inverse = [order.index(r) for r in range(row_count)]
    place = jnp.asarray(inverse, jnp.int32)[lax.axis_index("row")] + row_count
    ring = jnp.asarray(order, jnp.int32)
    col = lax.axis_index("col")
    f32 = jnp.float32
    bf16 = jnp.bfloat16

    def dot(a, b, ca, cb):
        return lax.dot_general(a, b, (((ca,), (cb,)), ((), ())), preferred_element_type=f32)

    def shaped(x):
        return x.reshape(rows_here, half, -1)

    row_ids = lax.axis_index("row") * rows_here + jnp.arange(rows_here, dtype=jnp.int32)
    col_ids = col * half + jnp.arange(half, dtype=jnp.int32)
    pair_mask = (
        present_rows(row_ids, chain_lengths, slot_size)[:, None, None]
        * present_rows(col_ids, chain_lengths, slot_size)[None, :, None]
    )
    w_left, w_right = w_in[:, : 2 * hidden], w_in[:, 2 * hidden : 4 * hidden]
    w_gate = w_in[:, 4 * hidden :]
    normalized_float32, standardized_pair, input_inverse_deviation = layer_norm_forward(
        pair.astype(f32), input_norm_gain, input_norm_bias
    )
    normed_flat = normalized_float32.astype(bf16).reshape(rows_here * half, channels)
    proj_right = shaped(dot(normed_flat, w_right, 1, 0))
    sig_right = jax.nn.sigmoid(proj_right[..., :hidden])
    val_right = proj_right[..., hidden:]
    right_proj = (pair_mask * sig_right * val_right).astype(bf16)
    right_all = ring_gather(right_proj, order, place)

    proj_left = shaped(dot(normed_flat, w_left, 1, 0))
    sig_left = jax.nn.sigmoid(proj_left[..., :hidden])
    val_left = proj_left[..., hidden:]
    left_proj = (pair_mask * sig_left * val_left).astype(bf16)
    gate = jax.nn.sigmoid(shaped(dot(normed_flat, w_gate, 1, 0)))
    grad_up = cotangent.astype(f32)
    grad_proj_out = (grad_up * gate).astype(bf16)
    grad_flat = grad_proj_out.reshape(rows_here * half, channels)

    other_out = swap_col(grad_proj_out)
    grad_out_all = jnp.where(
        col == 0,
        jnp.concatenate([grad_proj_out, other_out], axis=1),
        jnp.concatenate([other_out, grad_proj_out], axis=1),
    )
    triangle_norm_gradient = dot(
        grad_out_all.reshape(rows_here * 2 * half, channels), w_out, 1, 1
    ).reshape(rows_here, 2 * half, hidden)

    partial_tri = jnp.einsum(
        "ikh,jkh->ijh", left_proj, right_all, preferred_element_type=f32
    ).astype(bf16)
    triangle_product = partial_tri.astype(f32) + swap_col(partial_tri).astype(f32)
    triangle_output, standardized_triangle, triangle_inverse_deviation = layer_norm_forward(
        triangle_product, output_norm_gain, output_norm_bias
    )
    triangle_gradient = layer_norm_backward(
        triangle_norm_gradient, standardized_triangle, triangle_inverse_deviation, output_norm_gain
    ).astype(bf16)

    grad_right_all = jnp.einsum(
        "ijh,ikh->jkh", triangle_gradient, left_proj, preferred_element_type=f32
    ).astype(bf16)

    def part_of(position):
        start = ring[position % row_count] * rows_here
        return lax.dynamic_slice_in_dim(grad_right_all, start, rows_here, 0).astype(f32)

    grad_right = ring_scatter(part_of, order, place, rows_here)

    tri_norm = lax.dynamic_slice_in_dim(triangle_output, col * half, half, 1).astype(bf16)
    tri_flat = tri_norm.reshape(rows_here * half, hidden)
    projected = shaped(dot(tri_flat, w_out, 1, 0))
    update = (gate * projected).astype(bf16)
    grad_gate = (grad_up * projected * gate * (1.0 - gate)).astype(bf16)
    local_w_out = dot(tri_flat, grad_flat, 0, 0)
    grad_left = jnp.einsum("ijh,jkh->ikh", triangle_gradient, right_all, preferred_element_type=f32)
    early = jnp.concatenate(
        [
            grad_left * pair_mask * val_left * sig_left * (1.0 - sig_left),
            grad_left * pair_mask * sig_left,
        ],
        axis=-1,
    ).astype(bf16)
    early_flat = jnp.concatenate([early, grad_gate], axis=-1).reshape(rows_here * half, -1)
    w_early = jnp.concatenate([w_left, w_gate], axis=1)
    local_early = dot(normed_flat, early_flat, 0, 0)
    summed_early = sum_all(
        jnp.concatenate([local_early, local_w_out], axis=1).astype(bf16), row_count
    ).astype(f32)
    gradient_early = dot(early_flat, w_early, 1, 1)

    late_flat = (
        jnp.concatenate(
            [
                grad_right * pair_mask * val_right * sig_right * (1.0 - sig_right),
                grad_right * pair_mask * sig_right,
            ],
            axis=-1,
        )
        .astype(bf16)
        .reshape(rows_here * half, -1)
    )
    summed_late = sum_all(dot(normed_flat, late_flat, 0, 0).astype(bf16), row_count).astype(f32)
    normalized_gradient = shaped(gradient_early + dot(late_flat, w_right, 1, 1))
    pair_gradient = layer_norm_backward(
        normalized_gradient, standardized_pair, input_inverse_deviation, input_norm_gain
    ).astype(bf16)
    grad_w_in = jnp.concatenate(
        [summed_early[:, : 2 * hidden], summed_late, summed_early[:, 2 * hidden : 3 * hidden]],
        axis=1,
    )
    grad_w_out = summed_early[:, 3 * hidden :]
    return (update, pair_gradient, grad_w_in, grad_w_out)


def solution(mesh):
    placed = (
        P(("grp", "row"), "col", None),
        P(("grp", "row"), "col", None),
        P("grp"),
        P(),
        P(),
        P(),
        P(),
        P(),
        P(),
    )
    return jax.shard_map(
        shards,
        mesh=mesh,
        in_specs=placed,
        out_specs=(
            P(("grp", "row"), "col", None),
            P(("grp", "row"), "col", None),
            P("grp", None),
            P("grp", None),
        ),
        check_vma=False,
    )
```

time: 335 us -> 305 us (0.910)
  local copies, waits for them, and re-layouts: 25.4 us -> 126 us
  waiting for transfers between devices: 170 us -> 75.5 us
  blocking collectives: 66.4 us -> 0 us
  starting transfers between devices: 0.16 us -> 27.2 us
  matrix products: 30.6 us -> 36.7 us
    psum x1 -> x0, waiting for transfers between devices: 84.4 us -> none  [shards(): lax.psum(local_w_in.astype(jnp.bfloat16), ('row', 'col'))]
    dynamic_update_slice x0 -> x9, local copies, waits for them, and re-layouts: none -> 77.8 us  [put(): return lax.dynamic_update_slice_in_dim(whole, part, start, 0)]
    ppermute x0 -> x26, waiting for transfers between devices: none -> 75.5 us  [the longest x3 31.2 us: ring_gather(): ahead = lax.ppermute(ahead, 'row', forward)]
    all_gather x1 -> x0, waiting for transfers between devices: 72.9 us -> none  [shards(): lax.all_gather(right_proj, 'row', axis=0, tiled=True)]
    psum x1 -> x0, blocking collectives: 63.7 us -> none  [shards(): lax.psum(local_w_out.astype(jnp.bfloat16), ('row', 'col'))]
    ppermute x0 -> x26, starting transfers between devices: none -> 27.2 us  [the longest x6 8.16 us: sum_all(): lax.ppermute(x, 'row', [(r, r ^ step) for r in range(row_count)])]
    ppermute x0 -> x8, local copies, waits for them, and re-layouts: none -> 17.9 us  [the longest x3 6.8 us: ring_gather(): ahead = lax.ppermute(ahead, 'row', forward)]
    reduce_scatter x2 -> x0, waiting for transfers between devices: 12.3 us -> none  [the longest x1 7.06 us: shards(): lax.psum_scatter(partial_tri.astype(jnp.bfloat16), 'col', scatter_dimensi...]
  transfers between devices with their start and end apart: 4 -> 26, of which waited for: 4 -> 15; matrix products, arithmetic and copies ran while one was open for 5% -> 41% of each run, Pallas kernels for 0% -> 0%
where the time goes in v1:
time: 305 us; the launch traced here: 302 us
  local copies, waits for them, and re-layouts  126 us (41%)
  waiting for transfers between devices  75.5 us (25%)
  matrix products  36.7 us (12%)
  starting transfers between devices  27.2 us (9%)
  other arithmetic  25.2 us (8%)
  between operations  11.7 us (4%)
    dynamic_update_slice x9, local copies, waits for them, and re-layouts, put(): return lax.dynamic_update_slice_in_dim(whole, part, start, 0)  77.8 us
    ppermute x3, waiting for transfers between devices, ring_gather(): ahead = lax.ppermute(ahead, 'row', forward)  31.2 us
    ppermute x3, waiting for transfers between devices, ring_scatter(): lax.ppermute(up.astype(jnp.bfloat16), 'row', forward).astype(jnp.float32)  22.3 us
    dot_general x10, matrix products, dot(): lax.dot_general(a, b, (((ca,), (cb,)), ((), ())), preferred_element_type=...  18.2 us
    ppermute x6, waiting for transfers between devices, sum_all(): lax.ppermute(x, 'row', [(r, r ^ step) for r in range(row_count)])  12.6 us
    dot_general x1, local copies, waits for them, and re-layouts, shards(): jnp.einsum('ijh,ikh->jkh', triangle_gradient, left_proj, preferred_elemen...  9.13 us
    ppermute x6, starting transfers between devices, sum_all(): lax.ppermute(x, 'row', [(r, r ^ step) for r in range(row_count)])  8.16 us
    dot_general x1, matrix products, shards(): jnp.einsum('ikh,jkh->ijh', left_proj, right_all, preferred_element_type=f32)  6.91 us
  transfers between devices with their start and end apart: 26, of which 15 were waited for; matrix products, arithmetic and copies ran while one was open for 41% of the time, Pallas kernels for 0%

profile of v1, /device:TPU:0, one launch (start us, length us, event | category | flops | bytes accessed | tf_op | source)
XLA Modules:
  0.0 301.9 jit_solution(6070481609232983216)
XLA Ops:
  0.7 1.4 convert_reduce_fusion
  2.1 1.8 fusion.20
  3.9 1.8 fusion.61
  5.7 2.0 fusion.63
  8.0 2.9 multiply_convert_fusion.6
  10.9 3.0 %collective-permute-start = (bf16[22,88,128]{2,1,0:T(8,128)(2,1)S(1)}, bf16[22,88,128]{2,1,0:T(8,128)(2,1)S(1)}, u32[]{:S(2)}, u32[]{:S(2)}) collective-permute-start(bf16[22,88,128]{2,1,0:T(8,128)(2,1)S(1)} %get-tuple-element.25), channel_id=1, source_target_pairs={{0,4},{4,8},{8,12},{12,14},{14,10},{10,6},{6,2},{2,0},{1,5},{5,9},... | collective-permute-start | bytes 1486856 | tf_op jit(solution)/shard_map/ppermute | solution.py:74
  14.0 11.2 %collective-permute-done = bf16[22,88,128]{2,1,0:T(8,128)(2,1)S(1)} collective-permute-done((bf16[22,88,128]{2,1,0:T(8,128)(2,1)S(1)}, bf16[22,88,128]{2,1,0:T(8,128)(2,1)S(1)}, u32[]{:S(2)}, u32[]{:S(2)}) %collective-permute-start) | collective-permute-done | bytes 495648 | tf_op jit(solution)/shard_map/ppermute | solution.py:74
  25.2 1.8 collective-permute-start.2
  27.2 10.5 %collective-permute-done.2 = bf16[22,88,128]{2,1,0:T(8,128)(2,1)S(1)} collective-permute-done((bf16[22,88,128]{2,1,0:T(8,128)(2,1)S(1)}, bf16[22,88,128]{2,1,0:T(8,128)(2,1)S(1)}, u32[]{:S(2)}, u32[]{:S(2)}) %collective-permute-start.2) | collective-permute-done | bytes 495648 | tf_op jit(solution)/shard_map/ppermute | solution.py:74
  37.7 1.5 collective-permute-start.4
  39.8 9.5 %collective-permute-done.4 = bf16[22,88,128]{2,1,0:T(8,128)(2,1)S(1)} collective-permute-done((bf16[22,88,128]{2,1,0:T(8,128)(2,1)S(1)}, bf16[22,88,128]{2,1,0:T(8,128)(2,1)S(1)}, u32[]{:S(2)}, u32[]{:S(2)}) %collective-permute-start.4) | collective-permute-done | bytes 495648 | tf_op jit(solution)/shard_map/ppermute | solution.py:74
  67.4 1.4 copy.80
  69.0 3.2 %broadcast_in_dim.26 = bf16[176,88,128]{1,0,2:T(8,128)(2,1)} broadcast(bf16[]{:T(256)} %constant.142.clone.1), dimensions={} | broadcast | bytes 3964930 | tf_op jit(solution)/shard_map/broadcast_in_dim | solution.py:63
  72.2 9.3 %dynamic_update_slice.27 = bf16[176,88,128]{1,0,2:T(8,128)(2,1)} dynamic-update-slice(bf16[176,88,128]{1,0,2:T(8,128)(2,1)} %broadcast_in_dim.26, bf16[22,88,128]{1,0,2:T(8,128)(2,1)} %copy.71, s32[]{:T(128)S(6)} %select_n.194, s32[]{:T(128)} %constant.147.clone.1, s32[]{:T(128)} %constant.147.clone.1) | dynamic-update-slice | bytes 991236 | tf_op jit(solution)/shard_map/dynamic_update_slice | solution.py:68
  81.5 2.3 copy.72
  83.7 9.2 %dynamic_update_slice.28 = bf16[176,88,128]{1,0,2:T(8,128)(2,1)} dynamic-update-slice(bf16[176,88,128]{1,0,2:T(8,128)(2,1)} %dynamic_update_slice.27, bf16[22,88,128]{1,0,2:T(8,128)(2,1)} %copy.72, s32[]{:T(128)S(6)} %select_n.197, s32[]{:T(128)} %constant.147.clone.1, s32[]{:T(128)} %constant.147.clone.1) | dynamic-update-slice | bytes 991236 | tf_op jit(solution)/shard_map/dynamic_update_slice | solution.py:68
  92.9 2.3 copy.73
  95.2 9.2 %dynamic_update_slice.29 = bf16[176,88,128]{1,0,2:T(8,128)(2,1)} dynamic-update-slice(bf16[176,88,128]{1,0,2:T(8,128)(2,1)} %dynamic_update_slice.28, bf16[22,88,128]{1,0,2:T(8,128)(2,1)} %copy.73, s32[]{:T(128)S(6)} %select_n.200, s32[]{:T(128)} %constant.147.clone.1, s32[]{:T(128)} %constant.147.clone.1) | dynamic-update-slice | bytes 991236 | tf_op jit(solution)/shard_map/dynamic_update_slice | solution.py:68
  104.4 2.3 copy.74
  106.7 9.3 %dynamic_update_slice.30 = bf16[176,88,128]{1,0,2:T(8,128)(2,1)} dynamic-update-slice(bf16[176,88,128]{1,0,2:T(8,128)(2,1)} %dynamic_update_slice.29, bf16[22,88,128]{1,0,2:T(8,128)(2,1)} %copy.74, s32[]{:T(128)S(6)} %select_n.203, s32[]{:T(128)} %constant.147.clone.1, s32[]{:T(128)} %constant.147.clone.1) | dynamic-update-slice | bytes 991236 | tf_op jit(solution)/shard_map/dynamic_update_slice | solution.py:68
  116.0 2.3 copy.75
  118.2 9.2 %dynamic_update_slice.31 = bf16[176,88,128]{1,0,2:T(8,128)(2,1)} dynamic-update-slice(bf16[176,88,128]{1,0,2:T(8,128)(2,1)} %dynamic_update_slice.30, bf16[22,88,128]{1,0,2:T(8,128)(2,1)} %copy.75, s32[]{:T(128)S(6)} %select_n.206, s32[]{:T(128)} %constant.147.clone.1, s32[]{:T(128)} %constant.147.clone.1) | dynamic-update-slice | bytes 991236 | tf_op jit(solution)/shard_map/dynamic_update_slice | solution.py:68
  127.5 2.3 copy.76
  129.7 9.2 %dynamic_update_slice.32 = bf16[176,88,128]{1,0,2:T(8,128)(2,1)} dynamic-update-slice(bf16[176,88,128]{1,0,2:T(8,128)(2,1)} %dynamic_update_slice.31, bf16[22,88,128]{1,0,2:T(8,128)(2,1)} %copy.76, s32[]{:T(128)S(6)} %select_n.209, s32[]{:T(128)} %constant.147.clone.1, s32[]{:T(128)} %constant.147.clone.1) | dynamic-update-slice | bytes 991236 | tf_op jit(solution)/shard_map/dynamic_update_slice | solution.py:68
  138.9 2.3 copy.77
  141.2 9.2 %dynamic_update_slice.33 = bf16[176,88,128]{1,0,2:T(8,128)(2,1)} dynamic-update-slice(bf16[176,88,128]{1,0,2:T(8,128)(2,1)} %dynamic_update_slice.32, bf16[22,88,128]{1,0,2:T(8,128)(2,1)} %copy.77, s32[]{:T(128)S(6)} %select_n.212, s32[]{:T(128)} %constant.147.clone.1, s32[]{:T(128)} %constant.147.clone.1) | dynamic-update-slice | bytes 991236 | tf_op jit(solution)/shard_map/dynamic_update_slice | solution.py:68
  150.4 2.1 copy.78
  152.6 6.8 %dynamic_update_slice.34 = bf16[176,88,128]{1,0,2:T(8,128)(2,1)} dynamic-update-slice(bf16[176,88,128]{1,0,2:T(8,128)(2,1)} %dynamic_update_slice.33, bf16[11,88,128]{1,0,2:T(8,128)(2,1)} %copy.78, s32[]{:T(128)S(6)} %select_n.215, s32[]{:T(128)} %constant.147.clone.1, s32[]{:T(128)} %constant.147.clone.1) | dynamic-update-slice | bytes 495620 | tf_op jit(solution)/shard_map/dynamic_update_slice | solution.py:68
  159.4 2.1 copy.79
  161.5 6.3 %dynamic_update_slice.35 = bf16[176,88,128]{1,0,2:T(8,128)(2,1)} dynamic-update-slice(bf16[176,88,128]{1,0,2:T(8,128)(2,1)} %dynamic_update_slice.34, bf16[11,88,128]{1,0,2:T(8,128)(2,1)} %copy.79, s32[]{:T(128)S(6)} %select_n.216, s32[]{:T(128)} %constant.147.clone.1, s32[]{:T(128)} %constant.147.clone.1) | dynamic-update-slice | bytes 495620 | tf_op jit(solution)/shard_map/dynamic_update_slice | solution.py:68
  167.9 6.9 %fusion.87 = bf16[128,176,22]{1,2,0:T(8,128)(2,1)} fusion(bf16[176,88,128]{1,0,2:T(8,128)(2,1)} %dynamic_update_slice.35, bf16[22,88,128]{1,0,2:T(8,128)(2,1)S(1)} %copy.80), kind=kOutput, calls=%fused_computation.149 | convolution fusion | flops 87228416 | bytes 5451776 | tf_op jit(solution)/shard_map/ikh,jkh->ijh/dot_general | solution.py:175
  174.8 2.1 copy.81
  177.0 2.8 fusion.21
  180.3 2.1 fusion.1
  182.4 2.6 multiply_reduce_fusion.1
  185.0 4.4 %multiply_reduce_fusion.2 = (f32[22,176]{1,0:T(8,128)S(1)}, f32[22,176]{1,0:T(8,128)S(1)}, f32[22,176,128]{2,1,0:T(8,128)S(1)}, f32[22,176,128]{2,1,0:T(8,128)S(1)}) fusion(f32[128]{0:T(128)S(1)} %copy-done.20, f32[22,176]{1,0:T(8,128)S(1)} %add_rsqrt_fusion, f32[22,176]{1,0:T(8,128)S(1)} %broadcast_multiply_fusion.2, ...), kind=kOutput, calls=%fused_computation.8 | convolution fusion | flops 135791040 | bytes 7033857 | tf_op jit(solution)/shard_map/dot_general | solution.py:133
  190.7 2.9 multiply_convert_fusion
  193.5 2.9 copy.82
  196.4 5.7 %fusion.89 = bf16[128,88,176]{2,1,0:T(8,128)(2,1)} fusion(bf16[22,88,128]{1,0,2:T(8,128)(2,1)S(1)} %copy-done.6, bf16[22,176,128]{1,0,2:T(8,128)(2,1)} %copy.82), kind=kOutput, calls=%fused_computation.151 | convolution fusion | flops 87228416 | bytes 5451776 | tf_op jit(solution)/shard_map/ijh,ikh->jkh/dot_general | solution.py:186
  202.1 9.1 %copy.86 = bf16[128,88,176]{0,1,2:T(8,128)(2,1)} copy(bf16[128,88,176]{2,1,0:T(8,128)(2,1)} %fusion.89) | data formatting | bytes 7929856 | tf_op jit(solution)/shard_map/ijh,ikh->jkh/dot_general | solution.py:186
  211.2 1.4 dynamic-slice_bitcast_fusion.2
  212.7 1.3 collective-permute-start.10
  214.8 5.9 %collective-permute-done.10 = bf16[11,88,128]{2,1,0:T(8,128)(2,1)S(1)} collective-permute-done((bf16[11,88,128]{2,1,0:T(8,128)(2,1)S(1)}, bf16[11,88,128]{2,1,0:T(8,128)(2,1)S(1)}, u32[]{:S(2)}, u32[]{:S(2)}) %collective-permute-start.10) | collective-permute-done | bytes 247840 | tf_op jit(solution)/shard_map/ppermute | solution.py:91
  220.9 1.3 collective-permute-start.11
  223.1 10.1 %collective-permute-done.11 = bf16[22,88,128]{2,1,0:T(8,128)(2,1)S(1)} collective-permute-done((bf16[22,88,128]{2,1,0:T(8,128)(2,1)S(1)}, bf16[22,88,128]{2,1,0:T(8,128)(2,1)S(1)}, u32[]{:S(2)}, u32[]{:S(2)}) %collective-permute-start.11) | collective-permute-done | bytes 495648 | tf_op jit(solution)/shard_map/ppermute | solution.py:101
  234.5 1.3 collective-permute-start.12
  235.8 10.2 %collective-permute-done.12 = bf16[22,88,128]{2,1,0:T(8,128)(2,1)S(1)} collective-permute-done((bf16[22,88,128]{2,1,0:T(8,128)(2,1)S(1)}, bf16[22,88,128]{2,1,0:T(8,128)(2,1)S(1)}, u32[]{:S(2)}, u32[]{:S(2)}) %collective-permute-start.12) | collective-permute-done | bytes 495648 | tf_op jit(solution)/shard_map/ppermute | solution.py:101
  246.0 2.4 fusion.48
  249.5 5.9 %fusion.88 = f32[128,88,22]{1,2,0:T(8,128)} fusion(bf16[176,88,128]{1,0,2:T(8,128)(2,1)} %dynamic_update_slice.35, bf16[22,176,128]{1,0,2:T(8,128)(2,1)} %copy.82), kind=kOutput, calls=%fused_computation.150 | convolution fusion | flops 87228416 | bytes 5947392 | tf_op jit(solution)/shard_map/ijh,jkh->ikh/dot_general | solution.py:202
  255.4 1.8 copy.83
  259.3 1.3 fusion.46
  261.8 1.7 fusion.13
  263.5 2.4 fusion.24
  265.9 1.9 collective-permute-done.13
  267.8 2.5 collective-permute-done.17
  270.3 2.0 multiply_convert_fusion.2
  277.6 1.9 fusion.19
  281.7 2.8 collective-permute-done.23
  286.7 1.3 collective-permute-start.20
  288.9 1.9 collective-permute-start.25
  290.9 1.5 collective-permute-done.20
  292.4 1.8 collective-permute-start.21
  294.3 2.5 collective-permute-done.25
  296.8 3.7 %collective-permute-done.21 = bf16[128,512]{1,0:T(8,128)(2,1)S(1)} collective-permute-done((bf16[128,512]{1,0:T(8,128)(2,1)S(1)}, bf16[128,512]{1,0:T(8,128)(2,1)S(1)}, u32[]{:S(2)}, u32[]{:S(2)}) %collective-permute-start.21) | collective-permute-done | bytes 131104 | tf_op jit(solution)/shard_map/ppermute | solution.py:53
  (131 shorter events, 30.2 us)
Async XLA Ops:
  0.6 184.4 %copy-start = (bf16[128,128]{1,0:T(8,128)(2,1)S(1)}, bf16[128,128]{1,0:T(8,128)(2,1)}, u32[]{:S(2)}) copy-start(bf16[128,128]{1,0:T(8,128)(2,1)} %param.20) | copy-start | bytes 98308
  0.6 5.0 %copy-start.2 = (bf16[22,88,128]{2,1,0:T(8,128)(2,1)S(1)}, bf16[22,88,128]{2,1,0:T(8,128)(2,1)}, u32[]{:S(2)}) copy-start(bf16[22,88,128]{2,1,0:T(8,128)(2,1)} %param.12) | copy-start | bytes 1486852
  0.7 5.0 %copy-start.19 = (f32[128]{0:T(128)S(1)}, f32[128]{0:T(128)}, u32[]{:S(2)}) copy-start(f32[128]{0:T(128)} %param.15) | copy-start | bytes 1540
  0.7 5.0 %copy-start.21 = (f32[128]{0:T(128)S(1)}, f32[128]{0:T(128)}, u32[]{:S(2)}) copy-start(f32[128]{0:T(128)} %param.16) | copy-start | bytes 1540
  0.7 5.0 %copy-start.10 = (bf16[128,640]{1,0:T(8,128)(2,1)S(1)}, bf16[128,640]{1,0:T(8,128)(2,1)}, u32[]{:S(2)}) copy-start(bf16[128,640]{1,0:T(8,128)(2,1)} %param.17) | copy-start | bytes 491524
  3.9 3.9 %copy-start.23 = (s32[8]{0:T(128)S(1)}, s32[8]{0:T(128)}, u32[]{:S(2)}) copy-start(s32[8]{0:T(128)} %param.14) | copy-start | bytes 100
  8.0 46.4 %copy-start.24 = (s32[8]{0:T(128)S(1)}, s32[8]{0:T(128)}, u32[]{:S(2)}) copy-start(s32[8]{0:T(128)} %constant.164.clone) | copy-start | bytes 100
  8.0 52.3 %copy-start.18 = (s32[8]{0:T(128)S(1)}, s32[8]{0:T(128)}, u32[]{:S(2)}) copy-start(s32[8]{0:T(128)} %constant.165.clone) | copy-start | bytes 100
  10.9 14.3 %collective-permute-start = (bf16[22,88,128]{2,1,0:T(8,128)(2,1)S(1)}, bf16[22,88,128]{2,1,0:T(8,128)(2,1)S(1)}, u32[]{:S(2)}, u32[]{:S(2)}) collective-permute-start(bf16[22,88,128]{2,1,0:T(8,128)(2,1)S(1)} %get-tuple-element.25), channel_id=1, source_target_pairs={{0,4},{4,8},{8,12},{12,14},{14,10},{10,6},{6,2},{2,0},{1,5},{5,9},... | collective-permute-start | bytes 1486856 | tf_op jit(solution)/shard_map/ppermute | solution.py:74
  14.0 13.1 %collective-permute-start.1 = (bf16[22,88,128]{2,1,0:T(8,128)(2,1)S(1)}, bf16[22,88,128]{2,1,0:T(8,128)(2,1)S(1)}, u32[]{:S(2)}, u32[]{:S(2)}) collective-permute-start(bf16[22,88,128]{2,1,0:T(8,128)(2,1)S(1)} %get-tuple-element.25), channel_id=1, source_target_pairs={{0,2},{4,0},{8,4},{12,8},{14,12},{10,14},{6,10},{2,6},{1,3},{5,1},... | collective-permute-start | bytes 1486856 | tf_op jit(solution)/shard_map/ppermute | solution.py:75
  25.2 14.6 %copy-start.13 = (bf16[22,88,128]{2,1,0:T(8,128)(2,1)}, bf16[22,88,128]{2,1,0:T(8,128)(2,1)S(1)}, u32[]{:S(2)}) copy-start(bf16[22,88,128]{2,1,0:T(8,128)(2,1)S(1)} %collective-permute-done) | copy-start | bytes 1486852
  25.2 12.5 %collective-permute-start.2 = (bf16[22,88,128]{2,1,0:T(8,128)(2,1)S(1)}, bf16[22,88,128]{2,1,0:T(8,128)(2,1)S(1)}, u32[]{:S(2)}, u32[]{:S(2)}) collective-permute-start(bf16[22,88,128]{2,1,0:T(8,128)(2,1)S(1)} %collective-permute-done), channel_id=1, source_target_pairs={{0,4},{4,8},{8,12},{12,14},{14,10},{10,6},{6,2},{2,0},{1,5},{5,9},... | collective-permute-start | bytes 1486856 | tf_op jit(solution)/shard_map/ppermute | solution.py:74
  27.0 12.2 %copy-start.12 = (bf16[22,88,128]{2,1,0:T(8,128)(2,1)}, bf16[22,88,128]{2,1,0:T(8,128)(2,1)S(1)}, u32[]{:S(2)}) copy-start(bf16[22,88,128]{2,1,0:T(8,128)(2,1)S(1)} %collective-permute-done.1) | copy-start | bytes 1486852
  27.0 12.2 %collective-permute-start.3 = (bf16[22,88,128]{2,1,0:T(8,128)(2,1)S(1)}, bf16[22,88,128]{2,1,0:T(8,128)(2,1)S(1)}, u32[]{:S(2)}, u32[]{:S(2)}) collective-permute-start(bf16[22,88,128]{2,1,0:T(8,128)(2,1)S(1)} %collective-permute-done.1), channel_id=1, source_target_pairs={{0,2},{4,0},{8,4},{12,8},{14,12},{10,14},{6,10},{2,6},{1,3},{5,1},... | collective-permute-start | bytes 1486856 | tf_op jit(solution)/shard_map/ppermute | solution.py:75
  37.7 2.1 copy-start.14
  37.7 11.6 %collective-permute-start.4 = (bf16[22,88,128]{2,1,0:T(8,128)(2,1)S(1)}, bf16[22,88,128]{2,1,0:T(8,128)(2,1)S(1)}, u32[]{:S(2)}, u32[]{:S(2)}) collective-permute-start(bf16[22,88,128]{2,1,0:T(8,128)(2,1)S(1)} %collective-permute-done.2), channel_id=1, source_target_pairs={{0,4},{4,8},{8,12},{12,14},{14,10},{10,6},{6,2},{2,0},{1,5},{5,9},... | collective-permute-start | bytes 1486856 | tf_op jit(solution)/shard_map/ppermute | solution.py:74
  39.2 14.3 %copy-start.15 = (bf16[22,88,128]{2,1,0:T(8,128)(2,1)}, bf16[22,88,128]{2,1,0:T(8,128)(2,1)S(1)}, u32[]{:S(2)}) copy-start(bf16[22,88,128]{2,1,0:T(8,128)(2,1)S(1)} %collective-permute-done.3) | copy-start | bytes 1486852
  39.2 12.8 %collective-permute-start.5 = (bf16[22,88,128]{2,1,0:T(8,128)(2,1)S(1)}, bf16[22,88,128]{2,1,0:T(8,128)(2,1)S(1)}, u32[]{:S(2)}, u32[]{:S(2)}) collective-permute-start(bf16[22,88,128]{2,1,0:T(8,128)(2,1)S(1)} %collective-permute-done.3), channel_id=1, source_target_pairs={{0,2},{4,0},{8,4},{12,8},{14,12},{10,14},{6,10},{2,6},{1,3},{5,1},... | collective-permute-start | bytes 1486856 | tf_op jit(solution)/shard_map/ppermute | solution.py:75
  49.3 0.8 copy-start.7
  50.8 99.6 %collective-permute-start.6 = (bf16[11,88,128]{2,1,0:T(8,128)(2,1)}, bf16[11,88,128]{2,1,0:T(8,128)(2,1)}, u32[]{:S(2)}, u32[]{:S(2)}) collective-permute-start(bf16[11,88,128]{2,1,0:T(8,128)(2,1)} %slice.84), channel_id=1, source_target_pairs={{0,4},{4,8},{8,12},{12,14},{14,10},{10,6},{6,2},{2,0},{1,5},{5,9},... | collective-permute-start | bytes 743432 | tf_op jit(solution)/shard_map/ppermute | solution.py:78
  52.0 0.8 copy-start.8
  53.5 105.9 %collective-permute-start.7 = (bf16[11,88,128]{2,1,0:T(8,128)(2,1)}, bf16[11,88,128]{2,1,0:T(8,128)(2,1)}, u32[]{:S(2)}, u32[]{:S(2)}) collective-permute-start(bf16[11,88,128]{2,1,0:T(8,128)(2,1)} %slice.85), channel_id=1, source_target_pairs={{0,2},{4,0},{8,4},{12,8},{14,12},{10,14},{6,10},{2,6},{1,3},{5,1},... | collective-permute-start | bytes 743432 | tf_op jit(solution)/shard_map/ppermute | solution.py:79
  68.9 99.0 %copy-start.5 = (bf16[22,88,128]{1,0,2:T(8,128)(2,1)}, bf16[22,88,128]{1,0,2:T(8,128)(2,1)S(1)}, u32[]{:S(2)}) copy-start(bf16[22,88,128]{1,0,2:T(8,128)(2,1)S(1)} %copy.80) | copy-start | bytes 1486852
  176.9 3.4 %collective-permute-start.8 = (bf16[22,176,128]{2,1,0:T(8,128)(2,1)S(1)}, bf16[22,176,128]{2,1,0:T(8,128)(2,1)}, u32[]{:S(2)}, u32[]{:S(2)}) collective-permute-start(bf16[22,176,128]{2,1,0:T(8,128)(2,1)S(1)} %bitcast.104), channel_id=1, source_target_pairs={{0,1},{1,0},{2,3},{3,2},{4,5},{5,4},{6,7},{7,6},{8,9},{9,8},{10,11... | collective-permute-start | bytes 2973704 | tf_op jit(solution)/shard_map/ppermute | solution.py:43
  179.8 5.2 %collective-permute-start.9 = (bf16[22,88,128]{2,1,0:T(8,128)(2,1)}, bf16[22,88,128]{2,1,0:T(8,128)(2,1)}, u32[]{:S(2)}, u32[]{:S(2)}) collective-permute-start(bf16[22,88,128]{2,1,0:T(8,128)(2,1)} %get-tuple-element.34), channel_id=1, source_target_pairs={{0,1},{1,0},{2,3},{3,2},{4,5},{5,4},{6,7},{7,6},{8,9},{9,8},{10,11... | collective-permute-start | bytes 1486856 | tf_op jit(solution)/shard_map/ppermute | solution.py:43
  180.3 4.7 %copy-start.20 = (f32[128]{0:T(128)S(1)}, f32[128]{0:T(128)}, u32[]{:S(2)}) copy-start(f32[128]{0:T(128)} %param.18) | copy-start | bytes 1540
  189.4 1.3 copy-start.3
  193.5 2.9 copy-start.6
  212.7 8.0 %collective-permute-start.10 = (bf16[11,88,128]{2,1,0:T(8,128)(2,1)S(1)}, bf16[11,88,128]{2,1,0:T(8,128)(2,1)S(1)}, u32[]{:S(2)}, u32[]{:S(2)}) collective-permute-start(bf16[11,88,128]{2,1,0:T(8,128)(2,1)S(1)} %get-tuple-element.18), channel_id=1, source_target_pairs={{0,4},{4,8},{8,12},{12,14},{14,10},{10,6},{6,2},{2,0},{1,5},{5,9},... | collective-permute-start | bytes 743432 | tf_op jit(solution)/shard_map/ppermute | solution.py:91
  214.0 8.1 %collective-permute-start.14 = (bf16[11,88,128]{2,1,0:T(8,128)(2,1)S(1)}, bf16[11,88,128]{2,1,0:T(8,128)(2,1)S(1)}, u32[]{:S(2)}, u32[]{:S(2)}) collective-permute-start(bf16[11,88,128]{2,1,0:T(8,128)(2,1)S(1)} %get-tuple-element.19), channel_id=1, source_target_pairs={{0,2},{4,0},{8,4},{12,8},{14,12},{10,14},{6,10},{2,6},{1,3},{5,1},... | collective-permute-start | bytes 743432 | tf_op jit(solution)/shard_map/ppermute | solution.py:92
  220.9 12.4 %collective-permute-start.11 = (bf16[22,88,128]{2,1,0:T(8,128)(2,1)S(1)}, bf16[22,88,128]{2,1,0:T(8,128)(2,1)S(1)}, u32[]{:S(2)}, u32[]{:S(2)}) collective-permute-start(bf16[22,88,128]{2,1,0:T(8,128)(2,1)S(1)} %pad_maximum_fusion.1), channel_id=1, source_target_pairs={{0,4},{4,8},{8,12},{12,14},{14,10},{10,6},{6,2},{2,0},{1,5},{5,9},... | collective-permute-start | bytes 1486856 | tf_op jit(solution)/shard_map/ppermute | solution.py:101
  222.3 13.5 %collective-permute-start.15 = (bf16[22,88,128]{2,1,0:T(8,128)(2,1)S(1)}, bf16[22,88,128]{2,1,0:T(8,128)(2,1)S(1)}, u32[]{:S(2)}, u32[]{:S(2)}) collective-permute-start(bf16[22,88,128]{2,1,0:T(8,128)(2,1)S(1)} %pad_maximum_fusion.2), channel_id=1, source_target_pairs={{0,2},{4,0},{8,4},{12,8},{14,12},{10,14},{6,10},{2,6},{1,3},{5,1},... | collective-permute-start | bytes 1486856 | tf_op jit(solution)/shard_map/ppermute | solution.py:102
  234.5 11.5 %collective-permute-start.12 = (bf16[22,88,128]{2,1,0:T(8,128)(2,1)S(1)}, bf16[22,88,128]{2,1,0:T(8,128)(2,1)S(1)}, u32[]{:S(2)}, u32[]{:S(2)}) collective-permute-start(bf16[22,88,128]{2,1,0:T(8,128)(2,1)S(1)} %fusion.47), channel_id=1, source_target_pairs={{0,4},{4,8},{8,12},{12,14},{14,10},{10,6},{6,2},{2,0},{1,5},{5,9},... | collective-permute-start | bytes 1486856 | tf_op jit(solution)/shard_map/ppermute | solution.py:101
  248.4 10.9 %collective-permute-start.16 = (bf16[22,88,128]{2,1,0:T(8,128)(2,1)}, bf16[22,88,128]{2,1,0:T(8,128)(2,1)}, u32[]{:S(2)}, u32[]{:S(2)}) collective-permute-start(bf16[22,88,128]{2,1,0:T(8,128)(2,1)} %get-tuple-element.10), channel_id=1, source_target_pairs={{0,2},{4,0},{8,4},{12,8},{14,12},{10,14},{6,10},{2,6},{1,3},{5,1},... | collective-permute-start | bytes 1486856 | tf_op jit(solution)/shard_map/ppermute | solution.py:102
  255.4 6.4 %copy-start.22 = (f32[128]{0:T(128)S(1)}, f32[128]{0:T(128)}, u32[]{:S(2)}) copy-start(f32[128]{0:T(128)} %param.19) | copy-start | bytes 1540
  257.2 6.2 %copy-start.4 = (f32[22,176,128]{2,1,0:T(8,128)S(1)}, f32[22,176,128]{2,1,0:T(8,128)}, u32[]{:S(2)}) copy-start(f32[22,176,128]{2,1,0:T(8,128)} %copy-done.3) | copy-start | bytes 5947396
  257.2 6.2 %copy-start.9 = (f32[22,88,128]{2,1,0:T(8,128)S(1)}, f32[22,88,128]{2,1,0:T(8,128)}, u32[]{:S(2)}) copy-start(f32[22,88,128]{2,1,0:T(8,128)} %get-tuple-element.35) | copy-start | bytes 2973700
  257.3 10.5 %collective-permute-start.13 = (bf16[22,88,128]{2,1,0:T(8,128)(2,1)}, bf16[22,88,128]{2,1,0:T(8,128)(2,1)S(1)}, u32[]{:S(2)}, u32[]{:S(2)}) collective-permute-start(bf16[22,88,128]{2,1,0:T(8,128)(2,1)} %get-tuple-element.9), channel_id=1, source_target_pairs={{0,4},{4,8},{8,12},{12,14},{14,10},{10,6},{6,2},{2,0},{1,5},{5,9},... | collective-permute-start | bytes 1486856 | tf_op jit(solution)/shard_map/ppermute | solution.py:101
  260.6 9.7 %collective-permute-start.17 = (bf16[22,88,128]{2,1,0:T(8,128)(2,1)S(1)}, bf16[22,88,128]{2,1,0:T(8,128)(2,1)S(1)}, u32[]{:S(2)}, u32[]{:S(2)}) collective-permute-start(bf16[22,88,128]{2,1,0:T(8,128)(2,1)S(1)} %fusion.46), channel_id=1, source_target_pairs={{0,2},{4,0},{8,4},{12,8},{14,12},{10,14},{6,10},{2,6},{1,3},{5,1},... | collective-permute-start | bytes 1486856 | tf_op jit(solution)/shard_map/ppermute | solution.py:102
  263.4 11.2 %copy-start.16 = (bf16[128,128]{1,0:T(8,128)(2,1)}, bf16[128,128]{1,0:T(8,128)(2,1)S(1)}, u32[]{:S(2)}) copy-start(bf16[128,128]{1,0:T(8,128)(2,1)S(1)} %fusion.13) | copy-start | bytes 98308
  263.5 6.8 %copy-start.1 = (f32[22,88,256]{2,1,0:T(8,128)S(1)}, f32[22,88,256]{2,1,0:T(8,128)}, u32[]{:S(2)}) copy-start(f32[22,88,256]{2,1,0:T(8,128)} %fusion.63) | copy-start | bytes 5947396
  273.6 1.6 slice-start
  273.6 1.6 slice-start.1
  274.5 1.4 copy-start.11
  274.5 4.9 %collective-permute-start.22 = (bf16[128,256]{1,0:T(8,128)(2,1)S(1)}, bf16[128,256]{1,0:T(8,128)(2,1)S(1)}, u32[]{:S(2)}, u32[]{:S(2)}) collective-permute-start(bf16[128,256]{1,0:T(8,128)(2,1)S(1)} %fusion.12), channel_id=1, source_target_pairs={{0,1},{1,0},{2,3},{3,2},{4,5},{5,4},{6,7},{7,6},{8,9},{9,8},{10,11... | collective-permute-start | bytes 196616 | tf_op jit(solution)/shard_map/ppermute | solution.py:43
  274.7 6.1 %collective-permute-start.18 = (bf16[128,512]{1,0:T(8,128)(2,1)S(1)}, bf16[128,512]{1,0:T(8,128)(2,1)S(1)}, u32[]{:S(2)}, u32[]{:S(2)}) collective-permute-start(bf16[128,512]{1,0:T(8,128)(2,1)S(1)} %pad_maximum_fusion.4), channel_id=1, source_target_pairs={{0,1},{1,0},{2,3},{3,2},{4,5},{5,4},{6,7},{7,6},{8,9},{9,8},{10,11... | collective-permute-start | bytes 393224 | tf_op jit(solution)/shard_map/ppermute | solution.py:43
  276.4 4.3 %copy-start.17 = (bf16[128,128]{1,0:T(8,128)(2,1)S(1)}, bf16[128,128]{1,0:T(8,128)(2,1)}, u32[]{:S(2)}) copy-start(bf16[128,128]{1,0:T(8,128)(2,1)} %copy-done.16) | copy-start | bytes 98308
  279.5 5.0 %collective-permute-start.23 = (bf16[128,256]{1,0:T(8,128)(2,1)S(1)}, bf16[128,256]{1,0:T(8,128)(2,1)S(1)}, u32[]{:S(2)}, u32[]{:S(2)}) collective-permute-start(bf16[128,256]{1,0:T(8,128)(2,1)S(1)} %add_convert_fusion.9), channel_id=1, source_target_pairs={{0,2},{2,0},{4,6},{6,4},{8,10},{10,8},{12,14},{14,12},{1,3},{3,1},... | collective-permute-start | bytes 196616 | tf_op jit(solution)/shard_map/ppermute | solution.py:53
  280.8 5.9 %collective-permute-start.19 = (bf16[128,512]{1,0:T(8,128)(2,1)S(1)}, bf16[128,512]{1,0:T(8,128)(2,1)S(1)}, u32[]{:S(2)}, u32[]{:S(2)}) collective-permute-start(bf16[128,512]{1,0:T(8,128)(2,1)S(1)} %add_convert_fusion.5), channel_id=1, source_target_pairs={{0,2},{2,0},{4,6},{6,4},{8,10},{10,8},{12,14},{14,12},{1,3},{3,1},... | collective-permute-start | bytes 393224 | tf_op jit(solution)/shard_map/ppermute | solution.py:53
  284.5 4.4 %collective-permute-start.24 = (bf16[128,256]{1,0:T(8,128)(2,1)S(1)}, bf16[128,256]{1,0:T(8,128)(2,1)S(1)}, u32[]{:S(2)}, u32[]{:S(2)}) collective-permute-start(bf16[128,256]{1,0:T(8,128)(2,1)S(1)} %add_convert_fusion.8), channel_id=1, source_target_pairs={{0,4},{2,6},{4,0},{6,2},{8,12},{10,14},{12,8},{14,10},{1,5},{3,7},... | collective-permute-start | bytes 196616 | tf_op jit(solution)/shard_map/ppermute | solution.py:53
  286.7 5.7 %collective-permute-start.20 = (bf16[128,512]{1,0:T(8,128)(2,1)S(1)}, bf16[128,512]{1,0:T(8,128)(2,1)S(1)}, u32[]{:S(2)}, u32[]{:S(2)}) collective-permute-start(bf16[128,512]{1,0:T(8,128)(2,1)S(1)} %add_convert_fusion.4), channel_id=1, source_target_pairs={{0,4},{2,6},{4,0},{6,2},{8,12},{10,14},{12,8},{14,10},{1,5},{3,7},... | collective-permute-start | bytes 393224 | tf_op jit(solution)/shard_map/ppermute | solution.py:53
  288.9 7.8 %collective-permute-start.25 = (bf16[128,256]{1,0:T(8,128)(2,1)S(1)}, bf16[128,256]{1,0:T(8,128)(2,1)S(1)}, u32[]{:S(2)}, u32[]{:S(2)}) collective-permute-start(bf16[128,256]{1,0:T(8,128)(2,1)S(1)} %add_convert_fusion.7), channel_id=1, source_target_pairs={{0,8},{2,10},{4,12},{6,14},{8,0},{10,2},{12,4},{14,6},{1,9},{3,11}... | collective-permute-start | bytes 196616 | tf_op jit(solution)/shard_map/ppermute | solution.py:53
  292.4 8.0 %collective-permute-start.21 = (bf16[128,512]{1,0:T(8,128)(2,1)S(1)}, bf16[128,512]{1,0:T(8,128)(2,1)S(1)}, u32[]{:S(2)}, u32[]{:S(2)}) collective-permute-start(bf16[128,512]{1,0:T(8,128)(2,1)S(1)} %add_convert_fusion.3), channel_id=1, source_target_pairs={{0,8},{2,10},{4,12},{6,14},{8,0},{10,2},{12,4},{14,6},{1,9},{3,11}... | collective-permute-start | bytes 393224 | tf_op jit(solution)/shard_map/ppermute | solution.py:53

commit v2 on v1

v2 whole, which is shorter than its diff:
```python
import functools

import jax
import jax.numpy as jnp
from jax import lax
from jax.experimental import pallas as pl
from jax.experimental.pallas import tpu as pltpu
from jax.sharding import PartitionSpec as P

eps = 1e-05
f32 = jnp.float32
bf16 = jnp.bfloat16
VMEM = pl.BlockSpec(memory_space=pltpu.VMEM)
LIMIT = 48 * 1024 * 1024


def layer_norm_forward(values, norm_gain, shift_bias):
    average_value = jnp.mean(values, axis=-1, keepdims=True)
    centered_input = values - average_value
    inverse_deviation = lax.rsqrt(
        jnp.mean(centered_input * centered_input, axis=-1, keepdims=True) + eps
    )
    standardized_input = centered_input * inverse_deviation
    return (standardized_input * norm_gain + shift_bias, standardized_input, inverse_deviation)


def layer_norm_backward(output_gradient, standardized_input, inverse_deviation, norm_gain):
    scaled_output = output_gradient * norm_gain
    first_operand = jnp.mean(scaled_output, axis=-1, keepdims=True)
    second_operand = jnp.mean(scaled_output * standardized_input, axis=-1, keepdims=True)
    return inverse_deviation * (scaled_output - first_operand - standardized_input * second_operand)


def present_rows(positions, chain_lengths, slot_size):
    chain_ids = positions // slot_size
    offsets = positions - chain_ids * slot_size
    slots = jnp.arange(chain_lengths.shape[0], dtype=jnp.int32)
    lengths = jnp.sum(
        jnp.where(chain_ids[:, None] == slots[None, :], chain_lengths[None, :], 0), axis=1
    )
    return (offsets < lengths).astype(f32)


def ring_order(row_count):
    if row_count == 8:
        return [0, 2, 4, 6, 7, 5, 3, 1]
    return list(range(row_count))


def swap_col(x):
    return lax.ppermute(x, "col", [(0, 1), (1, 0)])


def sum_all(x, row_count):
    def add(a, b):
        return (a.astype(f32) + b.astype(f32)).astype(bf16)

    x = add(x, swap_col(x))
    step = 1
    while step < row_count:
        x = add(x, lax.ppermute(x, "row", [(r, r ^ step) for r in range(row_count)]))
        step *= 2
    return x


def cost(microseconds):
    return pl.CostEstimate(
        flops=int(microseconds * 1.1e9), bytes_accessed=1 << 20, transcendentals=0
    )


def params():
    return pltpu.CompilerParams(vmem_limit_bytes=LIMIT)


def triangle_kernel(count, left_ref, *refs):
    rights, out_ref, wide, rows = refs[:count], refs[count], refs[count + 1], refs[count + 2]
    here, short = left_ref.shape[0], rights[0].shape[0]
    rows[...] = jnp.zeros_like(rows)
    for half in range(count):
        wide[...] = rights[half][...].astype(f32)

        def body(i, carry, half=half):
            left = left_ref[i]
            for j in range(short):
                rows[pl.ds(j, 1), :] = jnp.sum(left * wide[j], axis=0, keepdims=True)
            out_ref[half, i] = rows[...].astype(bf16)
            return carry

        lax.fori_loop(0, here, body, 0)


def triangle(left, rights, padded):
    count, here = len(rights), left.shape[0]
    return pl.pallas_call(
        functools.partial(triangle_kernel, count),
        out_shape=jax.ShapeDtypeStruct((count, here, padded, left.shape[2]), bf16),
        in_specs=[VMEM] * (count + 1),
        out_specs=VMEM,
        scratch_shapes=[
            pltpu.VMEM(rights[0].shape, f32),
            pltpu.VMEM((padded, left.shape[2]), f32),
        ],
        compiler_params=params(),
        cost_estimate=cost(1.0 * count),
        name="triangle",
    )(left, *rights)


def triangle_gradient_kernel(where, mine, other, grads, w_out, gain, out_ref):
    here, padded, hidden = mine.shape[1:]
    flat = (here * padded, hidden)
    total = (mine[0].astype(f32) + other[0].astype(f32)).reshape(flat)
    average = jnp.mean(total, axis=-1, keepdims=True)
    centered = total - average
    inverse = lax.rsqrt(jnp.mean(centered * centered, axis=-1, keepdims=True) + eps)
    standard = centered * inverse
    grad_norm = lax.dot_general(
        grads[0].reshape(flat), w_out[...], (((1,), (1,)), ((), ())), preferred_element_type=f32
    )
    result = layer_norm_backward(grad_norm, standard, inverse, gain[...])
    out_ref[0] = result.astype(bf16).reshape(here, padded, hidden)


def triangle_gradient(where, mine, other, grads, w_out, gain):
    count, here, padded, hidden = mine.shape
    block = (1, here, padded, hidden)
    return pl.pallas_call(
        triangle_gradient_kernel,
        out_shape=jax.ShapeDtypeStruct(mine.shape, bf16),
        grid_spec=pltpu.PrefetchScalarGridSpec(
            num_scalar_prefetch=1,
            grid=(count,),
            in_specs=[
                pl.BlockSpec(block, lambda s, at: (s, 0, 0, 0)),
                pl.BlockSpec(block, lambda s, at: (s, 0, 0, 0)),
                pl.BlockSpec(block, lambda s, at: (at[s], 0, 0, 0)),
                pl.BlockSpec(w_out.shape, lambda s, at: (0, 0)),
                pl.BlockSpec(gain.shape, lambda s, at: (0, 0)),
            ],
            out_specs=pl.BlockSpec(block, lambda s, at: (s, 0, 0, 0)),
        ),
        compiler_params=params(),
        cost_estimate=cost(0.8 * count),
        name="triangle_gradient",
    )(where, mine, other, grads, w_out, gain)


def hop_kernel(count, carried, left_ref, *refs):
    grads, refs = refs[:count], refs[count:]
    arrived, refs = refs[: count * carried], refs[count * carried :]
    outs, wide = refs[:count], refs[count]
    here, short = left_ref.shape[0], outs[0].shape[0]
    for half in range(count):
        wide[...] = grads[half][0].astype(f32)

        def body(j, carry, half=half):
            if carried:
                total = arrived[half][j].astype(f32)
                for more in range(1, carried):
                    total += arrived[half + more * count][j].astype(f32)
            else:
                total = jnp.zeros(left_ref.shape[1:], f32)
            for i in range(here):
                total += wide[i, pl.ds(j, 1), :] * left_ref[i]
            outs[half][j] = total.astype(outs[half].dtype)
            return carry

        lax.fori_loop(0, short, body, 0)


def hop(left, grads, picks, arrived, short, dtype=bf16):
    here, half, hidden = left.shape
    count = len(grads)
    carried = len(arrived) // count
    whole = pl.BlockSpec(left.shape, lambda s: (0, 0, 0))
    part = pl.BlockSpec((short, half, hidden), lambda s: (0, 0, 0))

    def picked(g, pick):
        return pl.BlockSpec((1,) + g.shape[1:], lambda s: (pick, 0, 0, 0))

    return pl.pallas_call(
        functools.partial(hop_kernel, count, carried),
        grid=(1,),
        out_shape=[jax.ShapeDtypeStruct((short, half, hidden), dtype)] * count,
        in_specs=[whole]
        + [picked(g, pick) for g, pick in zip(grads, picks)]
        + [part] * len(arrived),
        out_specs=[part] * count,
        scratch_shapes=[pltpu.VMEM(grads[0].shape[1:], f32)],
        compiler_params=params(),
        cost_estimate=cost(1.0 * count),
        name="scatter_hop",
    )(left, *grads, *arrived)


def left_kernel(count, carried, grads, *refs):
    rights, refs = refs[:count], refs[count:]
    before, (out_ref, wide_right, wide_grad) = refs[:carried], refs[carried:]
    short = rights[0].shape[0]
    for half in range(count):
        wide_right[half] = rights[half][...].astype(f32)
        wide_grad[half] = grads[half].astype(f32)

    def rows(i, carry):
        def add(s, total):
            for j in range(short):
                total += wide_grad[s, i, pl.ds(j, 1), :] * wide_right[s, j]
            return total

        start = before[0][i] if carried else jnp.zeros(out_ref.shape[1:], f32)
        out_ref[i] = lax.fori_loop(0, count, add, start)
        return carry

    lax.fori_loop(0, out_ref.shape[0], rows, 0)


def left_gradient(grads, rights, before):
    count, here = grads.shape[:2]
    short, half, hidden = rights[0].shape
    return pl.pallas_call(
        functools.partial(left_kernel, count, len(before)),
        out_shape=jax.ShapeDtypeStruct((here, half, hidden), f32),
        in_specs=[VMEM] * (1 + count + len(before)),
        out_specs=VMEM,
        scratch_shapes=[
            pltpu.VMEM((count, short, half, hidden), f32),
            pltpu.VMEM(grads.shape, f32),
        ],
        compiler_params=params(),
        cost_estimate=cost(0.8 * count),
        name="left_gradient",
    )(grads, *rights, *before)


def shards(
    pair,
    cotangent,
    chain_lengths,
    input_norm_gain,
    input_norm_bias,
    w_in,
    output_norm_gain,
    output_norm_bias,
    w_out,
):
    rows_here = pair.shape[0]
    half = pair.shape[1]
    channels = pair.shape[2]
    hidden = w_out.shape[0]
    row_count = lax.axis_size("row")
    residues = rows_here * row_count
    slot_size = residues // chain_lengths.shape[0]
    order = ring_order(row_count)
    inverse = [order.index(r) for r in range(row_count)]
    place = jnp.asarray(inverse, jnp.int32)[lax.axis_index("row")]
    ring = jnp.asarray(order, jnp.int32)
    col = lax.axis_index("col")
    short = rows_here // 2
    padded = (short + 15) // 16 * 16
    forward = [(order[p], order[(p + 1) % row_count]) for p in range(row_count)]
    backward = [(order[p], order[(p - 1) % row_count]) for p in range(row_count)]

    def ahead(x):
        return lax.ppermute(x, "row", forward)

    def behind(x):
        return lax.ppermute(x, "row", backward)

    def dot(a, b, ca, cb):
        return lax.dot_general(a, b, (((ca,), (cb,)), ((), ())), preferred_element_type=f32)

    def shaped(x):
        return x.reshape(rows_here, half, -1)

    row_ids = lax.axis_index("row") * rows_here + jnp.arange(rows_here, dtype=jnp.int32)
    col_ids = col * half + jnp.arange(half, dtype=jnp.int32)
    pair_mask = (
        present_rows(row_ids, chain_lengths, slot_size)[:, None, None]
        * present_rows(col_ids, chain_lengths, slot_size)[None, :, None]
    )
    w_left, w_right = w_in[:, : 2 * hidden], w_in[:, 2 * hidden : 4 * hidden]
    w_gate = w_in[:, 4 * hidden :]
    normalized_float32, standardized_pair, input_inverse_deviation = layer_norm_forward(
        pair.astype(f32), input_norm_gain, input_norm_bias
    )
    normed_flat = normalized_float32.astype(bf16).reshape(rows_here * half, channels)
    proj_right = shaped(dot(normed_flat, w_right, 1, 0))
    sig_right = jax.nn.sigmoid(proj_right[..., :hidden])
    val_right = proj_right[..., hidden:]
    right_proj = (pair_mask * sig_right * val_right).astype(bf16)

    own = [right_proj[:short], right_proj[short:]]
    hops = row_count // 2
    chain1, chain2 = [], []
    a, b, c, d = own[0], own[1], own[1], own[0]
    for step in range(hops):
        a, b = ahead(a), behind(b)
        chain1 += [a, b]
        if step < hops - 1:
            c, d = ahead(c), behind(d)
            chain2 += [c, d]

    def half_index(offset, letter):
        return ring[(place + offset + row_count) % row_count] * 2 + letter

    early_hops = hops // 2
    groups = [own + chain1[: 2 * early_hops], chain1[2 * early_hops :], chain2]
    index1 = [half_index(sign * s, x) for s in range(1, hops + 1) for sign, x in ((-1, 0), (1, 1))]
    index2 = [half_index(sign * s, x) for s in range(1, hops) for sign, x in ((-1, 1), (1, 0))]
    indices = [
        [half_index(0, 0), half_index(0, 1)] + index1[: 2 * early_hops],
        index1[2 * early_hops :],
        index2,
    ]

    proj_left = shaped(dot(normed_flat, w_left, 1, 0))
    sig_left = jax.nn.sigmoid(proj_left[..., :hidden])
    val_left = proj_left[..., hidden:]
    left_proj = (pair_mask * sig_left * val_left).astype(bf16).astype(f32)
    gate = jax.nn.sigmoid(shaped(dot(normed_flat, w_gate, 1, 0)))
    grad_up = cotangent.astype(f32)
    grad_proj_out = (grad_up * gate).astype(bf16)
    grad_flat = grad_proj_out.reshape(rows_here * half, channels)

    mine_out = jnp.pad(
        grad_proj_out.reshape(rows_here, row_count, short, channels).transpose(1, 0, 2, 3),
        ((0, 0), (0, 0), (0, padded - short), (0, 0)),
    )
    out_halves = jnp.concatenate([mine_out, swap_col(mine_out)], axis=0)
    gain = output_norm_gain.reshape(1, hidden)

    def local_index(i):
        return (i // row_count) ^ col, i % row_count

    sums, others, grads = [], [], []
    for rights, index in zip(groups, indices):
        partial = triangle(left_proj, rights, padded)
        other = swap_col(partial)
        at = jnp.stack([x * row_count + y for x, y in map(local_index, index)]).astype(jnp.int32)
        sums.append(partial)
        others.append(other)
        grads.append(triangle_gradient(at, partial, other, out_halves, w_out, gain))

    def group1(s):
        at = 2 * (s - 1)
        if s <= early_hops:
            return [grads[0], grads[0]], [at + 2, at + 3]
        at -= 2 * early_hops
        return [grads[1], grads[1]], [at, at + 1]

    arrived1, arrived2 = [], []
    for s in range(hops, 0, -1):
        g, picks = group1(s)
        x, y = hop(left_proj, g, picks, arrived1, short)
        arrived1 = [behind(x), ahead(y)]
    for s in range(hops - 1, 0, -1):
        x, y = hop(left_proj, [grads[2]] * 2, [2 * s - 2, 2 * s - 1], arrived2, short)
        arrived2 = [behind(x), ahead(y)]
    arrived2 = [arrived2[1], arrived2[0]]

    tri_halves = jnp.concatenate(sums, axis=0).astype(f32) + jnp.concatenate(
        others, axis=0
    ).astype(f32)
    flat_index = jnp.stack(sum(indices, []))
    wanted = col * row_count + jnp.arange(row_count, dtype=jnp.int32)
    slot = jnp.argmax(flat_index[None, :] == wanted[:, None], axis=1)
    triangle_product = (
        tri_halves[slot][:, :, :short].transpose(1, 0, 2, 3).reshape(rows_here, half, hidden)
    )
    triangle_output, _, _ = layer_norm_forward(
        triangle_product, output_norm_gain, output_norm_bias
    )
    tri_flat = triangle_output.astype(bf16).reshape(rows_here * half, hidden)
    projected = shaped(dot(tri_flat, w_out, 1, 0))
    update = (gate * projected).astype(bf16)
    grad_gate = (grad_up * projected * gate * (1.0 - gate)).astype(bf16)
    local_w_out = dot(tri_flat, grad_flat, 0, 0)

    before = []
    for g, rights in zip(grads, groups):
        before = [left_gradient(g, rights, before)]
    grad_left = before[0]
    early = jnp.concatenate(
        [
            grad_left * pair_mask * val_left * sig_left * (1.0 - sig_left),
            grad_left * pair_mask * sig_left,
        ],
        axis=-1,
    ).astype(bf16)
    early_flat = jnp.concatenate([early, grad_gate], axis=-1).reshape(rows_here * half, -1)
    w_early = jnp.concatenate([w_left, w_gate], axis=1)
    local_early = dot(normed_flat, early_flat, 0, 0)
    summed_early = sum_all(
        jnp.concatenate([local_early, local_w_out], axis=1).astype(bf16), row_count
    ).astype(f32)
    gradient_early = dot(early_flat, w_early, 1, 1)

    x, y = hop(left_proj, [grads[0]] * 2, [0, 1], arrived1 + arrived2, short, f32)
    grad_right = jnp.concatenate([x, y], axis=0)
    late_flat = (
        jnp.concatenate(
            [
                grad_right * pair_mask * val_right * sig_right * (1.0 - sig_right),
                grad_right * pair_mask * sig_right,
            ],
            axis=-1,
        )
        .astype(bf16)
        .reshape(rows_here * half, -1)
    )
    summed_late = sum_all(dot(normed_flat, late_flat, 0, 0).astype(bf16), row_count).astype(f32)
    normalized_gradient = shaped(gradient_early + dot(late_flat, w_right, 1, 1))
    pair_gradient = layer_norm_backward(
        normalized_gradient, standardized_pair, input_inverse_deviation, input_norm_gain
    ).astype(bf16)
    grad_w_in = jnp.concatenate(
        [summed_early[:, : 2 * hidden], summed_late, summed_early[:, 2 * hidden : 3 * hidden]],
        axis=1,
    )
    grad_w_out = summed_early[:, 3 * hidden :]
    return (update, pair_gradient, grad_w_in, grad_w_out)


def solution(mesh):
    placed = (
        P(("grp", "row"), "col", None),
        P(("grp", "row"), "col", None),
        P("grp"),
        P(),
        P(),
        P(),
        P(),
        P(),
        P(),
    )
    return jax.shard_map(
        shards,
        mesh=mesh,
        in_specs=placed,
        out_specs=(
            P(("grp", "row"), "col", None),
            P(("grp", "row"), "col", None),
            P("grp", None),
            P("grp", None),
        ),
        check_vma=False,
    )
```

time: 305 us -> 202 us (0.66)
  local copies, waits for them, and re-layouts: 126 us -> 28 us
  Pallas kernels: 0 us -> 60.1 us
  waiting for transfers between devices: 75.5 us -> 25 us
  matrix products: 36.7 us -> 11.4 us
  starting transfers between devices: 27.2 us -> 38.8 us
    dynamic_update_slice x9 -> x0, local copies, waits for them, and re-layouts: 77.8 us -> none  [put(): return lax.dynamic_update_slice_in_dim(whole, part, start, 0)]
    pallas_call x0 -> x17, Pallas kernels: none -> 60.1 us  [the longest x3 22.6 us: triangle(): pl.pallas_call(functools.partial(triangle_kernel, count), out_shape=jax.S...]
    ppermute x16 -> x28, waiting for transfers between devices: 62.9 us -> 11.3 us  [the longest x14 6.56 us: ahead(): return lax.ppermute(x, 'row', forward)]
    dot_general x3 -> x0, matrix products: 18.5 us -> none  [the longest x1 6.91 us: shards(): jnp.einsum('ikh,jkh->ijh', left_proj, right_all, preferred_element_type=f32)]
    ppermute x8 -> x0, local copies, waits for them, and re-layouts: 17.9 us -> none  [the longest x3 6.8 us: ring_gather(): ahead = lax.ppermute(ahead, 'row', forward)]
    dot_general x3 -> x0, local copies, waits for them, and re-layouts: 13.1 us -> none  [the longest x1 9.13 us: shards(): jnp.einsum('ijh,ikh->jkh', triangle_gradient, left_proj, preferred_elemen...]
    ppermute x16 -> x28, starting transfers between devices: 17.9 us -> 30.1 us  [the longest x14 23.8 us: behind(): return lax.ppermute(x, 'row', backward)]
    convert_element_type x4 -> x1, local copies, waits for them, and re-layouts: 6.99 us -> 0.08 us  [shards(): grad_proj_out = (grad_up * gate).astype(bf16)]
  transfers between devices with their start and end apart: 26 -> 40, of which waited for: 15 -> 12; matrix products, arithmetic and copies ran while one was open for 41% -> 5% of each run, Pallas kernels for 0% -> 27%
where the time goes in v2:
time: 202 us; the launch traced here: 201 us
  Pallas kernels  60.1 us (30%)
  starting transfers between devices  38.8 us (19%)
  local copies, waits for them, and re-layouts  28 us (14%)
  waiting for transfers between devices  25 us (12%)
  other arithmetic  24 us (12%)
  between operations  13.5 us (7%)
  matrix products  11.4 us (6%)
    ppermute x14, starting transfers between devices, behind(): return lax.ppermute(x, 'row', backward)  23.8 us
    pallas_call x3, Pallas kernels, triangle(): pl.pallas_call(functools.partial(triangle_kernel, count), out_shape=jax.S...  22.6 us
    pallas_call x3, Pallas kernels, left_gradient(): pl.pallas_call(functools.partial(left_kernel, count, len(before)), out_sh...  15.8 us
    pallas_call x8, Pallas kernels, hop(): pl.pallas_call(functools.partial(hop_kernel, count, carried), grid=(1,),...  14.7 us
    ppermute x6, waiting for transfers between devices, sum_all(): lax.ppermute(x, 'row', [(r, r ^ step) for r in range(row_count)])  13.1 us
    dot_general x9, matrix products, dot(): lax.dot_general(a, b, (((ca,), (cb,)), ((), ())), preferred_element_type=...  11.4 us
    ppermute x6, starting transfers between devices, sum_all(): lax.ppermute(x, 'row', [(r, r ^ step) for r in range(row_count)])  7.15 us
    pallas_call x3, Pallas kernels, triangle_gradient(): pl.pallas_call(triangle_gradient_kernel, out_shape=jax.ShapeDtypeStruct(m...  7.03 us
  transfers between devices with their start and end apart: 40, of which 12 were waited for; matrix products, arithmetic and copies ran while one was open for 5% of the time, Pallas kernels for 27%

profile of v2, /device:TPU:0, one launch (start us, length us, event | category | flops | bytes accessed | tf_op | source)
XLA Modules:
  0.0 200.6 jit_solution(1980908508850390484)
XLA Ops:
  0.6 1.3 convert_reduce_fusion
  2.0 1.8 fusion.21
  3.9 1.8 fusion.50
  5.7 2.0 fusion.48
  8.1 2.1 %multiply_convert_fusion.5 = (bf16[22,88,128]{2,1,0:T(8,128)(2,1)S(1)}, f32[22,88,128]{2,1,0:T(8,128)S(1)}) fusion(f32[22,88,256]{2,1,0:T(8,128)} %fusion.48, f32[22,88]{1,0:T(8,128)S(1)} %broadcast_multiply_fusion.1, f32[22,88,256]{2,1,0:T(8,128)S(1)} %fusion.50), kind=kLoop, calls=%fused_computation.63 | loop fusion | flops 3221504 | bytes 5459520 | tf_op jit(solution)/shard_map/convert_element_type | solution.py:291
  10.3 3.0 %collective-permute-start.9 = (bf16[11,88,128]{2,1,0:T(8,128)(2,1)S(1)}, bf16[11,88,128]{2,1,0:T(8,128)(2,1)S(1)}, u32[]{:S(2)}, u32[]{:S(2)}) collective-permute-start(bf16[11,88,128]{2,1,0:T(8,128)(2,1)S(1)} %get-tuple-element.45.refs_0_), channel_id=1, source_target_pairs={{0,2},{4,0},{8,4},{12,8},{14,12},{10,14},{6,10},{2,6},{1,3},{5,1},... | collective-permute-start | bytes 743432 | tf_op jit(solution)/shard_map/ppermute | solution.py:268
  13.4 2.0 collective-permute-start.8
  15.4 4.7 %collective-permute-done.9.refs_1_ = bf16[11,88,128]{2,1,0:T(8,128)(2,1)S(1)} collective-permute-done((bf16[11,88,128]{2,1,0:T(8,128)(2,1)S(1)}, bf16[11,88,128]{2,1,0:T(8,128)(2,1)S(1)}, u32[]{:S(2)}, u32[]{:S(2)}) %collective-permute-start.9) | collective-permute-done | bytes 247840 | tf_op jit(solution)/shard_map/ppermute | solution.py:268
  20.2 2.0 collective-permute-start.11
  22.3 5.2 %collective-permute-done.8.refs_0_ = bf16[11,88,128]{2,1,0:T(8,128)(2,1)S(1)} collective-permute-done((bf16[11,88,128]{2,1,0:T(8,128)(2,1)S(1)}, bf16[11,88,128]{2,1,0:T(8,128)(2,1)S(1)}, u32[]{:S(2)}, u32[]{:S(2)}) %collective-permute-start.8) | collective-permute-done | bytes 247840 | tf_op jit(solution)/shard_map/ppermute | solution.py:265
  27.6 1.9 collective-permute-start.3
  43.4 1.6 collective-permute-start.13
  45.6 1.9 collective-permute-start.5
  48.4 9.1 %triangle.3.mine = bf16[6,22,16,128]{3,2,1,0:T(8,128)(2,1)S(1)} custom-call(f32[22,88,128]{2,1,0:T(8,128)S(1)} %get-tuple-element.52.left_ref, bf16[11,88,128]{2,1,0:T(8,128)(2,1)S(1)} %get-tuple-element.45.refs_0_, bf16[11,88,128]{2,1,0:T(8,128)(2,1)S(1)} %get-tuple-element.46.refs_1_, bf16[11,88,128]{2,1,0:T(8,128)(2,1)S(1)} %collective-permute-done.refs_2_, ...), custom_call_target="tpu_custom_call" | custom-call | flops 6600000000 | bytes 1048576 | tf_op jit(solution)/shard_map/triangle/pallas_call | solution.py:95
  58.5 1.9 collective-permute-start.7
  61.5 8.1 %triangle.5.mine = bf16[6,22,16,128]{3,2,1,0:T(8,128)(2,1)S(1)} custom-call(f32[22,88,128]{2,1,0:T(8,128)S(1)} %get-tuple-element.52.left_ref, bf16[11,88,128]{2,1,0:T(8,128)(2,1)S(1)} %collective-permute-done.8.refs_0_, bf16[11,88,128]{2,1,0:T(8,128)(2,1)S(1)} %collective-permute-done.9.refs_1_, bf16[11,88,128]{2,1,0:T(8,128)(2,1)S(1)} %copy-done.16, ...), custom_call_target="tpu_custom_call" | custom-call | flops 6600000000 | bytes 1048576 | tf_op jit(solution)/shard_map/triangle/pallas_call | solution.py:95
  69.7 5.4 %triangle.4.mine = bf16[4,22,16,128]{3,2,1,0:T(8,128)(2,1)S(1)} custom-call(f32[22,88,128]{2,1,0:T(8,128)S(1)} %get-tuple-element.52.left_ref, bf16[11,88,128]{2,1,0:T(8,128)(2,1)S(1)} %collective-permute-done.4.refs_0_, bf16[11,88,128]{2,1,0:T(8,128)(2,1)S(1)} %collective-permute-done.5.refs_1_, bf16[11,88,128]{2,1,0:T(8,128)(2,1)S(1)} %collective-permute-done.6.refs_2_, ...), custom_call_target="tpu_custom_call" | custom-call | flops 4400000000 | bytes 1048576 | tf_op jit(solution)/shard_map/triangle/pallas_call | solution.py:95
  76.9 2.1 %convert_add_fusion = f32[16,22,16,128]{3,2,1,0:T(8,128)} fusion(bf16[6,22,16,128]{3,2,1,0:T(8,128)(2,1)S(1)} %triangle.5.mine, bf16[4,22,16,128]{3,2,1,0:T(8,128)(2,1)S(1)} %triangle.4.mine, bf16[6,22,16,128]{3,2,1,0:T(8,128)(2,1)S(1)} %triangle.3.mine, bf16[6,22,16,128]{3,2,1,0:T(8,128)(2,1)S(1)} %collective-permute-done.16.other, ...), kind=kLoop, calls=%fused_computation.1 | loop fusion | flops 5046272 | bytes 5767168 | tf_op jit(solution)/shard_map/add | solution.py:362
  79.7 3.7 %gather_fusion = f32[8,22,16,128]{3,2,1,0:T(8,128)} fusion(f32[16,22,16,128]{3,2,1,0:T(8,128)} %convert_add_fusion, s32[1024]{0:T(1024)S(1)} %pad_clamp_fusion), kind=kCustom, calls=%fused_computation | custom fusion | bytes 2883616 | tf_op jit(solution)/shard_map/gather | solution.py:369
  83.4 2.5 %fusion.61 = f32[22,8,11]{2,0,1:T(8,128)} fusion(f32[8,22,16,128]{3,2,1,0:T(8,128)} %gather_fusion), kind=kLoop, calls=%fused_computation.121 | loop fusion | flops 245872 | bytes 998976 | tf_op jit(solution)/shard_map/reduce_sum | solution.py:18
  85.9 1.6 copy.47
  89.5 1.6 copy.50
  91.1 2.6 %slice_bitcast_fusion = f32[22,8,11,128]{3,2,0,1:T(8,128)} fusion(f32[8,22,16,128]{3,2,1,0:T(8,128)} %gather_fusion), kind=kLoop, calls=%fused_computation.4 | loop fusion | bytes 1982464 | tf_op jit(solution)/shard_map/transpose | solution.py:369
  93.7 1.5 reshape.293
  95.1 2.9 %multiply_reduce_fusion = f32[22,8,11]{2,0,1:T(8,128)} fusion(f32[22,8,11]{2,0,1:T(8,128)} %copy.50, f32[8,22,16,128]{3,2,1,0:T(8,128)} %gather_fusion), kind=kLoop, calls=%fused_computation.6 | loop fusion | flops 741488 | bytes 1006720 | tf_op jit(solution)/shard_map/reduce_sum | solution.py:21
  98.0 1.6 copy.51
  100.5 2.7 %copy.46 = f32[22,8,11,128]{3,0,2,1:T(8,128)} copy(f32[22,8,11,128]{3,2,0,1:T(8,128)} %slice_bitcast_fusion) | data formatting | bytes 1982464 | tf_op jit(solution)/shard_map/transpose | solution.py:369
  103.8 1.5 reshape.294
  105.3 2.0 fusion.14
  108.5 1.9 fusion.25
  112.8 2.2 %fusion.10 = bf16[128,128]{1,0:T(8,128)(2,1)} fusion(bf16[22,88,128]{2,1,0:T(8,128)(2,1)} %copy-done.46, bf16[22,88,128]{2,0,1:T(8,128)(2,1)} %copy-done.41), kind=kOutput, calls=%fused_computation.25 | convolution fusion | flops 63455232 | bytes 1024000 | tf_op jit(solution)/shard_map/dot_general | solution.py:271
  115.0 1.5 pad_maximum_fusion.1.grads
  116.5 1.9 triangle_gradient.4.grads.refs_0_.refs_1_
  118.4 1.9 scatter_hop.8
  120.4 1.6 collective-permute-start.18
  122.5 2.6 %triangle_gradient.3.grads.refs_0_.refs_1_ = bf16[6,22,16,128]{3,2,1,0:T(8,128)(2,1)S(1)} custom-call(s32[6]{0:T(128)S(1)} %copy-done.8, bf16[6,22,16,128]{3,2,1,0:T(8,128)(2,1)S(1)} %triangle.5.mine, bf16[6,22,16,128]{3,2,1,0:T(8,128)(2,1)S(1)} %collective-permute-done.16.other, bf16[16,22,16,128]{3,2,1,0:T(8,128)(2,1)S(1)} %pad_maximum_fusion.1.grads, ...), custom_call_target="tpu_custom_call" | custom-call | flops 5280000000 | bytes 1048576 | tf_op jit(solution)/shard_map/triangle_gradient/pallas_call | solution.py:128
  125.0 1.9 scatter_hop.12
  127.0 1.6 collective-permute-start.26
  129.0 2.6 %triangle_gradient.5.grads.refs_0_.refs_1_ = bf16[6,22,16,128]{3,2,1,0:T(8,128)(2,1)S(1)} custom-call(s32[6]{0:T(128)S(1)} %stack.116.where, bf16[6,22,16,128]{3,2,1,0:T(8,128)(2,1)S(1)} %triangle.3.mine, bf16[6,22,16,128]{3,2,1,0:T(8,128)(2,1)S(1)} %collective-permute-done.14.other, bf16[16,22,16,128]{3,2,1,0:T(8,128)(2,1)S(1)} %pad_maximum_fusion.1.grads, ...), custom_call_target="tpu_custom_call" | custom-call | flops 5280000000 | bytes 1048576 | tf_op jit(solution)/shard_map/triangle_gradient/pallas_call | solution.py:128
  131.7 1.8 scatter_hop.9
  133.5 1.6 collective-permute-start.20
  135.5 6.5 %left_gradient.3.refs_4_ = f32[22,88,128]{2,1,0:T(8,128)S(1)} custom-call(bf16[6,22,16,128]{3,2,1,0:T(8,128)(2,1)S(1)} %triangle_gradient.5.grads.refs_0_.refs_1_, bf16[11,88,128]{2,1,0:T(8,128)(2,1)S(1)} %copy-done.3, bf16[11,88,128]{2,1,0:T(8,128)(2,1)S(1)} %copy-done.5, bf16[11,88,128]{2,1,0:T(8,128)(2,1)S(1)} %copy-done.19, ...), custom_call_target="tpu_custom_call" | custom-call | flops 5280000000 | bytes 1048576 | tf_op jit(solution)/shard_map/left_gradient/pallas_call | solution.py:221
  142.1 1.8 scatter_hop.13
  143.9 1.6 collective-permute-start.28
  146.0 1.8 scatter_hop.10
  147.8 1.6 collective-permute-start.22
  149.9 3.7 %left_gradient.4.refs_6_ = f32[22,88,128]{2,1,0:T(8,128)S(1)} custom-call(bf16[4,22,16,128]{3,2,1,0:T(8,128)(2,1)S(1)} %triangle_gradient.4.grads.refs_0_.refs_1_, bf16[11,88,128]{2,1,0:T(8,128)(2,1)S(1)} %copy-done.28, bf16[11,88,128]{2,1,0:T(8,128)(2,1)S(1)} %copy-done.30, bf16[11,88,128]{2,1,0:T(8,128)(2,1)S(1)} %copy-done.32, ...), custom_call_target="tpu_custom_call" | custom-call | flops 3520000000 | bytes 1048576 | tf_op jit(solution)/shard_map/left_gradient/pallas_call | solution.py:221
  154.0 1.8 scatter_hop.14
  156.3 1.6 collective-permute-start.31
  158.7 1.8 scatter_hop.11
  160.5 1.6 collective-permute-start.24
  162.6 5.5 %left_gradient.5 = f32[22,88,128]{2,1,0:T(8,128)S(1)} custom-call(bf16[6,22,16,128]{3,2,1,0:T(8,128)(2,1)S(1)} %triangle_gradient.3.grads.refs_0_.refs_1_, bf16[11,88,128]{2,1,0:T(8,128)(2,1)S(1)} %copy-done.12, bf16[11,88,128]{2,1,0:T(8,128)(2,1)S(1)} %copy-done.10, bf16[11,88,128]{2,1,0:T(8,128)(2,1)S(1)} %copy-done.17, ...), custom_call_target="tpu_custom_call" | custom-call | flops 5280000000 | bytes 1048576 | tf_op jit(solution)/shard_map/left_gradient/pallas_call | solution.py:221
  168.3 2.0 scatter_hop.15
  170.4 1.1 multiply_convert_fusion.1
  176.9 1.9 fusion.20
  178.8 1.7 collective-permute-start.37
  181.0 2.3 %collective-permute-done.37 = bf16[128,256]{1,0:T(8,128)(2,1)S(1)} collective-permute-done((bf16[128,256]{1,0:T(8,128)(2,1)S(1)}, bf16[128,256]{1,0:T(8,128)(2,1)S(1)}, u32[]{:S(2)}, u32[]{:S(2)}) %collective-permute-start.37) | collective-permute-done | bytes 65568 | tf_op jit(solution)/shard_map/ppermute | solution.py:61
  183.3 1.2 collective-permute-start.38
  184.4 1.5 collective-permute-done.33
  185.9 1.4 collective-permute-start.34
  188.7 3.0 %collective-permute-done.34 = bf16[128,512]{1,0:T(8,128)(2,1)S(1)} collective-permute-done((bf16[128,512]{1,0:T(8,128)(2,1)S(1)}, bf16[128,512]{1,0:T(8,128)(2,1)S(1)}, u32[]{:S(2)}, u32[]{:S(2)}) %collective-permute-start.34) | collective-permute-done | bytes 131104 | tf_op jit(solution)/shard_map/ppermute | solution.py:61
  191.7 1.3 collective-permute-start.35
  193.0 2.4 %collective-permute-done.39 = bf16[128,256]{1,0:T(8,128)(2,1)S(1)} collective-permute-done((bf16[128,256]{1,0:T(8,128)(2,1)S(1)}, bf16[128,256]{1,0:T(8,128)(2,1)S(1)}, u32[]{:S(2)}, u32[]{:S(2)}) %collective-permute-start.39) | collective-permute-done | bytes 65568 | tf_op jit(solution)/shard_map/ppermute | solution.py:61
  195.4 3.8 %collective-permute-done.35 = bf16[128,512]{1,0:T(8,128)(2,1)S(1)} collective-permute-done((bf16[128,512]{1,0:T(8,128)(2,1)S(1)}, bf16[128,512]{1,0:T(8,128)(2,1)S(1)}, u32[]{:S(2)}, u32[]{:S(2)}) %collective-permute-start.35) | collective-permute-done | bytes 131104 | tf_op jit(solution)/shard_map/ppermute | solution.py:61
  (240 shorter events, 29.4 us)
Async XLA Ops:
  5.7 4.5 %copy-start.38 = (f32[22,88,256]{2,1,0:T(8,128)}, f32[22,88,256]{2,1,0:T(8,128)S(1)}, u32[]{:S(2)}) copy-start(f32[22,88,256]{2,1,0:T(8,128)S(1)} %fusion.50) | copy-start | bytes 5947396
  8.1 22.2 %copy-start.65 = (s32[8]{0:T(128)S(1)}, s32[8]{0:T(128)}, u32[]{:S(2)}) copy-start(s32[8]{0:T(128)} %constant.341.clone) | copy-start | bytes 100
  8.1 28.8 %copy-start.57 = (s32[8]{0:T(128)S(1)}, s32[8]{0:T(128)}, u32[]{:S(2)}) copy-start(s32[8]{0:T(128)} %constant.342.clone) | copy-start | bytes 100
  10.2 37.3 %copy-start.2 = (bf16[11,88,128]{2,1,0:T(8,128)(2,1)}, bf16[11,88,128]{2,1,0:T(8,128)(2,1)S(1)}, u32[]{:S(2)}) copy-start(bf16[11,88,128]{2,1,0:T(8,128)(2,1)S(1)} %get-tuple-element.45.refs_0_) | copy-start | bytes 743428
  10.3 9.9 %collective-permute-start.9 = (bf16[11,88,128]{2,1,0:T(8,128)(2,1)S(1)}, bf16[11,88,128]{2,1,0:T(8,128)(2,1)S(1)}, u32[]{:S(2)}, u32[]{:S(2)}) collective-permute-start(bf16[11,88,128]{2,1,0:T(8,128)(2,1)S(1)} %get-tuple-element.45.refs_0_), channel_id=1, source_target_pairs={{0,2},{4,0},{8,4},{12,8},{14,12},{10,14},{6,10},{2,6},{1,3},{5,1},... | collective-permute-start | bytes 743432 | tf_op jit(solution)/shard_map/ppermute | solution.py:268
  13.3 8.9 %collective-permute-start = (bf16[11,88,128]{2,1,0:T(8,128)(2,1)S(1)}, bf16[11,88,128]{2,1,0:T(8,128)(2,1)S(1)}, u32[]{:S(2)}, u32[]{:S(2)}) collective-permute-start(bf16[11,88,128]{2,1,0:T(8,128)(2,1)S(1)} %get-tuple-element.45.refs_0_), channel_id=1, source_target_pairs={{0,4},{4,8},{8,12},{12,14},{14,10},{10,6},{6,2},{2,0},{1,5},{5,9},... | collective-permute-start | bytes 743432 | tf_op jit(solution)/shard_map/ppermute | solution.py:265
  13.4 14.1 %collective-permute-start.8 = (bf16[11,88,128]{2,1,0:T(8,128)(2,1)S(1)}, bf16[11,88,128]{2,1,0:T(8,128)(2,1)S(1)}, u32[]{:S(2)}, u32[]{:S(2)}) collective-permute-start(bf16[11,88,128]{2,1,0:T(8,128)(2,1)S(1)} %get-tuple-element.46.refs_1_), channel_id=1, source_target_pairs={{0,4},{4,8},{8,12},{12,14},{14,10},{10,6},{6,2},{2,0},{1,5},{5,9},... | collective-permute-start | bytes 743432 | tf_op jit(solution)/shard_map/ppermute | solution.py:265
  15.4 12.2 %collective-permute-start.1 = (bf16[11,88,128]{2,1,0:T(8,128)(2,1)S(1)}, bf16[11,88,128]{2,1,0:T(8,128)(2,1)S(1)}, u32[]{:S(2)}, u32[]{:S(2)}) collective-permute-start(bf16[11,88,128]{2,1,0:T(8,128)(2,1)S(1)} %get-tuple-element.46.refs_1_), channel_id=1, source_target_pairs={{0,2},{4,0},{8,4},{12,8},{14,12},{10,14},{6,10},{2,6},{1,3},{5,1},... | collective-permute-start | bytes 743432 | tf_op jit(solution)/shard_map/ppermute | solution.py:268
  20.2 40.3 %copy-start.9 = (bf16[11,88,128]{2,1,0:T(8,128)(2,1)}, bf16[11,88,128]{2,1,0:T(8,128)(2,1)S(1)}, u32[]{:S(2)}) copy-start(bf16[11,88,128]{2,1,0:T(8,128)(2,1)S(1)} %collective-permute-done.9.refs_1_) | copy-start | bytes 743428
  20.2 23.2 %collective-permute-start.11 = (bf16[11,88,128]{2,1,0:T(8,128)(2,1)S(1)}, bf16[11,88,128]{2,1,0:T(8,128)(2,1)S(1)}, u32[]{:S(2)}, u32[]{:S(2)}) collective-permute-start(bf16[11,88,128]{2,1,0:T(8,128)(2,1)S(1)} %collective-permute-done.9.refs_1_), channel_id=1, source_target_pairs={{0,2},{4,0},{8,4},{12,8},{14,12},{10,14},{6,10},{2,6},{1,3},{5,1},... | collective-permute-start | bytes 743432 | tf_op jit(solution)/shard_map/ppermute | solution.py:268
  22.2 35.4 %copy-start.18 = (bf16[11,88,128]{2,1,0:T(8,128)(2,1)}, bf16[11,88,128]{2,1,0:T(8,128)(2,1)S(1)}, u32[]{:S(2)}) copy-start(bf16[11,88,128]{2,1,0:T(8,128)(2,1)S(1)} %collective-permute-done.refs_2_) | copy-start | bytes 743428
  22.2 22.8 %collective-permute-start.2 = (bf16[11,88,128]{2,1,0:T(8,128)(2,1)S(1)}, bf16[11,88,128]{2,1,0:T(8,128)(2,1)}, u32[]{:S(2)}, u32[]{:S(2)}) collective-permute-start(bf16[11,88,128]{2,1,0:T(8,128)(2,1)S(1)} %collective-permute-done.refs_2_), channel_id=1, source_target_pairs={{0,4},{4,8},{8,12},{12,14},{14,10},{10,6},{6,2},{2,0},{1,5},{5,9},... | collective-permute-start | bytes 743432 | tf_op jit(solution)/shard_map/ppermute | solution.py:265
  27.5 32.9 %copy-start.11 = (bf16[11,88,128]{2,1,0:T(8,128)(2,1)}, bf16[11,88,128]{2,1,0:T(8,128)(2,1)S(1)}, u32[]{:S(2)}) copy-start(bf16[11,88,128]{2,1,0:T(8,128)(2,1)S(1)} %collective-permute-done.8.refs_0_) | copy-start | bytes 743428
  27.5 18.0 %collective-permute-start.10 = (bf16[11,88,128]{2,1,0:T(8,128)(2,1)S(1)}, bf16[11,88,128]{2,1,0:T(8,128)(2,1)S(1)}, u32[]{:S(2)}, u32[]{:S(2)}) collective-permute-start(bf16[11,88,128]{2,1,0:T(8,128)(2,1)S(1)} %collective-permute-done.8.refs_0_), channel_id=1, source_target_pairs={{0,4},{4,8},{8,12},{12,14},{14,10},{10,6},{6,2},{2,0},{1,5},{5,9},... | collective-permute-start | bytes 743432 | tf_op jit(solution)/shard_map/ppermute | solution.py:265
  27.6 18.0 %collective-permute-start.3 = (bf16[11,88,128]{2,1,0:T(8,128)(2,1)S(1)}, bf16[11,88,128]{2,1,0:T(8,128)(2,1)}, u32[]{:S(2)}, u32[]{:S(2)}) collective-permute-start(bf16[11,88,128]{2,1,0:T(8,128)(2,1)S(1)} %collective-permute-done.1.refs_3_), channel_id=1, source_target_pairs={{0,2},{4,0},{8,4},{12,8},{14,12},{10,14},{6,10},{2,6},{1,3},{5,1},... | collective-permute-start | bytes 743432 | tf_op jit(solution)/shard_map/ppermute | solution.py:268
  43.4 17.1 %copy-start.13 = (bf16[11,88,128]{2,1,0:T(8,128)(2,1)}, bf16[11,88,128]{2,1,0:T(8,128)(2,1)S(1)}, u32[]{:S(2)}) copy-start(bf16[11,88,128]{2,1,0:T(8,128)(2,1)S(1)} %collective-permute-done.11.refs_3_) | copy-start | bytes 743428
  43.4 17.0 %collective-permute-start.13 = (bf16[11,88,128]{2,1,0:T(8,128)(2,1)S(1)}, bf16[11,88,128]{2,1,0:T(8,128)(2,1)S(1)}, u32[]{:S(2)}, u32[]{:S(2)}) collective-permute-start(bf16[11,88,128]{2,1,0:T(8,128)(2,1)S(1)} %collective-permute-done.11.refs_3_), channel_id=1, source_target_pairs={{0,2},{4,0},{8,4},{12,8},{14,12},{10,14},{6,10},{2,6},{1,3},{5,1},... | collective-permute-start | bytes 743432 | tf_op jit(solution)/shard_map/ppermute | solution.py:268
  45.0 13.3 %collective-permute-start.4 = (bf16[11,88,128]{2,1,0:T(8,128)(2,1)}, bf16[11,88,128]{2,1,0:T(8,128)(2,1)S(1)}, u32[]{:S(2)}, u32[]{:S(2)}) collective-permute-start(bf16[11,88,128]{2,1,0:T(8,128)(2,1)} %collective-permute-done.2.refs_4_), channel_id=1, source_target_pairs={{0,4},{4,8},{8,12},{12,14},{14,10},{10,6},{6,2},{2,0},{1,5},{5,9},... | collective-permute-start | bytes 743432 | tf_op jit(solution)/shard_map/ppermute | solution.py:265
  45.5 12.1 %copy-start.15 = (bf16[11,88,128]{2,1,0:T(8,128)(2,1)}, bf16[11,88,128]{2,1,0:T(8,128)(2,1)S(1)}, u32[]{:S(2)}) copy-start(bf16[11,88,128]{2,1,0:T(8,128)(2,1)S(1)} %collective-permute-done.10.refs_2_) | copy-start | bytes 743428
  45.5 14.9 %collective-permute-start.12 = (bf16[11,88,128]{2,1,0:T(8,128)(2,1)S(1)}, bf16[11,88,128]{2,1,0:T(8,128)(2,1)S(1)}, u32[]{:S(2)}, u32[]{:S(2)}) collective-permute-start(bf16[11,88,128]{2,1,0:T(8,128)(2,1)S(1)} %collective-permute-done.10.refs_2_), channel_id=1, source_target_pairs={{0,4},{4,8},{8,12},{12,14},{14,10},{10,6},{6,2},{2,0},{1,5},{5,9},... | collective-permute-start | bytes 743432 | tf_op jit(solution)/shard_map/ppermute | solution.py:265
  45.6 12.9 %collective-permute-start.5 = (bf16[11,88,128]{2,1,0:T(8,128)(2,1)}, bf16[11,88,128]{2,1,0:T(8,128)(2,1)S(1)}, u32[]{:S(2)}, u32[]{:S(2)}) collective-permute-start(bf16[11,88,128]{2,1,0:T(8,128)(2,1)} %collective-permute-done.3.refs_5_), channel_id=1, source_target_pairs={{0,2},{4,0},{8,4},{12,8},{14,12},{10,14},{6,10},{2,6},{1,3},{5,1},... | collective-permute-start | bytes 743432 | tf_op jit(solution)/shard_map/ppermute | solution.py:268
  58.3 18.0 %collective-permute-start.14 = (bf16[6,22,16,128]{3,2,1,0:T(8,128)(2,1)S(1)}, bf16[6,22,16,128]{3,2,1,0:T(8,128)(2,1)S(1)}, u32[]{:S(2)}, u32[]{:S(2)}) collective-permute-start(bf16[6,22,16,128]{3,2,1,0:T(8,128)(2,1)S(1)} %triangle.3.mine), channel_id=1, source_target_pairs={{0,1},{1,0},{2,3},{3,2},{4,5},{5,4},{6,7},{7,6},{8,9},{9,8},{10,11... | collective-permute-start | bytes 1622024 | tf_op jit(solution)/shard_map/ppermute | solution.py:51
  58.3 11.3 %copy-start.27 = (bf16[11,88,128]{2,1,0:T(8,128)(2,1)}, bf16[11,88,128]{2,1,0:T(8,128)(2,1)S(1)}, u32[]{:S(2)}) copy-start(bf16[11,88,128]{2,1,0:T(8,128)(2,1)S(1)} %collective-permute-done.4.refs_0_) | copy-start | bytes 743428
  58.3 11.3 %collective-permute-start.6 = (bf16[11,88,128]{2,1,0:T(8,128)(2,1)S(1)}, bf16[11,88,128]{2,1,0:T(8,128)(2,1)S(1)}, u32[]{:S(2)}, u32[]{:S(2)}) collective-permute-start(bf16[11,88,128]{2,1,0:T(8,128)(2,1)S(1)} %collective-permute-done.4.refs_0_), channel_id=1, source_target_pairs={{0,4},{4,8},{8,12},{12,14},{14,10},{10,6},{6,2},{2,0},{1,5},{5,9},... | collective-permute-start | bytes 743432 | tf_op jit(solution)/shard_map/ppermute | solution.py:265
  58.5 11.2 %copy-start.29 = (bf16[11,88,128]{2,1,0:T(8,128)(2,1)}, bf16[11,88,128]{2,1,0:T(8,128)(2,1)S(1)}, u32[]{:S(2)}) copy-start(bf16[11,88,128]{2,1,0:T(8,128)(2,1)S(1)} %collective-permute-done.5.refs_1_) | copy-start | bytes 743428
  58.5 11.1 %collective-permute-start.7 = (bf16[11,88,128]{2,1,0:T(8,128)(2,1)S(1)}, bf16[11,88,128]{2,1,0:T(8,128)(2,1)S(1)}, u32[]{:S(2)}, u32[]{:S(2)}) collective-permute-start(bf16[11,88,128]{2,1,0:T(8,128)(2,1)S(1)} %collective-permute-done.5.refs_1_), channel_id=1, source_target_pairs={{0,2},{4,0},{8,4},{12,8},{14,12},{10,14},{6,10},{2,6},{1,3},{5,1},... | collective-permute-start | bytes 743432 | tf_op jit(solution)/shard_map/ppermute | solution.py:268
  60.4 9.1 %copy-start.23 = (bf16[11,88,128]{2,1,0:T(8,128)(2,1)}, bf16[11,88,128]{2,1,0:T(8,128)(2,1)S(1)}, u32[]{:S(2)}) copy-start(bf16[11,88,128]{2,1,0:T(8,128)(2,1)S(1)} %collective-permute-done.13.refs_5_) | copy-start | bytes 743428
  61.5 8.1 %copy-start.25 = (bf16[11,88,128]{2,1,0:T(8,128)(2,1)}, bf16[11,88,128]{2,1,0:T(8,128)(2,1)S(1)}, u32[]{:S(2)}) copy-start(bf16[11,88,128]{2,1,0:T(8,128)(2,1)S(1)} %collective-permute-done.12.refs_4_) | copy-start | bytes 743428
  69.5 6.8 %collective-permute-start.16 = (bf16[6,22,16,128]{3,2,1,0:T(8,128)(2,1)S(1)}, bf16[6,22,16,128]{3,2,1,0:T(8,128)(2,1)S(1)}, u32[]{:S(2)}, u32[]{:S(2)}) collective-permute-start(bf16[6,22,16,128]{3,2,1,0:T(8,128)(2,1)S(1)} %triangle.5.mine), channel_id=1, source_target_pairs={{0,1},{1,0},{2,3},{3,2},{4,5},{5,4},{6,7},{7,6},{8,9},{9,8},{10,11... | collective-permute-start | bytes 1622024 | tf_op jit(solution)/shard_map/ppermute | solution.py:51
  69.6 5.4 %copy-start.31 = (bf16[11,88,128]{2,1,0:T(8,128)(2,1)}, bf16[11,88,128]{2,1,0:T(8,128)(2,1)S(1)}, u32[]{:S(2)}) copy-start(bf16[11,88,128]{2,1,0:T(8,128)(2,1)S(1)} %collective-permute-done.6.refs_2_) | copy-start | bytes 743428
  69.7 5.4 %copy-start.33 = (bf16[11,88,128]{2,1,0:T(8,128)(2,1)}, bf16[11,88,128]{2,1,0:T(8,128)(2,1)S(1)}, u32[]{:S(2)}) copy-start(bf16[11,88,128]{2,1,0:T(8,128)(2,1)S(1)} %collective-permute-done.7.refs_3_) | copy-start | bytes 743428
  75.1 1.8 collective-permute-start.15
  98.0 7.2 %copy-start.7 = (f32[128]{0:T(128)S(1)}, f32[128]{0:T(128)}, u32[]{:S(2)}) copy-start(f32[128]{0:T(128)} %param.17) | copy-start | bytes 1540
  103.1 4.9 %copy-start.6 = (bf16[128,128]{1,0:T(8,128)(2,1)S(1)}, bf16[128,128]{1,0:T(8,128)(2,1)}, u32[]{:S(2)}) copy-start(bf16[128,128]{1,0:T(8,128)(2,1)} %w_out.5) | copy-start | bytes 98308
  111.6 3.4 %collective-permute-start.17 = (bf16[8,22,16,128]{3,2,1,0:T(8,128)(2,1)}, bf16[8,22,16,128]{3,2,1,0:T(8,128)(2,1)}, u32[]{:S(2)}, u32[]{:S(2)}) collective-permute-start(bf16[8,22,16,128]{3,2,1,0:T(8,128)(2,1)} %pad.4), channel_id=1, source_target_pairs={{0,1},{1,0},{2,3},{3,2},{4,5},{5,4},{6,7},{7,6},{8,9},{9,8},{10,11... | collective-permute-start | bytes 2162696 | tf_op jit(solution)/shard_map/ppermute | solution.py:51
  120.4 11.3 %collective-permute-start.18 = (bf16[11,88,128]{2,1,0:T(8,128)(2,1)S(1)}, bf16[11,88,128]{2,1,0:T(8,128)(2,1)S(1)}, u32[]{:S(2)}, u32[]{:S(2)}) collective-permute-start(bf16[11,88,128]{2,1,0:T(8,128)(2,1)S(1)} %get-tuple-element.22), channel_id=1, source_target_pairs={{0,2},{4,0},{8,4},{12,8},{14,12},{10,14},{6,10},{2,6},{1,3},{5,1},... | collective-permute-start | bytes 743432 | tf_op jit(solution)/shard_map/ppermute | solution.py:268
  122.0 9.7 %collective-permute-start.19 = (bf16[11,88,128]{2,1,0:T(8,128)(2,1)S(1)}, bf16[11,88,128]{2,1,0:T(8,128)(2,1)S(1)}, u32[]{:S(2)}, u32[]{:S(2)}) collective-permute-start(bf16[11,88,128]{2,1,0:T(8,128)(2,1)S(1)} %get-tuple-element.23), channel_id=1, source_target_pairs={{0,4},{4,8},{8,12},{12,14},{14,10},{10,6},{6,2},{2,0},{1,5},{5,9},... | collective-permute-start | bytes 743432 | tf_op jit(solution)/shard_map/ppermute | solution.py:265
  127.0 15.1 %collective-permute-start.26 = (bf16[11,88,128]{2,1,0:T(8,128)(2,1)S(1)}, bf16[11,88,128]{2,1,0:T(8,128)(2,1)S(1)}, u32[]{:S(2)}, u32[]{:S(2)}) collective-permute-start(bf16[11,88,128]{2,1,0:T(8,128)(2,1)S(1)} %get-tuple-element.30), channel_id=1, source_target_pairs={{0,2},{4,0},{8,4},{12,8},{14,12},{10,14},{6,10},{2,6},{1,3},{5,1},... | collective-permute-start | bytes 743432 | tf_op jit(solution)/shard_map/ppermute | solution.py:268
  128.6 13.5 %collective-permute-start.27 = (bf16[11,88,128]{2,1,0:T(8,128)(2,1)S(1)}, bf16[11,88,128]{2,1,0:T(8,128)(2,1)S(1)}, u32[]{:S(2)}, u32[]{:S(2)}) collective-permute-start(bf16[11,88,128]{2,1,0:T(8,128)(2,1)S(1)} %get-tuple-element.31), channel_id=1, source_target_pairs={{0,4},{4,8},{8,12},{12,14},{14,10},{10,6},{6,2},{2,0},{1,5},{5,9},... | collective-permute-start | bytes 743432 | tf_op jit(solution)/shard_map/ppermute | solution.py:265
  133.5 12.6 %collective-permute-start.20 = (bf16[11,88,128]{2,1,0:T(8,128)(2,1)S(1)}, bf16[11,88,128]{2,1,0:T(8,128)(2,1)S(1)}, u32[]{:S(2)}, u32[]{:S(2)}) collective-permute-start(bf16[11,88,128]{2,1,0:T(8,128)(2,1)S(1)} %get-tuple-element.24), channel_id=1, source_target_pairs={{0,2},{4,0},{8,4},{12,8},{14,12},{10,14},{6,10},{2,6},{1,3},{5,1},... | collective-permute-start | bytes 743432 | tf_op jit(solution)/shard_map/ppermute | solution.py:268
  135.1 10.9 %collective-permute-start.21 = (bf16[11,88,128]{2,1,0:T(8,128)(2,1)S(1)}, bf16[11,88,128]{2,1,0:T(8,128)(2,1)S(1)}, u32[]{:S(2)}, u32[]{:S(2)}) collective-permute-start(bf16[11,88,128]{2,1,0:T(8,128)(2,1)S(1)} %get-tuple-element.25), channel_id=1, source_target_pairs={{0,4},{4,8},{8,12},{12,14},{14,10},{10,6},{6,2},{2,0},{1,5},{5,9},... | collective-permute-start | bytes 743432 | tf_op jit(solution)/shard_map/ppermute | solution.py:265
  143.9 9.8 %collective-permute-start.28 = (bf16[11,88,128]{2,1,0:T(8,128)(2,1)S(1)}, bf16[11,88,128]{2,1,0:T(8,128)(2,1)S(1)}, u32[]{:S(2)}, u32[]{:S(2)}) collective-permute-start(bf16[11,88,128]{2,1,0:T(8,128)(2,1)S(1)} %get-tuple-element.32), channel_id=1, source_target_pairs={{0,2},{4,0},{8,4},{12,8},{14,12},{10,14},{6,10},{2,6},{1,3},{5,1},... | collective-permute-start | bytes 743432 | tf_op jit(solution)/shard_map/ppermute | solution.py:268
  145.5 4.4 %copy-start.34 = (bf16[11,88,128]{2,1,0:T(8,128)(2,1)S(1)}, bf16[11,88,128]{2,1,0:T(8,128)(2,1)}, u32[]{:S(2)}) copy-start(bf16[11,88,128]{2,1,0:T(8,128)(2,1)} %copy-done.33) | copy-start | bytes 743428
  145.5 8.5 %collective-permute-start.29 = (bf16[11,88,128]{2,1,0:T(8,128)(2,1)S(1)}, bf16[11,88,128]{2,1,0:T(8,128)(2,1)S(1)}, u32[]{:S(2)}, u32[]{:S(2)}) collective-permute-start(bf16[11,88,128]{2,1,0:T(8,128)(2,1)S(1)} %get-tuple-element.33), channel_id=1, source_target_pairs={{0,4},{4,8},{8,12},{12,14},{14,10},{10,6},{6,2},{2,0},{1,5},{5,9},... | collective-permute-start | bytes 743432 | tf_op jit(solution)/shard_map/ppermute | solution.py:265
  147.8 10.1 %collective-permute-start.22 = (bf16[11,88,128]{2,1,0:T(8,128)(2,1)S(1)}, bf16[11,88,128]{2,1,0:T(8,128)(2,1)S(1)}, u32[]{:S(2)}, u32[]{:S(2)}) collective-permute-start(bf16[11,88,128]{2,1,0:T(8,128)(2,1)S(1)} %get-tuple-element.26), channel_id=1, source_target_pairs={{0,2},{4,0},{8,4},{12,8},{14,12},{10,14},{6,10},{2,6},{1,3},{5,1},... | collective-permute-start | bytes 743432 | tf_op jit(solution)/shard_map/ppermute | solution.py:268
  149.4 9.3 %collective-permute-start.23 = (bf16[11,88,128]{2,1,0:T(8,128)(2,1)S(1)}, bf16[11,88,128]{2,1,0:T(8,128)(2,1)S(1)}, u32[]{:S(2)}, u32[]{:S(2)}) collective-permute-start(bf16[11,88,128]{2,1,0:T(8,128)(2,1)S(1)} %get-tuple-element.27), channel_id=1, source_target_pairs={{0,4},{4,8},{8,12},{12,14},{14,10},{10,6},{6,2},{2,0},{1,5},{5,9},... | collective-permute-start | bytes 743432 | tf_op jit(solution)/shard_map/ppermute | solution.py:265
  155.8 12.4 %collective-permute-start.30 = (bf16[11,88,128]{2,1,0:T(8,128)(2,1)S(1)}, bf16[11,88,128]{2,1,0:T(8,128)(2,1)S(1)}, u32[]{:S(2)}, u32[]{:S(2)}) collective-permute-start(bf16[11,88,128]{2,1,0:T(8,128)(2,1)S(1)} %get-tuple-element.34), channel_id=1, source_target_pairs={{0,4},{4,8},{8,12},{12,14},{14,10},{10,6},{6,2},{2,0},{1,5},{5,9},... | collective-permute-start | bytes 743432 | tf_op jit(solution)/shard_map/ppermute | solution.py:265
  156.3 6.3 %copy-start.10 = (bf16[11,88,128]{2,1,0:T(8,128)(2,1)S(1)}, bf16[11,88,128]{2,1,0:T(8,128)(2,1)}, u32[]{:S(2)}) copy-start(bf16[11,88,128]{2,1,0:T(8,128)(2,1)} %copy-done.9) | copy-start | bytes 743428
  156.3 6.3 %copy-start.12 = (bf16[11,88,128]{2,1,0:T(8,128)(2,1)S(1)}, bf16[11,88,128]{2,1,0:T(8,128)(2,1)}, u32[]{:S(2)}) copy-start(bf16[11,88,128]{2,1,0:T(8,128)(2,1)} %copy-done.11) | copy-start | bytes 743428
  156.3 6.3 %copy-start.14 = (bf16[11,88,128]{2,1,0:T(8,128)(2,1)S(1)}, bf16[11,88,128]{2,1,0:T(8,128)(2,1)}, u32[]{:S(2)}) copy-start(bf16[11,88,128]{2,1,0:T(8,128)(2,1)} %copy-done.13) | copy-start | bytes 743428
  156.3 6.3 %copy-start.17 = (bf16[11,88,128]{2,1,0:T(8,128)(2,1)S(1)}, bf16[11,88,128]{2,1,0:T(8,128)(2,1)}, u32[]{:S(2)}) copy-start(bf16[11,88,128]{2,1,0:T(8,128)(2,1)} %copy-done.15) | copy-start | bytes 743428
  156.3 6.3 %copy-start.24 = (bf16[11,88,128]{2,1,0:T(8,128)(2,1)S(1)}, bf16[11,88,128]{2,1,0:T(8,128)(2,1)}, u32[]{:S(2)}) copy-start(bf16[11,88,128]{2,1,0:T(8,128)(2,1)} %copy-done.23) | copy-start | bytes 743428
  156.3 6.3 %copy-start.26 = (bf16[11,88,128]{2,1,0:T(8,128)(2,1)S(1)}, bf16[11,88,128]{2,1,0:T(8,128)(2,1)}, u32[]{:S(2)}) copy-start(bf16[11,88,128]{2,1,0:T(8,128)(2,1)} %copy-done.25) | copy-start | bytes 743428
  156.3 11.9 %collective-permute-start.31 = (bf16[11,88,128]{2,1,0:T(8,128)(2,1)S(1)}, bf16[11,88,128]{2,1,0:T(8,128)(2,1)S(1)}, u32[]{:S(2)}, u32[]{:S(2)}) collective-permute-start(bf16[11,88,128]{2,1,0:T(8,128)(2,1)S(1)} %get-tuple-element.35), channel_id=1, source_target_pairs={{0,2},{4,0},{8,4},{12,8},{14,12},{10,14},{6,10},{2,6},{1,3},{5,1},... | collective-permute-start | bytes 743432 | tf_op jit(solution)/shard_map/ppermute | solution.py:268
  160.5 7.7 %collective-permute-start.24 = (bf16[11,88,128]{2,1,0:T(8,128)(2,1)S(1)}, bf16[11,88,128]{2,1,0:T(8,128)(2,1)S(1)}, u32[]{:S(2)}, u32[]{:S(2)}) collective-permute-start(bf16[11,88,128]{2,1,0:T(8,128)(2,1)S(1)} %get-tuple-element.28), channel_id=1, source_target_pairs={{0,2},{4,0},{8,4},{12,8},{14,12},{10,14},{6,10},{2,6},{1,3},{5,1},... | collective-permute-start | bytes 743432 | tf_op jit(solution)/shard_map/ppermute | solution.py:268
  162.1 6.2 %collective-permute-start.25 = (bf16[11,88,128]{2,1,0:T(8,128)(2,1)S(1)}, bf16[11,88,128]{2,1,0:T(8,128)(2,1)S(1)}, u32[]{:S(2)}, u32[]{:S(2)}) collective-permute-start(bf16[11,88,128]{2,1,0:T(8,128)(2,1)S(1)} %get-tuple-element.29), channel_id=1, source_target_pairs={{0,4},{4,8},{8,12},{12,14},{14,10},{10,6},{6,2},{2,0},{1,5},{5,9},... | collective-permute-start | bytes 743432 | tf_op jit(solution)/shard_map/ppermute | solution.py:265
  173.8 4.9 %collective-permute-start.36 = (bf16[128,256]{1,0:T(8,128)(2,1)S(1)}, bf16[128,256]{1,0:T(8,128)(2,1)S(1)}, u32[]{:S(2)}, u32[]{:S(2)}) collective-permute-start(bf16[128,256]{1,0:T(8,128)(2,1)S(1)} %fusion.9), channel_id=1, source_target_pairs={{0,1},{1,0},{2,3},{3,2},{4,5},{5,4},{6,7},{7,6},{8,9},{9,8},{10,11... | collective-permute-start | bytes 196616 | tf_op jit(solution)/shard_map/ppermute | solution.py:51
  176.4 4.0 %collective-permute-start.32 = (bf16[128,512]{1,0:T(8,128)(2,1)S(1)}, bf16[128,512]{1,0:T(8,128)(2,1)S(1)}, u32[]{:S(2)}, u32[]{:S(2)}) collective-permute-start(bf16[128,512]{1,0:T(8,128)(2,1)S(1)} %pad_maximum_fusion.3), channel_id=1, source_target_pairs={{0,1},{1,0},{2,3},{3,2},{4,5},{5,4},{6,7},{7,6},{8,9},{9,8},{10,11... | collective-permute-start | bytes 393224 | tf_op jit(solution)/shard_map/ppermute | solution.py:51
  178.8 4.5 %collective-permute-start.37 = (bf16[128,256]{1,0:T(8,128)(2,1)S(1)}, bf16[128,256]{1,0:T(8,128)(2,1)S(1)}, u32[]{:S(2)}, u32[]{:S(2)}) collective-permute-start(bf16[128,256]{1,0:T(8,128)(2,1)S(1)} %add_convert_fusion.7), channel_id=1, source_target_pairs={{0,2},{2,0},{4,6},{6,4},{8,10},{10,8},{12,14},{14,12},{1,3},{3,1},... | collective-permute-start | bytes 196616 | tf_op jit(solution)/shard_map/ppermute | solution.py:61
  180.5 5.4 %collective-permute-start.33 = (bf16[128,512]{1,0:T(8,128)(2,1)S(1)}, bf16[128,512]{1,0:T(8,128)(2,1)S(1)}, u32[]{:S(2)}, u32[]{:S(2)}) collective-permute-start(bf16[128,512]{1,0:T(8,128)(2,1)S(1)} %add_convert_fusion.3), channel_id=1, source_target_pairs={{0,2},{2,0},{4,6},{6,4},{8,10},{10,8},{12,14},{14,12},{1,3},{3,1},... | collective-permute-start | bytes 393224 | tf_op jit(solution)/shard_map/ppermute | solution.py:61
  183.3 4.3 %collective-permute-start.38 = (bf16[128,256]{1,0:T(8,128)(2,1)S(1)}, bf16[128,256]{1,0:T(8,128)(2,1)S(1)}, u32[]{:S(2)}, u32[]{:S(2)}) collective-permute-start(bf16[128,256]{1,0:T(8,128)(2,1)S(1)} %add_convert_fusion.6), channel_id=1, source_target_pairs={{0,4},{2,6},{4,0},{6,2},{8,12},{10,14},{12,8},{14,10},{1,5},{3,7},... | collective-permute-start | bytes 196616 | tf_op jit(solution)/shard_map/ppermute | solution.py:61
  185.9 5.7 %collective-permute-start.34 = (bf16[128,512]{1,0:T(8,128)(2,1)S(1)}, bf16[128,512]{1,0:T(8,128)(2,1)S(1)}, u32[]{:S(2)}, u32[]{:S(2)}) collective-permute-start(bf16[128,512]{1,0:T(8,128)(2,1)S(1)} %add_convert_fusion.2), channel_id=1, source_target_pairs={{0,4},{2,6},{4,0},{6,2},{8,12},{10,14},{12,8},{14,10},{1,5},{3,7},... | collective-permute-start | bytes 393224 | tf_op jit(solution)/shard_map/ppermute | solution.py:61
  187.6 7.8 %collective-permute-start.39 = (bf16[128,256]{1,0:T(8,128)(2,1)S(1)}, bf16[128,256]{1,0:T(8,128)(2,1)S(1)}, u32[]{:S(2)}, u32[]{:S(2)}) collective-permute-start(bf16[128,256]{1,0:T(8,128)(2,1)S(1)} %add_convert_fusion.5), channel_id=1, source_target_pairs={{0,8},{2,10},{4,12},{6,14},{8,0},{10,2},{12,4},{14,6},{1,9},{3,11}... | collective-permute-start | bytes 196616 | tf_op jit(solution)/shard_map/ppermute | solution.py:61
  191.7 7.5 %collective-permute-start.35 = (bf16[128,512]{1,0:T(8,128)(2,1)S(1)}, bf16[128,512]{1,0:T(8,128)(2,1)S(1)}, u32[]{:S(2)}, u32[]{:S(2)}) collective-permute-start(bf16[128,512]{1,0:T(8,128)(2,1)S(1)} %add_convert_fusion.1), channel_id=1, source_target_pairs={{0,8},{2,10},{4,12},{6,14},{8,0},{10,2},{12,4},{14,6},{1,9},{3,11}... | collective-permute-start | bytes 393224 | tf_op jit(solution)/shard_map/ppermute | solution.py:61
  (44 other events, 102.6 us)

commit v3 on v0

v3 whole, which is shorter than its diff:
```python
import functools

import jax
import jax.numpy as jnp
from jax import lax
from jax.experimental import pallas as pl
from jax.experimental.pallas import tpu as pltpu
from jax.sharding import PartitionSpec as P

eps = 1e-05
f32 = jnp.float32
bf16 = jnp.bfloat16
VMEM = pl.BlockSpec(memory_space=pltpu.VMEM)
SMEM = pl.BlockSpec(memory_space=pltpu.SMEM)
ANY = pl.BlockSpec(memory_space=pl.ANY)
MIB = 1 << 20


def layer_norm_backward(output_gradient, standardized_input, inverse_deviation, norm_gain):
    scaled_output = output_gradient * norm_gain
    first_operand = jnp.mean(scaled_output, axis=-1, keepdims=True)
    second_operand = jnp.mean(scaled_output * standardized_input, axis=-1, keepdims=True)
    return inverse_deviation * (scaled_output - first_operand - standardized_input * second_operand)


def standardize(values):
    centered = values - jnp.mean(values, axis=-1, keepdims=True)
    inverse = lax.rsqrt(jnp.mean(centered * centered, axis=-1, keepdims=True) + eps)
    return centered * inverse, inverse


def dot(a, b, ca, cb):
    return lax.dot_general(a, b, (((ca,), (cb,)), ((), ())), preferred_element_type=f32)


def ring_order(row_count):
    if row_count == 8:
        return [0, 2, 4, 6, 7, 5, 3, 1]
    return list(range(row_count))


def swap_col(x):
    return lax.ppermute(x, "col", [(0, 1), (1, 0)])


def sum_all(x, row_count):
    def add(a, b):
        return (a.astype(f32) + b.astype(f32)).astype(bf16)

    x = add(x, swap_col(x))
    step = 1
    while step < row_count:
        x = add(x, lax.ppermute(x, "row", [(r, r ^ step) for r in range(row_count)]))
        step *= 2
    return x


def call(kernel, name, microseconds, args, specs, outs, scratch=(), after=()):
    held = sum(a.size * a.dtype.itemsize for a, s in zip(args, specs) if s is VMEM)
    held += sum(int(o.size) * o.dtype.itemsize for o in outs)
    held += sum(int(s.inner_aval.size) * 4 for s in scratch)

    def body(*refs):
        kernel(*refs[: len(args)], *refs[len(args) + len(after) :])

    return pl.pallas_call(
        body,
        out_shape=list(outs),
        in_specs=list(specs) + [ANY] * len(after),
        out_specs=[VMEM] * len(outs),
        scratch_shapes=list(scratch),
        compiler_params=pltpu.CompilerParams(vmem_limit_bytes=min(56 * MIB, held * 5 // 4 + 6 * MIB)),
        cost_estimate=pl.CostEstimate(
            flops=int(microseconds * 1.1e9), bytes_accessed=MIB, transcendentals=0
        ),
        name=name,
    )(*args, *after)


def shape_of(dims, dtype):
    return jax.ShapeDtypeStruct(dims, dtype)


def present_row(lengths, slot, position):
    return (position % slot < lengths[position // slot]).astype(f32)


def present_columns(lengths, slot, half):
    at = lax.axis_index("col") * half + lax.broadcasted_iota(jnp.int32, (half, 128), 0)
    chain = at // slot
    held = jnp.zeros((half, 128), jnp.int32)
    for c in range(lengths.shape[0]):
        held = jnp.where(chain == c, lengths[c], held)
    return (at - chain * slot < held).astype(f32)


def first_row(here):
    return lax.axis_index("row") * here


def input_kernel(slot, lengths, pair, gain, bias, w, right_a, right_b, normed, mask):
    here, half, hidden = pair.shape
    short = here // 2
    mask[...] = present_columns(lengths, slot, half)

    def body(t, carry):
        for out, i in ((right_a, t), (right_b, t + short)):
            standard, _ = standardize(pair[i].astype(f32))
            values = (standard * gain[...] + bias[...]).astype(bf16)
            normed[i] = values
            proj = dot(values, w[...], 1, 0)
            shown = mask[...] * present_row(lengths, slot, first_row(here) + i)
            gated = jax.nn.sigmoid(proj[:, :hidden]) * proj[:, hidden:]
            out[t] = (shown * gated).astype(bf16)
        return carry

    lax.fori_loop(0, short, body, 0)


def left_kernel(slot, lengths, normed, cotangent, w, left, outs, mask):
    here, half, hidden = normed.shape
    halves, _, padded, _ = outs.shape
    short = half // halves
    mask[...] = present_columns(lengths, slot, half)

    def body(i, carry):
        proj = dot(normed[i], w[...], 1, 0)
        shown = mask[...] * present_row(lengths, slot, first_row(here) + i)
        gated = shown * jax.nn.sigmoid(proj[:, :hidden]) * proj[:, hidden : 2 * hidden]
        left[i] = gated.astype(bf16).astype(f32)
        grads = cotangent[i].astype(f32) * jax.nn.sigmoid(proj[:, 2 * hidden :])
        empty = jnp.zeros((padded - short, hidden), f32)
        for m in range(halves):
            part = grads[m * short : (m + 1) * short]
            outs[m, i] = jnp.concatenate([part, empty], axis=0).astype(bf16)
        return carry

    lax.fori_loop(0, here, body, 0)


def triangle_kernel(count, present, left, *refs):
    rights, (out, right, partial, rows) = refs[:count], refs[count:]
    here, half, hidden = left.shape
    short = rights[0].shape[0]
    padded = out.shape[2]
    for s in range(count):
        right[...] = rights[s][...].astype(f32)
        rows[...] = jnp.zeros_like(rows)

        def body(j, carry):
            held = right[j]
            for i in range(here):
                product = (left[i] * held).reshape(half // 8, 8, hidden)
                partial[pl.ds(8 * i, 8), :] = jnp.sum(product, axis=0)
            total = partial[pl.ds(0, here, stride=8), :]
            for sub in range(1, 8):
                total += partial[pl.ds(sub, here, stride=8), :]
            rows[pl.ds(j, here, stride=padded), :] = total
            return carry

        lax.fori_loop(0, present[s], body, 0)
        out[s] = rows[...].astype(bf16).reshape(here, padded, hidden)


def triangle(present, left, rights, padded):
    count, (here, half, hidden) = len(rights), left.shape
    return call(
        functools.partial(triangle_kernel, count),
        "triangle",
        0.7 * count,
        [present, left, *rights],
        [SMEM] + [VMEM] * (count + 1),
        [shape_of((count, here, padded, hidden), bf16)],
        [
            pltpu.VMEM(rights[0].shape, f32),
            pltpu.VMEM((here * 8, hidden), f32),
            pltpu.VMEM((here * padded, hidden), f32),
        ],
    )[0]


def triangle_norm_kernel(where, mine, other, outs, w_out, gain, bias, grad, normed):
    count, here, padded, hidden = mine.shape
    flat = (here * padded, hidden)

    def body(s, carry):
        total = (mine[s].astype(f32) + other[s].astype(f32)).reshape(flat)
        standard, inverse = standardize(total)
        normed[s] = (standard * gain[...] + bias[...]).astype(bf16).reshape(here, padded, hidden)
        grad_norm = dot(outs[where[s]].reshape(flat), w_out[...], 1, 1)
        result = layer_norm_backward(grad_norm, standard, inverse, gain[...])
        grad[s] = result.astype(bf16).reshape(here, padded, hidden)
        return carry

    lax.fori_loop(0, count, body, 0)


def triangle_norm(where, mine, other, outs, w_out, gain, bias):
    return call(
        triangle_norm_kernel,
        "triangle_norm",
        0.4 * mine.shape[0],
        [where, mine, other, outs, w_out, gain, bias],
        [SMEM] + [VMEM] * 6,
        [shape_of(mine.shape, bf16)] * 2,
    )


def hop_kernel(picks, carried, present, left, *refs):
    count = len(picks)
    grads, refs = refs[:count], refs[count:]
    arrived, refs = refs[: count * carried], refs[count * carried :]
    outs, wide = refs[:count], refs[count]
    here, half, hidden = left.shape
    short = outs[0].shape[0]
    for s in range(count):
        wide[...] = grads[s][picks[s]].astype(f32)
        out = outs[s]

        def body(pair, carry, s=s, out=out):
            at = [jnp.minimum(2 * pair + x, short - 1) for x in range(2)]
            totals = []
            for j in at:
                total = jnp.zeros((half, hidden), f32)
                for more in range(carried):
                    total += arrived[s + more * count][j].astype(f32)
                totals.append(total)
            for i in range(here):
                held = left[i]
                for x in range(2):
                    totals[x] += wide[i, pl.ds(at[x], 1), :] * held
            for x in range(2):
                out[at[x]] = totals[x].astype(out.dtype)
            return carry

        def clear(j, carry, out=out):
            out[j] = jnp.zeros((half, hidden), out.dtype)
            return carry

        pairs = (present[s] + 1) // 2
        lax.fori_loop(0, pairs, body, 0)
        lax.fori_loop(2 * pairs, short, clear, 0)


def hop(present, left, grads, picks, arrived, short, dtype=bf16, after=()):
    here, half, hidden = left.shape
    count = len(grads)
    carried = len(arrived) // count
    return call(
        functools.partial(hop_kernel, picks, carried),
        "scatter_hop",
        0.7 * count,
        [present, left, *grads, *arrived],
        [SMEM] + [VMEM] * (1 + count + len(arrived)),
        [shape_of((short, half, hidden), dtype)] * count,
        [pltpu.VMEM(grads[0].shape[1:], f32)],
        after,
    )


def left_gradient_kernel(count, carried, present, grads, *refs):
    rights, refs = refs[:count], refs[count:]
    before, (out, right, wide) = refs[:carried], refs[carried:]
    here = out.shape[0]
    short = rights[0].shape[0]
    right[short] = jnp.zeros(right.shape[1:], f32)
    if carried:
        out[...] = before[0][...]
    else:
        out[...] = jnp.zeros_like(out)
    for s in range(count):
        right[pl.ds(0, short)] = rights[s][...].astype(f32)
        wide[...] = grads[s].astype(f32)

        def rows(t, carry):
            def add(pair, totals):
                totals = list(totals)
                for j in (2 * pair, 2 * pair + 1):
                    held = right[j]
                    for x in range(2):
                        totals[x] += wide[2 * t + x, pl.ds(j, 1), :] * held
                return tuple(totals)

            start = (out[2 * t], out[2 * t + 1])
            one, two = lax.fori_loop(0, (present[s] + 1) // 2, add, start)
            out[2 * t] = one
            out[2 * t + 1] = two
            return carry

        lax.fori_loop(0, here // 2, rows, 0)


def left_gradient(present, grads, rights, before, after=()):
    count, here = grads.shape[:2]
    short, half, hidden = rights[0].shape
    return call(
        functools.partial(left_gradient_kernel, count, len(before)),
        "left_gradient",
        0.7 * count,
        [present, grads, *rights, *before],
        [SMEM] + [VMEM] * (1 + count + len(before)),
        [shape_of((here, half, hidden), f32)],
        [pltpu.VMEM((short + 1, half, hidden), f32), pltpu.VMEM(grads.shape[1:], f32)],
        after,
    )[0]


def output_kernel(
    slot, counts, lengths, slots, normed, cotangent, grad_left, w, w_out, outs, *refs
):
    norms, (update, gradient, weights, mask, picked, flat, total) = (
        refs[: len(counts)],
        refs[len(counts) :],
    )
    here, half, hidden = normed.shape
    halves, _, padded, _ = picked.shape
    short = half // halves
    mask[...] = present_columns(lengths, slot, half)
    total[...] = jnp.zeros_like(total)
    for m in range(halves):
        low = 0
        for norm, count in zip(norms, counts):

            @pl.when((slots[m] >= low) & (slots[m] < low + count))
            def _(m=m, norm=norm, low=low):
                picked[m] = norm[slots[m] - low]

            low += count

    def body(i, carry):
        values = normed[i]
        proj = dot(values, w[...], 1, 0)
        sig_left = jax.nn.sigmoid(proj[:, :hidden])
        val_left = proj[:, hidden : 2 * hidden]
        gate = jax.nn.sigmoid(proj[:, 2 * hidden :])
        tri = picked[:, i].reshape(halves * padded, hidden)
        product = dot(tri, w_out[...], 1, 0)
        for m in range(halves):
            flat[pl.ds(m * short, short), :] = product[m * padded : m * padded + short]
        projected = flat[...]
        update[i] = (gate * projected).astype(bf16)
        grad_gate = cotangent[i].astype(f32) * projected * gate * (1.0 - gate)
        shown = mask[...] * present_row(lengths, slot, first_row(here) + i)
        masked = grad_left[i] * shown
        grads = jnp.concatenate(
            [masked * val_left * sig_left * (1.0 - sig_left), masked * sig_left, grad_gate], axis=1
        ).astype(bf16)
        gradient[i] = dot(grads, w[...], 1, 1)
        total[:, : 3 * hidden] += dot(values, grads, 0, 0)
        total[:, 3 * hidden :] += dot(tri, outs[:halves, i].reshape(halves * padded, hidden), 0, 0)
        return carry

    lax.fori_loop(0, here, body, 0)
    weights[...] = total[...].astype(bf16)


def right_gradient_kernel(slot, lengths, normed, w, own_a, own_b, *refs):
    arrived, (grads, weights, mask, total) = refs[:4], refs[4:]
    here, half, hidden = normed.shape
    short = here // 2
    mask[...] = present_columns(lengths, slot, half)
    total[...] = jnp.zeros_like(total)

    def body(t, carry):
        parts = ((own_a, arrived[:2], t), (own_b, arrived[2:], t + short))
        for own, others, j in parts:
            values = normed[j]
            proj = dot(values, w[...], 1, 0)
            sig_right = jax.nn.sigmoid(proj[:, :hidden])
            val_right = proj[:, hidden:]
            shown = mask[...] * present_row(lengths, slot, first_row(here) + j)
            masked = shown * (own[t] + others[0][t].astype(f32) + others[1][t].astype(f32))
            result = jnp.concatenate(
                [masked * val_right * sig_right * (1.0 - sig_right), masked * sig_right], axis=1
            ).astype(bf16)
            grads[j] = result
            total[...] += dot(values, result, 0, 0)
        return carry

    lax.fori_loop(0, short, body, 0)
    weights[...] = total[...].astype(bf16)


def pair_gradient_kernel(pair, grads, gradient, gain, w, out):
    def body(t, carry):
        for i in (2 * t, 2 * t + 1):
            standard, inverse = standardize(pair[i].astype(f32))
            total = gradient[i] + dot(grads[i], w[...], 1, 1)
            out[i] = layer_norm_backward(total, standard, inverse, gain[...]).astype(bf16)
        return carry

    lax.fori_loop(0, pair.shape[0] // 2, body, 0)


def shards(
    pair,
    cotangent,
    chain_lengths,
    input_norm_gain,
    input_norm_bias,
    w_in,
    output_norm_gain,
    output_norm_bias,
    w_out,
):
    here, half, channels = pair.shape
    hidden = w_out.shape[0]
    row_count = lax.axis_size("row")
    slot = here * row_count // chain_lengths.shape[0]
    order = ring_order(row_count)
    place = jnp.asarray([order.index(r) for r in range(row_count)], jnp.int32)[
        lax.axis_index("row")
    ]
    ring = jnp.asarray(order, jnp.int32)
    col = lax.axis_index("col")
    short = here // 2
    padded = (short + 15) // 16 * 16
    forward = [(order[p], order[(p + 1) % row_count]) for p in range(row_count)]
    backward = [(order[p], order[(p - 1) % row_count]) for p in range(row_count)]
    w_left, w_right = w_in[:, : 2 * hidden], w_in[:, 2 * hidden : 4 * hidden]
    w_early = jnp.concatenate([w_left, w_in[:, 4 * hidden :]], axis=1)
    in_gain, in_bias = input_norm_gain.reshape(1, -1), input_norm_bias.reshape(1, -1)
    out_gain, out_bias = output_norm_gain.reshape(1, -1), output_norm_bias.reshape(1, -1)
    block = (here, half, hidden)
    half_block = (short, half, hidden)
    mask = pltpu.VMEM((half, 128), f32)

    def ahead(x):
        return lax.ppermute(x, "row", forward)

    def behind(x):
        return lax.ppermute(x, "row", backward)

    right_a, right_b, normed = call(
        functools.partial(input_kernel, slot),
        "input_side",
        3.0,
        [chain_lengths, pair, in_gain, in_bias, w_right],
        [SMEM] + [VMEM] * 4,
        [shape_of(half_block, bf16)] * 2 + [shape_of(block, bf16)],
        [mask],
    )

    hops = row_count // 2
    chain1, chain2 = [], []
    a, b, c, d = right_a, right_b, right_b, right_a
    for step in range(hops):
        a, b = ahead(a), behind(b)
        chain1 += [a, b]
        if step < hops - 1:
            c, d = ahead(c), behind(d)
            chain2 += [c, d]

    def half_index(offset, letter):
        return ring[(place + offset + row_count) % row_count] * 2 + letter

    early_hops = hops // 2
    groups = [[right_a, right_b] + chain1[: 2 * early_hops], chain1[2 * early_hops :], chain2]
    index1 = [half_index(sign * s, x) for s in range(1, hops + 1) for sign, x in ((-1, 0), (1, 1))]
    index2 = [half_index(sign * s, x) for s in range(1, hops) for sign, x in ((-1, 1), (1, 0))]
    own = [half_index(0, 0), half_index(0, 1)]
    indices = [own + index1[: 2 * early_hops], index1[2 * early_hops :], index2]
    indices = [jnp.stack(index).astype(jnp.int32) for index in indices]
    presents = [
        jnp.clip(chain_lengths[i * short // slot] - i * short % slot, 0, short) for i in indices
    ]

    left, mine_out = call(
        functools.partial(left_kernel, slot),
        "left_side",
        4.0,
        [chain_lengths, normed, cotangent, w_early],
        [SMEM] + [VMEM] * 3,
        [shape_of(block, f32), shape_of((row_count, here, padded, hidden), bf16)],
        [mask],
    )
    outs = jnp.concatenate([mine_out, swap_col(mine_out)], axis=0)

    norms, grads = [], []
    for rights, index, present in zip(groups, indices, presents):
        partial = triangle(present, left, rights, padded)
        at = ((index // row_count) ^ col) * row_count + index % row_count
        grad, norm = triangle_norm(
            at, partial, swap_col(partial), outs, w_out, out_gain, out_bias
        )
        grads.append(grad)
        norms.append(norm)

    def group1(s):
        at = 2 * (s - 1)
        if s <= early_hops:
            return 0, [at + 2, at + 3]
        at -= 2 * early_hops
        return 1, [at, at + 1]

    def chosen(g, picks):
        return presents[g][picks[0] : picks[1] + 1]

    arrived1, arrived2 = [], []
    for s in range(hops, 0, -1):
        g, picks = group1(s)
        x, y = hop(chosen(g, picks), left, [grads[g]] * 2, picks, arrived1, short)
        arrived1 = [behind(x), ahead(y)]
        if s == hops:
            first_hop = x
    for s in range(hops - 1, 0, -1):
        picks = [2 * s - 2, 2 * s - 1]
        x, y = hop(chosen(2, picks), left, [grads[2]] * 2, picks, arrived2, short)
        arrived2 = [behind(x), ahead(y)]

    own_a, own_b = hop(
        presents[0][:2], left, [grads[0]] * 2, [0, 1], [], short, f32, after=[first_hop]
    )
    before = []
    for g, rights, present in zip(grads, groups, presents):
        before = [left_gradient(present, g, rights, before, after=[first_hop])]
    flat_index = jnp.concatenate(indices)
    wanted = col * row_count + jnp.arange(row_count, dtype=jnp.int32)
    slots = jnp.argmax(flat_index[None, :] == wanted[:, None], axis=1).astype(jnp.int32)
    update, gradient, early = call(
        functools.partial(output_kernel, slot, [len(g) for g in groups]),
        "output_side",
        6.0,
        [chain_lengths, slots, normed, cotangent, before[0], w_early, w_out, outs, *norms],
        [SMEM] * 2 + [VMEM] * 9,
        [
            shape_of(block, bf16),
            shape_of(block, f32),
            shape_of((channels, 4 * hidden), bf16),
        ],
        [
            mask,
            pltpu.VMEM((row_count, here, padded, hidden), bf16),
            pltpu.VMEM((half, hidden), f32),
            pltpu.VMEM((channels, 4 * hidden), f32),
        ],
    )
    summed_early = sum_all(early, row_count).astype(f32)

    late, weights = call(
        functools.partial(right_gradient_kernel, slot),
        "right_gradient",
        3.0,
        [chain_lengths, normed, w_right, own_a, own_b]
        + [arrived1[0], arrived2[1], arrived1[1], arrived2[0]],
        [SMEM] + [VMEM] * 8,
        [
            shape_of((here, half, 2 * hidden), bf16),
            shape_of((channels, 2 * hidden), bf16),
        ],
        [mask, pltpu.VMEM((channels, 2 * hidden), f32)],
    )
    summed_late = sum_all(weights, row_count).astype(f32)
    (pair_gradient,) = call(
        pair_gradient_kernel,
        "pair_gradient",
        3.0,
        [pair, late, gradient, in_gain, w_right],
        [VMEM] * 5,
        [shape_of(block, bf16)],
    )
    grad_w_in = jnp.concatenate(
        [summed_early[:, : 2 * hidden], summed_late, summed_early[:, 2 * hidden : 3 * hidden]],
        axis=1,
    )
    grad_w_out = summed_early[:, 3 * hidden :]
    return (update, pair_gradient, grad_w_in, grad_w_out)


def solution(mesh):
    placed = (
        P(("grp", "row"), "col", None),
        P(("grp", "row"), "col", None),
        P("grp"),
        P(),
        P(),
        P(),
        P(),
        P(),
        P(),
    )
    return jax.shard_map(
        shards,
        mesh=mesh,
        in_specs=placed,
        out_specs=(
            P(("grp", "row"), "col", None),
            P(("grp", "row"), "col", None),
            P("grp", None),
            P("grp", None),
        ),
        check_vma=False,
    )
```

time: 335 us -> 180 us (0.54)
  waiting for transfers between devices: 170 us -> 31 us
  Pallas kernels: 0 us -> 87.7 us
  blocking collectives: 66.4 us -> 0 us
  starting transfers between devices: 0.16 us -> 34.3 us
  matrix products: 30.6 us -> 0 us
  other arithmetic: 27.7 us -> 1.95 us
  local copies, waits for them, and re-layouts: 25.4 us -> 11.3 us
    pallas_call x0 -> x22, Pallas kernels: none -> 87.7 us  [call(): pl.pallas_call(body, out_shape=list(outs), in_specs=list(specs) + [ANY] *...]
    psum x1 -> x0, waiting for transfers between devices: 84.4 us -> none  [shards(): lax.psum(local_w_in.astype(jnp.bfloat16), ('row', 'col'))]
    all_gather x1 -> x0, waiting for transfers between devices: 72.9 us -> none  [shards(): lax.all_gather(right_proj, 'row', axis=0, tiled=True)]
    psum x1 -> x0, blocking collectives: 63.7 us -> none  [shards(): lax.psum(local_w_out.astype(jnp.bfloat16), ('row', 'col'))]
    ppermute x0 -> x40, starting transfers between devices: none -> 34.3 us  [the longest x14 16.1 us: ahead(): return lax.ppermute(x, 'row', forward)]
    ppermute x0 -> x40, waiting for transfers between devices: none -> 31 us  [the longest x14 15 us: ahead(): return lax.ppermute(x, 'row', forward)]
    dot_general x9 -> x0, matrix products: 30.6 us -> none  [the longest x1 5.73 us: shards(): jnp.einsum('ikh,jkh->ijh', left_proj, lax.all_gather(right_proj, 'row', a...]
    reduce_scatter x2 -> x0, waiting for transfers between devices: 12.3 us -> none  [the longest x1 7.06 us: shards(): lax.psum_scatter(partial_tri.astype(jnp.bfloat16), 'col', scatter_dimensi...]
  transfers between devices with their start and end apart: 4 -> 40, of which waited for: 4 -> 14; matrix products, arithmetic and copies ran while one was open for 5% -> 4% of each run, Pallas kernels for 0% -> 46%
where the time goes in v3:
time: 180 us; the launch traced here: 179 us
  Pallas kernels  87.7 us (49%)
  starting transfers between devices  34.3 us (19%)
  waiting for transfers between devices  31 us (17%)
  between operations  12.7 us (7%)
  local copies, waits for them, and re-layouts  11.3 us (6%)
  other arithmetic  1.95 us (1%)
    pallas_call x22, Pallas kernels, call(): pl.pallas_call(body, out_shape=list(outs), in_specs=list(specs) + [ANY] *...  87.7 us
    ppermute x14, starting transfers between devices, ahead(): return lax.ppermute(x, 'row', forward)  16.1 us
    ppermute x14, waiting for transfers between devices, ahead(): return lax.ppermute(x, 'row', forward)  15 us
    ppermute x14, starting transfers between devices, behind(): return lax.ppermute(x, 'row', backward)  13.9 us
    ppermute x6, waiting for transfers between devices, sum_all(): lax.ppermute(x, 'row', [(r, r ^ step) for r in range(row_count)])  10.8 us
    unnamed x37, local copies, waits for them, and re-layouts  4.39 us
    ppermute x14, waiting for transfers between devices, behind(): return lax.ppermute(x, 'row', backward)  4.12 us
    ppermute x6, starting transfers between devices, sum_all(): lax.ppermute(x, 'row', [(r, r ^ step) for r in range(row_count)])  3.92 us
  transfers between devices with their start and end apart: 40, of which 14 were waited for; matrix products, arithmetic and copies ran while one was open for 4% of the time, Pallas kernels for 46%

profile of v3, /device:TPU:0, one launch (start us, length us, event | category | flops | bytes accessed | tf_op | source)
XLA Modules:
  0.0 178.9 jit_solution(11788910692184707119)
XLA Ops:
  0.6 0.9 fusion.15
  1.5 0.6 copy-done
  2.2 1.0 copy-done.3
  3.2 0.7 copy-done.6
  3.9 0.7 copy-done.9
  4.5 5.0 %input_side.1 = (bf16[11,88,128]{2,1,0:T(8,128)(2,1)}, bf16[11,88,128]{2,1,0:T(8,128)(2,1)}, bf16[22,88,128]{2,1,0:T(8,128)(2,1)S(1)}) custom-call(s32[8]{0:T(128)S(1)} %copy-done, bf16[22,88,128]{2,1,0:T(8,128)(2,1)S(1)} %copy-done.3, f32[1,128]{1,0:T(1,128)S(1)} %bitcast.42, f32[1,128]{1,0:T(1,128)S(1)} %bitcast.35, ...), custom_call_target="tpu_custom_call" | custom-call | flops 3300000000 | bytes 1048576 | tf_op jit(solution)/shard_map/input_side/pallas_call | solution.py:66
  9.5 3.0 %collective-permute-start.1 = (bf16[11,88,128]{2,1,0:T(8,128)(2,1)}, bf16[11,88,128]{2,1,0:T(8,128)(2,1)S(1)}, u32[]{:S(2)}, u32[]{:S(2)}) collective-permute-start(bf16[11,88,128]{2,1,0:T(8,128)(2,1)} %get-tuple-element.41.refs_2_), channel_id=1, source_target_pairs={{0,2},{4,0},{8,4},{12,8},{14,12},{10,14},{6,10},{2,6},{1,3},{5,1},... | collective-permute-start | bytes 743432 | tf_op jit(solution)/shard_map/ppermute | solution.py:432
  12.6 2.0 %collective-permute-start = (bf16[11,88,128]{2,1,0:T(8,128)(2,1)}, bf16[11,88,128]{2,1,0:T(8,128)(2,1)S(1)}, u32[]{:S(2)}, u32[]{:S(2)}) collective-permute-start(bf16[11,88,128]{2,1,0:T(8,128)(2,1)} %get-tuple-element.40.refs_3_), channel_id=1, source_target_pairs={{0,4},{4,8},{8,12},{12,14},{14,10},{10,6},{6,2},{2,0},{1,5},{5,9},... | collective-permute-start | bytes 743432 | tf_op jit(solution)/shard_map/ppermute | solution.py:429
  14.7 4.4 %left_side.1 = (f32[22,88,128]{2,1,0:T(8,128)S(1)}, bf16[8,22,16,128]{3,2,1,0:T(8,128)(2,1)S(1)}) custom-call(s32[8]{0:T(128)S(1)} %copy-done.1, bf16[22,88,128]{2,1,0:T(8,128)(2,1)S(1)} %get-tuple-element.38.refs_1_.refs_2_, bf16[22,88,128]{2,1,0:T(8,128)(2,1)S(1)} %copy-done.2, bf16[128,384]{1,0:T(8,128)(2,1)S(1)} %pad_maximum_fusion.1.refs_3_.refs_5_), custom_call_target="tpu_custom_call" | custom-call | flops 4400000000 | bytes 1048576 | tf_op jit(solution)/shard_map/left_side/pallas_call | solution.py:66
  19.2 0.7 dynamic_slice.37
  25.9 0.7 fusion.19
  32.3 0.6 gather_fusion
  35.1 2.0 %collective-permute-start.2 = (bf16[11,88,128]{2,1,0:T(8,128)(2,1)S(1)}, bf16[11,88,128]{2,1,0:T(8,128)(2,1)}, u32[]{:S(2)}, u32[]{:S(2)}) collective-permute-start(bf16[11,88,128]{2,1,0:T(8,128)(2,1)S(1)} %collective-permute-done.refs_2_), channel_id=1, source_target_pairs={{0,4},{4,8},{8,12},{12,14},{14,10},{10,6},{6,2},{2,0},{1,5},{5,9},... | collective-permute-start | bytes 743432 | tf_op jit(solution)/shard_map/ppermute | solution.py:429
  37.1 2.0 %collective-permute-start.9 = (bf16[11,88,128]{2,1,0:T(8,128)(2,1)}, bf16[11,88,128]{2,1,0:T(8,128)(2,1)}, u32[]{:S(2)}, u32[]{:S(2)}) collective-permute-start(bf16[11,88,128]{2,1,0:T(8,128)(2,1)} %collective-permute-done.8.refs_4_), channel_id=1, source_target_pairs={{0,4},{4,8},{8,12},{12,14},{14,10},{10,6},{6,2},{2,0},{1,5},{5,9},... | collective-permute-start | bytes 743432 | tf_op jit(solution)/shard_map/ppermute | solution.py:429
  39.3 0.7 iota_reduce_fusion
  40.0 4.0 %collective-permute-done.2.refs_4_ = bf16[11,88,128]{2,1,0:T(8,128)(2,1)} collective-permute-done((bf16[11,88,128]{2,1,0:T(8,128)(2,1)S(1)}, bf16[11,88,128]{2,1,0:T(8,128)(2,1)}, u32[]{:S(2)}, u32[]{:S(2)}) %collective-permute-start.2) | collective-permute-done | bytes 247840 | tf_op jit(solution)/shard_map/ppermute | solution.py:429
  44.0 2.0 %collective-permute-start.4 = (bf16[11,88,128]{2,1,0:T(8,128)(2,1)}, bf16[11,88,128]{2,1,0:T(8,128)(2,1)S(1)}, u32[]{:S(2)}, u32[]{:S(2)}) collective-permute-start(bf16[11,88,128]{2,1,0:T(8,128)(2,1)} %collective-permute-done.2.refs_4_), channel_id=1, source_target_pairs={{0,4},{4,8},{8,12},{12,14},{14,10},{10,6},{6,2},{2,0},{1,5},{5,9},... | collective-permute-start | bytes 743432 | tf_op jit(solution)/shard_map/ppermute | solution.py:429
  46.1 3.2 %collective-permute-done.9.refs_6_ = bf16[11,88,128]{2,1,0:T(8,128)(2,1)} collective-permute-done((bf16[11,88,128]{2,1,0:T(8,128)(2,1)}, bf16[11,88,128]{2,1,0:T(8,128)(2,1)}, u32[]{:S(2)}, u32[]{:S(2)}) %collective-permute-start.9) | collective-permute-done | bytes 247840 | tf_op jit(solution)/shard_map/ppermute | solution.py:429
  49.3 2.0 %collective-permute-start.10 = (bf16[11,88,128]{2,1,0:T(8,128)(2,1)}, bf16[11,88,128]{2,1,0:T(8,128)(2,1)S(1)}, u32[]{:S(2)}, u32[]{:S(2)}) collective-permute-start(bf16[11,88,128]{2,1,0:T(8,128)(2,1)} %collective-permute-done.9.refs_6_), channel_id=1, source_target_pairs={{0,4},{4,8},{8,12},{12,14},{14,10},{10,6},{6,2},{2,0},{1,5},{5,9},... | collective-permute-start | bytes 743432 | tf_op jit(solution)/shard_map/ppermute | solution.py:429
  51.4 1.2 copy-done.12
  52.6 5.6 %triangle.5.refs_1_ = bf16[6,22,16,128]{3,2,1,0:T(8,128)(2,1)S(1)} custom-call(s32[6]{0:T(128)S(1)} %get-tuple-element.85.refs_0_, f32[22,88,128]{2,1,0:T(8,128)S(1)} %copy-done.12, bf16[11,88,128]{2,1,0:T(8,128)(2,1)} %get-tuple-element.41.refs_2_, bf16[11,88,128]{2,1,0:T(8,128)(2,1)} %get-tuple-element.40.refs_3_, ...), custom_call_target="tpu_custom_call" | custom-call | flops 4619999744 | bytes 1048576 | tf_op jit(solution)/shard_map/triangle/pallas_call | solution.py:66
  58.3 1.2 collective-permute-done.10.refs_2_
  59.5 1.8 %collective-permute-start.14 = (bf16[11,88,128]{2,1,0:T(8,128)(2,1)S(1)}, bf16[11,88,128]{2,1,0:T(8,128)(2,1)S(1)}, u32[]{:S(2)}, u32[]{:S(2)}) collective-permute-start(bf16[11,88,128]{2,1,0:T(8,128)(2,1)S(1)} %collective-permute-done.10.refs_2_), channel_id=1, source_target_pairs={{0,4},{4,8},{8,12},{12,14},{14,10},{10,6},{6,2},{2,0},{1,5},{5,9},... | collective-permute-start | bytes 743432 | tf_op jit(solution)/shard_map/ppermute | solution.py:429
  61.5 6.1 %triangle.3.refs_1_ = bf16[6,22,16,128]{3,2,1,0:T(8,128)(2,1)S(1)} custom-call(s32[6]{0:T(128)S(1)} %get-tuple-element.87.refs_0_, f32[22,88,128]{2,1,0:T(8,128)S(1)} %copy-done.12, bf16[11,88,128]{2,1,0:T(8,128)(2,1)S(1)} %collective-permute-done.refs_2_, bf16[11,88,128]{2,1,0:T(8,128)(2,1)S(1)} %collective-permute-done.1.refs_3_, ...), custom_call_target="tpu_custom_call" | custom-call | flops 4619999744 | bytes 1048576 | tf_op jit(solution)/shard_map/triangle/pallas_call | solution.py:66
  67.7 1.3 constant_dynamic-update-slice_fusion.refs_3_.refs_7_
  69.4 4.3 %triangle.4.refs_1_ = bf16[4,22,16,128]{3,2,1,0:T(8,128)(2,1)S(1)} custom-call(s32[4]{0:T(128)S(1)} %fusion.12.refs_0_, f32[22,88,128]{2,1,0:T(8,128)S(1)} %copy-done.13, bf16[11,88,128]{2,1,0:T(8,128)(2,1)S(1)} %collective-permute-done.10.refs_2_, bf16[11,88,128]{2,1,0:T(8,128)(2,1)S(1)} %collective-permute-done.13.refs_3_, ...), custom_call_target="tpu_custom_call" | custom-call | flops 3080000000 | bytes 1048576 | tf_op jit(solution)/shard_map/triangle/pallas_call | solution.py:66
  73.9 2.5 %triangle_norm.5 = (bf16[6,22,16,128]{3,2,1,0:T(8,128)(2,1)S(1)}, bf16[6,22,16,128]{3,2,1,0:T(8,128)(2,1)S(1)}) custom-call(s32[6]{0:T(128)S(1)} %get-tuple-element.84.refs_0_, bf16[6,22,16,128]{3,2,1,0:T(8,128)(2,1)S(1)} %triangle.5.refs_1_, bf16[6,22,16,128]{3,2,1,0:T(8,128)(2,1)S(1)} %collective-permute-done.17.refs_2_, ...), custom_call_target="tpu_custom_call" | custom-call | flops 2640000000 | bytes 1048576 | tf_op jit(solution)/shard_map/triangle_norm/pallas_call | solution.py:66
  76.5 2.5 %triangle_norm.3 = (bf16[6,22,16,128]{3,2,1,0:T(8,128)(2,1)S(1)}, bf16[6,22,16,128]{3,2,1,0:T(8,128)(2,1)S(1)}) custom-call(s32[6]{0:T(128)S(1)} %get-tuple-element.86.refs_0_, bf16[6,22,16,128]{3,2,1,0:T(8,128)(2,1)S(1)} %triangle.3.refs_1_, bf16[6,22,16,128]{3,2,1,0:T(8,128)(2,1)S(1)} %collective-permute-done.6.refs_2_, ...), custom_call_target="tpu_custom_call" | custom-call | flops 2640000000 | bytes 1048576 | tf_op jit(solution)/shard_map/triangle_norm/pallas_call | solution.py:66
  79.0 2.1 %scatter_hop.13 = (bf16[11,88,128]{2,1,0:T(8,128)(2,1)S(1)}, bf16[11,88,128]{2,1,0:T(8,128)(2,1)S(1)}) custom-call(s32[2]{0:T(128)S(1)} %get-tuple-element.76.refs_0_, f32[22,88,128]{2,1,0:T(8,128)S(1)} %copy-done.13, bf16[6,22,16,128]{3,2,1,0:T(8,128)(2,1)S(1)} %get-tuple-element.43.refs_1_.refs_2_.refs_3_, ...), custom_call_target="tpu_custom_call" | custom-call | flops 1540000000 | bytes 1048576 | tf_op jit(solution)/shard_map/scatter_hop/pallas_call | solution.py:66
  81.1 2.2 %collective-permute-start.25 = (bf16[11,88,128]{2,1,0:T(8,128)(2,1)S(1)}, bf16[11,88,128]{2,1,0:T(8,128)(2,1)S(1)}, u32[]{:S(2)}, u32[]{:S(2)}) collective-permute-start(bf16[11,88,128]{2,1,0:T(8,128)(2,1)S(1)} %get-tuple-element.59), channel_id=1, source_target_pairs={{0,2},{4,0},{8,4},{12,8},{14,12},{10,14},{6,10},{2,6},{1,3},{5,1},... | collective-permute-start | bytes 743432 | tf_op jit(solution)/shard_map/ppermute | solution.py:432
  83.3 1.9 %triangle_norm.4 = (bf16[4,22,16,128]{3,2,1,0:T(8,128)(2,1)S(1)}, bf16[4,22,16,128]{3,2,1,0:T(8,128)(2,1)S(1)}) custom-call(s32[4]{0:T(128)S(1)} %get-tuple-element.70.refs_0_, bf16[4,22,16,128]{3,2,1,0:T(8,128)(2,1)S(1)} %triangle.4.refs_1_, bf16[4,22,16,128]{3,2,1,0:T(8,128)(2,1)S(1)} %collective-permute-done.16.refs_2_, ...), custom_call_target="tpu_custom_call" | custom-call | flops 1760000000 | bytes 1048576 | tf_op jit(solution)/shard_map/triangle_norm/pallas_call | solution.py:66
  85.2 2.4 %scatter_hop.8 = (bf16[11,88,128]{2,1,0:T(8,128)(2,1)S(1)}, bf16[11,88,128]{2,1,0:T(8,128)(2,1)S(1)}) custom-call(s32[2]{0:T(128)S(1)} %get-tuple-element.80.refs_0_, f32[22,88,128]{2,1,0:T(8,128)S(1)} %copy-done.13, bf16[4,22,16,128]{3,2,1,0:T(8,128)(2,1)S(1)} %get-tuple-element.44.refs_2_.refs_3_.refs_1_, ...), custom_call_target="tpu_custom_call" | custom-call | flops 1540000000 | bytes 1048576 | tf_op jit(solution)/shard_map/scatter_hop/pallas_call | solution.py:66
  87.6 1.6 collective-permute-start.18
  89.7 7.7 %left_gradient.3.refs_6_ = f32[22,88,128]{2,1,0:T(8,128)S(1)} custom-call(s32[6]{0:T(128)S(1)} %get-tuple-element.85.refs_0_, bf16[6,22,16,128]{3,2,1,0:T(8,128)(2,1)S(1)} %get-tuple-element.45.refs_1_.refs_2_.refs_3_, bf16[11,88,128]{2,1,0:T(8,128)(2,1)} %get-tuple-element.41.refs_2_, bf16[11,88,128]{2,1,0:T(8,128)(2,1)} %get-tuple-element.40.refs_3_, ...), custom_call_target="tpu_custom_call" | custom-call | flops 4619999744 | bytes 1048576 | tf_op jit(solution)/shard_map/left_gradient/pallas_call | solution.py:66
  97.4 5.8 %left_gradient.4.refs_8_ = f32[22,88,128]{2,1,0:T(8,128)S(1)} custom-call(s32[4]{0:T(128)S(1)} %fusion.12.refs_0_, bf16[4,22,16,128]{3,2,1,0:T(8,128)(2,1)S(1)} %get-tuple-element.44.refs_2_.refs_3_.refs_1_, bf16[11,88,128]{2,1,0:T(8,128)(2,1)S(1)} %collective-permute-done.10.refs_2_, bf16[11,88,128]{2,1,0:T(8,128)(2,1)S(1)} %collective-permute-done.13.refs_3_, ...), custom_call_target="tpu_custom_call" | custom-call | flops 3080000000 | bytes 1048576 | tf_op jit(solution)/shard_map/left_gradient/pallas_call | solution.py:66
  103.3 8.3 %left_gradient.5.refs_4_ = f32[22,88,128]{2,1,0:T(8,128)S(1)} custom-call(s32[6]{0:T(128)S(1)} %get-tuple-element.87.refs_0_, bf16[6,22,16,128]{3,2,1,0:T(8,128)(2,1)S(1)} %get-tuple-element.43.refs_1_.refs_2_.refs_3_, bf16[11,88,128]{2,1,0:T(8,128)(2,1)S(1)} %collective-permute-done.refs_2_, bf16[11,88,128]{2,1,0:T(8,128)(2,1)S(1)} %collective-permute-done.1.refs_3_, ...), custom_call_target="tpu_custom_call" | custom-call | flops 4619999744 | bytes 1048576 | tf_op jit(solution)/shard_map/left_gradient/pallas_call | solution.py:66
  111.6 2.0 %scatter_hop.10 = (bf16[11,88,128]{2,1,0:T(8,128)(2,1)S(1)}, bf16[11,88,128]{2,1,0:T(8,128)(2,1)S(1)}) custom-call(s32[2]{0:T(128)S(1)} %get-tuple-element.79.refs_0_, f32[22,88,128]{2,1,0:T(8,128)S(1)} %copy-done.13, bf16[4,22,16,128]{3,2,1,0:T(8,128)(2,1)S(1)} %get-tuple-element.44.refs_2_.refs_3_.refs_1_, ...), custom_call_target="tpu_custom_call" | custom-call | flops 1540000000 | bytes 1048576 | tf_op jit(solution)/shard_map/scatter_hop/pallas_call | solution.py:66
  113.6 1.5 collective-permute-start.20
  115.7 9.2 %output_side.1 = (bf16[22,88,128]{2,1,0:T(8,128)(2,1)}, f32[22,88,128]{2,1,0:T(8,128)S(1)}, bf16[128,512]{1,0:T(8,128)(2,1)S(1)}) custom-call(s32[8]{0:T(128)S(1)} %copy-done.1, s32[8]{0:T(128)S(1)} %get-tuple-element.37.refs_1_, bf16[22,88,128]{2,1,0:T(8,128)(2,1)S(1)} %copy-done.15, bf16[22,88,128]{2,1,0:T(8,128)(2,1)S(1)} %copy-done.2, ...), custom_call_target="tpu_custom_call" | custom-call | flops 6600000000 | bytes 1048576 | tf_op jit(solution)/shard_map/output_side/pallas_call | solution.py:66
  124.9 2.1 %scatter_hop.14 = (bf16[11,88,128]{2,1,0:T(8,128)(2,1)S(1)}, bf16[11,88,128]{2,1,0:T(8,128)(2,1)S(1)}) custom-call(s32[2]{0:T(128)S(1)} %get-tuple-element.77.refs_0_, f32[22,88,128]{2,1,0:T(8,128)S(1)} %copy-done.13, bf16[6,22,16,128]{3,2,1,0:T(8,128)(2,1)S(1)} %get-tuple-element.43.refs_1_.refs_2_.refs_3_, ...), custom_call_target="tpu_custom_call" | custom-call | flops 1540000000 | bytes 1048576 | tf_op jit(solution)/shard_map/scatter_hop/pallas_call | solution.py:66
  127.0 1.5 collective-permute-start.27
  129.1 1.8 %scatter_hop.11 = (bf16[11,88,128]{2,1,0:T(8,128)(2,1)S(1)}, bf16[11,88,128]{2,1,0:T(8,128)(2,1)S(1)}) custom-call(s32[2]{0:T(128)S(1)} %get-tuple-element.81.refs_0_, f32[22,88,128]{2,1,0:T(8,128)S(1)} %copy-done.13, bf16[6,22,16,128]{3,2,1,0:T(8,128)(2,1)S(1)} %get-tuple-element.45.refs_1_.refs_2_.refs_3_, ...), custom_call_target="tpu_custom_call" | custom-call | flops 1540000000 | bytes 1048576 | tf_op jit(solution)/shard_map/scatter_hop/pallas_call | solution.py:66
  130.9 1.5 collective-permute-start.22
  133.0 1.5 collective-permute-start.33
  134.5 1.3 collective-permute-done.27.refs_4_
  135.8 1.5 collective-permute-done.28.refs_5_
  137.3 1.8 %scatter_hop.15 = (bf16[11,88,128]{2,1,0:T(8,128)(2,1)S(1)}, bf16[11,88,128]{2,1,0:T(8,128)(2,1)S(1)}) custom-call(s32[2]{0:T(128)S(1)} %get-tuple-element.78.refs_0_, f32[22,88,128]{2,1,0:T(8,128)S(1)} %copy-done.13, bf16[6,22,16,128]{3,2,1,0:T(8,128)(2,1)S(1)} %get-tuple-element.43.refs_1_.refs_2_.refs_3_, ...), custom_call_target="tpu_custom_call" | custom-call | flops 1540000000 | bytes 1048576 | tf_op jit(solution)/shard_map/scatter_hop/pallas_call | solution.py:66
  139.6 1.6 collective-permute-start.31
  141.2 1.4 collective-permute-done.23.refs_5_
  142.6 1.8 %scatter_hop.12 = (bf16[11,88,128]{2,1,0:T(8,128)(2,1)S(1)}, bf16[11,88,128]{2,1,0:T(8,128)(2,1)S(1)}) custom-call(s32[2]{0:T(128)S(1)} %get-tuple-element.82.refs_0_, f32[22,88,128]{2,1,0:T(8,128)S(1)} %copy-done.13, bf16[6,22,16,128]{3,2,1,0:T(8,128)(2,1)S(1)} %get-tuple-element.45.refs_1_.refs_2_.refs_3_, ...), custom_call_target="tpu_custom_call" | custom-call | flops 1540000000 | bytes 1048576 | tf_op jit(solution)/shard_map/scatter_hop/pallas_call | solution.py:66
  144.5 0.7 collective-permute-start.24
  145.2 1.3 collective-permute-start.30
  146.5 1.8 %scatter_hop.9 = (f32[11,88,128]{2,1,0:T(8,128)S(1)}, f32[11,88,128]{2,1,0:T(8,128)S(1)}) custom-call(s32[2]{0:T(128)S(1)} %get-tuple-element.83.refs_0_, f32[22,88,128]{2,1,0:T(8,128)S(1)} %copy-done.13, bf16[6,22,16,128]{3,2,1,0:T(8,128)(2,1)S(1)} %get-tuple-element.45.refs_1_.refs_2_.refs_3_, ...), custom_call_target="tpu_custom_call" | custom-call | flops 1540000000 | bytes 1048576 | tf_op jit(solution)/shard_map/scatter_hop/pallas_call | solution.py:66
  148.4 0.8 collective-permute-start.34
  149.2 1.5 collective-permute-done.29.refs_6_
  150.7 2.4 %collective-permute-done.24.refs_5_ = bf16[11,88,128]{2,1,0:T(8,128)(2,1)S(1)} collective-permute-done((bf16[11,88,128]{2,1,0:T(8,128)(2,1)S(1)}, bf16[11,88,128]{2,1,0:T(8,128)(2,1)S(1)}, u32[]{:S(2)}, u32[]{:S(2)}) %collective-permute-start.24) | collective-permute-done | bytes 247840 | tf_op jit(solution)/shard_map/ppermute | solution.py:432
  153.1 2.2 %collective-permute-done.30.refs_7_ = bf16[11,88,128]{2,1,0:T(8,128)(2,1)S(1)} collective-permute-done((bf16[11,88,128]{2,1,0:T(8,128)(2,1)S(1)}, bf16[11,88,128]{2,1,0:T(8,128)(2,1)S(1)}, u32[]{:S(2)}, u32[]{:S(2)}) %collective-permute-start.30) | collective-permute-done | bytes 247840 | tf_op jit(solution)/shard_map/ppermute | solution.py:429
  155.3 4.4 %right_gradient.1 = (bf16[22,88,256]{2,1,0:T(8,128)(2,1)S(1)}, bf16[128,256]{1,0:T(8,128)(2,1)S(1)}) custom-call(s32[8]{0:T(128)S(1)} %copy-done.1, bf16[22,88,128]{2,1,0:T(8,128)(2,1)S(1)} %copy-done.15, bf16[128,256]{1,0:T(8,128)(2,1)S(1)} %get-tuple-element.75.refs_4_.refs_2_, f32[11,88,128]{2,1,0:T(8,128)S(1)} %get-tuple-element.51.refs_3_, ...), custom_call_target="tpu_custom_call" | custom-call | flops 3300000000 | bytes 1048576 | tf_op jit(solution)/shard_map/right_gradient/pallas_call | solution.py:66
  160.0 1.1 collective-permute-done.36
  161.5 6.7 %collective-permute-done.35 = bf16[128,512]{1,0:T(8,128)(2,1)S(1)} collective-permute-done((bf16[128,512]{1,0:T(8,128)(2,1)S(1)}, bf16[128,512]{1,0:T(8,128)(2,1)S(1)}, u32[]{:S(2)}, u32[]{:S(2)}) %collective-permute-start.35) | collective-permute-done | bytes 131104 | tf_op jit(solution)/shard_map/ppermute | solution.py:53
  169.0 3.6 %collective-permute-done.38 = bf16[128,256]{1,0:T(8,128)(2,1)S(1)} collective-permute-done((bf16[128,256]{1,0:T(8,128)(2,1)S(1)}, bf16[128,256]{1,0:T(8,128)(2,1)S(1)}, u32[]{:S(2)}, u32[]{:S(2)}) %collective-permute-start.38) | collective-permute-done | bytes 65568 | tf_op jit(solution)/shard_map/ppermute | solution.py:53
  172.6 1.1 collective-permute-start.39
  173.8 3.9 %pair_gradient.1 = bf16[22,88,128]{2,1,0:T(8,128)(2,1)} custom-call(bf16[22,88,128]{2,1,0:T(8,128)(2,1)S(1)} %copy-done.4, bf16[22,88,256]{2,1,0:T(8,128)(2,1)S(1)} %get-tuple-element.66.refs_1_, f32[22,88,128]{2,1,0:T(8,128)S(1)} %get-tuple-element.67.refs_2_, f32[1,128]{1,0:T(1,128)S(1)} %bitcast.43, bf16[128,256]{1,0:T(8,128)(2,1)S(1)} %get-tuple-element.75.refs_4_.refs_2_), custom_call_target="tpu_custom_call" | custom-call | flops 3300000000 | bytes 1048576 | tf_op jit(solution)/shard_map/pair_gradient/pallas_call | solution.py:66
  178.2 0.7 pad_maximum_fusion
  (115 shorter events, 8.3 us)
Async XLA Ops:
  1.5 0.7 copy-start
  2.2 1.0 copy-start.3
  3.2 0.7 copy-start.6
  3.9 0.7 copy-start.9
  4.5 10.1 %slice-start = ((bf16[128,640]{1,0:T(8,128)(2,1)}), bf16[128,128]{1,0:T(8,128)(2,1)S(1)}, s32[]{:S(2)}) async-start(bf16[128,640]{1,0:T(8,128)(2,1)} %param.16), calls=%async_computation | async-start | bytes 65536 | tf_op jit(solution)/shard_map/slice | solution.py:421
  4.5 10.1 %copy-start.1 = (s32[8]{0:T(128)S(1)}, s32[8]{0:T(128)}, u32[]{:S(2)}) copy-start(s32[8]{0:T(128)} %refs_0_.8) | copy-start | bytes 100
  4.5 10.1 %copy-start.2 = (bf16[22,88,128]{2,1,0:T(8,128)(2,1)S(1)}, bf16[22,88,128]{2,1,0:T(8,128)(2,1)}, u32[]{:S(2)}) copy-start(bf16[22,88,128]{2,1,0:T(8,128)(2,1)} %refs_3_.1) | copy-start | bytes 1486852
  9.5 9.5 %copy-start.14 = (bf16[22,88,128]{2,1,0:T(8,128)(2,1)}, bf16[22,88,128]{2,1,0:T(8,128)(2,1)S(1)}, u32[]{:S(2)}) copy-start(bf16[22,88,128]{2,1,0:T(8,128)(2,1)S(1)} %get-tuple-element.38.refs_1_.refs_2_) | copy-start | bytes 1486852
  9.5 27.6 %collective-permute-start.1 = (bf16[11,88,128]{2,1,0:T(8,128)(2,1)}, bf16[11,88,128]{2,1,0:T(8,128)(2,1)S(1)}, u32[]{:S(2)}, u32[]{:S(2)}) collective-permute-start(bf16[11,88,128]{2,1,0:T(8,128)(2,1)} %get-tuple-element.41.refs_2_), channel_id=1, source_target_pairs={{0,2},{4,0},{8,4},{12,8},{14,12},{10,14},{6,10},{2,6},{1,3},{5,1},... | collective-permute-start | bytes 743432 | tf_op jit(solution)/shard_map/ppermute | solution.py:432
  12.5 24.6 %collective-permute-start.8 = (bf16[11,88,128]{2,1,0:T(8,128)(2,1)}, bf16[11,88,128]{2,1,0:T(8,128)(2,1)}, u32[]{:S(2)}, u32[]{:S(2)}) collective-permute-start(bf16[11,88,128]{2,1,0:T(8,128)(2,1)} %get-tuple-element.41.refs_2_), channel_id=1, source_target_pairs={{0,4},{4,8},{8,12},{12,14},{14,10},{10,6},{6,2},{2,0},{1,5},{5,9},... | collective-permute-start | bytes 743432 | tf_op jit(solution)/shard_map/ppermute | solution.py:429
  12.6 22.5 %collective-permute-start = (bf16[11,88,128]{2,1,0:T(8,128)(2,1)}, bf16[11,88,128]{2,1,0:T(8,128)(2,1)S(1)}, u32[]{:S(2)}, u32[]{:S(2)}) collective-permute-start(bf16[11,88,128]{2,1,0:T(8,128)(2,1)} %get-tuple-element.40.refs_3_), channel_id=1, source_target_pairs={{0,4},{4,8},{8,12},{12,14},{14,10},{10,6},{6,2},{2,0},{1,5},{5,9},... | collective-permute-start | bytes 743432 | tf_op jit(solution)/shard_map/ppermute | solution.py:429
  14.6 24.6 %collective-permute-start.11 = (bf16[11,88,128]{2,1,0:T(8,128)(2,1)}, bf16[11,88,128]{2,1,0:T(8,128)(2,1)}, u32[]{:S(2)}, u32[]{:S(2)}) collective-permute-start(bf16[11,88,128]{2,1,0:T(8,128)(2,1)} %get-tuple-element.40.refs_3_), channel_id=1, source_target_pairs={{0,2},{4,0},{8,4},{12,8},{14,12},{10,14},{6,10},{2,6},{1,3},{5,1},... | collective-permute-start | bytes 743432 | tf_op jit(solution)/shard_map/ppermute | solution.py:432
  14.6 4.5 %copy-start.17 = (s32[8]{0:T(128)S(1)}, s32[8]{0:T(128)}, u32[]{:S(2)}) copy-start(s32[8]{0:T(128)} %constant.212.clone) | copy-start | bytes 100
  14.6 11.3 %copy-start.16 = (s32[8]{0:T(128)S(1)}, s32[8]{0:T(128)}, u32[]{:S(2)}) copy-start(s32[8]{0:T(128)} %constant.213.clone) | copy-start | bytes 100
  19.1 15.8 %copy-start.11 = (f32[22,88,128]{2,1,0:T(8,128)}, f32[22,88,128]{2,1,0:T(8,128)S(1)}, u32[]{:S(2)}) copy-start(f32[22,88,128]{2,1,0:T(8,128)S(1)} %get-tuple-element.39.refs_1_) | copy-start | bytes 2973700
  19.1 48.6 %collective-permute-start.7 = (bf16[8,22,16,128]{3,2,1,0:T(8,128)(2,1)S(1)}, bf16[8,22,16,128]{3,2,1,0:T(8,128)(2,1)}, u32[]{:S(2)}, u32[]{:S(2)}) collective-permute-start(bf16[8,22,16,128]{3,2,1,0:T(8,128)(2,1)S(1)} %get-tuple-element.42), channel_id=1, source_target_pairs={{0,1},{1,0},{2,3},{3,2},{4,5},{5,4},{6,7},{7,6},{8,9},{9,8},{10,11... | collective-permute-start | bytes 2162696 | tf_op jit(solution)/shard_map/ppermute | solution.py:43
  35.1 8.9 %collective-permute-start.2 = (bf16[11,88,128]{2,1,0:T(8,128)(2,1)S(1)}, bf16[11,88,128]{2,1,0:T(8,128)(2,1)}, u32[]{:S(2)}, u32[]{:S(2)}) collective-permute-start(bf16[11,88,128]{2,1,0:T(8,128)(2,1)S(1)} %collective-permute-done.refs_2_), channel_id=1, source_target_pairs={{0,4},{4,8},{8,12},{12,14},{14,10},{10,6},{6,2},{2,0},{1,5},{5,9},... | collective-permute-start | bytes 743432 | tf_op jit(solution)/shard_map/ppermute | solution.py:429
  37.1 9.0 %collective-permute-start.3 = (bf16[11,88,128]{2,1,0:T(8,128)(2,1)S(1)}, bf16[11,88,128]{2,1,0:T(8,128)(2,1)}, u32[]{:S(2)}, u32[]{:S(2)}) collective-permute-start(bf16[11,88,128]{2,1,0:T(8,128)(2,1)S(1)} %collective-permute-done.1.refs_3_), channel_id=1, source_target_pairs={{0,2},{4,0},{8,4},{12,8},{14,12},{10,14},{6,10},{2,6},{1,3},{5,1},... | collective-permute-start | bytes 743432 | tf_op jit(solution)/shard_map/ppermute | solution.py:432
  37.1 12.2 %collective-permute-start.9 = (bf16[11,88,128]{2,1,0:T(8,128)(2,1)}, bf16[11,88,128]{2,1,0:T(8,128)(2,1)}, u32[]{:S(2)}, u32[]{:S(2)}) collective-permute-start(bf16[11,88,128]{2,1,0:T(8,128)(2,1)} %collective-permute-done.8.refs_4_), channel_id=1, source_target_pairs={{0,4},{4,8},{8,12},{12,14},{14,10},{10,6},{6,2},{2,0},{1,5},{5,9},... | collective-permute-start | bytes 743432 | tf_op jit(solution)/shard_map/ppermute | solution.py:429
  39.1 12.2 %collective-permute-start.12 = (bf16[11,88,128]{2,1,0:T(8,128)(2,1)}, bf16[11,88,128]{2,1,0:T(8,128)(2,1)}, u32[]{:S(2)}, u32[]{:S(2)}) collective-permute-start(bf16[11,88,128]{2,1,0:T(8,128)(2,1)} %collective-permute-done.11.refs_5_), channel_id=1, source_target_pairs={{0,2},{4,0},{8,4},{12,8},{14,12},{10,14},{6,10},{2,6},{1,3},{5,1},... | collective-permute-start | bytes 743432 | tf_op jit(solution)/shard_map/ppermute | solution.py:432
  44.0 14.3 %collective-permute-start.4 = (bf16[11,88,128]{2,1,0:T(8,128)(2,1)}, bf16[11,88,128]{2,1,0:T(8,128)(2,1)S(1)}, u32[]{:S(2)}, u32[]{:S(2)}) collective-permute-start(bf16[11,88,128]{2,1,0:T(8,128)(2,1)} %collective-permute-done.2.refs_4_), channel_id=1, source_target_pairs={{0,4},{4,8},{8,12},{12,14},{14,10},{10,6},{6,2},{2,0},{1,5},{5,9},... | collective-permute-start | bytes 743432 | tf_op jit(solution)/shard_map/ppermute | solution.py:429
  46.1 15.4 %collective-permute-start.5 = (bf16[11,88,128]{2,1,0:T(8,128)(2,1)}, bf16[11,88,128]{2,1,0:T(8,128)(2,1)S(1)}, u32[]{:S(2)}, u32[]{:S(2)}) collective-permute-start(bf16[11,88,128]{2,1,0:T(8,128)(2,1)} %collective-permute-done.3.refs_5_), channel_id=1, source_target_pairs={{0,2},{4,0},{8,4},{12,8},{14,12},{10,14},{6,10},{2,6},{1,3},{5,1},... | collective-permute-start | bytes 743432 | tf_op jit(solution)/shard_map/ppermute | solution.py:432
  49.3 10.2 %collective-permute-start.10 = (bf16[11,88,128]{2,1,0:T(8,128)(2,1)}, bf16[11,88,128]{2,1,0:T(8,128)(2,1)S(1)}, u32[]{:S(2)}, u32[]{:S(2)}) collective-permute-start(bf16[11,88,128]{2,1,0:T(8,128)(2,1)} %collective-permute-done.9.refs_6_), channel_id=1, source_target_pairs={{0,4},{4,8},{8,12},{12,14},{14,10},{10,6},{6,2},{2,0},{1,5},{5,9},... | collective-permute-start | bytes 743432 | tf_op jit(solution)/shard_map/ppermute | solution.py:429
  51.4 9.9 %collective-permute-start.13 = (bf16[11,88,128]{2,1,0:T(8,128)(2,1)}, bf16[11,88,128]{2,1,0:T(8,128)(2,1)S(1)}, u32[]{:S(2)}, u32[]{:S(2)}) collective-permute-start(bf16[11,88,128]{2,1,0:T(8,128)(2,1)} %collective-permute-done.12.refs_7_), channel_id=1, source_target_pairs={{0,2},{4,0},{8,4},{12,8},{14,12},{10,14},{6,10},{2,6},{1,3},{5,1},... | collective-permute-start | bytes 743432 | tf_op jit(solution)/shard_map/ppermute | solution.py:432
  51.4 1.2 copy-start.12
  58.2 15.7 %collective-permute-start.17 = (bf16[6,22,16,128]{3,2,1,0:T(8,128)(2,1)S(1)}, bf16[6,22,16,128]{3,2,1,0:T(8,128)(2,1)S(1)}, u32[]{:S(2)}, u32[]{:S(2)}) collective-permute-start(bf16[6,22,16,128]{3,2,1,0:T(8,128)(2,1)S(1)} %triangle.5.refs_1_), channel_id=1, source_target_pairs={{0,1},{1,0},{2,3},{3,2},{4,5},{5,4},{6,7},{7,6},{8,9},{9,8},{10,11... | collective-permute-start | bytes 1622024 | tf_op jit(solution)/shard_map/ppermute | solution.py:43
  59.5 9.6 %collective-permute-start.14 = (bf16[11,88,128]{2,1,0:T(8,128)(2,1)S(1)}, bf16[11,88,128]{2,1,0:T(8,128)(2,1)S(1)}, u32[]{:S(2)}, u32[]{:S(2)}) collective-permute-start(bf16[11,88,128]{2,1,0:T(8,128)(2,1)S(1)} %collective-permute-done.10.refs_2_), channel_id=1, source_target_pairs={{0,4},{4,8},{8,12},{12,14},{14,10},{10,6},{6,2},{2,0},{1,5},{5,9},... | collective-permute-start | bytes 743432 | tf_op jit(solution)/shard_map/ppermute | solution.py:429
  61.3 8.1 %collective-permute-start.15 = (bf16[11,88,128]{2,1,0:T(8,128)(2,1)S(1)}, bf16[11,88,128]{2,1,0:T(8,128)(2,1)S(1)}, u32[]{:S(2)}, u32[]{:S(2)}) collective-permute-start(bf16[11,88,128]{2,1,0:T(8,128)(2,1)S(1)} %collective-permute-done.13.refs_3_), channel_id=1, source_target_pairs={{0,2},{4,0},{8,4},{12,8},{14,12},{10,14},{6,10},{2,6},{1,3},{5,1},... | collective-permute-start | bytes 743432 | tf_op jit(solution)/shard_map/ppermute | solution.py:432
  67.6 1.8 %copy-start.13 = (f32[22,88,128]{2,1,0:T(8,128)S(1)}, f32[22,88,128]{2,1,0:T(8,128)}, u32[]{:S(2)}) copy-start(f32[22,88,128]{2,1,0:T(8,128)} %copy-done.11) | copy-start | bytes 2973700
  67.6 8.9 %collective-permute-start.6 = (bf16[6,22,16,128]{3,2,1,0:T(8,128)(2,1)S(1)}, bf16[6,22,16,128]{3,2,1,0:T(8,128)(2,1)S(1)}, u32[]{:S(2)}, u32[]{:S(2)}) collective-permute-start(bf16[6,22,16,128]{3,2,1,0:T(8,128)(2,1)S(1)} %triangle.3.refs_1_), channel_id=1, source_target_pairs={{0,1},{1,0},{2,3},{3,2},{4,5},{5,4},{6,7},{7,6},{8,9},{9,8},{10,11... | collective-permute-start | bytes 1622024 | tf_op jit(solution)/shard_map/ppermute | solution.py:43
  69.0 4.9 %copy-start.5 = (bf16[128,128]{1,0:T(8,128)(2,1)S(1)}, bf16[128,128]{1,0:T(8,128)(2,1)}, u32[]{:S(2)}) copy-start(bf16[128,128]{1,0:T(8,128)(2,1)} %refs_6_.1) | copy-start | bytes 98308
  69.0 4.9 %copy-start.7 = (f32[128]{0:T(128)S(1)}, f32[128]{0:T(128)}, u32[]{:S(2)}) copy-start(f32[128]{0:T(128)} %param.17) | copy-start | bytes 1540
  69.1 4.9 %copy-start.8 = (f32[128]{0:T(128)S(1)}, f32[128]{0:T(128)}, u32[]{:S(2)}) copy-start(f32[128]{0:T(128)} %param.18) | copy-start | bytes 1540
  73.7 9.6 %collective-permute-start.16 = (bf16[4,22,16,128]{3,2,1,0:T(8,128)(2,1)S(1)}, bf16[4,22,16,128]{3,2,1,0:T(8,128)(2,1)S(1)}, u32[]{:S(2)}, u32[]{:S(2)}) collective-permute-start(bf16[4,22,16,128]{3,2,1,0:T(8,128)(2,1)S(1)} %triangle.4.refs_1_), channel_id=1, source_target_pairs={{0,1},{1,0},{2,3},{3,2},{4,5},{5,4},{6,7},{7,6},{8,9},{9,8},{10,11... | collective-permute-start | bytes 1081352 | tf_op jit(solution)/shard_map/ppermute | solution.py:43
  81.1 43.7 %collective-permute-start.25 = (bf16[11,88,128]{2,1,0:T(8,128)(2,1)S(1)}, bf16[11,88,128]{2,1,0:T(8,128)(2,1)S(1)}, u32[]{:S(2)}, u32[]{:S(2)}) collective-permute-start(bf16[11,88,128]{2,1,0:T(8,128)(2,1)S(1)} %get-tuple-element.59), channel_id=1, source_target_pairs={{0,2},{4,0},{8,4},{12,8},{14,12},{10,14},{6,10},{2,6},{1,3},{5,1},... | collective-permute-start | bytes 743432 | tf_op jit(solution)/shard_map/ppermute | solution.py:432
  83.3 41.5 %collective-permute-start.26 = (bf16[11,88,128]{2,1,0:T(8,128)(2,1)S(1)}, bf16[11,88,128]{2,1,0:T(8,128)(2,1)S(1)}, u32[]{:S(2)}, u32[]{:S(2)}) collective-permute-start(bf16[11,88,128]{2,1,0:T(8,128)(2,1)S(1)} %get-tuple-element.60), channel_id=1, source_target_pairs={{0,4},{4,8},{8,12},{12,14},{14,10},{10,6},{6,2},{2,0},{1,5},{5,9},... | collective-permute-start | bytes 743432 | tf_op jit(solution)/shard_map/ppermute | solution.py:429
  87.6 23.9 %collective-permute-start.18 = (bf16[11,88,128]{2,1,0:T(8,128)(2,1)S(1)}, bf16[11,88,128]{2,1,0:T(8,128)(2,1)S(1)}, u32[]{:S(2)}, u32[]{:S(2)}) collective-permute-start(bf16[11,88,128]{2,1,0:T(8,128)(2,1)S(1)} %get-tuple-element.46.refs_8_.refs_7_.refs_9_.refs_4_), channel_id=1, source_target_pairs={{0,2},{4,0},{8,4},{12,8},{14,12},{10,14},{6,10},{2,6},{1,3},{5,1},... | collective-permute-start | bytes 743432 | tf_op jit(solution)/shard_map/ppermute | solution.py:432
  89.3 22.3 %collective-permute-start.19 = (bf16[11,88,128]{2,1,0:T(8,128)(2,1)S(1)}, bf16[11,88,128]{2,1,0:T(8,128)(2,1)S(1)}, u32[]{:S(2)}, u32[]{:S(2)}) collective-permute-start(bf16[11,88,128]{2,1,0:T(8,128)(2,1)S(1)} %get-tuple-element.53), channel_id=1, source_target_pairs={{0,4},{4,8},{8,12},{12,14},{14,10},{10,6},{6,2},{2,0},{1,5},{5,9},... | collective-permute-start | bytes 743432 | tf_op jit(solution)/shard_map/ppermute | solution.py:429
  111.6 4.1 %copy-start.15 = (bf16[22,88,128]{2,1,0:T(8,128)(2,1)S(1)}, bf16[22,88,128]{2,1,0:T(8,128)(2,1)}, u32[]{:S(2)}) copy-start(bf16[22,88,128]{2,1,0:T(8,128)(2,1)} %copy-done.14) | copy-start | bytes 1486852
  113.6 15.5 %collective-permute-start.20 = (bf16[11,88,128]{2,1,0:T(8,128)(2,1)S(1)}, bf16[11,88,128]{2,1,0:T(8,128)(2,1)S(1)}, u32[]{:S(2)}, u32[]{:S(2)}) collective-permute-start(bf16[11,88,128]{2,1,0:T(8,128)(2,1)S(1)} %get-tuple-element.54), channel_id=1, source_target_pairs={{0,2},{4,0},{8,4},{12,8},{14,12},{10,14},{6,10},{2,6},{1,3},{5,1},... | collective-permute-start | bytes 743432 | tf_op jit(solution)/shard_map/ppermute | solution.py:432
  115.1 14.0 %collective-permute-start.21 = (bf16[11,88,128]{2,1,0:T(8,128)(2,1)S(1)}, bf16[11,88,128]{2,1,0:T(8,128)(2,1)S(1)}, u32[]{:S(2)}, u32[]{:S(2)}) collective-permute-start(bf16[11,88,128]{2,1,0:T(8,128)(2,1)S(1)} %get-tuple-element.55), channel_id=1, source_target_pairs={{0,4},{4,8},{8,12},{12,14},{14,10},{10,6},{6,2},{2,0},{1,5},{5,9},... | collective-permute-start | bytes 743432 | tf_op jit(solution)/shard_map/ppermute | solution.py:429
  124.8 8.1 %collective-permute-start.32 = (bf16[128,512]{1,0:T(8,128)(2,1)S(1)}, bf16[128,512]{1,0:T(8,128)(2,1)S(1)}, u32[]{:S(2)}, u32[]{:S(2)}) collective-permute-start(bf16[128,512]{1,0:T(8,128)(2,1)S(1)} %get-tuple-element.68), channel_id=1, source_target_pairs={{0,1},{1,0},{2,3},{3,2},{4,5},{5,4},{6,7},{7,6},{8,9},{9,8},{10,11... | collective-permute-start | bytes 393224 | tf_op jit(solution)/shard_map/ppermute | solution.py:43
  127.0 8.8 %collective-permute-start.27 = (bf16[11,88,128]{2,1,0:T(8,128)(2,1)S(1)}, bf16[11,88,128]{2,1,0:T(8,128)(2,1)S(1)}, u32[]{:S(2)}, u32[]{:S(2)}) collective-permute-start(bf16[11,88,128]{2,1,0:T(8,128)(2,1)S(1)} %get-tuple-element.61), channel_id=1, source_target_pairs={{0,2},{4,0},{8,4},{12,8},{14,12},{10,14},{6,10},{2,6},{1,3},{5,1},... | collective-permute-start | bytes 743432 | tf_op jit(solution)/shard_map/ppermute | solution.py:432
  128.5 8.8 %collective-permute-start.28 = (bf16[11,88,128]{2,1,0:T(8,128)(2,1)S(1)}, bf16[11,88,128]{2,1,0:T(8,128)(2,1)S(1)}, u32[]{:S(2)}, u32[]{:S(2)}) collective-permute-start(bf16[11,88,128]{2,1,0:T(8,128)(2,1)S(1)} %get-tuple-element.62), channel_id=1, source_target_pairs={{0,4},{4,8},{8,12},{12,14},{14,10},{10,6},{6,2},{2,0},{1,5},{5,9},... | collective-permute-start | bytes 743432 | tf_op jit(solution)/shard_map/ppermute | solution.py:429
  130.9 10.3 %collective-permute-start.22 = (bf16[11,88,128]{2,1,0:T(8,128)(2,1)S(1)}, bf16[11,88,128]{2,1,0:T(8,128)(2,1)S(1)}, u32[]{:S(2)}, u32[]{:S(2)}) collective-permute-start(bf16[11,88,128]{2,1,0:T(8,128)(2,1)S(1)} %get-tuple-element.56), channel_id=1, source_target_pairs={{0,2},{4,0},{8,4},{12,8},{14,12},{10,14},{6,10},{2,6},{1,3},{5,1},... | collective-permute-start | bytes 743432 | tf_op jit(solution)/shard_map/ppermute | solution.py:432
  132.4 10.2 %collective-permute-start.23 = (bf16[11,88,128]{2,1,0:T(8,128)(2,1)S(1)}, bf16[11,88,128]{2,1,0:T(8,128)(2,1)S(1)}, u32[]{:S(2)}, u32[]{:S(2)}) collective-permute-start(bf16[11,88,128]{2,1,0:T(8,128)(2,1)S(1)} %get-tuple-element.57), channel_id=1, source_target_pairs={{0,4},{4,8},{8,12},{12,14},{14,10},{10,6},{6,2},{2,0},{1,5},{5,9},... | collective-permute-start | bytes 743432 | tf_op jit(solution)/shard_map/ppermute | solution.py:429
  133.0 15.3 %collective-permute-start.33 = (bf16[128,512]{1,0:T(8,128)(2,1)S(1)}, bf16[128,512]{1,0:T(8,128)(2,1)S(1)}, u32[]{:S(2)}, u32[]{:S(2)}) collective-permute-start(bf16[128,512]{1,0:T(8,128)(2,1)S(1)} %add_convert_fusion.3), channel_id=1, source_target_pairs={{0,2},{2,0},{4,6},{6,4},{8,10},{10,8},{12,14},{14,12},{1,3},{3,1},... | collective-permute-start | bytes 393224 | tf_op jit(solution)/shard_map/ppermute | solution.py:53
  139.2 11.6 %collective-permute-start.29 = (bf16[11,88,128]{2,1,0:T(8,128)(2,1)S(1)}, bf16[11,88,128]{2,1,0:T(8,128)(2,1)S(1)}, u32[]{:S(2)}, u32[]{:S(2)}) collective-permute-start(bf16[11,88,128]{2,1,0:T(8,128)(2,1)S(1)} %get-tuple-element.63), channel_id=1, source_target_pairs={{0,4},{4,8},{8,12},{12,14},{14,10},{10,6},{6,2},{2,0},{1,5},{5,9},... | collective-permute-start | bytes 743432 | tf_op jit(solution)/shard_map/ppermute | solution.py:429
  139.6 11.1 %collective-permute-start.31 = (bf16[11,88,128]{2,1,0:T(8,128)(2,1)S(1)}, bf16[11,88,128]{2,1,0:T(8,128)(2,1)S(1)}, u32[]{:S(2)}, u32[]{:S(2)}) collective-permute-start(bf16[11,88,128]{2,1,0:T(8,128)(2,1)S(1)} %get-tuple-element.65), channel_id=1, source_target_pairs={{0,2},{4,0},{8,4},{12,8},{14,12},{10,14},{6,10},{2,6},{1,3},{5,1},... | collective-permute-start | bytes 743432 | tf_op jit(solution)/shard_map/ppermute | solution.py:432
  144.5 8.7 %collective-permute-start.24 = (bf16[11,88,128]{2,1,0:T(8,128)(2,1)S(1)}, bf16[11,88,128]{2,1,0:T(8,128)(2,1)S(1)}, u32[]{:S(2)}, u32[]{:S(2)}) collective-permute-start(bf16[11,88,128]{2,1,0:T(8,128)(2,1)S(1)} %get-tuple-element.58), channel_id=1, source_target_pairs={{0,2},{4,0},{8,4},{12,8},{14,12},{10,14},{6,10},{2,6},{1,3},{5,1},... | collective-permute-start | bytes 743432 | tf_op jit(solution)/shard_map/ppermute | solution.py:432
  145.2 10.1 %collective-permute-start.30 = (bf16[11,88,128]{2,1,0:T(8,128)(2,1)S(1)}, bf16[11,88,128]{2,1,0:T(8,128)(2,1)S(1)}, u32[]{:S(2)}, u32[]{:S(2)}) collective-permute-start(bf16[11,88,128]{2,1,0:T(8,128)(2,1)S(1)} %get-tuple-element.64), channel_id=1, source_target_pairs={{0,4},{4,8},{8,12},{12,14},{14,10},{10,6},{6,2},{2,0},{1,5},{5,9},... | collective-permute-start | bytes 743432 | tf_op jit(solution)/shard_map/ppermute | solution.py:429
  148.4 11.5 %collective-permute-start.34 = (bf16[128,512]{1,0:T(8,128)(2,1)S(1)}, bf16[128,512]{1,0:T(8,128)(2,1)S(1)}, u32[]{:S(2)}, u32[]{:S(2)}) collective-permute-start(bf16[128,512]{1,0:T(8,128)(2,1)S(1)} %add_convert_fusion.2), channel_id=1, source_target_pairs={{0,4},{2,6},{4,0},{6,2},{8,12},{10,14},{12,8},{14,10},{1,5},{3,7},... | collective-permute-start | bytes 393224 | tf_op jit(solution)/shard_map/ppermute | solution.py:53
  159.8 14.0 %copy-start.4 = (bf16[22,88,128]{2,1,0:T(8,128)(2,1)S(1)}, bf16[22,88,128]{2,1,0:T(8,128)(2,1)}, u32[]{:S(2)}) copy-start(bf16[22,88,128]{2,1,0:T(8,128)(2,1)} %refs_0_.9) | copy-start | bytes 1486852
  159.8 14.0 %copy-start.10 = (f32[128]{0:T(128)S(1)}, f32[128]{0:T(128)}, u32[]{:S(2)}) copy-start(f32[128]{0:T(128)} %param.14) | copy-start | bytes 1540
  159.8 1.3 collective-permute-start.36
  159.9 8.3 %collective-permute-start.35 = (bf16[128,512]{1,0:T(8,128)(2,1)S(1)}, bf16[128,512]{1,0:T(8,128)(2,1)S(1)}, u32[]{:S(2)}, u32[]{:S(2)}) collective-permute-start(bf16[128,512]{1,0:T(8,128)(2,1)S(1)} %add_convert_fusion.1), channel_id=1, source_target_pairs={{0,8},{2,10},{4,12},{6,14},{8,0},{10,2},{12,4},{14,6},{1,9},{3,11}... | collective-permute-start | bytes 393224 | tf_op jit(solution)/shard_map/ppermute | solution.py:53
  161.2 7.1 %collective-permute-start.37 = (bf16[128,256]{1,0:T(8,128)(2,1)S(1)}, bf16[128,256]{1,0:T(8,128)(2,1)S(1)}, u32[]{:S(2)}, u32[]{:S(2)}) collective-permute-start(bf16[128,256]{1,0:T(8,128)(2,1)S(1)} %add_convert_fusion.7), channel_id=1, source_target_pairs={{0,2},{2,0},{4,6},{6,4},{8,10},{10,8},{12,14},{14,12},{1,3},{3,1},... | collective-permute-start | bytes 196616 | tf_op jit(solution)/shard_map/ppermute | solution.py:53
  168.3 4.3 %collective-permute-start.38 = (bf16[128,256]{1,0:T(8,128)(2,1)S(1)}, bf16[128,256]{1,0:T(8,128)(2,1)S(1)}, u32[]{:S(2)}, u32[]{:S(2)}) collective-permute-start(bf16[128,256]{1,0:T(8,128)(2,1)S(1)} %add_convert_fusion.6), channel_id=1, source_target_pairs={{0,4},{2,6},{4,0},{6,2},{8,12},{10,14},{12,8},{14,10},{1,5},{3,7},... | collective-permute-start | bytes 196616 | tf_op jit(solution)/shard_map/ppermute | solution.py:53
  172.6 5.5 %collective-permute-start.39 = (bf16[128,256]{1,0:T(8,128)(2,1)S(1)}, bf16[128,256]{1,0:T(8,128)(2,1)S(1)}, u32[]{:S(2)}, u32[]{:S(2)}) collective-permute-start(bf16[128,256]{1,0:T(8,128)(2,1)S(1)} %add_convert_fusion.5), channel_id=1, source_target_pairs={{0,8},{2,10},{4,12},{6,14},{8,0},{10,2},{12,4},{14,6},{1,9},{3,11}... | collective-permute-start | bytes 196616 | tf_op jit(solution)/shard_map/ppermute | solution.py:53

commit v4 on v3

v4 whole, which is shorter than its diff:
```python
import functools

import jax
import jax.numpy as jnp
from jax import lax
from jax.experimental import pallas as pl
from jax.experimental.pallas import tpu as pltpu
from jax.sharding import PartitionSpec as P

eps = 1e-05
f32 = jnp.float32
bf16 = jnp.bfloat16
VMEM = pl.BlockSpec(memory_space=pltpu.VMEM)
SMEM = pl.BlockSpec(memory_space=pltpu.SMEM)
ANY = pl.BlockSpec(memory_space=pl.ANY)
MIB = 1 << 20


def layer_norm_backward(output_gradient, standardized_input, inverse_deviation, norm_gain):
    scaled_output = output_gradient * norm_gain
    first_operand = jnp.mean(scaled_output, axis=-1, keepdims=True)
    second_operand = jnp.mean(scaled_output * standardized_input, axis=-1, keepdims=True)
    return inverse_deviation * (scaled_output - first_operand - standardized_input * second_operand)


def standardize(values):
    centered = values - jnp.mean(values, axis=-1, keepdims=True)
    inverse = lax.rsqrt(jnp.mean(centered * centered, axis=-1, keepdims=True) + eps)
    return centered * inverse, inverse


def dot(a, b, ca, cb):
    return lax.dot_general(a, b, (((ca,), (cb,)), ((), ())), preferred_element_type=f32)


def ring_order(row_count):
    if row_count == 8:
        return [0, 2, 4, 6, 7, 5, 3, 1]
    return list(range(row_count))


def ring_place(row_count, row):
    if row_count == 8:
        return jnp.where(row % 2 == 0, row // 2, row_count - 1 - row // 2)
    return row


def ring_row(row_count, place):
    if row_count == 8:
        return jnp.where(place < row_count // 2, 2 * place, 2 * (row_count - 1 - place) + 1)
    return place


def half_index(row_count, offset, letter):
    place = ring_place(row_count, lax.axis_index("row"))
    return ring_row(row_count, (place + offset + row_count) % row_count) * 2 + letter


def arrival_slot(row_count, index):
    hops = row_count // 2
    letter = index % 2
    apart = ring_place(row_count, index // 2) - ring_place(row_count, lax.axis_index("row"))
    apart = (apart + row_count) % row_count
    near = jnp.where(letter == 0, row_count - apart, apart)
    first = 2 * near + letter
    second = 2 + 2 * hops + 2 * (row_count - near - 1) + 1 - letter
    return jnp.where(apart == 0, letter, jnp.where(near <= hops, first, second))


def present_count(row_count, lengths, slot, short, where):
    start = half_index(row_count, *where) * short
    return jnp.clip(lengths[start // slot] - start % slot, 0, short)


def swap_col(x):
    return lax.ppermute(x, "col", [(0, 1), (1, 0)])


def sum_all(x, row_count):
    def add(a, b):
        return (a.astype(f32) + b.astype(f32)).astype(bf16)

    x = add(x, swap_col(x))
    step = 1
    while step < row_count:
        x = add(x, lax.ppermute(x, "row", [(r, r ^ step) for r in range(row_count)]))
        step *= 2
    return x


def call(kernel, name, microseconds, args, specs, outs, scratch=(), after=()):
    held = sum(a.size * a.dtype.itemsize for a, s in zip(args, specs) if s is VMEM)
    held += sum(int(o.size) * o.dtype.itemsize for o in outs)
    held += sum(int(s.inner_aval.size) * 4 for s in scratch)

    def body(*refs):
        kernel(*refs[: len(args)], *refs[len(args) + len(after) :])

    return pl.pallas_call(
        body,
        out_shape=list(outs),
        in_specs=list(specs) + [ANY] * len(after),
        out_specs=[VMEM] * len(outs),
        scratch_shapes=list(scratch),
        compiler_params=pltpu.CompilerParams(vmem_limit_bytes=min(56 * MIB, held * 5 // 4 + 6 * MIB)),
        cost_estimate=pl.CostEstimate(
            flops=int(microseconds * 1.1e9), bytes_accessed=MIB, transcendentals=0
        ),
        name=name,
    )(*args, *after)


def shape_of(dims, dtype):
    return jax.ShapeDtypeStruct(dims, dtype)


def present_row(lengths, slot, position):
    return (position % slot < lengths[position // slot]).astype(f32)


def present_columns(lengths, slot, half):
    at = lax.axis_index("col") * half + lax.broadcasted_iota(jnp.int32, (half, 128), 0)
    chain = at // slot
    held = jnp.zeros((half, 128), jnp.int32)
    for c in range(lengths.shape[0]):
        held = jnp.where(chain == c, lengths[c], held)
    return (at - chain * slot < held).astype(f32)


def first_row(here):
    return lax.axis_index("row") * here


def input_kernel(slot, lengths, pair, gain, bias, w, right_a, right_b, normed, mask):
    here, half, hidden = pair.shape
    short = here // 2
    mask[...] = present_columns(lengths, slot, half)

    for out, first in ((right_a, 0), (right_b, short)):
        for t in range(short):
            i = first + t
            standard, _ = standardize(pair[i].astype(f32))
            values = (standard * gain[...] + bias[...]).astype(bf16)
            normed[i] = values
            proj = dot(values, w[:, 2 * hidden : 4 * hidden], 1, 0)
            shown = mask[...] * present_row(lengths, slot, first_row(here) + i)
            gated = jax.nn.sigmoid(proj[:, :hidden]) * proj[:, hidden:]
            out[t] = (shown * gated).astype(bf16)


def by_rows(here, body):
    def step(t, carry):
        for x in range(here // 2):
            body(t * (here // 2) + x)
        return carry

    lax.fori_loop(0, 2, step, 0)


def left_kernel(slot, lengths, normed, cotangent, w, left, outs, mask):
    here, half, hidden = normed.shape
    halves, _, padded, _ = outs.shape
    short = half // halves
    mask[...] = present_columns(lengths, slot, half)

    def body(i):
        proj = dot(normed[i], w[:, : 2 * hidden], 1, 0)
        shown = mask[...] * present_row(lengths, slot, first_row(here) + i)
        gated = shown * jax.nn.sigmoid(proj[:, :hidden]) * proj[:, hidden:]
        left[i] = gated.astype(bf16).astype(f32)
        gate = jax.nn.sigmoid(dot(normed[i], w[:, 4 * hidden :], 1, 0))
        grads = cotangent[i].astype(f32) * gate
        empty = jnp.zeros((padded - short, hidden), f32)
        for m in range(halves):
            part = grads[m * short : (m + 1) * short]
            outs[m, i] = jnp.concatenate([part, empty], axis=0).astype(bf16)

    by_rows(here, body)


def triangle_kernel(row_count, slot, places, lengths, left, *refs):
    count = len(places)
    rights, (out, right, partial, rows) = refs[:count], refs[count:]
    here, half, hidden = left.shape
    short = rights[0].shape[0]
    padded = out.shape[2]
    for s in range(count):
        right[...] = rights[s][...].astype(f32)
        rows[...] = jnp.zeros_like(rows)

        def body(j, carry):
            held = right[j]
            for i in range(here):
                product = (left[i] * held).reshape(half // 8, 8, hidden)
                partial[pl.ds(8 * i, 8), :] = jnp.sum(product, axis=0)
            total = partial[pl.ds(0, here, stride=8), :]
            for sub in range(1, 8):
                total += partial[pl.ds(sub, here, stride=8), :]
            rows[pl.ds(j, here, stride=padded), :] = total
            return carry

        present = present_count(row_count, lengths, slot, short, places[s])
        lax.fori_loop(0, present, body, 0)
        out[s] = rows[...].astype(bf16).reshape(here, padded, hidden)


def triangle(row_count, slot, places, lengths, left, rights, padded, after=()):
    count, (here, half, hidden) = len(rights), left.shape
    return call(
        functools.partial(triangle_kernel, row_count, slot, places),
        "triangle",
        0.7 * count,
        [lengths, left, *rights],
        [SMEM] + [VMEM] * (count + 1),
        [shape_of((count, here, padded, hidden), bf16)],
        [
            pltpu.VMEM(rights[0].shape, f32),
            pltpu.VMEM((here * 8, hidden), f32),
            pltpu.VMEM((here * padded, hidden), f32),
        ],
        after,
    )[0]


def triangle_norm_kernel(row_count, places, mine, other, outs, w_out, gain, bias, grad, normed):
    count, here, padded, hidden = mine.shape
    flat = (here * padded, hidden)

    for s in range(count):
        index = half_index(row_count, *places[s])
        near = ((index // row_count) ^ lax.axis_index("col")) * row_count + index % row_count
        total = (mine[s].astype(f32) + other[s].astype(f32)).reshape(flat)
        standard, inverse = standardize(total)
        normed[s] = (standard * gain[...] + bias[...]).astype(bf16).reshape(here, padded, hidden)
        grad_norm = dot(outs[near].reshape(flat), w_out[...], 1, 1)
        result = layer_norm_backward(grad_norm, standard, inverse, gain[...])
        grad[s] = result.astype(bf16).reshape(here, padded, hidden)


def triangle_norm(row_count, places, mine, other, outs, w_out, gain, bias):
    return call(
        functools.partial(triangle_norm_kernel, row_count, places),
        "triangle_norm",
        0.4 * mine.shape[0],
        [mine, other, outs, w_out, gain, bias],
        [VMEM] * 6,
        [shape_of(mine.shape, bf16)] * 2,
    )


def hop_kernel(row_count, slot, places, picks, carried, lengths, left, *refs):
    count = len(picks)
    grads, refs = refs[:count], refs[count:]
    arrived, refs = refs[: count * carried], refs[count * carried :]
    outs, wide = refs[:count], refs[count]
    here, half, hidden = left.shape
    short = outs[0].shape[0]
    for s in range(count):
        wide[...] = grads[s][picks[s]].astype(f32)
        out = outs[s]

        def body(pair, carry, s=s, out=out):
            at = [jnp.minimum(2 * pair + x, short - 1) for x in range(2)]
            totals = []
            for j in at:
                total = jnp.zeros((half, hidden), f32)
                for more in range(carried):
                    total += arrived[s + more * count][j].astype(f32)
                totals.append(total)
            for i in range(here):
                held = left[i]
                for x in range(2):
                    totals[x] += wide[i, pl.ds(at[x], 1), :] * held
            for x in range(2):
                out[at[x]] = totals[x].astype(out.dtype)
            return carry

        def clear(j, carry, out=out):
            out[j] = jnp.zeros((half, hidden), out.dtype)
            return carry

        present = present_count(row_count, lengths, slot, short, places[s])
        pairs = (present + 1) // 2
        lax.fori_loop(0, pairs, body, 0)
        lax.fori_loop(2 * pairs, short, clear, 0)


def hop(row_count, slot, places, lengths, left, grads, picks, arrived, short, dtype=bf16, after=()):
    here, half, hidden = left.shape
    count = len(grads)
    carried = len(arrived) // count
    return call(
        functools.partial(hop_kernel, row_count, slot, places, picks, carried),
        "scatter_hop",
        0.7 * count,
        [lengths, left, *grads, *arrived],
        [SMEM] + [VMEM] * (1 + count + len(arrived)),
        [shape_of((short, half, hidden), dtype)] * count,
        [pltpu.VMEM(grads[0].shape[1:], f32)],
        after,
    )


def left_gradient_kernel(picks, carried, grads, *refs):
    count = len(picks)
    rights, refs = refs[:count], refs[count:]
    before, (out, right, wide) = refs[:carried], refs[carried:]
    here, half, hidden = out.shape
    short = rights[0].shape[0]
    for s in range(count):
        right[s] = rights[s][...].astype(f32)
        wide[s] = grads[picks[s]].astype(f32)

    def row(i, carry):
        total = before[0][i] if carried else jnp.zeros((half, hidden), f32)
        for s in range(count):
            for j in range(short):
                total += wide[s, i, pl.ds(j, 1), :] * right[s, j]
        out[i] = total
        return carry

    lax.fori_loop(0, here, row, 0)


def left_gradient(grads, picks, rights, before, after=()):
    count, here = len(picks), grads.shape[1]
    short, half, hidden = rights[0].shape
    return call(
        functools.partial(left_gradient_kernel, picks, len(before)),
        "left_gradient",
        0.9 * count,
        [grads, *rights, *before],
        [VMEM] * (1 + count + len(before)),
        [shape_of((here, half, hidden), f32)],
        [
            pltpu.VMEM((count, short, half, hidden), f32),
            pltpu.VMEM((count,) + grads.shape[1:], f32),
        ],
        after,
    )[0]


def output_kernel(
    row_count, slot, counts, lengths, normed, cotangent, grad_left, w, w_out, outs, *refs
):
    norms, (update, gradient, weights, mask, picked, total) = (
        refs[: len(counts)],
        refs[len(counts) :],
    )
    here, half, hidden = normed.shape
    halves, _, padded, _ = picked.shape
    short = half // halves
    mask[...] = present_columns(lengths, slot, half)
    total[...] = jnp.zeros_like(total)
    for m in range(halves):
        low = 0
        stands = arrival_slot(row_count, lax.axis_index("col") * row_count + m)
        for norm, count in zip(norms, counts):

            @pl.when((stands >= low) & (stands < low + count))
            def _(m=m, norm=norm, low=low, stands=stands):
                picked[m] = norm[stands - low]

            low += count

    def body(i):
        values = normed[i]
        proj = dot(values, w[:, : 2 * hidden], 1, 0)
        sig_left = jax.nn.sigmoid(proj[:, :hidden])
        val_left = proj[:, hidden:]
        gate = jax.nn.sigmoid(dot(values, w[:, 4 * hidden :], 1, 0))
        tri = picked[:, i].reshape(halves * padded, hidden)
        product = dot(tri, w_out[...], 1, 0)
        projected = jnp.concatenate(
            [product[m * padded : m * padded + short] for m in range(halves)], axis=0
        )
        update[i] = (gate * projected).astype(bf16)
        grad_gate = (cotangent[i].astype(f32) * projected * gate * (1.0 - gate)).astype(bf16)
        shown = mask[...] * present_row(lengths, slot, first_row(here) + i)
        masked = grad_left[i] * shown
        grads = jnp.concatenate(
            [masked * val_left * sig_left * (1.0 - sig_left), masked * sig_left], axis=1
        ).astype(bf16)
        gradient[i] = dot(grads, w[:, : 2 * hidden], 1, 1) + dot(
            grad_gate, w[:, 4 * hidden :], 1, 1
        )
        total[:, : 2 * hidden] += dot(values, grads, 0, 0)
        total[:, 2 * hidden : 3 * hidden] += dot(values, grad_gate, 0, 0)
        total[:, 3 * hidden :] += dot(tri, outs[:halves, i].reshape(halves * padded, hidden), 0, 0)

    by_rows(here, body)
    weights[...] = total[...].astype(bf16)


def right_gradient_kernel(slot, lengths, normed, w, own_a, own_b, *refs):
    arrived, (grads, weights, mask, total) = refs[:4], refs[4:]
    here, half, hidden = normed.shape
    short = here // 2
    mask[...] = present_columns(lengths, slot, half)
    total[...] = jnp.zeros_like(total)

    for own, others, first in ((own_a, arrived[:2], 0), (own_b, arrived[2:], short)):
        for t in range(short):
            j = first + t
            values = normed[j]
            proj = dot(values, w[:, 2 * hidden : 4 * hidden], 1, 0)
            sig_right = jax.nn.sigmoid(proj[:, :hidden])
            val_right = proj[:, hidden:]
            shown = mask[...] * present_row(lengths, slot, first_row(here) + j)
            masked = shown * (own[t] + others[0][t].astype(f32) + others[1][t].astype(f32))
            result = jnp.concatenate(
                [masked * val_right * sig_right * (1.0 - sig_right), masked * sig_right], axis=1
            ).astype(bf16)
            grads[j] = result
            total[...] += dot(values, result, 0, 0)
    weights[...] = total[...].astype(bf16)


def pair_gradient_kernel(pair, grads, gradient, gain, w, out):
    hidden = pair.shape[2]

    def body(i):
        standard, inverse = standardize(pair[i].astype(f32))
        total = gradient[i] + dot(grads[i], w[:, 2 * hidden : 4 * hidden], 1, 1)
        out[i] = layer_norm_backward(total, standard, inverse, gain[...]).astype(bf16)

    by_rows(pair.shape[0], body)


def shards(
    pair,
    cotangent,
    chain_lengths,
    input_norm_gain,
    input_norm_bias,
    w_in,
    output_norm_gain,
    output_norm_bias,
    w_out,
):
    here, half, channels = pair.shape
    hidden = w_out.shape[0]
    row_count = lax.axis_size("row")
    slot = here * row_count // chain_lengths.shape[0]
    order = ring_order(row_count)
    short = here // 2
    padded = (short + 15) // 16 * 16
    forward = [(order[p], order[(p + 1) % row_count]) for p in range(row_count)]
    backward = [(order[p], order[(p - 1) % row_count]) for p in range(row_count)]
    in_gain, in_bias = input_norm_gain.reshape(1, -1), input_norm_bias.reshape(1, -1)
    out_gain, out_bias = output_norm_gain.reshape(1, -1), output_norm_bias.reshape(1, -1)
    block = (here, half, hidden)
    half_block = (short, half, hidden)
    mask = pltpu.VMEM((half, 128), f32)

    def ahead(x):
        return lax.ppermute(x, "row", forward)

    def behind(x):
        return lax.ppermute(x, "row", backward)

    right_a, right_b, normed = call(
        functools.partial(input_kernel, slot),
        "input_side",
        3.0,
        [chain_lengths, pair, in_gain, in_bias, w_in],
        [SMEM] + [VMEM] * 4,
        [shape_of(half_block, bf16)] * 2 + [shape_of(block, bf16)],
        [mask],
    )

    hops = row_count // 2
    chain1, chain2 = [], []
    a, b, c, d = right_a, right_b, right_b, right_a
    for step in range(hops):
        a, b = ahead(a), behind(b)
        chain1 += [a, b]
        if step < hops - 1:
            c, d = ahead(c), behind(d)
            chain2 += [c, d]

    early_hops = hops // 2
    groups = [[right_a, right_b] + chain1[: 2 * early_hops], chain1[2 * early_hops :], chain2]
    places1 = [p for s in range(1, hops + 1) for p in ((-s, 0), (s, 1))]
    places2 = [p for s in range(1, hops) for p in ((-s, 1), (s, 0))]
    places = [[(0, 0), (0, 1)] + places1[: 2 * early_hops], places1[2 * early_hops :], places2]

    left, mine_out = call(
        functools.partial(left_kernel, slot),
        "left_side",
        4.0,
        [chain_lengths, normed, cotangent, w_in],
        [SMEM] + [VMEM] * 3,
        [shape_of(block, f32), shape_of((row_count, here, padded, hidden), bf16)],
        [mask],
    )
    outs = jnp.concatenate([mine_out, swap_col(mine_out)], axis=0)

    norms, grads = [], []

    def triangle_group(g, after=()):
        partial = triangle(
            row_count, slot, places[g], chain_lengths, left, groups[g], padded, after
        )
        grad, norm = triangle_norm(
            row_count, places[g], partial, swap_col(partial), outs, w_out, out_gain, out_bias
        )
        grads.append(grad)
        norms.append(norm)

    def scatter(g, picks, arrived, dtype=bf16, after=()):
        return hop(
            row_count,
            slot,
            [places[g][pick] for pick in picks],
            chain_lengths,
            left,
            [grads[g]] * 2,
            picks,
            arrived,
            short,
            dtype,
            after,
        )

    def group1(s):
        at = 2 * (s - 1)
        if s <= early_hops:
            return 0, [at + 2, at + 3]
        at -= 2 * early_hops
        return 1, [at, at + 1]

    pieces = []

    def add_left(g, picks, after):
        rights = [groups[g][pick] for pick in picks]
        pieces[:] = [left_gradient(grads[g], picks, rights, pieces[:], after)]

    arrived1, arrived2 = [], []
    triangle_group(0)
    triangle_group(1)
    g, picks = group1(hops)
    x, y = scatter(g, picks, arrived1)
    arrived1 = [behind(x), ahead(y)]
    add_left(0, list(range(len(groups[0]))), [x])
    triangle_group(2, pieces)
    waiting = [
        (g, [at, at + 1]) for g in (1, 2) for at in range(0, len(groups[g]), 2)
    ]
    for s in range(hops - 1, 0, -1):
        x, y = scatter(2, [2 * s - 2, 2 * s - 1], arrived2, after=pieces)
        arrived2 = [behind(x), ahead(y)]
        if waiting:
            add_left(*waiting.pop(0), [x])
        g, picks = group1(s)
        x, y = scatter(g, picks, arrived1, after=pieces)
        arrived1 = [behind(x), ahead(y)]
        if waiting:
            add_left(*waiting.pop(0), [x])
    while waiting:
        add_left(*waiting.pop(0), [x])
    own_a, own_b = scatter(0, [0, 1], [], f32, after=[x])
    update, gradient, early = call(
        functools.partial(output_kernel, row_count, slot, [len(g) for g in groups]),
        "output_side",
        6.0,
        [chain_lengths, normed, cotangent, pieces[0], w_in, w_out, outs, *norms],
        [SMEM] + [VMEM] * 9,
        [
            shape_of(block, bf16),
            shape_of(block, f32),
            shape_of((channels, 4 * hidden), bf16),
        ],
        [
            mask,
            pltpu.VMEM((row_count, here, padded, hidden), bf16),
            pltpu.VMEM((channels, 4 * hidden), f32),
        ],
    )
    summed_early = sum_all(early, row_count).astype(f32)

    late, weights = call(
        functools.partial(right_gradient_kernel, slot),
        "right_gradient",
        3.0,
        [chain_lengths, normed, w_in, own_a, own_b]
        + [arrived1[0], arrived2[1], arrived1[1], arrived2[0]],
        [SMEM] + [VMEM] * 8,
        [
            shape_of((here, half, 2 * hidden), bf16),
            shape_of((channels, 2 * hidden), bf16),
        ],
        [mask, pltpu.VMEM((channels, 2 * hidden), f32)],
    )
    summed_late = sum_all(weights, row_count).astype(f32)
    (pair_gradient,) = call(
        pair_gradient_kernel,
        "pair_gradient",
        3.0,
        [pair, late, gradient, in_gain, w_in],
        [VMEM] * 5,
        [shape_of(block, bf16)],
    )
    grad_w_in = jnp.concatenate(
        [summed_early[:, : 2 * hidden], summed_late, summed_early[:, 2 * hidden : 3 * hidden]],
        axis=1,
    )
    grad_w_out = summed_early[:, 3 * hidden :]
    return (update, pair_gradient, grad_w_in, grad_w_out)


def solution(mesh):
    placed = (
        P(("grp", "row"), "col", None),
        P(("grp", "row"), "col", None),
        P("grp"),
        P(),
        P(),
        P(),
        P(),
        P(),
        P(),
    )
    return jax.shard_map(
        shards,
        mesh=mesh,
        in_specs=placed,
        out_specs=(
            P(("grp", "row"), "col", None),
            P(("grp", "row"), "col", None),
            P("grp", None),
            P("grp", None),
        ),
        check_vma=False,
    )
```

time: 180 us -> 141 us (0.78)
  Pallas kernels: 87.7 us -> 65.7 us
  between operations: 12.7 us -> 1.06 us
  starting transfers between devices: 34.3 us -> 41.5 us
  local copies, waits for them, and re-layouts: 11.3 us -> 5.34 us
  waiting for transfers between devices: 31 us -> 26.3 us
    pallas_call x22 -> x25, Pallas kernels: 87.7 us -> 65.7 us  [call(): pl.pallas_call(body, out_shape=list(outs), in_specs=list(specs) + [ANY] *...]
    ppermute x14, waiting for transfers between devices: 15 us -> 4.63 us  [ahead(): return lax.ppermute(x, 'row', forward)]
    ppermute x14, waiting for transfers between devices: 4.12 us -> 11.4 us  [behind(): return lax.ppermute(x, 'row', backward)]
    ppermute x14, starting transfers between devices: 13.9 us -> 21 us  [behind(): return lax.ppermute(x, 'row', backward)]
    ppermute x14, starting transfers between devices: 16.1 us -> 10.4 us  [ahead(): return lax.ppermute(x, 'row', forward)]
    ppermute x6, starting transfers between devices: 3.92 us -> 9.13 us  [sum_all(): lax.ppermute(x, 'row', [(r, r ^ step) for r in range(row_count)])]
    gather x3 -> x0, local copies, waits for them, and re-layouts: 1.93 us -> none  [shards(): chain_lengths[i * short // slot] - i * short % slot]
    unnamed x37 -> x27, local copies, waits for them, and re-layouts: 4.39 us -> 4.52 us
  transfers between devices with their start and end apart: 40 -> 40, of which waited for: 14 -> 11; matrix products, arithmetic and copies ran while one was open for 4% -> 0% of each run, Pallas kernels for 46% -> 42%
where the time goes in v4:
time: 141 us
  Pallas kernels  65.7 us (47%)
  starting transfers between devices  41.5 us (29%)
  waiting for transfers between devices  26.3 us (19%)
  local copies, waits for them, and re-layouts  5.34 us (4%)
    pallas_call x25, Pallas kernels, call(): pl.pallas_call(body, out_shape=list(outs), in_specs=list(specs) + [ANY] *...  65.7 us
    ppermute x14, starting transfers between devices, behind(): return lax.ppermute(x, 'row', backward)  21 us
    ppermute x14, waiting for transfers between devices, behind(): return lax.ppermute(x, 'row', backward)  11.4 us
    ppermute x14, starting transfers between devices, ahead(): return lax.ppermute(x, 'row', forward)  10.4 us
    ppermute x6, waiting for transfers between devices, sum_all(): lax.ppermute(x, 'row', [(r, r ^ step) for r in range(row_count)])  10.3 us
    ppermute x6, starting transfers between devices, sum_all(): lax.ppermute(x, 'row', [(r, r ^ step) for r in range(row_count)])  9.13 us
    ppermute x14, waiting for transfers between devices, ahead(): return lax.ppermute(x, 'row', forward)  4.63 us
    unnamed x27, local copies, waits for them, and re-layouts  4.52 us
  transfers between devices with their start and end apart: 40, of which 11 were waited for; matrix products, arithmetic and copies ran while one was open for 0% of the time, Pallas kernels for 42%

profile of v4, /device:TPU:0, one launch (start us, length us, event | category | flops | bytes accessed | tf_op | source)
XLA Modules:
  0.0 140.8 jit_solution(9489355678949828600)
XLA Ops:
  0.6 1.0 copy-done.1
  1.7 0.9 copy-done.3
  2.6 0.7 copy-done.6
  3.2 0.7 copy-done.9
  3.9 0.7 copy-done.11
  4.6 1.5 %input_side.1 = (bf16[11,88,128]{2,1,0:T(8,128)(2,1)S(1)}, bf16[11,88,128]{2,1,0:T(8,128)(2,1)S(1)}, bf16[22,88,128]{2,1,0:T(8,128)(2,1)S(1)}) custom-call(s32[8]{0:T(128)S(1)} %copy-done.9, bf16[22,88,128]{2,1,0:T(8,128)(2,1)S(1)} %copy-done.1, f32[1,128]{1,0:T(1,128)S(1)} %bitcast.11, f32[1,128]{1,0:T(1,128)S(1)} %bitcast.4, bf16[128,640]{1,0:T(8,128)(2,1)S(1)} %copy-done.3), custom_call_target="tpu_custom_call" | custom-call | flops 3300000000 | bytes 1048576 | tf_op jit(solution)/shard_map/input_side/pallas_call | solution.py:99
  6.0 3.0 %collective-permute-start.7 = (bf16[11,88,128]{2,1,0:T(8,128)(2,1)S(1)}, bf16[11,88,128]{2,1,0:T(8,128)(2,1)S(1)}, u32[]{:S(2)}, u32[]{:S(2)}) collective-permute-start(bf16[11,88,128]{2,1,0:T(8,128)(2,1)S(1)} %get-tuple-element.38.refs_3_.refs_2_), channel_id=1, source_target_pairs={{0,2},{4,0},{8,4},{12,8},{14,12},{10,14},{6,10},{2,6},{1,3},{5,1},... | collective-permute-start | bytes 743432 | tf_op jit(solution)/shard_map/ppermute | solution.py:460
  9.2 5.9 %collective-permute-done.7.refs_5_.refs_4_ = bf16[11,88,128]{2,1,0:T(8,128)(2,1)S(1)} collective-permute-done((bf16[11,88,128]{2,1,0:T(8,128)(2,1)S(1)}, bf16[11,88,128]{2,1,0:T(8,128)(2,1)S(1)}, u32[]{:S(2)}, u32[]{:S(2)}) %collective-permute-start.7) | collective-permute-done | bytes 247840 | tf_op jit(solution)/shard_map/ppermute | solution.py:460
  15.1 1.7 %collective-permute-start.9 = (bf16[11,88,128]{2,1,0:T(8,128)(2,1)S(1)}, bf16[11,88,128]{2,1,0:T(8,128)(2,1)S(1)}, u32[]{:S(2)}, u32[]{:S(2)}) collective-permute-start(bf16[11,88,128]{2,1,0:T(8,128)(2,1)S(1)} %collective-permute-done.7.refs_5_.refs_4_), channel_id=1, source_target_pairs={{0,2},{4,0},{8,4},{12,8},{14,12},{10,14},{6,10},{2,6},{1,3},{5,1},... | collective-permute-start | bytes 743432 | tf_op jit(solution)/shard_map/ppermute | solution.py:460
  17.1 1.7 %collective-permute-start = (bf16[11,88,128]{2,1,0:T(8,128)(2,1)S(1)}, bf16[11,88,128]{2,1,0:T(8,128)(2,1)S(1)}, u32[]{:S(2)}, u32[]{:S(2)}) collective-permute-start(bf16[11,88,128]{2,1,0:T(8,128)(2,1)S(1)} %get-tuple-element.38.refs_3_.refs_2_), channel_id=1, source_target_pairs={{0,4},{4,8},{8,12},{12,14},{14,10},{10,6},{6,2},{2,0},{1,5},{5,9},... | collective-permute-start | bytes 743432 | tf_op jit(solution)/shard_map/ppermute | solution.py:457
  19.1 4.9 %collective-permute-done.9.refs_7_.refs_6_ = bf16[11,88,128]{2,1,0:T(8,128)(2,1)S(1)} collective-permute-done((bf16[11,88,128]{2,1,0:T(8,128)(2,1)S(1)}, bf16[11,88,128]{2,1,0:T(8,128)(2,1)S(1)}, u32[]{:S(2)}, u32[]{:S(2)}) %collective-permute-start.9) | collective-permute-done | bytes 247840 | tf_op jit(solution)/shard_map/ppermute | solution.py:460
  24.0 1.7 %collective-permute-start.13 = (bf16[11,88,128]{2,1,0:T(8,128)(2,1)S(1)}, bf16[11,88,128]{2,1,0:T(8,128)(2,1)S(1)}, u32[]{:S(2)}, u32[]{:S(2)}) collective-permute-start(bf16[11,88,128]{2,1,0:T(8,128)(2,1)S(1)} %collective-permute-done.9.refs_7_.refs_6_), channel_id=1, source_target_pairs={{0,2},{4,0},{8,4},{12,8},{14,12},{10,14},{6,10},{2,6},{1,3},{5,1},... | collective-permute-start | bytes 743432 | tf_op jit(solution)/shard_map/ppermute | solution.py:460
  26.1 1.4 %left_side.1 = (f32[22,88,128]{2,1,0:T(8,128)S(1)}, bf16[8,22,16,128]{3,2,1,0:T(8,128)(2,1)S(1)}) custom-call(s32[8]{0:T(128)S(1)} %copy-done.10, bf16[22,88,128]{2,1,0:T(8,128)(2,1)S(1)} %get-tuple-element.36.refs_1_, bf16[22,88,128]{2,1,0:T(8,128)(2,1)S(1)} %copy-done, bf16[128,640]{1,0:T(8,128)(2,1)S(1)} %copy-done.4), custom_call_target="tpu_custom_call" | custom-call | flops 4400000000 | bytes 1048576 | tf_op jit(solution)/shard_map/left_side/pallas_call | solution.py:99
  27.6 3.4 %collective-permute-done.refs_2_.refs_1_ = bf16[11,88,128]{2,1,0:T(8,128)(2,1)S(1)} collective-permute-done((bf16[11,88,128]{2,1,0:T(8,128)(2,1)S(1)}, bf16[11,88,128]{2,1,0:T(8,128)(2,1)S(1)}, u32[]{:S(2)}, u32[]{:S(2)}) %collective-permute-start) | collective-permute-done | bytes 247840 | tf_op jit(solution)/shard_map/ppermute | solution.py:457
  31.4 1.7 %collective-permute-start.3 = (bf16[11,88,128]{2,1,0:T(8,128)(2,1)S(1)}, bf16[11,88,128]{2,1,0:T(8,128)(2,1)S(1)}, u32[]{:S(2)}, u32[]{:S(2)}) collective-permute-start(bf16[11,88,128]{2,1,0:T(8,128)(2,1)S(1)} %collective-permute-done.1.refs_3_.refs_2_), channel_id=1, source_target_pairs={{0,2},{4,0},{8,4},{12,8},{14,12},{10,14},{6,10},{2,6},{1,3},{5,1},... | collective-permute-start | bytes 743432 | tf_op jit(solution)/shard_map/ppermute | solution.py:460
  33.6 2.5 %collective-permute-start.15 = (bf16[11,88,128]{2,1,0:T(8,128)(2,1)S(1)}, bf16[11,88,128]{2,1,0:T(8,128)(2,1)S(1)}, u32[]{:S(2)}, u32[]{:S(2)}) collective-permute-start(bf16[11,88,128]{2,1,0:T(8,128)(2,1)S(1)} %collective-permute-done.13.refs_3_.refs_2_), channel_id=1, source_target_pairs={{0,2},{4,0},{8,4},{12,8},{14,12},{10,14},{6,10},{2,6},{1,3},{5,1},... | collective-permute-start | bytes 743432 | tf_op jit(solution)/shard_map/ppermute | solution.py:460
  36.7 5.3 %triangle.3.refs_0_ = bf16[6,22,16,128]{3,2,1,0:T(8,128)(2,1)S(1)} custom-call(s32[8]{0:T(128)S(1)} %copy-done.10, f32[22,88,128]{2,1,0:T(8,128)S(1)} %get-tuple-element.37.refs_1_, bf16[11,88,128]{2,1,0:T(8,128)(2,1)S(1)} %get-tuple-element.39.refs_2_.refs_1_, bf16[11,88,128]{2,1,0:T(8,128)(2,1)S(1)} %get-tuple-element.38.refs_3_.refs_2_, ...), custom_call_target="tpu_custom_call" | custom-call | flops 4619999744 | bytes 1048576 | tf_op jit(solution)/shard_map/triangle/pallas_call | solution.py:99
  42.2 1.6 %collective-permute-start.4 = (bf16[11,88,128]{2,1,0:T(8,128)(2,1)S(1)}, bf16[11,88,128]{2,1,0:T(8,128)(2,1)S(1)}, u32[]{:S(2)}, u32[]{:S(2)}) collective-permute-start(bf16[11,88,128]{2,1,0:T(8,128)(2,1)S(1)} %collective-permute-done.2.refs_4_.refs_1_), channel_id=1, source_target_pairs={{0,4},{4,8},{8,12},{12,14},{14,10},{10,6},{6,2},{2,0},{1,5},{5,9},... | collective-permute-start | bytes 743432 | tf_op jit(solution)/shard_map/ppermute | solution.py:457
  43.8 1.1 collective-permute-start.5
  44.9 4.7 %triangle.4.refs_0_ = bf16[4,22,16,128]{3,2,1,0:T(8,128)(2,1)S(1)} custom-call(s32[8]{0:T(128)S(1)} %copy-done.10, f32[22,88,128]{2,1,0:T(8,128)S(1)} %get-tuple-element.37.refs_1_, bf16[11,88,128]{2,1,0:T(8,128)(2,1)S(1)} %collective-permute-done.12.refs_2_.refs_1_, bf16[11,88,128]{2,1,0:T(8,128)(2,1)S(1)} %collective-permute-done.13.refs_3_.refs_2_, ...), custom_call_target="tpu_custom_call" | custom-call | flops 3080000000 | bytes 1048576 | tf_op jit(solution)/shard_map/triangle/pallas_call | solution.py:99
  50.4 1.4 %triangle_norm.3 = (bf16[6,22,16,128]{3,2,1,0:T(8,128)(2,1)S(1)}, bf16[6,22,16,128]{3,2,1,0:T(8,128)(2,1)S(1)}) custom-call(bf16[6,22,16,128]{3,2,1,0:T(8,128)(2,1)S(1)} %triangle.3.refs_0_, bf16[6,22,16,128]{3,2,1,0:T(8,128)(2,1)S(1)} %collective-permute-done.10.refs_1_, bf16[16,22,16,128]{3,2,1,0:T(8,128)(2,1)S(1)} %constant_dynamic-update-slice_fusion.refs_2_.refs_6_, ...), custom_call_target="tpu_custom_call" | custom-call | flops 2640000000 | bytes 1048576 | tf_op jit(solution)/shard_map/triangle_norm/pallas_call | solution.py:99
  51.8 1.0 triangle_norm.4
  52.8 2.4 %scatter_hop.8 = (bf16[11,88,128]{2,1,0:T(8,128)(2,1)S(1)}, bf16[11,88,128]{2,1,0:T(8,128)(2,1)S(1)}) custom-call(s32[8]{0:T(128)S(1)} %copy-done.10, f32[22,88,128]{2,1,0:T(8,128)S(1)} %get-tuple-element.37.refs_1_, bf16[4,22,16,128]{3,2,1,0:T(8,128)(2,1)S(1)} %get-tuple-element.42.refs_2_.refs_3_.refs_0_, ...), custom_call_target="tpu_custom_call" | custom-call | flops 1540000000 | bytes 1048576 | tf_op jit(solution)/shard_map/scatter_hop/pallas_call | solution.py:99
  55.2 6.7 %left_gradient.6.refs_8_.refs_4_.refs_3_ = f32[22,88,128]{2,1,0:T(8,128)S(1)} custom-call(bf16[6,22,16,128]{3,2,1,0:T(8,128)(2,1)S(1)} %get-tuple-element.41.refs_0_.refs_2_.refs_3_, bf16[11,88,128]{2,1,0:T(8,128)(2,1)S(1)} %get-tuple-element.39.refs_2_.refs_1_, bf16[11,88,128]{2,1,0:T(8,128)(2,1)S(1)} %get-tuple-element.38.refs_3_.refs_2_, ...), custom_call_target="tpu_custom_call" | custom-call | flops 5939999744 | bytes 1048576 | tf_op jit(solution)/shard_map/left_gradient/pallas_call | solution.py:99
  61.9 4.6 %triangle.5.refs_0_ = bf16[6,22,16,128]{3,2,1,0:T(8,128)(2,1)S(1)} custom-call(s32[8]{0:T(128)S(1)} %copy-done.10, f32[22,88,128]{2,1,0:T(8,128)S(1)} %get-tuple-element.37.refs_1_, bf16[11,88,128]{2,1,0:T(8,128)(2,1)S(1)} %collective-permute-done.refs_2_.refs_1_, bf16[11,88,128]{2,1,0:T(8,128)(2,1)S(1)} %collective-permute-done.1.refs_3_.refs_2_, ...), custom_call_target="tpu_custom_call" | custom-call | flops 4619999744 | bytes 1048576 | tf_op jit(solution)/shard_map/triangle/pallas_call | solution.py:99
  66.6 1.2 collective-permute-start.18
  67.9 0.8 collective-permute-start.19
  68.6 1.4 %triangle_norm.5 = (bf16[6,22,16,128]{3,2,1,0:T(8,128)(2,1)S(1)}, bf16[6,22,16,128]{3,2,1,0:T(8,128)(2,1)S(1)}) custom-call(bf16[6,22,16,128]{3,2,1,0:T(8,128)(2,1)S(1)} %triangle.5.refs_0_, bf16[6,22,16,128]{3,2,1,0:T(8,128)(2,1)S(1)} %collective-permute-done.17.refs_1_, bf16[16,22,16,128]{3,2,1,0:T(8,128)(2,1)S(1)} %constant_dynamic-update-slice_fusion.refs_2_.refs_6_, ...), custom_call_target="tpu_custom_call" | custom-call | flops 2640000000 | bytes 1048576 | tf_op jit(solution)/shard_map/triangle_norm/pallas_call | solution.py:99
  70.1 1.6 %scatter_hop.9 = (bf16[11,88,128]{2,1,0:T(8,128)(2,1)S(1)}, bf16[11,88,128]{2,1,0:T(8,128)(2,1)S(1)}) custom-call(s32[8]{0:T(128)S(1)} %copy-done.10, f32[22,88,128]{2,1,0:T(8,128)S(1)} %get-tuple-element.37.refs_1_, bf16[6,22,16,128]{3,2,1,0:T(8,128)(2,1)S(1)} %get-tuple-element.44.refs_2_.refs_3_.refs_0_, ...), custom_call_target="tpu_custom_call" | custom-call | flops 1540000000 | bytes 1048576 | tf_op jit(solution)/shard_map/scatter_hop/pallas_call | solution.py:99
  71.7 0.6 collective-permute-start.21
  72.2 1.6 %collective-permute-start.20 = (bf16[11,88,128]{2,1,0:T(8,128)(2,1)S(1)}, bf16[11,88,128]{2,1,0:T(8,128)(2,1)S(1)}, u32[]{:S(2)}, u32[]{:S(2)}) collective-permute-start(bf16[11,88,128]{2,1,0:T(8,128)(2,1)S(1)} %get-tuple-element.45.refs_4_), channel_id=1, source_target_pairs={{0,2},{4,0},{8,4},{12,8},{14,12},{10,14},{6,10},{2,6},{1,3},{5,1},... | collective-permute-start | bytes 743432 | tf_op jit(solution)/shard_map/ppermute | solution.py:460
  73.8 2.0 %left_gradient.7.refs_6_.refs_3_ = f32[22,88,128]{2,1,0:T(8,128)S(1)} custom-call(bf16[4,22,16,128]{3,2,1,0:T(8,128)(2,1)S(1)} %get-tuple-element.42.refs_2_.refs_3_.refs_0_, bf16[11,88,128]{2,1,0:T(8,128)(2,1)S(1)} %collective-permute-done.12.refs_2_.refs_1_, bf16[11,88,128]{2,1,0:T(8,128)(2,1)S(1)} %collective-permute-done.13.refs_3_.refs_2_, ...), custom_call_target="tpu_custom_call" | custom-call | flops 1980000000 | bytes 1048576 | tf_op jit(solution)/shard_map/left_gradient/pallas_call | solution.py:99
  75.8 0.9 collective-permute-done.19.refs_5_
  76.7 2.4 %scatter_hop.10 = (bf16[11,88,128]{2,1,0:T(8,128)(2,1)S(1)}, bf16[11,88,128]{2,1,0:T(8,128)(2,1)S(1)}) custom-call(s32[8]{0:T(128)S(1)} %copy-done.10, f32[22,88,128]{2,1,0:T(8,128)S(1)} %get-tuple-element.37.refs_1_, bf16[4,22,16,128]{3,2,1,0:T(8,128)(2,1)S(1)} %get-tuple-element.42.refs_2_.refs_3_.refs_0_, ...), custom_call_target="tpu_custom_call" | custom-call | flops 1540000000 | bytes 1048576 | tf_op jit(solution)/shard_map/scatter_hop/pallas_call | solution.py:99
  79.1 1.0 collective-permute-start.23
  80.1 1.1 collective-permute-start.22
  81.2 2.0 %left_gradient.8.refs_6_.refs_3_ = f32[22,88,128]{2,1,0:T(8,128)S(1)} custom-call(bf16[4,22,16,128]{3,2,1,0:T(8,128)(2,1)S(1)} %get-tuple-element.42.refs_2_.refs_3_.refs_0_, bf16[11,88,128]{2,1,0:T(8,128)(2,1)S(1)} %collective-permute-done.14.refs_4_.refs_1_, bf16[11,88,128]{2,1,0:T(8,128)(2,1)S(1)} %collective-permute-done.15.refs_5_.refs_2_, ...), custom_call_target="tpu_custom_call" | custom-call | flops 1980000000 | bytes 1048576 | tf_op jit(solution)/shard_map/left_gradient/pallas_call | solution.py:99
  83.3 1.7 %scatter_hop.11 = (bf16[11,88,128]{2,1,0:T(8,128)(2,1)S(1)}, bf16[11,88,128]{2,1,0:T(8,128)(2,1)S(1)}) custom-call(s32[8]{0:T(128)S(1)} %copy-done.10, f32[22,88,128]{2,1,0:T(8,128)S(1)} %get-tuple-element.37.refs_1_, bf16[6,22,16,128]{3,2,1,0:T(8,128)(2,1)S(1)} %get-tuple-element.44.refs_2_.refs_3_.refs_0_, ...), custom_call_target="tpu_custom_call" | custom-call | flops 1540000000 | bytes 1048576 | tf_op jit(solution)/shard_map/scatter_hop/pallas_call | solution.py:99
  85.0 1.3 collective-permute-start.25
  86.2 0.8 collective-permute-start.24
  87.1 2.0 %left_gradient.9.refs_6_.refs_3_ = f32[22,88,128]{2,1,0:T(8,128)S(1)} custom-call(bf16[6,22,16,128]{3,2,1,0:T(8,128)(2,1)S(1)} %get-tuple-element.44.refs_2_.refs_3_.refs_0_, bf16[11,88,128]{2,1,0:T(8,128)(2,1)S(1)} %collective-permute-done.refs_2_.refs_1_, bf16[11,88,128]{2,1,0:T(8,128)(2,1)S(1)} %collective-permute-done.1.refs_3_.refs_2_, ...), custom_call_target="tpu_custom_call" | custom-call | flops 1980000000 | bytes 1048576 | tf_op jit(solution)/shard_map/left_gradient/pallas_call | solution.py:99
  89.1 1.8 %scatter_hop.12 = (bf16[11,88,128]{2,1,0:T(8,128)(2,1)S(1)}, bf16[11,88,128]{2,1,0:T(8,128)(2,1)S(1)}) custom-call(s32[8]{0:T(128)S(1)} %copy-done.10, f32[22,88,128]{2,1,0:T(8,128)S(1)} %get-tuple-element.37.refs_1_, bf16[6,22,16,128]{3,2,1,0:T(8,128)(2,1)S(1)} %get-tuple-element.41.refs_0_.refs_2_.refs_3_, ...), custom_call_target="tpu_custom_call" | custom-call | flops 1540000000 | bytes 1048576 | tf_op jit(solution)/shard_map/scatter_hop/pallas_call | solution.py:99
  91.0 1.7 %collective-permute-start.27 = (bf16[11,88,128]{2,1,0:T(8,128)(2,1)S(1)}, bf16[11,88,128]{2,1,0:T(8,128)(2,1)S(1)}, u32[]{:S(2)}, u32[]{:S(2)}) collective-permute-start(bf16[11,88,128]{2,1,0:T(8,128)(2,1)S(1)} %get-tuple-element.58), channel_id=1, source_target_pairs={{0,4},{4,8},{8,12},{12,14},{14,10},{10,6},{6,2},{2,0},{1,5},{5,9},... | collective-permute-start | bytes 743432 | tf_op jit(solution)/shard_map/ppermute | solution.py:457
  93.0 2.0 %left_gradient.10.refs_6_.refs_3_ = f32[22,88,128]{2,1,0:T(8,128)S(1)} custom-call(bf16[6,22,16,128]{3,2,1,0:T(8,128)(2,1)S(1)} %get-tuple-element.44.refs_2_.refs_3_.refs_0_, bf16[11,88,128]{2,1,0:T(8,128)(2,1)S(1)} %collective-permute-done.2.refs_4_.refs_1_, bf16[11,88,128]{2,1,0:T(8,128)(2,1)S(1)} %collective-permute-done.3.refs_5_.refs_2_, ...), custom_call_target="tpu_custom_call" | custom-call | flops 1980000000 | bytes 1048576 | tf_op jit(solution)/shard_map/left_gradient/pallas_call | solution.py:99
  95.1 2.0 %scatter_hop.13 = (bf16[11,88,128]{2,1,0:T(8,128)(2,1)S(1)}, bf16[11,88,128]{2,1,0:T(8,128)(2,1)S(1)}) custom-call(s32[8]{0:T(128)S(1)} %copy-done.10, f32[22,88,128]{2,1,0:T(8,128)S(1)} %get-tuple-element.37.refs_1_, bf16[6,22,16,128]{3,2,1,0:T(8,128)(2,1)S(1)} %get-tuple-element.44.refs_2_.refs_3_.refs_0_, ...), custom_call_target="tpu_custom_call" | custom-call | flops 1540000000 | bytes 1048576 | tf_op jit(solution)/shard_map/scatter_hop/pallas_call | solution.py:99
  97.1 2.0 %collective-permute-start.31 = (bf16[11,88,128]{2,1,0:T(8,128)(2,1)S(1)}, bf16[11,88,128]{2,1,0:T(8,128)(2,1)S(1)}, u32[]{:S(2)}, u32[]{:S(2)}) collective-permute-start(bf16[11,88,128]{2,1,0:T(8,128)(2,1)S(1)} %get-tuple-element.53.refs_4_), channel_id=1, source_target_pairs={{0,2},{4,0},{8,4},{12,8},{14,12},{10,14},{6,10},{2,6},{1,3},{5,1},... | collective-permute-start | bytes 743432 | tf_op jit(solution)/shard_map/ppermute | solution.py:460
  99.0 2.0 %left_gradient.11.refs_3_.refs_6_ = f32[22,88,128]{2,1,0:T(8,128)S(1)} custom-call(bf16[6,22,16,128]{3,2,1,0:T(8,128)(2,1)S(1)} %get-tuple-element.44.refs_2_.refs_3_.refs_0_, bf16[11,88,128]{2,1,0:T(8,128)(2,1)S(1)} %collective-permute-done.4.refs_6_.refs_1_, bf16[11,88,128]{2,1,0:T(8,128)(2,1)S(1)} %collective-permute-done.5.refs_7_.refs_2_, ...), custom_call_target="tpu_custom_call" | custom-call | flops 1980000000 | bytes 1048576 | tf_op jit(solution)/shard_map/left_gradient/pallas_call | solution.py:99
  101.1 1.8 %scatter_hop.14 = (bf16[11,88,128]{2,1,0:T(8,128)(2,1)S(1)}, bf16[11,88,128]{2,1,0:T(8,128)(2,1)S(1)}) custom-call(s32[8]{0:T(128)S(1)} %copy-done.10, f32[22,88,128]{2,1,0:T(8,128)S(1)} %get-tuple-element.37.refs_1_, bf16[6,22,16,128]{3,2,1,0:T(8,128)(2,1)S(1)} %get-tuple-element.41.refs_0_.refs_2_.refs_3_, ...), custom_call_target="tpu_custom_call" | custom-call | flops 1540000000 | bytes 1048576 | tf_op jit(solution)/shard_map/scatter_hop/pallas_call | solution.py:99
  103.1 2.1 %collective-permute-start.28 = (bf16[11,88,128]{2,1,0:T(8,128)(2,1)S(1)}, bf16[11,88,128]{2,1,0:T(8,128)(2,1)S(1)}, u32[]{:S(2)}, u32[]{:S(2)}) collective-permute-start(bf16[11,88,128]{2,1,0:T(8,128)(2,1)S(1)} %get-tuple-element.59.refs_4_), channel_id=1, source_target_pairs={{0,2},{4,0},{8,4},{12,8},{14,12},{10,14},{6,10},{2,6},{1,3},{5,1},... | collective-permute-start | bytes 743432 | tf_op jit(solution)/shard_map/ppermute | solution.py:460
  105.3 6.4 %output_side.1 = (bf16[22,88,128]{2,1,0:T(8,128)(2,1)}, f32[22,88,128]{2,1,0:T(8,128)S(1)}, bf16[128,512]{1,0:T(8,128)(2,1)S(1)}) custom-call(s32[8]{0:T(128)S(1)} %copy-done.10, bf16[22,88,128]{2,1,0:T(8,128)(2,1)S(1)} %get-tuple-element.36.refs_1_, bf16[22,88,128]{2,1,0:T(8,128)(2,1)S(1)} %copy-done, f32[22,88,128]{2,1,0:T(8,128)S(1)} %left_gradient.11.refs_3_.refs_6_, ...), custom_call_target="tpu_custom_call" | custom-call | flops 6600000000 | bytes 1048576 | tf_op jit(solution)/shard_map/output_side/pallas_call | solution.py:99
  111.7 2.1 %scatter_hop.15 = (f32[11,88,128]{2,1,0:T(8,128)S(1)}, f32[11,88,128]{2,1,0:T(8,128)S(1)}) custom-call(s32[8]{0:T(128)S(1)} %copy-done.10, f32[22,88,128]{2,1,0:T(8,128)S(1)} %get-tuple-element.37.refs_1_, bf16[6,22,16,128]{3,2,1,0:T(8,128)(2,1)S(1)} %get-tuple-element.41.refs_0_.refs_2_.refs_3_, ...), custom_call_target="tpu_custom_call" | custom-call | flops 1540000000 | bytes 1048576 | tf_op jit(solution)/shard_map/scatter_hop/pallas_call | solution.py:99
  113.8 2.0 %right_gradient.1 = (bf16[22,88,256]{2,1,0:T(8,128)(2,1)S(1)}, bf16[128,256]{1,0:T(8,128)(2,1)S(1)}) custom-call(s32[8]{0:T(128)S(1)} %copy-done.10, bf16[22,88,128]{2,1,0:T(8,128)(2,1)S(1)} %get-tuple-element.36.refs_1_, bf16[128,640]{1,0:T(8,128)(2,1)S(1)} %copy-done.4, f32[11,88,128]{2,1,0:T(8,128)S(1)} %get-tuple-element.60.refs_3_, ...), custom_call_target="tpu_custom_call" | custom-call | flops 3300000000 | bytes 1048576 | tf_op jit(solution)/shard_map/right_gradient/pallas_call | solution.py:99
  116.5 1.8 %collective-permute-start.33 = (bf16[128,512]{1,0:T(8,128)(2,1)S(1)}, bf16[128,512]{1,0:T(8,128)(2,1)S(1)}, u32[]{:S(2)}, u32[]{:S(2)}) collective-permute-start(bf16[128,512]{1,0:T(8,128)(2,1)S(1)} %add_convert_fusion.3), channel_id=1, source_target_pairs={{0,2},{2,0},{4,6},{6,4},{8,10},{10,8},{12,14},{14,12},{1,3},{3,1},... | collective-permute-start | bytes 393224 | tf_op jit(solution)/shard_map/ppermute | solution.py:86
  118.3 0.9 collective-permute-start.37
  119.2 3.3 %pair_gradient.1 = bf16[22,88,128]{2,1,0:T(8,128)(2,1)} custom-call(bf16[22,88,128]{2,1,0:T(8,128)(2,1)S(1)} %copy-done.2, bf16[22,88,256]{2,1,0:T(8,128)(2,1)S(1)} %get-tuple-element.64.refs_1_, f32[22,88,128]{2,1,0:T(8,128)S(1)} %get-tuple-element.65.refs_2_, f32[1,128]{1,0:T(1,128)S(1)} %bitcast.12, bf16[128,640]{1,0:T(8,128)(2,1)S(1)} %copy-done.4), custom_call_target="tpu_custom_call" | custom-call | flops 3300000000 | bytes 1048576 | tf_op jit(solution)/shard_map/pair_gradient/pallas_call | solution.py:99
  122.5 0.9 collective-permute-done.37
  123.4 1.8 %collective-permute-start.38 = (bf16[128,256]{1,0:T(8,128)(2,1)S(1)}, bf16[128,256]{1,0:T(8,128)(2,1)S(1)}, u32[]{:S(2)}, u32[]{:S(2)}) collective-permute-start(bf16[128,256]{1,0:T(8,128)(2,1)S(1)} %add_convert_fusion.6), channel_id=1, source_target_pairs={{0,4},{2,6},{4,0},{6,2},{8,12},{10,14},{12,8},{14,10},{1,5},{3,7},... | collective-permute-start | bytes 196616 | tf_op jit(solution)/shard_map/ppermute | solution.py:86
  125.6 2.8 %collective-permute-done.38 = bf16[128,256]{1,0:T(8,128)(2,1)S(1)} collective-permute-done((bf16[128,256]{1,0:T(8,128)(2,1)S(1)}, bf16[128,256]{1,0:T(8,128)(2,1)S(1)}, u32[]{:S(2)}, u32[]{:S(2)}) %collective-permute-start.38) | collective-permute-done | bytes 65568 | tf_op jit(solution)/shard_map/ppermute | solution.py:86
  128.5 2.4 %collective-permute-start.39 = (bf16[128,256]{1,0:T(8,128)(2,1)S(1)}, bf16[128,256]{1,0:T(8,128)(2,1)S(1)}, u32[]{:S(2)}, u32[]{:S(2)}) collective-permute-start(bf16[128,256]{1,0:T(8,128)(2,1)S(1)} %add_convert_fusion.5), channel_id=1, source_target_pairs={{0,8},{2,10},{4,12},{6,14},{8,0},{10,2},{12,4},{14,6},{1,9},{3,11}... | collective-permute-start | bytes 196616 | tf_op jit(solution)/shard_map/ppermute | solution.py:86
  131.1 1.9 %collective-permute-start.35 = (bf16[128,512]{1,0:T(8,128)(2,1)S(1)}, bf16[128,512]{1,0:T(8,128)(2,1)S(1)}, u32[]{:S(2)}, u32[]{:S(2)}) collective-permute-start(bf16[128,512]{1,0:T(8,128)(2,1)S(1)} %add_convert_fusion.1), channel_id=1, source_target_pairs={{0,8},{2,10},{4,12},{6,14},{8,0},{10,2},{12,4},{14,6},{1,9},{3,11}... | collective-permute-start | bytes 393224 | tf_op jit(solution)/shard_map/ppermute | solution.py:86
  133.0 4.7 %collective-permute-done.39 = bf16[128,256]{1,0:T(8,128)(2,1)S(1)} collective-permute-done((bf16[128,256]{1,0:T(8,128)(2,1)S(1)}, bf16[128,256]{1,0:T(8,128)(2,1)S(1)}, u32[]{:S(2)}, u32[]{:S(2)}) %collective-permute-start.39) | collective-permute-done | bytes 65568 | tf_op jit(solution)/shard_map/ppermute | solution.py:86
  137.7 1.6 %collective-permute-done.35 = bf16[128,512]{1,0:T(8,128)(2,1)S(1)} collective-permute-done((bf16[128,512]{1,0:T(8,128)(2,1)S(1)}, bf16[128,512]{1,0:T(8,128)(2,1)S(1)}, u32[]{:S(2)}, u32[]{:S(2)}) %collective-permute-start.35) | collective-permute-done | bytes 131104 | tf_op jit(solution)/shard_map/ppermute | solution.py:86
  139.4 0.6 fusion.2
  140.1 0.7 pad_maximum_fusion
  (80 shorter events, 5.8 us)
Async XLA Ops:
  0.6 1.0 copy-start.1
  1.7 0.9 copy-start.3
  2.6 0.7 copy-start.6
  3.2 0.7 copy-start.9
  3.9 0.7 copy-start.11
  4.6 21.5 %copy-start = (bf16[22,88,128]{2,1,0:T(8,128)(2,1)S(1)}, bf16[22,88,128]{2,1,0:T(8,128)(2,1)}, u32[]{:S(2)}) copy-start(bf16[22,88,128]{2,1,0:T(8,128)(2,1)} %refs_2_.4) | copy-start | bytes 1486852
  4.6 21.5 %copy-start.4 = (bf16[128,640]{1,0:T(8,128)(2,1)S(1)}, bf16[128,640]{1,0:T(8,128)(2,1)}, u32[]{:S(2)}) copy-start(bf16[128,640]{1,0:T(8,128)(2,1)} %refs_4_.5) | copy-start | bytes 491524
  4.6 21.5 %copy-start.10 = (s32[8]{0:T(128)S(1)}, s32[8]{0:T(128)}, u32[]{:S(2)}) copy-start(s32[8]{0:T(128)} %refs_0_.30) | copy-start | bytes 100
  6.0 9.1 %collective-permute-start.7 = (bf16[11,88,128]{2,1,0:T(8,128)(2,1)S(1)}, bf16[11,88,128]{2,1,0:T(8,128)(2,1)S(1)}, u32[]{:S(2)}, u32[]{:S(2)}) collective-permute-start(bf16[11,88,128]{2,1,0:T(8,128)(2,1)S(1)} %get-tuple-element.38.refs_3_.refs_2_), channel_id=1, source_target_pairs={{0,2},{4,0},{8,4},{12,8},{14,12},{10,14},{6,10},{2,6},{1,3},{5,1},... | collective-permute-start | bytes 743432 | tf_op jit(solution)/shard_map/ppermute | solution.py:460
  9.0 7.7 %collective-permute-start.6 = (bf16[11,88,128]{2,1,0:T(8,128)(2,1)S(1)}, bf16[11,88,128]{2,1,0:T(8,128)(2,1)S(1)}, u32[]{:S(2)}, u32[]{:S(2)}) collective-permute-start(bf16[11,88,128]{2,1,0:T(8,128)(2,1)S(1)} %get-tuple-element.39.refs_2_.refs_1_), channel_id=1, source_target_pairs={{0,4},{4,8},{8,12},{12,14},{14,10},{10,6},{6,2},{2,0},{1,5},{5,9},... | collective-permute-start | bytes 743432 | tf_op jit(solution)/shard_map/ppermute | solution.py:457
  15.1 8.9 %collective-permute-start.9 = (bf16[11,88,128]{2,1,0:T(8,128)(2,1)S(1)}, bf16[11,88,128]{2,1,0:T(8,128)(2,1)S(1)}, u32[]{:S(2)}, u32[]{:S(2)}) collective-permute-start(bf16[11,88,128]{2,1,0:T(8,128)(2,1)S(1)} %collective-permute-done.7.refs_5_.refs_4_), channel_id=1, source_target_pairs={{0,2},{4,0},{8,4},{12,8},{14,12},{10,14},{6,10},{2,6},{1,3},{5,1},... | collective-permute-start | bytes 743432 | tf_op jit(solution)/shard_map/ppermute | solution.py:460
  16.8 8.9 %collective-permute-start.8 = (bf16[11,88,128]{2,1,0:T(8,128)(2,1)S(1)}, bf16[11,88,128]{2,1,0:T(8,128)(2,1)S(1)}, u32[]{:S(2)}, u32[]{:S(2)}) collective-permute-start(bf16[11,88,128]{2,1,0:T(8,128)(2,1)S(1)} %collective-permute-done.6.refs_4_.refs_3_), channel_id=1, source_target_pairs={{0,4},{4,8},{8,12},{12,14},{14,10},{10,6},{6,2},{2,0},{1,5},{5,9},... | collective-permute-start | bytes 743432 | tf_op jit(solution)/shard_map/ppermute | solution.py:457
  17.1 13.9 %collective-permute-start = (bf16[11,88,128]{2,1,0:T(8,128)(2,1)S(1)}, bf16[11,88,128]{2,1,0:T(8,128)(2,1)S(1)}, u32[]{:S(2)}, u32[]{:S(2)}) collective-permute-start(bf16[11,88,128]{2,1,0:T(8,128)(2,1)S(1)} %get-tuple-element.38.refs_3_.refs_2_), channel_id=1, source_target_pairs={{0,4},{4,8},{8,12},{12,14},{14,10},{10,6},{6,2},{2,0},{1,5},{5,9},... | collective-permute-start | bytes 743432 | tf_op jit(solution)/shard_map/ppermute | solution.py:457
  18.9 12.5 %collective-permute-start.1 = (bf16[11,88,128]{2,1,0:T(8,128)(2,1)S(1)}, bf16[11,88,128]{2,1,0:T(8,128)(2,1)S(1)}, u32[]{:S(2)}, u32[]{:S(2)}) collective-permute-start(bf16[11,88,128]{2,1,0:T(8,128)(2,1)S(1)} %get-tuple-element.39.refs_2_.refs_1_), channel_id=1, source_target_pairs={{0,2},{4,0},{8,4},{12,8},{14,12},{10,14},{6,10},{2,6},{1,3},{5,1},... | collective-permute-start | bytes 743432 | tf_op jit(solution)/shard_map/ppermute | solution.py:460
  24.0 9.6 %collective-permute-start.13 = (bf16[11,88,128]{2,1,0:T(8,128)(2,1)S(1)}, bf16[11,88,128]{2,1,0:T(8,128)(2,1)S(1)}, u32[]{:S(2)}, u32[]{:S(2)}) collective-permute-start(bf16[11,88,128]{2,1,0:T(8,128)(2,1)S(1)} %collective-permute-done.9.refs_7_.refs_6_), channel_id=1, source_target_pairs={{0,2},{4,0},{8,4},{12,8},{14,12},{10,14},{6,10},{2,6},{1,3},{5,1},... | collective-permute-start | bytes 743432 | tf_op jit(solution)/shard_map/ppermute | solution.py:460
  25.7 10.6 %collective-permute-start.12 = (bf16[11,88,128]{2,1,0:T(8,128)(2,1)S(1)}, bf16[11,88,128]{2,1,0:T(8,128)(2,1)S(1)}, u32[]{:S(2)}, u32[]{:S(2)}) collective-permute-start(bf16[11,88,128]{2,1,0:T(8,128)(2,1)S(1)} %collective-permute-done.8.refs_6_.refs_5_), channel_id=1, source_target_pairs={{0,4},{4,8},{8,12},{12,14},{14,10},{10,6},{6,2},{2,0},{1,5},{5,9},... | collective-permute-start | bytes 743432 | tf_op jit(solution)/shard_map/ppermute | solution.py:457
  27.5 22.2 %collective-permute-start.11 = (bf16[8,22,16,128]{3,2,1,0:T(8,128)(2,1)S(1)}, bf16[8,22,16,128]{3,2,1,0:T(8,128)(2,1)S(1)}, u32[]{:S(2)}, u32[]{:S(2)}) collective-permute-start(bf16[8,22,16,128]{3,2,1,0:T(8,128)(2,1)S(1)} %get-tuple-element.40), channel_id=1, source_target_pairs={{0,1},{1,0},{2,3},{3,2},{4,5},{5,4},{6,7},{7,6},{8,9},{9,8},{10,11... | collective-permute-start | bytes 2162696 | tf_op jit(solution)/shard_map/ppermute | solution.py:76
  31.0 10.9 %collective-permute-start.2 = (bf16[11,88,128]{2,1,0:T(8,128)(2,1)S(1)}, bf16[11,88,128]{2,1,0:T(8,128)(2,1)S(1)}, u32[]{:S(2)}, u32[]{:S(2)}) collective-permute-start(bf16[11,88,128]{2,1,0:T(8,128)(2,1)S(1)} %collective-permute-done.refs_2_.refs_1_), channel_id=1, source_target_pairs={{0,4},{4,8},{8,12},{12,14},{14,10},{10,6},{6,2},{2,0},{1,5},{5,9},... | collective-permute-start | bytes 743432 | tf_op jit(solution)/shard_map/ppermute | solution.py:457
  31.4 10.8 %collective-permute-start.3 = (bf16[11,88,128]{2,1,0:T(8,128)(2,1)S(1)}, bf16[11,88,128]{2,1,0:T(8,128)(2,1)S(1)}, u32[]{:S(2)}, u32[]{:S(2)}) collective-permute-start(bf16[11,88,128]{2,1,0:T(8,128)(2,1)S(1)} %collective-permute-done.1.refs_3_.refs_2_), channel_id=1, source_target_pairs={{0,2},{4,0},{8,4},{12,8},{14,12},{10,14},{6,10},{2,6},{1,3},{5,1},... | collective-permute-start | bytes 743432 | tf_op jit(solution)/shard_map/ppermute | solution.py:460
  33.6 10.2 %collective-permute-start.15 = (bf16[11,88,128]{2,1,0:T(8,128)(2,1)S(1)}, bf16[11,88,128]{2,1,0:T(8,128)(2,1)S(1)}, u32[]{:S(2)}, u32[]{:S(2)}) collective-permute-start(bf16[11,88,128]{2,1,0:T(8,128)(2,1)S(1)} %collective-permute-done.13.refs_3_.refs_2_), channel_id=1, source_target_pairs={{0,2},{4,0},{8,4},{12,8},{14,12},{10,14},{6,10},{2,6},{1,3},{5,1},... | collective-permute-start | bytes 743432 | tf_op jit(solution)/shard_map/ppermute | solution.py:460
  36.3 8.6 %collective-permute-start.14 = (bf16[11,88,128]{2,1,0:T(8,128)(2,1)S(1)}, bf16[11,88,128]{2,1,0:T(8,128)(2,1)S(1)}, u32[]{:S(2)}, u32[]{:S(2)}) collective-permute-start(bf16[11,88,128]{2,1,0:T(8,128)(2,1)S(1)} %collective-permute-done.12.refs_2_.refs_1_), channel_id=1, source_target_pairs={{0,4},{4,8},{8,12},{12,14},{14,10},{10,6},{6,2},{2,0},{1,5},{5,9},... | collective-permute-start | bytes 743432 | tf_op jit(solution)/shard_map/ppermute | solution.py:457
  42.0 8.0 %collective-permute-start.10 = (bf16[6,22,16,128]{3,2,1,0:T(8,128)(2,1)S(1)}, bf16[6,22,16,128]{3,2,1,0:T(8,128)(2,1)S(1)}, u32[]{:S(2)}, u32[]{:S(2)}) collective-permute-start(bf16[6,22,16,128]{3,2,1,0:T(8,128)(2,1)S(1)} %triangle.3.refs_0_), channel_id=1, source_target_pairs={{0,1},{1,0},{2,3},{3,2},{4,5},{5,4},{6,7},{7,6},{8,9},{9,8},{10,11... | collective-permute-start | bytes 1622024 | tf_op jit(solution)/shard_map/ppermute | solution.py:76
  42.2 19.7 %collective-permute-start.4 = (bf16[11,88,128]{2,1,0:T(8,128)(2,1)S(1)}, bf16[11,88,128]{2,1,0:T(8,128)(2,1)S(1)}, u32[]{:S(2)}, u32[]{:S(2)}) collective-permute-start(bf16[11,88,128]{2,1,0:T(8,128)(2,1)S(1)} %collective-permute-done.2.refs_4_.refs_1_), channel_id=1, source_target_pairs={{0,4},{4,8},{8,12},{12,14},{14,10},{10,6},{6,2},{2,0},{1,5},{5,9},... | collective-permute-start | bytes 743432 | tf_op jit(solution)/shard_map/ppermute | solution.py:457
  43.8 18.0 %collective-permute-start.5 = (bf16[11,88,128]{2,1,0:T(8,128)(2,1)S(1)}, bf16[11,88,128]{2,1,0:T(8,128)(2,1)S(1)}, u32[]{:S(2)}, u32[]{:S(2)}) collective-permute-start(bf16[11,88,128]{2,1,0:T(8,128)(2,1)S(1)} %collective-permute-done.3.refs_5_.refs_2_), channel_id=1, source_target_pairs={{0,2},{4,0},{8,4},{12,8},{14,12},{10,14},{6,10},{2,6},{1,3},{5,1},... | collective-permute-start | bytes 743432 | tf_op jit(solution)/shard_map/ppermute | solution.py:460
  49.6 0.8 copy-start.5
  49.6 0.8 copy-start.7
  49.6 0.7 copy-start.8
  49.6 2.2 %collective-permute-start.16 = (bf16[4,22,16,128]{3,2,1,0:T(8,128)(2,1)S(1)}, bf16[4,22,16,128]{3,2,1,0:T(8,128)(2,1)S(1)}, u32[]{:S(2)}, u32[]{:S(2)}) collective-permute-start(bf16[4,22,16,128]{3,2,1,0:T(8,128)(2,1)S(1)} %triangle.4.refs_0_), channel_id=1, source_target_pairs={{0,1},{1,0},{2,3},{3,2},{4,5},{5,4},{6,7},{7,6},{8,9},{9,8},{10,11... | collective-permute-start | bytes 1081352 | tf_op jit(solution)/shard_map/ppermute | solution.py:76
  66.5 2.2 %collective-permute-start.17 = (bf16[6,22,16,128]{3,2,1,0:T(8,128)(2,1)S(1)}, bf16[6,22,16,128]{3,2,1,0:T(8,128)(2,1)S(1)}, u32[]{:S(2)}, u32[]{:S(2)}) collective-permute-start(bf16[6,22,16,128]{3,2,1,0:T(8,128)(2,1)S(1)} %triangle.5.refs_0_), channel_id=1, source_target_pairs={{0,1},{1,0},{2,3},{3,2},{4,5},{5,4},{6,7},{7,6},{8,9},{9,8},{10,11... | collective-permute-start | bytes 1622024 | tf_op jit(solution)/shard_map/ppermute | solution.py:76
  66.6 10.1 %collective-permute-start.18 = (bf16[11,88,128]{2,1,0:T(8,128)(2,1)S(1)}, bf16[11,88,128]{2,1,0:T(8,128)(2,1)S(1)}, u32[]{:S(2)}, u32[]{:S(2)}) collective-permute-start(bf16[11,88,128]{2,1,0:T(8,128)(2,1)S(1)} %get-tuple-element.43.refs_7_), channel_id=1, source_target_pairs={{0,2},{4,0},{8,4},{12,8},{14,12},{10,14},{6,10},{2,6},{1,3},{5,1},... | collective-permute-start | bytes 743432 | tf_op jit(solution)/shard_map/ppermute | solution.py:460
  67.9 8.8 %collective-permute-start.19 = (bf16[11,88,128]{2,1,0:T(8,128)(2,1)S(1)}, bf16[11,88,128]{2,1,0:T(8,128)(2,1)S(1)}, u32[]{:S(2)}, u32[]{:S(2)}) collective-permute-start(bf16[11,88,128]{2,1,0:T(8,128)(2,1)S(1)} %get-tuple-element.46), channel_id=1, source_target_pairs={{0,4},{4,8},{8,12},{12,14},{14,10},{10,6},{6,2},{2,0},{1,5},{5,9},... | collective-permute-start | bytes 743432 | tf_op jit(solution)/shard_map/ppermute | solution.py:457
  71.7 11.6 %collective-permute-start.21 = (bf16[11,88,128]{2,1,0:T(8,128)(2,1)S(1)}, bf16[11,88,128]{2,1,0:T(8,128)(2,1)S(1)}, u32[]{:S(2)}, u32[]{:S(2)}) collective-permute-start(bf16[11,88,128]{2,1,0:T(8,128)(2,1)S(1)} %get-tuple-element.48), channel_id=1, source_target_pairs={{0,4},{4,8},{8,12},{12,14},{14,10},{10,6},{6,2},{2,0},{1,5},{5,9},... | collective-permute-start | bytes 743432 | tf_op jit(solution)/shard_map/ppermute | solution.py:457
  72.2 11.0 %collective-permute-start.20 = (bf16[11,88,128]{2,1,0:T(8,128)(2,1)S(1)}, bf16[11,88,128]{2,1,0:T(8,128)(2,1)S(1)}, u32[]{:S(2)}, u32[]{:S(2)}) collective-permute-start(bf16[11,88,128]{2,1,0:T(8,128)(2,1)S(1)} %get-tuple-element.45.refs_4_), channel_id=1, source_target_pairs={{0,2},{4,0},{8,4},{12,8},{14,12},{10,14},{6,10},{2,6},{1,3},{5,1},... | collective-permute-start | bytes 743432 | tf_op jit(solution)/shard_map/ppermute | solution.py:460
  79.1 9.9 %collective-permute-start.23 = (bf16[11,88,128]{2,1,0:T(8,128)(2,1)S(1)}, bf16[11,88,128]{2,1,0:T(8,128)(2,1)S(1)}, u32[]{:S(2)}, u32[]{:S(2)}) collective-permute-start(bf16[11,88,128]{2,1,0:T(8,128)(2,1)S(1)} %get-tuple-element.50), channel_id=1, source_target_pairs={{0,4},{4,8},{8,12},{12,14},{14,10},{10,6},{6,2},{2,0},{1,5},{5,9},... | collective-permute-start | bytes 743432 | tf_op jit(solution)/shard_map/ppermute | solution.py:457
  80.1 9.0 %collective-permute-start.22 = (bf16[11,88,128]{2,1,0:T(8,128)(2,1)S(1)}, bf16[11,88,128]{2,1,0:T(8,128)(2,1)S(1)}, u32[]{:S(2)}, u32[]{:S(2)}) collective-permute-start(bf16[11,88,128]{2,1,0:T(8,128)(2,1)S(1)} %get-tuple-element.47.refs_4_), channel_id=1, source_target_pairs={{0,2},{4,0},{8,4},{12,8},{14,12},{10,14},{6,10},{2,6},{1,3},{5,1},... | collective-permute-start | bytes 743432 | tf_op jit(solution)/shard_map/ppermute | solution.py:460
  85.0 10.1 %collective-permute-start.25 = (bf16[11,88,128]{2,1,0:T(8,128)(2,1)S(1)}, bf16[11,88,128]{2,1,0:T(8,128)(2,1)S(1)}, u32[]{:S(2)}, u32[]{:S(2)}) collective-permute-start(bf16[11,88,128]{2,1,0:T(8,128)(2,1)S(1)} %get-tuple-element.52), channel_id=1, source_target_pairs={{0,4},{4,8},{8,12},{12,14},{14,10},{10,6},{6,2},{2,0},{1,5},{5,9},... | collective-permute-start | bytes 743432 | tf_op jit(solution)/shard_map/ppermute | solution.py:457
  86.2 8.8 %collective-permute-start.24 = (bf16[11,88,128]{2,1,0:T(8,128)(2,1)S(1)}, bf16[11,88,128]{2,1,0:T(8,128)(2,1)S(1)}, u32[]{:S(2)}, u32[]{:S(2)}) collective-permute-start(bf16[11,88,128]{2,1,0:T(8,128)(2,1)S(1)} %get-tuple-element.49.refs_4_), channel_id=1, source_target_pairs={{0,2},{4,0},{8,4},{12,8},{14,12},{10,14},{6,10},{2,6},{1,3},{5,1},... | collective-permute-start | bytes 743432 | tf_op jit(solution)/shard_map/ppermute | solution.py:460
  91.0 10.1 %collective-permute-start.27 = (bf16[11,88,128]{2,1,0:T(8,128)(2,1)S(1)}, bf16[11,88,128]{2,1,0:T(8,128)(2,1)S(1)}, u32[]{:S(2)}, u32[]{:S(2)}) collective-permute-start(bf16[11,88,128]{2,1,0:T(8,128)(2,1)S(1)} %get-tuple-element.58), channel_id=1, source_target_pairs={{0,4},{4,8},{8,12},{12,14},{14,10},{10,6},{6,2},{2,0},{1,5},{5,9},... | collective-permute-start | bytes 743432 | tf_op jit(solution)/shard_map/ppermute | solution.py:457
  92.6 8.4 %collective-permute-start.26 = (bf16[11,88,128]{2,1,0:T(8,128)(2,1)S(1)}, bf16[11,88,128]{2,1,0:T(8,128)(2,1)S(1)}, u32[]{:S(2)}, u32[]{:S(2)}) collective-permute-start(bf16[11,88,128]{2,1,0:T(8,128)(2,1)S(1)} %get-tuple-element.51.refs_4_), channel_id=1, source_target_pairs={{0,2},{4,0},{8,4},{12,8},{14,12},{10,14},{6,10},{2,6},{1,3},{5,1},... | collective-permute-start | bytes 743432 | tf_op jit(solution)/shard_map/ppermute | solution.py:460
  97.1 16.7 %collective-permute-start.31 = (bf16[11,88,128]{2,1,0:T(8,128)(2,1)S(1)}, bf16[11,88,128]{2,1,0:T(8,128)(2,1)S(1)}, u32[]{:S(2)}, u32[]{:S(2)}) collective-permute-start(bf16[11,88,128]{2,1,0:T(8,128)(2,1)S(1)} %get-tuple-element.53.refs_4_), channel_id=1, source_target_pairs={{0,2},{4,0},{8,4},{12,8},{14,12},{10,14},{6,10},{2,6},{1,3},{5,1},... | collective-permute-start | bytes 743432 | tf_op jit(solution)/shard_map/ppermute | solution.py:460
  102.9 10.9 %collective-permute-start.30 = (bf16[11,88,128]{2,1,0:T(8,128)(2,1)S(1)}, bf16[11,88,128]{2,1,0:T(8,128)(2,1)S(1)}, u32[]{:S(2)}, u32[]{:S(2)}) collective-permute-start(bf16[11,88,128]{2,1,0:T(8,128)(2,1)S(1)} %get-tuple-element.63), channel_id=1, source_target_pairs={{0,4},{4,8},{8,12},{12,14},{14,10},{10,6},{6,2},{2,0},{1,5},{5,9},... | collective-permute-start | bytes 743432 | tf_op jit(solution)/shard_map/ppermute | solution.py:457
  103.1 10.7 %collective-permute-start.28 = (bf16[11,88,128]{2,1,0:T(8,128)(2,1)S(1)}, bf16[11,88,128]{2,1,0:T(8,128)(2,1)S(1)}, u32[]{:S(2)}, u32[]{:S(2)}) collective-permute-start(bf16[11,88,128]{2,1,0:T(8,128)(2,1)S(1)} %get-tuple-element.59.refs_4_), channel_id=1, source_target_pairs={{0,2},{4,0},{8,4},{12,8},{14,12},{10,14},{6,10},{2,6},{1,3},{5,1},... | collective-permute-start | bytes 743432 | tf_op jit(solution)/shard_map/ppermute | solution.py:460
  105.1 8.7 %collective-permute-start.29 = (bf16[11,88,128]{2,1,0:T(8,128)(2,1)S(1)}, bf16[11,88,128]{2,1,0:T(8,128)(2,1)S(1)}, u32[]{:S(2)}, u32[]{:S(2)}) collective-permute-start(bf16[11,88,128]{2,1,0:T(8,128)(2,1)S(1)} %get-tuple-element.62), channel_id=1, source_target_pairs={{0,4},{4,8},{8,12},{12,14},{14,10},{10,6},{6,2},{2,0},{1,5},{5,9},... | collective-permute-start | bytes 743432 | tf_op jit(solution)/shard_map/ppermute | solution.py:457
  111.7 4.8 %collective-permute-start.32 = (bf16[128,512]{1,0:T(8,128)(2,1)S(1)}, bf16[128,512]{1,0:T(8,128)(2,1)S(1)}, u32[]{:S(2)}, u32[]{:S(2)}) collective-permute-start(bf16[128,512]{1,0:T(8,128)(2,1)S(1)} %get-tuple-element.66), channel_id=1, source_target_pairs={{0,1},{1,0},{2,3},{3,2},{4,5},{5,4},{6,7},{7,6},{8,9},{9,8},{10,11... | collective-permute-start | bytes 393224 | tf_op jit(solution)/shard_map/ppermute | solution.py:76
  113.8 5.4 %copy-start.2 = (bf16[22,88,128]{2,1,0:T(8,128)(2,1)S(1)}, bf16[22,88,128]{2,1,0:T(8,128)(2,1)}, u32[]{:S(2)}) copy-start(bf16[22,88,128]{2,1,0:T(8,128)(2,1)} %refs_0_.31) | copy-start | bytes 1486852
  113.8 5.4 %copy-start.12 = (f32[128]{0:T(128)S(1)}, f32[128]{0:T(128)}, u32[]{:S(2)}) copy-start(f32[128]{0:T(128)} %param.12) | copy-start | bytes 1540
  115.9 2.5 %collective-permute-start.36 = (bf16[128,256]{1,0:T(8,128)(2,1)S(1)}, bf16[128,256]{1,0:T(8,128)(2,1)S(1)}, u32[]{:S(2)}, u32[]{:S(2)}) collective-permute-start(bf16[128,256]{1,0:T(8,128)(2,1)S(1)} %get-tuple-element.67), channel_id=1, source_target_pairs={{0,1},{1,0},{2,3},{3,2},{4,5},{5,4},{6,7},{7,6},{8,9},{9,8},{10,11... | collective-permute-start | bytes 196616 | tf_op jit(solution)/shard_map/ppermute | solution.py:76
  116.5 8.7 %collective-permute-start.33 = (bf16[128,512]{1,0:T(8,128)(2,1)S(1)}, bf16[128,512]{1,0:T(8,128)(2,1)S(1)}, u32[]{:S(2)}, u32[]{:S(2)}) collective-permute-start(bf16[128,512]{1,0:T(8,128)(2,1)S(1)} %add_convert_fusion.3), channel_id=1, source_target_pairs={{0,2},{2,0},{4,6},{6,4},{8,10},{10,8},{12,14},{14,12},{1,3},{3,1},... | collective-permute-start | bytes 393224 | tf_op jit(solution)/shard_map/ppermute | solution.py:86
  118.3 5.1 %collective-permute-start.37 = (bf16[128,256]{1,0:T(8,128)(2,1)S(1)}, bf16[128,256]{1,0:T(8,128)(2,1)S(1)}, u32[]{:S(2)}, u32[]{:S(2)}) collective-permute-start(bf16[128,256]{1,0:T(8,128)(2,1)S(1)} %add_convert_fusion.7), channel_id=1, source_target_pairs={{0,2},{2,0},{4,6},{6,4},{8,10},{10,8},{12,14},{14,12},{1,3},{3,1},... | collective-permute-start | bytes 196616 | tf_op jit(solution)/shard_map/ppermute | solution.py:86
  123.4 5.0 %collective-permute-start.38 = (bf16[128,256]{1,0:T(8,128)(2,1)S(1)}, bf16[128,256]{1,0:T(8,128)(2,1)S(1)}, u32[]{:S(2)}, u32[]{:S(2)}) collective-permute-start(bf16[128,256]{1,0:T(8,128)(2,1)S(1)} %add_convert_fusion.6), channel_id=1, source_target_pairs={{0,4},{2,6},{4,0},{6,2},{8,12},{10,14},{12,8},{14,10},{1,5},{3,7},... | collective-permute-start | bytes 196616 | tf_op jit(solution)/shard_map/ppermute | solution.py:86
  125.3 5.8 %collective-permute-start.34 = (bf16[128,512]{1,0:T(8,128)(2,1)S(1)}, bf16[128,512]{1,0:T(8,128)(2,1)S(1)}, u32[]{:S(2)}, u32[]{:S(2)}) collective-permute-start(bf16[128,512]{1,0:T(8,128)(2,1)S(1)} %add_convert_fusion.2), channel_id=1, source_target_pairs={{0,4},{2,6},{4,0},{6,2},{8,12},{10,14},{12,8},{14,10},{1,5},{3,7},... | collective-permute-start | bytes 393224 | tf_op jit(solution)/shard_map/ppermute | solution.py:86
  128.5 9.2 %collective-permute-start.39 = (bf16[128,256]{1,0:T(8,128)(2,1)S(1)}, bf16[128,256]{1,0:T(8,128)(2,1)S(1)}, u32[]{:S(2)}, u32[]{:S(2)}) collective-permute-start(bf16[128,256]{1,0:T(8,128)(2,1)S(1)} %add_convert_fusion.5), channel_id=1, source_target_pairs={{0,8},{2,10},{4,12},{6,14},{8,0},{10,2},{12,4},{14,6},{1,9},{3,11}... | collective-permute-start | bytes 196616 | tf_op jit(solution)/shard_map/ppermute | solution.py:86
  131.1 8.3 %collective-permute-start.35 = (bf16[128,512]{1,0:T(8,128)(2,1)S(1)}, bf16[128,512]{1,0:T(8,128)(2,1)S(1)}, u32[]{:S(2)}, u32[]{:S(2)}) collective-permute-start(bf16[128,512]{1,0:T(8,128)(2,1)S(1)} %add_convert_fusion.1), channel_id=1, source_target_pairs={{0,8},{2,10},{4,12},{6,14},{8,0},{10,2},{12,4},{14,6},{1,9},{3,11}... | collective-permute-start | bytes 393224 | tf_op jit(solution)/shard_map/ppermute | solution.py:86

commit v5 on v4

--- a/solution.py
+++ b/solution.py
@@ -62,8 +62,8 @@
     apart = ring_place(row_count, index // 2) - ring_place(row_count, lax.axis_index("row"))
     apart = (apart + row_count) % row_count
     near = jnp.where(letter == 0, row_count - apart, apart)
-    first = 2 * near + letter
-    second = 2 + 2 * hops + 2 * (row_count - near - 1) + 1 - letter
+    first = 4 * near - 2 + letter
+    second = 4 * (row_count - near) - 2 + 3 - letter
     return jnp.where(apart == 0, letter, jnp.where(near <= hops, first, second))
 
 
@@ -76,20 +76,28 @@
     return lax.ppermute(x, "col", [(0, 1), (1, 0)])
 
 
+def add(a, b):
+    return (a.astype(f32) + b.astype(f32)).astype(bf16)
+
+
 def sum_all(x, row_count):
-    def add(a, b):
-        return (a.astype(f32) + b.astype(f32)).astype(bf16)
-
-    x = add(x, swap_col(x))
+    other = swap_col(x)
     step = 1
     while step < row_count:
-        x = add(x, lax.ppermute(x, "row", [(r, r ^ step) for r in range(row_count)]))
+        x = add(x, other)
+        other = lax.ppermute(x, "row", [(r, r ^ step) for r in range(row_count)])
         step *= 2
-    return x
+    return x, other
+
+
+def whole_of(x):
+    return pl.BlockSpec(x.shape, lambda step: (0,) * x.ndim)
 
 
 def call(kernel, name, microseconds, args, specs, outs, scratch=(), after=()):
-    held = sum(a.size * a.dtype.itemsize for a, s in zip(args, specs) if s is VMEM)
+    held = sum(a.size * a.dtype.itemsize for a, s in zip(args, specs) if s is not SMEM)
+    after = [x for x in after if x is not None]
+    streamed = any(s is not SMEM and s is not VMEM for s in specs)
     held += sum(int(o.size) * o.dtype.itemsize for o in outs)
     held += sum(int(s.inner_aval.size) * 4 for s in scratch)
 
@@ -98,6 +106,7 @@
 
     return pl.pallas_call(
         body,
+        grid=(1,) if streamed else (),
         out_shape=list(outs),
         in_specs=list(specs) + [ANY] * len(after),
         out_specs=[VMEM] * len(outs),
@@ -131,21 +140,18 @@
     return lax.axis_index("row") * here
 
 
-def input_kernel(slot, lengths, pair, gain, bias, w, right_a, right_b, normed, mask):
+def input_kernel(slot, lengths, pair, gain, bias, w, right, normed, mask):
     here, half, hidden = pair.shape
-    short = here // 2
     mask[...] = present_columns(lengths, slot, half)
 
-    for out, first in ((right_a, 0), (right_b, short)):
-        for t in range(short):
-            i = first + t
-            standard, _ = standardize(pair[i].astype(f32))
-            values = (standard * gain[...] + bias[...]).astype(bf16)
-            normed[i] = values
-            proj = dot(values, w[:, 2 * hidden : 4 * hidden], 1, 0)
-            shown = mask[...] * present_row(lengths, slot, first_row(here) + i)
-            gated = jax.nn.sigmoid(proj[:, :hidden]) * proj[:, hidden:]
-            out[t] = (shown * gated).astype(bf16)
+    for i in range(here):
+        standard, _ = standardize(pair[i].astype(f32))
+        values = (standard * gain[...] + bias[...]).astype(bf16)
+        normed[i] = values
+        proj = dot(values, w[:, 2 * hidden : 4 * hidden], 1, 0)
+        shown = mask[...] * present_row(lengths, slot, first_row(here) + i)
+        gated = jax.nn.sigmoid(proj[:, :hidden]) * proj[:, hidden:]
+        right[i] = (shown * gated).astype(bf16)
 
 
 def by_rows(here, body):
@@ -178,14 +184,13 @@
     by_rows(here, body)
 
 
-def triangle_kernel(row_count, slot, places, lengths, left, *refs):
-    count = len(places)
-    rights, (out, right, partial, rows) = refs[:count], refs[count:]
+def triangle_kernel(row_count, slot, halves, arrays, lengths, left, *refs):
+    rights, (out, right, partial, rows) = refs[:arrays], refs[arrays:]
     here, half, hidden = left.shape
-    short = rights[0].shape[0]
     padded = out.shape[2]
-    for s in range(count):
-        right[...] = rights[s][...].astype(f32)
+    short = right.shape[0]
+    for s, (array, first, place) in enumerate(halves):
+        right[...] = rights[array][pl.ds(first, short)].astype(f32)
         rows[...] = jnp.zeros_like(rows)
 
         def body(j, carry):
@@ -199,22 +204,22 @@
             rows[pl.ds(j, here, stride=padded), :] = total
             return carry
 
-        present = present_count(row_count, lengths, slot, short, places[s])
+        present = present_count(row_count, lengths, slot, short, place)
         lax.fori_loop(0, present, body, 0)
         out[s] = rows[...].astype(bf16).reshape(here, padded, hidden)
 
 
-def triangle(row_count, slot, places, lengths, left, rights, padded, after=()):
-    count, (here, half, hidden) = len(rights), left.shape
+def triangle(row_count, slot, halves, lengths, left, rights, padded, after):
+    count, (here, half, hidden) = len(halves), left.shape
     return call(
-        functools.partial(triangle_kernel, row_count, slot, places),
+        functools.partial(triangle_kernel, row_count, slot, halves, len(rights)),
         "triangle",
-        0.7 * count,
+        0.9 * count,
         [lengths, left, *rights],
-        [SMEM] + [VMEM] * (count + 1),
+        [SMEM] + [VMEM] * (len(rights) + 1),
         [shape_of((count, here, padded, hidden), bf16)],
         [
-            pltpu.VMEM(rights[0].shape, f32),
+            pltpu.VMEM((here // 2, half, hidden), f32),
             pltpu.VMEM((here * 8, hidden), f32),
             pltpu.VMEM((here * padded, hidden), f32),
         ],
@@ -237,7 +242,7 @@
         grad[s] = result.astype(bf16).reshape(here, padded, hidden)
 
 
-def triangle_norm(row_count, places, mine, other, outs, w_out, gain, bias):
+def triangle_norm(row_count, places, mine, other, outs, w_out, gain, bias, after):
     return call(
         functools.partial(triangle_norm_kernel, row_count, places),
         "triangle_norm",
@@ -245,6 +250,8 @@
         [mine, other, outs, w_out, gain, bias],
         [VMEM] * 6,
         [shape_of(mine.shape, bf16)] * 2,
+        (),
+        after,
     )
 
 
@@ -301,15 +308,16 @@
     )
 
 
-def left_gradient_kernel(picks, carried, grads, *refs):
+def left_gradient_kernel(halves, picks, arrays, carried, grads, *refs):
     count = len(picks)
-    rights, refs = refs[:count], refs[count:]
+    rights, refs = refs[:arrays], refs[arrays:]
     before, (out, right, wide) = refs[:carried], refs[carried:]
     here, half, hidden = out.shape
-    short = rights[0].shape[0]
-    for s in range(count):
-        right[s] = rights[s][...].astype(f32)
-        wide[s] = grads[picks[s]].astype(f32)
+    short = here // 2
+    for s, pick in enumerate(picks):
+        array, first, _ = halves[pick]
+        right[s] = rights[array][pl.ds(first, short)].astype(f32)
+        wide[s] = grads[pick].astype(f32)
 
     def row(i, carry):
         total = before[0][i] if carried else jnp.zeros((half, hidden), f32)
@@ -322,18 +330,18 @@
     lax.fori_loop(0, here, row, 0)
 
 
-def left_gradient(grads, picks, rights, before, after=()):
+def left_gradient(halves, picks, grads, rights, before, after):
     count, here = len(picks), grads.shape[1]
-    short, half, hidden = rights[0].shape
+    half, hidden = rights[0].shape[1:]
     return call(
-        functools.partial(left_gradient_kernel, picks, len(before)),
+        functools.partial(left_gradient_kernel, halves, picks, len(rights), len(before)),
         "left_gradient",
         0.9 * count,
         [grads, *rights, *before],
-        [VMEM] * (1 + count + len(before)),
+        [VMEM] * (1 + len(rights) + len(before)),
         [shape_of((here, half, hidden), f32)],
         [
-            pltpu.VMEM((count, short, half, hidden), f32),
+            pltpu.VMEM((count, here // 2, half, hidden), f32),
             pltpu.VMEM((count,) + grads.shape[1:], f32),
         ],
         after,
@@ -427,6 +435,15 @@
     by_rows(pair.shape[0], body)
 
 
+def weights_kernel(early, mine, other, w_in, w_out):
+    hidden = w_out.shape[0]
+    w_in[:, : 2 * hidden] = early[:, : 2 * hidden].astype(f32)
+    late = mine[...].astype(f32) + other[...].astype(f32)
+    w_in[:, 2 * hidden : 4 * hidden] = late.astype(bf16).astype(f32)
+    w_in[:, 4 * hidden :] = early[:, 2 * hidden : 3 * hidden].astype(f32)
+    w_out[...] = early[:, 3 * hidden :].astype(f32)
+
+
 def shards(
     pair,
     cotangent,
@@ -450,7 +467,6 @@
     in_gain, in_bias = input_norm_gain.reshape(1, -1), input_norm_bias.reshape(1, -1)
     out_gain, out_bias = output_norm_gain.reshape(1, -1), output_norm_bias.reshape(1, -1)
     block = (here, half, hidden)
-    half_block = (short, half, hidden)
     mask = pltpu.VMEM((half, 128), f32)
 
     def ahead(x):
@@ -459,31 +475,28 @@
     def behind(x):
         return lax.ppermute(x, "row", backward)
 
-    right_a, right_b, normed = call(
+    right, normed = call(
         functools.partial(input_kernel, slot),
         "input_side",
         3.0,
         [chain_lengths, pair, in_gain, in_bias, w_in],
-        [SMEM] + [VMEM] * 4,
-        [shape_of(half_block, bf16)] * 2 + [shape_of(block, bf16)],
+        [SMEM] + [whole_of(x) for x in (pair, in_gain, in_bias, w_in)],
+        [shape_of(block, bf16)] * 2,
         [mask],
     )
 
     hops = row_count // 2
-    chain1, chain2 = [], []
-    a, b, c, d = right_a, right_b, right_b, right_a
-    for step in range(hops):
-        a, b = ahead(a), behind(b)
-        chain1 += [a, b]
-        if step < hops - 1:
-            c, d = ahead(c), behind(d)
-            chain2 += [c, d]
-
-    early_hops = hops // 2
-    groups = [[right_a, right_b] + chain1[: 2 * early_hops], chain1[2 * early_hops :], chain2]
-    places1 = [p for s in range(1, hops + 1) for p in ((-s, 0), (s, 1))]
-    places2 = [p for s in range(1, hops) for p in ((-s, 1), (s, 0))]
-    places = [[(0, 0), (0, 1)] + places1[: 2 * early_hops], places1[2 * early_hops :], places2]
+    groups = [[right]]
+    halves = [[(0, 0, (0, 0)), (0, short, (0, 1))]]
+    x = y = right
+    for s in range(1, hops):
+        x, y = ahead(x), behind(y)
+        groups.append([x, y])
+        halves.append(
+            [(0, 0, (-s, 0)), (1, short, (s, 1)), (0, short, (-s, 1)), (1, 0, (s, 0))]
+        )
+    groups.append([ahead(x[:short]), behind(y[short:])])
+    halves.append([(0, 0, (-hops, 0)), (1, 0, (hops, 1))])
 
     left, mine_out = call(
         functools.partial(left_kernel, slot),
@@ -496,95 +509,112 @@
     )
     outs = jnp.concatenate([mine_out, swap_col(mine_out)], axis=0)
 
-    norms, grads = [], []
-
-    def triangle_group(g, after=()):
-        partial = triangle(
-            row_count, slot, places[g], chain_lengths, left, groups[g], padded, after
+    norms, grads, partials, others = [], [], [], []
+    last = [left]
+    pieces = []
+
+    def triangles(s):
+        partials.append(
+            triangle(row_count, slot, halves[s], chain_lengths, left, groups[s], padded, last)
         )
+        others.append(swap_col(partials[s]))
+        last[:] = [partials[s]]
+
+    def normal(s):
+        places = [place for _, _, place in halves[s]]
         grad, norm = triangle_norm(
-            row_count, places[g], partial, swap_col(partial), outs, w_out, out_gain, out_bias
+            row_count, places, partials[s], others[s], outs, w_out, out_gain, out_bias, last
         )
         grads.append(grad)
         norms.append(norm)
-
-    def scatter(g, picks, arrived, dtype=bf16, after=()):
-        return hop(
+        last[:] = [grad]
+
+    def add_left(s, picks=None):
+        picks = list(range(len(halves[s]))) if picks is None else picks
+        pieces[:] = [
+            left_gradient(halves[s], picks, grads[s], groups[s], pieces[:], last)
+        ]
+        last[:] = pieces
+
+    def scatter(s, picks, arrived, dtype=bf16):
+        x, y = hop(
             row_count,
             slot,
-            [places[g][pick] for pick in picks],
+            [halves[s][pick][2] for pick in picks],
             chain_lengths,
             left,
-            [grads[g]] * 2,
+            [grads[s]] * 2,
             picks,
             arrived,
             short,
             dtype,
-            after,
+            last,
         )
-
-    def group1(s):
-        at = 2 * (s - 1)
-        if s <= early_hops:
-            return 0, [at + 2, at + 3]
-        at -= 2 * early_hops
-        return 1, [at, at + 1]
-
-    pieces = []
-
-    def add_left(g, picks, after):
-        rights = [groups[g][pick] for pick in picks]
-        pieces[:] = [left_gradient(grads[g], picks, rights, pieces[:], after)]
-
-    arrived1, arrived2 = [], []
-    triangle_group(0)
-    triangle_group(1)
-    g, picks = group1(hops)
-    x, y = scatter(g, picks, arrived1)
-    arrived1 = [behind(x), ahead(y)]
-    add_left(0, list(range(len(groups[0]))), [x])
-    triangle_group(2, pieces)
-    waiting = [
-        (g, [at, at + 1]) for g in (1, 2) for at in range(0, len(groups[g]), 2)
-    ]
+        last[:] = [x]
+        return x, y
+
+    arrived = {0: [], 2: []}
+
+    def send(s, chain):
+        x, y = scatter(s, [chain, chain + 1], arrived[chain])
+        arrived[chain] = [behind(x), ahead(y)]
+
+    def output_side():
+        results = call(
+            functools.partial(output_kernel, row_count, slot, [len(h) for h in halves]),
+            "output_side",
+            6.0,
+            [chain_lengths, normed, cotangent, pieces[0], w_in, w_out, outs, *norms],
+            [SMEM] + [VMEM] * (6 + len(norms)),
+            [
+                shape_of(block, bf16),
+                shape_of(block, f32),
+                shape_of((channels, 4 * hidden), bf16),
+            ],
+            [
+                mask,
+                pltpu.VMEM((row_count, here, padded, hidden), bf16),
+                pltpu.VMEM((channels, 4 * hidden), f32),
+            ],
+            last,
+        )
+        last[:] = results[:1]
+        return results
+
+    triangles(0)
+    for s in range(1, hops):
+        triangles(s)
+        normal(s - 1)
+        add_left(s - 1)
+    normal(hops - 1)
+    send(hops - 1, 2)
+    triangles(hops)
+    add_left(hops - 1, [0, 1])
+    normal(hops)
+    send(hops, 0)
+    add_left(hops - 1, [2, 3])
+    fillers = [lambda: add_left(hops), None, output_side, lambda: scatter(0, [0, 1], [], f32)]
+    results = []
     for s in range(hops - 1, 0, -1):
-        x, y = scatter(2, [2 * s - 2, 2 * s - 1], arrived2, after=pieces)
-        arrived2 = [behind(x), ahead(y)]
-        if waiting:
-            add_left(*waiting.pop(0), [x])
-        g, picks = group1(s)
-        x, y = scatter(g, picks, arrived1, after=pieces)
-        arrived1 = [behind(x), ahead(y)]
-        if waiting:
-            add_left(*waiting.pop(0), [x])
-    while waiting:
-        add_left(*waiting.pop(0), [x])
-    own_a, own_b = scatter(0, [0, 1], [], f32, after=[x])
-    update, gradient, early = call(
-        functools.partial(output_kernel, row_count, slot, [len(g) for g in groups]),
-        "output_side",
-        6.0,
-        [chain_lengths, normed, cotangent, pieces[0], w_in, w_out, outs, *norms],
-        [SMEM] + [VMEM] * 9,
-        [
-            shape_of(block, bf16),
-            shape_of(block, f32),
-            shape_of((channels, 4 * hidden), bf16),
-        ],
-        [
-            mask,
-            pltpu.VMEM((row_count, here, padded, hidden), bf16),
-            pltpu.VMEM((channels, 4 * hidden), f32),
-        ],
-    )
-    summed_early = sum_all(early, row_count).astype(f32)
+        if s > 1:
+            send(s - 1, 2)
+        if fillers:
+            results.append(fillers.pop(0)())
+        send(s, 0)
+        if s == hops - 1:
+            fillers.pop(0)
+    while fillers:
+        results.append(fillers.pop(0)())
+    _, (update, gradient, early), (own_a, own_b) = results
+    arrived1, arrived2 = arrived[0], [arrived[2][1], arrived[2][0]]
+    summed_early = add(*sum_all(early, row_count))
 
     late, weights = call(
         functools.partial(right_gradient_kernel, slot),
         "right_gradient",
         3.0,
         [chain_lengths, normed, w_in, own_a, own_b]
-        + [arrived1[0], arrived2[1], arrived1[1], arrived2[0]],
+        + [arrived1[0], arrived2[0], arrived1[1], arrived2[1]],
         [SMEM] + [VMEM] * 8,
         [
             shape_of((here, half, 2 * hidden), bf16),
@@ -592,7 +622,7 @@
         ],
         [mask, pltpu.VMEM((channels, 2 * hidden), f32)],
     )
-    summed_late = sum_all(weights, row_count).astype(f32)
+    terms = sum_all(weights, row_count)
     (pair_gradient,) = call(
         pair_gradient_kernel,
         "pair_gradient",
@@ -601,11 +631,14 @@
         [VMEM] * 5,
         [shape_of(block, bf16)],
     )
-    grad_w_in = jnp.concatenate(
-        [summed_early[:, : 2 * hidden], summed_late, summed_early[:, 2 * hidden : 3 * hidden]],
-        axis=1,
-    )
-    grad_w_out = summed_early[:, 3 * hidden :]
+    grad_w_in, grad_w_out = call(
+        weights_kernel,
+        "weight_gradients",
+        0.5,
+        [summed_early, *terms],
+        [VMEM] * 3,
+        [shape_of(w_in.shape, f32), shape_of(w_out.shape, f32)],
+    )
     return (update, pair_gradient, grad_w_in, grad_w_out)
 
 

time: 141 us -> 146 us (1.035)
  waiting for transfers between devices: 26.3 us -> 37.7 us
  starting transfers between devices: 41.5 us -> 34.4 us
  Pallas kernels: 65.7 us -> 67.7 us
    ppermute x14 -> x11, waiting for transfers between devices: 11.4 us -> 24 us  [behind(): return lax.ppermute(x, 'row', backward)]
    ppermute x14 -> x11, starting transfers between devices: 21 us -> 10.9 us  [behind(): return lax.ppermute(x, 'row', backward)]
    ppermute x14 -> x11, starting transfers between devices: 10.4 us -> 15.6 us  [ahead(): return lax.ppermute(x, 'row', forward)]
    ppermute x6, starting transfers between devices: 9.13 us -> 6.72 us  [sum_all(): other = lax.ppermute(x, 'row', [(r, r ^ step) for r in range(row_count)])]
    ppermute x14 -> x11, waiting for transfers between devices: 4.63 us -> 2.23 us  [ahead(): return lax.ppermute(x, 'row', forward)]
    pallas_call x25 -> x30, Pallas kernels: 65.7 us -> 67.7 us  [call(): pl.pallas_call(body, grid=(1,) if streamed else (), out_shape=list(outs),...]
    unnamed x27 -> x29, local copies, waits for them, and re-layouts: 4.52 us -> 5.55 us
  transfers between devices with their start and end apart: 40 -> 36, of which waited for: 11 -> 12; matrix products, arithmetic and copies ran while one was open for 0% -> 0% of each run, Pallas kernels for 42% -> 43%
where the time goes in v5:
time: 146 us; the launch traced here: 147 us
  Pallas kernels  67.7 us (46%)
  waiting for transfers between devices  37.7 us (26%)
  starting transfers between devices  34.4 us (24%)
  local copies, waits for them, and re-layouts  5.76 us (4%)
    pallas_call x30, Pallas kernels, call(): pl.pallas_call(body, grid=(1,) if streamed else (), out_shape=list(outs),...  67.7 us
    ppermute x11, waiting for transfers between devices, behind(): return lax.ppermute(x, 'row', backward)  24 us
    ppermute x11, starting transfers between devices, ahead(): return lax.ppermute(x, 'row', forward)  15.6 us
    ppermute x6, waiting for transfers between devices, sum_all(): other = lax.ppermute(x, 'row', [(r, r ^ step) for r in range(row_count)])  11.4 us
    ppermute x11, starting transfers between devices, behind(): return lax.ppermute(x, 'row', backward)  10.9 us
    ppermute x6, starting transfers between devices, sum_all(): other = lax.ppermute(x, 'row', [(r, r ^ step) for r in range(row_count)])  6.72 us
    unnamed x29, local copies, waits for them, and re-layouts  5.55 us
  transfers between devices with their start and end apart: 36, of which 12 were waited for; matrix products, arithmetic and copies ran while one was open for 0% of the time, Pallas kernels for 43%

profile of v5, /device:TPU:0, one launch (start us, length us, event | category | flops | bytes accessed | tf_op | source)
XLA Modules:
  0.0 146.8 jit_solution(17134137613595127165)
XLA Ops:
  0.6 1.0 copy-done.1
  1.7 0.9 copy-done.3
  2.6 0.7 copy-done.6
  3.2 0.7 copy-done.9
  3.9 0.7 copy-done.11
  4.6 1.5 input_side.1
  6.0 3.0 %collective-permute-start.4 = (bf16[22,88,128]{2,1,0:T(8,128)(2,1)S(1)}, bf16[22,88,128]{2,1,0:T(8,128)(2,1)S(1)}, u32[]{:S(2)}, u32[]{:S(2)}) collective-permute-start(bf16[22,88,128]{2,1,0:T(8,128)(2,1)S(1)} %get-tuple-element.43.refs_2_.refs_1_), channel_id=1, source_target_pairs={{0,2},{4,0},{8,4},{12,8},{14,12},{10,14},{6,10},{2,6},{1,3},{5,1},... | collective-permute-start | bytes 1486856 | tf_op jit(solution)/shard_map/ppermute | solution.py:476
  9.2 1.4 left_side.1
  10.7 2.7 %triangle.5.refs_4_.refs_0_ = bf16[2,22,16,128]{3,2,1,0:T(8,128)(2,1)S(1)} custom-call(s32[8]{0:T(128)S(1)} %copy-done.10, f32[22,88,128]{2,1,0:T(8,128)S(1)} %get-tuple-element.42.refs_1_.refs_3_, bf16[22,88,128]{2,1,0:T(8,128)(2,1)S(1)} %get-tuple-element.43.refs_2_.refs_1_, f32[22,88,128]{2,1,0:T(8,128)S(1)} %get-tuple-element.42.refs_1_.refs_3_), custom_call_target="tpu_custom_call" | custom-call | flops 1980000000 | bytes 1048576 | tf_op jit(solution)/shard_map/triangle/pallas_call | solution.py:107
  13.4 0.6 collective-permute-start.10
  14.0 6.4 %collective-permute-done.4.refs_3_.refs_2_ = bf16[22,88,128]{2,1,0:T(8,128)(2,1)S(1)} collective-permute-done((bf16[22,88,128]{2,1,0:T(8,128)(2,1)S(1)}, bf16[22,88,128]{2,1,0:T(8,128)(2,1)S(1)}, u32[]{:S(2)}, u32[]{:S(2)}) %collective-permute-start.4) | collective-permute-done | bytes 495648 | tf_op jit(solution)/shard_map/ppermute | solution.py:476
  20.4 1.7 %collective-permute-start.5 = (bf16[22,88,128]{2,1,0:T(8,128)(2,1)S(1)}, bf16[22,88,128]{2,1,0:T(8,128)(2,1)S(1)}, u32[]{:S(2)}, u32[]{:S(2)}) collective-permute-start(bf16[22,88,128]{2,1,0:T(8,128)(2,1)S(1)} %collective-permute-done.4.refs_3_.refs_2_), channel_id=1, source_target_pairs={{0,2},{4,0},{8,4},{12,8},{14,12},{10,14},{6,10},{2,6},{1,3},{5,1},... | collective-permute-start | bytes 1486856 | tf_op jit(solution)/shard_map/ppermute | solution.py:476
  22.4 4.8 %triangle.6.refs_6_.refs_0_ = bf16[4,22,16,128]{3,2,1,0:T(8,128)(2,1)S(1)} custom-call(s32[8]{0:T(128)S(1)} %copy-done.10, f32[22,88,128]{2,1,0:T(8,128)S(1)} %get-tuple-element.42.refs_1_.refs_3_, bf16[22,88,128]{2,1,0:T(8,128)(2,1)S(1)} %collective-permute-done.refs_2_.refs_1_, bf16[22,88,128]{2,1,0:T(8,128)(2,1)S(1)} %collective-permute-done.4.refs_3_.refs_2_, ...), custom_call_target="tpu_custom_call" | custom-call | flops 3960000000 | bytes 1048576 | tf_op jit(solution)/shard_map/triangle/pallas_call | solution.py:107
  28.5 2.0 %left_gradient.6.refs_4_.refs_3_ = f32[22,88,128]{2,1,0:T(8,128)S(1)} custom-call(bf16[2,22,16,128]{3,2,1,0:T(8,128)(2,1)S(1)} %get-tuple-element.45.refs_0_.refs_2_.refs_3_, bf16[22,88,128]{2,1,0:T(8,128)(2,1)S(1)} %get-tuple-element.43.refs_2_.refs_1_, bf16[2,22,16,128]{3,2,1,0:T(8,128)(2,1)S(1)} %get-tuple-element.45.refs_0_.refs_2_.refs_3_), custom_call_target="tpu_custom_call" | custom-call | flops 1980000000 | bytes 1048576 | tf_op jit(solution)/shard_map/left_gradient/pallas_call | solution.py:107
  30.5 2.4 %collective-permute-done.5.refs_3_.refs_2_ = bf16[22,88,128]{2,1,0:T(8,128)(2,1)S(1)} collective-permute-done((bf16[22,88,128]{2,1,0:T(8,128)(2,1)S(1)}, bf16[22,88,128]{2,1,0:T(8,128)(2,1)S(1)}, u32[]{:S(2)}, u32[]{:S(2)}) %collective-permute-start.5) | collective-permute-done | bytes 495648 | tf_op jit(solution)/shard_map/ppermute | solution.py:476
  32.9 1.1 collective-permute-done.1.refs_2_.refs_1_
  34.0 4.0 %triangle.7.refs_6_.refs_0_ = bf16[4,22,16,128]{3,2,1,0:T(8,128)(2,1)S(1)} custom-call(s32[8]{0:T(128)S(1)} %copy-done.10, f32[22,88,128]{2,1,0:T(8,128)S(1)} %get-tuple-element.42.refs_1_.refs_3_, bf16[22,88,128]{2,1,0:T(8,128)(2,1)S(1)} %collective-permute-done.1.refs_2_.refs_1_, bf16[22,88,128]{2,1,0:T(8,128)(2,1)S(1)} %collective-permute-done.5.refs_3_.refs_2_, ...), custom_call_target="tpu_custom_call" | custom-call | flops 3960000000 | bytes 1048576 | tf_op jit(solution)/shard_map/triangle/pallas_call | solution.py:107
  38.0 1.5 %collective-permute-start.6 = (bf16[22,88,128]{2,1,0:T(8,128)(2,1)S(1)}, bf16[22,88,128]{2,1,0:T(8,128)(2,1)S(1)}, u32[]{:S(2)}, u32[]{:S(2)}) collective-permute-start(bf16[22,88,128]{2,1,0:T(8,128)(2,1)S(1)} %collective-permute-done.5.refs_3_.refs_2_), channel_id=1, source_target_pairs={{0,2},{4,0},{8,4},{12,8},{14,12},{10,14},{6,10},{2,6},{1,3},{5,1},... | collective-permute-start | bytes 1486856 | tf_op jit(solution)/shard_map/ppermute | solution.py:476
  39.6 0.5 collective-permute-start.2
  40.1 1.0 triangle_norm.6
  41.1 3.9 %left_gradient.7.refs_4_.refs_3_ = f32[22,88,128]{2,1,0:T(8,128)S(1)} custom-call(bf16[4,22,16,128]{3,2,1,0:T(8,128)(2,1)S(1)} %get-tuple-element.46.refs_0_.refs_4_.refs_2_.refs_3_, bf16[22,88,128]{2,1,0:T(8,128)(2,1)S(1)} %collective-permute-done.refs_2_.refs_1_, bf16[22,88,128]{2,1,0:T(8,128)(2,1)S(1)} %collective-permute-done.4.refs_3_.refs_2_, ...), custom_call_target="tpu_custom_call" | custom-call | flops 3960000000 | bytes 1048576 | tf_op jit(solution)/shard_map/left_gradient/pallas_call | solution.py:107
  45.0 6.8 %collective-permute-done.6.refs_3_.refs_2_ = bf16[22,88,128]{2,1,0:T(8,128)(2,1)S(1)} collective-permute-done((bf16[22,88,128]{2,1,0:T(8,128)(2,1)S(1)}, bf16[22,88,128]{2,1,0:T(8,128)(2,1)S(1)}, u32[]{:S(2)}, u32[]{:S(2)}) %collective-permute-start.6) | collective-permute-done | bytes 495648 | tf_op jit(solution)/shard_map/ppermute | solution.py:476
  51.8 1.5 %collective-permute-start.7 = (bf16[11,88,128]{2,1,0:T(8,128)(2,1)S(1)}, bf16[11,88,128]{2,1,0:T(8,128)(2,1)S(1)}, u32[]{:S(2)}, u32[]{:S(2)}) collective-permute-start(bf16[11,88,128]{2,1,0:T(8,128)(2,1)S(1)} %slice.9), channel_id=1, source_target_pairs={{0,2},{4,0},{8,4},{12,8},{14,12},{10,14},{6,10},{2,6},{1,3},{5,1},... | collective-permute-start | bytes 743432 | tf_op jit(solution)/shard_map/ppermute | solution.py:476
  53.3 0.6 collective-permute-start.3
  53.9 2.8 %triangle.8.refs_6_.refs_0_ = bf16[4,22,16,128]{3,2,1,0:T(8,128)(2,1)S(1)} custom-call(s32[8]{0:T(128)S(1)} %copy-done.10, f32[22,88,128]{2,1,0:T(8,128)S(1)} %get-tuple-element.42.refs_1_.refs_3_, bf16[22,88,128]{2,1,0:T(8,128)(2,1)S(1)} %collective-permute-done.2.refs_2_.refs_1_, bf16[22,88,128]{2,1,0:T(8,128)(2,1)S(1)} %collective-permute-done.6.refs_3_.refs_2_, ...), custom_call_target="tpu_custom_call" | custom-call | flops 3960000000 | bytes 1048576 | tf_op jit(solution)/shard_map/triangle/pallas_call | solution.py:107
  56.8 1.0 triangle_norm.7
  57.8 3.9 %left_gradient.8.refs_6_.refs_3_ = f32[22,88,128]{2,1,0:T(8,128)S(1)} custom-call(bf16[4,22,16,128]{3,2,1,0:T(8,128)(2,1)S(1)} %get-tuple-element.47.refs_0_.refs_4_.refs_2_.refs_3_, bf16[22,88,128]{2,1,0:T(8,128)(2,1)S(1)} %collective-permute-done.1.refs_2_.refs_1_, bf16[22,88,128]{2,1,0:T(8,128)(2,1)S(1)} %collective-permute-done.5.refs_3_.refs_2_, ...), custom_call_target="tpu_custom_call" | custom-call | flops 3960000000 | bytes 1048576 | tf_op jit(solution)/shard_map/left_gradient/pallas_call | solution.py:107
  61.7 1.0 triangle_norm.8
  62.7 1.6 %scatter_hop.8 = (bf16[11,88,128]{2,1,0:T(8,128)(2,1)S(1)}, bf16[11,88,128]{2,1,0:T(8,128)(2,1)S(1)}) custom-call(s32[8]{0:T(128)S(1)} %copy-done.10, f32[22,88,128]{2,1,0:T(8,128)S(1)} %get-tuple-element.42.refs_1_.refs_3_, bf16[4,22,16,128]{3,2,1,0:T(8,128)(2,1)S(1)} %get-tuple-element.48.refs_2_.refs_3_.refs_4_.refs_0_, ...), custom_call_target="tpu_custom_call" | custom-call | flops 1540000000 | bytes 1048576 | tf_op jit(solution)/shard_map/scatter_hop/pallas_call | solution.py:107
  64.3 1.7 %collective-permute-start.14 = (bf16[11,88,128]{2,1,0:T(8,128)(2,1)S(1)}, bf16[11,88,128]{2,1,0:T(8,128)(2,1)S(1)}, u32[]{:S(2)}, u32[]{:S(2)}) collective-permute-start(bf16[11,88,128]{2,1,0:T(8,128)(2,1)S(1)} %get-tuple-element.49.refs_4_), channel_id=1, source_target_pairs={{0,2},{4,0},{8,4},{12,8},{14,12},{10,14},{6,10},{2,6},{1,3},{5,1},... | collective-permute-start | bytes 743432 | tf_op jit(solution)/shard_map/ppermute | solution.py:476
  66.0 1.5 %triangle.9.refs_4_.refs_0_ = bf16[2,22,16,128]{3,2,1,0:T(8,128)(2,1)S(1)} custom-call(s32[8]{0:T(128)S(1)} %copy-done.10, f32[22,88,128]{2,1,0:T(8,128)S(1)} %get-tuple-element.42.refs_1_.refs_3_, bf16[11,88,128]{2,1,0:T(8,128)(2,1)S(1)} %collective-permute-done.3.refs_2_.refs_1_, bf16[11,88,128]{2,1,0:T(8,128)(2,1)S(1)} %collective-permute-done.7.refs_3_.refs_2_, ...), custom_call_target="tpu_custom_call" | custom-call | flops 1980000000 | bytes 1048576 | tf_op jit(solution)/shard_map/triangle/pallas_call | solution.py:107
  67.8 0.6 collective-permute-start.15
  68.4 2.0 %left_gradient.9.refs_6_.refs_3_ = f32[22,88,128]{2,1,0:T(8,128)S(1)} custom-call(bf16[4,22,16,128]{3,2,1,0:T(8,128)(2,1)S(1)} %get-tuple-element.48.refs_2_.refs_3_.refs_4_.refs_0_, bf16[22,88,128]{2,1,0:T(8,128)(2,1)S(1)} %collective-permute-done.2.refs_2_.refs_1_, bf16[22,88,128]{2,1,0:T(8,128)(2,1)S(1)} %collective-permute-done.6.refs_3_.refs_2_, ...), custom_call_target="tpu_custom_call" | custom-call | flops 1980000000 | bytes 1048576 | tf_op jit(solution)/shard_map/left_gradient/pallas_call | solution.py:107
  71.0 1.5 %scatter_hop.9 = (bf16[11,88,128]{2,1,0:T(8,128)(2,1)S(1)}, bf16[11,88,128]{2,1,0:T(8,128)(2,1)S(1)}) custom-call(s32[8]{0:T(128)S(1)} %copy-done.10, f32[22,88,128]{2,1,0:T(8,128)S(1)} %get-tuple-element.42.refs_1_.refs_3_, bf16[2,22,16,128]{3,2,1,0:T(8,128)(2,1)S(1)} %get-tuple-element.50.refs_2_.refs_3_.refs_4_.refs_0_, ...), custom_call_target="tpu_custom_call" | custom-call | flops 1540000000 | bytes 1048576 | tf_op jit(solution)/shard_map/scatter_hop/pallas_call | solution.py:107
  72.5 3.2 %collective-permute-start.19 = (bf16[11,88,128]{2,1,0:T(8,128)(2,1)S(1)}, bf16[11,88,128]{2,1,0:T(8,128)(2,1)S(1)}, u32[]{:S(2)}, u32[]{:S(2)}) collective-permute-start(bf16[11,88,128]{2,1,0:T(8,128)(2,1)S(1)} %get-tuple-element.60), channel_id=1, source_target_pairs={{0,4},{4,8},{8,12},{12,14},{14,10},{10,6},{6,2},{2,0},{1,5},{5,9},... | collective-permute-start | bytes 743432 | tf_op jit(solution)/shard_map/ppermute | solution.py:473
  75.7 2.0 %left_gradient.10.refs_6_.refs_3_ = f32[22,88,128]{2,1,0:T(8,128)S(1)} custom-call(bf16[4,22,16,128]{3,2,1,0:T(8,128)(2,1)S(1)} %get-tuple-element.48.refs_2_.refs_3_.refs_4_.refs_0_, bf16[22,88,128]{2,1,0:T(8,128)(2,1)S(1)} %collective-permute-done.2.refs_2_.refs_1_, bf16[22,88,128]{2,1,0:T(8,128)(2,1)S(1)} %collective-permute-done.6.refs_3_.refs_2_, ...), custom_call_target="tpu_custom_call" | custom-call | flops 1980000000 | bytes 1048576 | tf_op jit(solution)/shard_map/left_gradient/pallas_call | solution.py:107
  77.7 2.5 %scatter_hop.10 = (bf16[11,88,128]{2,1,0:T(8,128)(2,1)S(1)}, bf16[11,88,128]{2,1,0:T(8,128)(2,1)S(1)}) custom-call(s32[8]{0:T(128)S(1)} %copy-done.10, f32[22,88,128]{2,1,0:T(8,128)S(1)} %get-tuple-element.42.refs_1_.refs_3_, bf16[4,22,16,128]{3,2,1,0:T(8,128)(2,1)S(1)} %get-tuple-element.47.refs_0_.refs_4_.refs_2_.refs_3_, ...), custom_call_target="tpu_custom_call" | custom-call | flops 1540000000 | bytes 1048576 | tf_op jit(solution)/shard_map/scatter_hop/pallas_call | solution.py:107
  80.2 3.3 %collective-permute-start.17 = (bf16[11,88,128]{2,1,0:T(8,128)(2,1)S(1)}, bf16[11,88,128]{2,1,0:T(8,128)(2,1)S(1)}, u32[]{:S(2)}, u32[]{:S(2)}) collective-permute-start(bf16[11,88,128]{2,1,0:T(8,128)(2,1)S(1)} %get-tuple-element.59), channel_id=1, source_target_pairs={{0,4},{4,8},{8,12},{12,14},{14,10},{10,6},{6,2},{2,0},{1,5},{5,9},... | collective-permute-start | bytes 743432 | tf_op jit(solution)/shard_map/ppermute | solution.py:473
  83.5 2.0 %left_gradient.11.refs_6_.refs_3_ = f32[22,88,128]{2,1,0:T(8,128)S(1)} custom-call(bf16[2,22,16,128]{3,2,1,0:T(8,128)(2,1)S(1)} %get-tuple-element.50.refs_2_.refs_3_.refs_4_.refs_0_, bf16[11,88,128]{2,1,0:T(8,128)(2,1)S(1)} %collective-permute-done.3.refs_2_.refs_1_, bf16[11,88,128]{2,1,0:T(8,128)(2,1)S(1)} %collective-permute-done.7.refs_3_.refs_2_, ...), custom_call_target="tpu_custom_call" | custom-call | flops 1980000000 | bytes 1048576 | tf_op jit(solution)/shard_map/left_gradient/pallas_call | solution.py:107
  85.6 1.6 %scatter_hop.11 = (bf16[11,88,128]{2,1,0:T(8,128)(2,1)S(1)}, bf16[11,88,128]{2,1,0:T(8,128)(2,1)S(1)}) custom-call(s32[8]{0:T(128)S(1)} %copy-done.10, f32[22,88,128]{2,1,0:T(8,128)S(1)} %get-tuple-element.42.refs_1_.refs_3_, bf16[4,22,16,128]{3,2,1,0:T(8,128)(2,1)S(1)} %get-tuple-element.48.refs_2_.refs_3_.refs_4_.refs_0_, ...), custom_call_target="tpu_custom_call" | custom-call | flops 1540000000 | bytes 1048576 | tf_op jit(solution)/shard_map/scatter_hop/pallas_call | solution.py:107
  87.2 2.1 %collective-permute-start.21 = (bf16[11,88,128]{2,1,0:T(8,128)(2,1)S(1)}, bf16[11,88,128]{2,1,0:T(8,128)(2,1)S(1)}, u32[]{:S(2)}, u32[]{:S(2)}) collective-permute-start(bf16[11,88,128]{2,1,0:T(8,128)(2,1)S(1)} %get-tuple-element.64), channel_id=1, source_target_pairs={{0,4},{4,8},{8,12},{12,14},{14,10},{10,6},{6,2},{2,0},{1,5},{5,9},... | collective-permute-start | bytes 743432 | tf_op jit(solution)/shard_map/ppermute | solution.py:473
  89.3 1.7 %collective-permute-done.16.refs_4_ = bf16[11,88,128]{2,1,0:T(8,128)(2,1)S(1)} collective-permute-done((bf16[11,88,128]{2,1,0:T(8,128)(2,1)S(1)}, bf16[11,88,128]{2,1,0:T(8,128)(2,1)S(1)}, u32[]{:S(2)}, u32[]{:S(2)}) %collective-permute-start.16) | collective-permute-done | bytes 247840 | tf_op jit(solution)/shard_map/ppermute | solution.py:476
  91.0 2.5 %scatter_hop.12 = (bf16[11,88,128]{2,1,0:T(8,128)(2,1)S(1)}, bf16[11,88,128]{2,1,0:T(8,128)(2,1)S(1)}) custom-call(s32[8]{0:T(128)S(1)} %copy-done.10, f32[22,88,128]{2,1,0:T(8,128)S(1)} %get-tuple-element.42.refs_1_.refs_3_, bf16[4,22,16,128]{3,2,1,0:T(8,128)(2,1)S(1)} %get-tuple-element.46.refs_0_.refs_4_.refs_2_.refs_3_, ...), custom_call_target="tpu_custom_call" | custom-call | flops 1540000000 | bytes 1048576 | tf_op jit(solution)/shard_map/scatter_hop/pallas_call | solution.py:107
  93.5 6.5 %output_side.1 = (bf16[22,88,128]{2,1,0:T(8,128)(2,1)}, f32[22,88,128]{2,1,0:T(8,128)S(1)}, bf16[128,512]{1,0:T(8,128)(2,1)S(1)}) custom-call(s32[8]{0:T(128)S(1)} %copy-done.10, bf16[22,88,128]{2,1,0:T(8,128)(2,1)S(1)} %get-tuple-element.41.refs_1_, bf16[22,88,128]{2,1,0:T(8,128)(2,1)S(1)} %copy-done, f32[22,88,128]{2,1,0:T(8,128)S(1)} %left_gradient.11.refs_6_.refs_3_, ...), custom_call_target="tpu_custom_call" | custom-call | flops 6600000000 | bytes 1048576 | tf_op jit(solution)/shard_map/output_side/pallas_call | solution.py:107
  100.0 1.0 copy-done.13
  101.1 1.9 %scatter_hop.13 = (bf16[11,88,128]{2,1,0:T(8,128)(2,1)S(1)}, bf16[11,88,128]{2,1,0:T(8,128)(2,1)S(1)}) custom-call(s32[8]{0:T(128)S(1)} %copy-done.10, f32[22,88,128]{2,1,0:T(8,128)S(1)} %get-tuple-element.42.refs_1_.refs_3_, bf16[4,22,16,128]{3,2,1,0:T(8,128)(2,1)S(1)} %get-tuple-element.47.refs_0_.refs_4_.refs_2_.refs_3_, ...), custom_call_target="tpu_custom_call" | custom-call | flops 1540000000 | bytes 1048576 | tf_op jit(solution)/shard_map/scatter_hop/pallas_call | solution.py:107
  103.0 1.8 %collective-permute-start.23 = (bf16[11,88,128]{2,1,0:T(8,128)(2,1)S(1)}, bf16[11,88,128]{2,1,0:T(8,128)(2,1)S(1)}, u32[]{:S(2)}, u32[]{:S(2)}) collective-permute-start(bf16[11,88,128]{2,1,0:T(8,128)(2,1)S(1)} %get-tuple-element.68), channel_id=1, source_target_pairs={{0,4},{4,8},{8,12},{12,14},{14,10},{10,6},{6,2},{2,0},{1,5},{5,9},... | collective-permute-start | bytes 743432 | tf_op jit(solution)/shard_map/ppermute | solution.py:473
  105.0 0.6 collective-permute-start.27
  105.6 1.4 collective-permute-start.25
  107.1 2.7 %scatter_hop.14 = (f32[11,88,128]{2,1,0:T(8,128)S(1)}, f32[11,88,128]{2,1,0:T(8,128)S(1)}) custom-call(s32[8]{0:T(128)S(1)} %copy-done.10, f32[22,88,128]{2,1,0:T(8,128)S(1)} %get-tuple-element.42.refs_1_.refs_3_, bf16[2,22,16,128]{3,2,1,0:T(8,128)(2,1)S(1)} %get-tuple-element.45.refs_0_.refs_2_.refs_3_, ...), custom_call_target="tpu_custom_call" | custom-call | flops 1540000000 | bytes 1048576 | tf_op jit(solution)/shard_map/scatter_hop/pallas_call | solution.py:107
  109.7 0.7 collective-permute-done.23.refs_5_
  110.4 3.1 %collective-permute-done.22.refs_4_ = bf16[11,88,128]{2,1,0:T(8,128)(2,1)S(1)} collective-permute-done((bf16[11,88,128]{2,1,0:T(8,128)(2,1)S(1)}, bf16[11,88,128]{2,1,0:T(8,128)(2,1)S(1)}, u32[]{:S(2)}, u32[]{:S(2)}) %collective-permute-start.22) | collective-permute-done | bytes 247840 | tf_op jit(solution)/shard_map/ppermute | solution.py:476
  113.5 2.5 %scatter_hop.15 = (bf16[11,88,128]{2,1,0:T(8,128)(2,1)S(1)}, bf16[11,88,128]{2,1,0:T(8,128)(2,1)S(1)}) custom-call(s32[8]{0:T(128)S(1)} %copy-done.10, f32[22,88,128]{2,1,0:T(8,128)S(1)} %get-tuple-element.42.refs_1_.refs_3_, bf16[4,22,16,128]{3,2,1,0:T(8,128)(2,1)S(1)} %get-tuple-element.46.refs_0_.refs_4_.refs_2_.refs_3_, ...), custom_call_target="tpu_custom_call" | custom-call | flops 1540000000 | bytes 1048576 | tf_op jit(solution)/shard_map/scatter_hop/pallas_call | solution.py:107
  116.5 1.6 %collective-permute-start.26 = (bf16[11,88,128]{2,1,0:T(8,128)(2,1)S(1)}, bf16[11,88,128]{2,1,0:T(8,128)(2,1)S(1)}, u32[]{:S(2)}, u32[]{:S(2)}) collective-permute-start(bf16[11,88,128]{2,1,0:T(8,128)(2,1)S(1)} %get-tuple-element.71), channel_id=1, source_target_pairs={{0,4},{4,8},{8,12},{12,14},{14,10},{10,6},{6,2},{2,0},{1,5},{5,9},... | collective-permute-start | bytes 743432 | tf_op jit(solution)/shard_map/ppermute | solution.py:473
  118.7 3.6 %collective-permute-done.24.refs_5_ = bf16[11,88,128]{2,1,0:T(8,128)(2,1)S(1)} collective-permute-done((bf16[11,88,128]{2,1,0:T(8,128)(2,1)S(1)}, bf16[11,88,128]{2,1,0:T(8,128)(2,1)S(1)}, u32[]{:S(2)}, u32[]{:S(2)}) %collective-permute-start.24) | collective-permute-done | bytes 247840 | tf_op jit(solution)/shard_map/ppermute | solution.py:476
  122.7 2.0 %right_gradient.1 = (bf16[22,88,256]{2,1,0:T(8,128)(2,1)S(1)}, bf16[128,256]{1,0:T(8,128)(2,1)S(1)}) custom-call(s32[8]{0:T(128)S(1)} %copy-done.10, bf16[22,88,128]{2,1,0:T(8,128)(2,1)S(1)} %get-tuple-element.41.refs_1_, bf16[128,640]{1,0:T(8,128)(2,1)S(1)} %copy-done.4, f32[11,88,128]{2,1,0:T(8,128)S(1)} %get-tuple-element.66.refs_6_.refs_3_, ...), custom_call_target="tpu_custom_call" | custom-call | flops 3300000000 | bytes 1048576 | tf_op jit(solution)/shard_map/right_gradient/pallas_call | solution.py:107
  124.9 1.7 %collective-permute-start.30 = (bf16[128,512]{1,0:T(8,128)(2,1)S(1)}, bf16[128,512]{1,0:T(8,128)(2,1)S(1)}, u32[]{:S(2)}, u32[]{:S(2)}) collective-permute-start(bf16[128,512]{1,0:T(8,128)(2,1)S(1)} %add_convert_fusion.2), channel_id=1, source_target_pairs={{0,4},{2,6},{4,0},{6,2},{8,12},{10,14},{12,8},{14,10},{1,5},{3,7},... | collective-permute-start | bytes 393224 | tf_op jit(solution)/shard_map/ppermute | solution.py:88
  127.0 3.8 %collective-permute-done.30 = bf16[128,512]{1,0:T(8,128)(2,1)S(1)} collective-permute-done((bf16[128,512]{1,0:T(8,128)(2,1)S(1)}, bf16[128,512]{1,0:T(8,128)(2,1)S(1)}, u32[]{:S(2)}, u32[]{:S(2)}) %collective-permute-start.30) | collective-permute-done | bytes 131104 | tf_op jit(solution)/shard_map/ppermute | solution.py:88
  130.9 2.1 %collective-permute-start.31 = (bf16[128,512]{1,0:T(8,128)(2,1)S(1)}, bf16[128,512]{1,0:T(8,128)(2,1)S(1)}, u32[]{:S(2)}, u32[]{:S(2)}) collective-permute-start(bf16[128,512]{1,0:T(8,128)(2,1)S(1)} %add_convert_fusion.1), channel_id=1, source_target_pairs={{0,8},{2,10},{4,12},{6,14},{8,0},{10,2},{12,4},{14,6},{1,9},{3,11}... | collective-permute-start | bytes 393224 | tf_op jit(solution)/shard_map/ppermute | solution.py:88
  133.0 1.8 %collective-permute-start.34 = (bf16[128,256]{1,0:T(8,128)(2,1)S(1)}, bf16[128,256]{1,0:T(8,128)(2,1)S(1)}, u32[]{:S(2)}, u32[]{:S(2)}) collective-permute-start(bf16[128,256]{1,0:T(8,128)(2,1)S(1)} %add_convert_fusion.5), channel_id=1, source_target_pairs={{0,4},{2,6},{4,0},{6,2},{8,12},{10,14},{12,8},{14,10},{1,5},{3,7},... | collective-permute-start | bytes 196616 | tf_op jit(solution)/shard_map/ppermute | solution.py:88
  134.8 5.0 %collective-permute-done.31 = bf16[128,512]{1,0:T(8,128)(2,1)S(1)} collective-permute-done((bf16[128,512]{1,0:T(8,128)(2,1)S(1)}, bf16[128,512]{1,0:T(8,128)(2,1)S(1)}, u32[]{:S(2)}, u32[]{:S(2)}) %collective-permute-start.31) | collective-permute-done | bytes 131104 | tf_op jit(solution)/shard_map/ppermute | solution.py:88
  140.1 3.3 %pair_gradient.1 = bf16[22,88,128]{2,1,0:T(8,128)(2,1)} custom-call(bf16[22,88,128]{2,1,0:T(8,128)(2,1)S(1)} %copy-done.2, bf16[22,88,256]{2,1,0:T(8,128)(2,1)S(1)} %get-tuple-element.72.refs_1_, f32[22,88,128]{2,1,0:T(8,128)S(1)} %get-tuple-element.73.refs_2_, f32[1,128]{1,0:T(1,128)S(1)} %bitcast.16, bf16[128,640]{1,0:T(8,128)(2,1)S(1)} %copy-done.4), custom_call_target="tpu_custom_call" | custom-call | flops 3300000000 | bytes 1048576 | tf_op jit(solution)/shard_map/pair_gradient/pallas_call | solution.py:107
  143.4 2.6 %collective-permute-done.35.refs_2_ = bf16[128,256]{1,0:T(8,128)(2,1)S(1)} collective-permute-done((bf16[128,256]{1,0:T(8,128)(2,1)S(1)}, bf16[128,256]{1,0:T(8,128)(2,1)S(1)}, u32[]{:S(2)}, u32[]{:S(2)}) %collective-permute-start.35) | collective-permute-done | bytes 65568 | tf_op jit(solution)/shard_map/ppermute | solution.py:88
  146.0 0.8 weight_gradients.1
  (77 shorter events, 5.7 us)
Async XLA Ops:
  0.6 1.0 copy-start.1
  1.7 0.9 copy-start.3
  2.6 0.7 copy-start.6
  3.2 0.7 copy-start.9
  3.9 0.7 copy-start.11
  4.6 4.6 %copy-start = (bf16[22,88,128]{2,1,0:T(8,128)(2,1)S(1)}, bf16[22,88,128]{2,1,0:T(8,128)(2,1)}, u32[]{:S(2)}) copy-start(bf16[22,88,128]{2,1,0:T(8,128)(2,1)} %refs_2_.4) | copy-start | bytes 1486852
  4.6 4.6 %copy-start.4 = (bf16[128,640]{1,0:T(8,128)(2,1)S(1)}, bf16[128,640]{1,0:T(8,128)(2,1)}, u32[]{:S(2)}) copy-start(bf16[128,640]{1,0:T(8,128)(2,1)} %refs_4_.5) | copy-start | bytes 491524
  4.6 4.6 %copy-start.10 = (s32[8]{0:T(128)S(1)}, s32[8]{0:T(128)}, u32[]{:S(2)}) copy-start(s32[8]{0:T(128)} %refs_0_.34) | copy-start | bytes 100
  6.0 14.4 %collective-permute-start.4 = (bf16[22,88,128]{2,1,0:T(8,128)(2,1)S(1)}, bf16[22,88,128]{2,1,0:T(8,128)(2,1)S(1)}, u32[]{:S(2)}, u32[]{:S(2)}) collective-permute-start(bf16[22,88,128]{2,1,0:T(8,128)(2,1)S(1)} %get-tuple-element.43.refs_2_.refs_1_), channel_id=1, source_target_pairs={{0,2},{4,0},{8,4},{12,8},{14,12},{10,14},{6,10},{2,6},{1,3},{5,1},... | collective-permute-start | bytes 1486856 | tf_op jit(solution)/shard_map/ppermute | solution.py:476
  9.0 13.1 %collective-permute-start = (bf16[22,88,128]{2,1,0:T(8,128)(2,1)S(1)}, bf16[22,88,128]{2,1,0:T(8,128)(2,1)S(1)}, u32[]{:S(2)}, u32[]{:S(2)}) collective-permute-start(bf16[22,88,128]{2,1,0:T(8,128)(2,1)S(1)} %get-tuple-element.43.refs_2_.refs_1_), channel_id=1, source_target_pairs={{0,4},{4,8},{8,12},{12,14},{14,10},{10,6},{6,2},{2,0},{1,5},{5,9},... | collective-permute-start | bytes 1486856 | tf_op jit(solution)/shard_map/ppermute | solution.py:473
  10.6 16.7 %collective-permute-start.9 = (bf16[8,22,16,128]{3,2,1,0:T(8,128)(2,1)S(1)}, bf16[8,22,16,128]{3,2,1,0:T(8,128)(2,1)S(1)}, u32[]{:S(2)}, u32[]{:S(2)}) collective-permute-start(bf16[8,22,16,128]{3,2,1,0:T(8,128)(2,1)S(1)} %get-tuple-element.44), channel_id=1, source_target_pairs={{0,1},{1,0},{2,3},{3,2},{4,5},{5,4},{6,7},{7,6},{8,9},{9,8},{10,11... | collective-permute-start | bytes 2162696 | tf_op jit(solution)/shard_map/ppermute | solution.py:76
  13.4 14.2 %collective-permute-start.10 = (bf16[2,22,16,128]{3,2,1,0:T(8,128)(2,1)S(1)}, bf16[2,22,16,128]{3,2,1,0:T(8,128)(2,1)S(1)}, u32[]{:S(2)}, u32[]{:S(2)}) collective-permute-start(bf16[2,22,16,128]{3,2,1,0:T(8,128)(2,1)S(1)} %triangle.5.refs_4_.refs_0_), channel_id=1, source_target_pairs={{0,1},{1,0},{2,3},{3,2},{4,5},{5,4},{6,7},{7,6},{8,9},{9,8},{10,11... | collective-permute-start | bytes 540680 | tf_op jit(solution)/shard_map/ppermute | solution.py:76
  20.4 12.5 %collective-permute-start.5 = (bf16[22,88,128]{2,1,0:T(8,128)(2,1)S(1)}, bf16[22,88,128]{2,1,0:T(8,128)(2,1)S(1)}, u32[]{:S(2)}, u32[]{:S(2)}) collective-permute-start(bf16[22,88,128]{2,1,0:T(8,128)(2,1)S(1)} %collective-permute-done.4.refs_3_.refs_2_), channel_id=1, source_target_pairs={{0,2},{4,0},{8,4},{12,8},{14,12},{10,14},{6,10},{2,6},{1,3},{5,1},... | collective-permute-start | bytes 1486856 | tf_op jit(solution)/shard_map/ppermute | solution.py:476
  22.1 11.9 %collective-permute-start.1 = (bf16[22,88,128]{2,1,0:T(8,128)(2,1)S(1)}, bf16[22,88,128]{2,1,0:T(8,128)(2,1)S(1)}, u32[]{:S(2)}, u32[]{:S(2)}) collective-permute-start(bf16[22,88,128]{2,1,0:T(8,128)(2,1)S(1)} %collective-permute-done.refs_2_.refs_1_), channel_id=1, source_target_pairs={{0,4},{4,8},{8,12},{12,14},{14,10},{10,6},{6,2},{2,0},{1,5},{5,9},... | collective-permute-start | bytes 1486856 | tf_op jit(solution)/shard_map/ppermute | solution.py:473
  27.2 0.8 copy-start.5
  27.2 0.8 copy-start.7
  27.2 0.7 copy-start.8
  27.3 12.9 %collective-permute-start.8 = (bf16[4,22,16,128]{3,2,1,0:T(8,128)(2,1)S(1)}, bf16[4,22,16,128]{3,2,1,0:T(8,128)(2,1)S(1)}, u32[]{:S(2)}, u32[]{:S(2)}) collective-permute-start(bf16[4,22,16,128]{3,2,1,0:T(8,128)(2,1)S(1)} %triangle.6.refs_6_.refs_0_), channel_id=1, source_target_pairs={{0,1},{1,0},{2,3},{3,2},{4,5},{5,4},{6,7},{7,6},{8,9},{9,8},{10,11... | collective-permute-start | bytes 1081352 | tf_op jit(solution)/shard_map/ppermute | solution.py:76
  37.9 18.8 %collective-permute-start.12 = (bf16[4,22,16,128]{3,2,1,0:T(8,128)(2,1)S(1)}, bf16[4,22,16,128]{3,2,1,0:T(8,128)(2,1)S(1)}, u32[]{:S(2)}, u32[]{:S(2)}) collective-permute-start(bf16[4,22,16,128]{3,2,1,0:T(8,128)(2,1)S(1)} %triangle.7.refs_6_.refs_0_), channel_id=1, source_target_pairs={{0,1},{1,0},{2,3},{3,2},{4,5},{5,4},{6,7},{7,6},{8,9},{9,8},{10,11... | collective-permute-start | bytes 1081352 | tf_op jit(solution)/shard_map/ppermute | solution.py:76
  38.0 13.7 %collective-permute-start.6 = (bf16[22,88,128]{2,1,0:T(8,128)(2,1)S(1)}, bf16[22,88,128]{2,1,0:T(8,128)(2,1)S(1)}, u32[]{:S(2)}, u32[]{:S(2)}) collective-permute-start(bf16[22,88,128]{2,1,0:T(8,128)(2,1)S(1)} %collective-permute-done.5.refs_3_.refs_2_), channel_id=1, source_target_pairs={{0,2},{4,0},{8,4},{12,8},{14,12},{10,14},{6,10},{2,6},{1,3},{5,1},... | collective-permute-start | bytes 1486856 | tf_op jit(solution)/shard_map/ppermute | solution.py:476
  39.6 13.7 %collective-permute-start.2 = (bf16[22,88,128]{2,1,0:T(8,128)(2,1)S(1)}, bf16[22,88,128]{2,1,0:T(8,128)(2,1)S(1)}, u32[]{:S(2)}, u32[]{:S(2)}) collective-permute-start(bf16[22,88,128]{2,1,0:T(8,128)(2,1)S(1)} %collective-permute-done.1.refs_2_.refs_1_), channel_id=1, source_target_pairs={{0,4},{4,8},{8,12},{12,14},{14,10},{10,6},{6,2},{2,0},{1,5},{5,9},... | collective-permute-start | bytes 1486856 | tf_op jit(solution)/shard_map/ppermute | solution.py:473
  51.8 14.3 %collective-permute-start.7 = (bf16[11,88,128]{2,1,0:T(8,128)(2,1)S(1)}, bf16[11,88,128]{2,1,0:T(8,128)(2,1)S(1)}, u32[]{:S(2)}, u32[]{:S(2)}) collective-permute-start(bf16[11,88,128]{2,1,0:T(8,128)(2,1)S(1)} %slice.9), channel_id=1, source_target_pairs={{0,2},{4,0},{8,4},{12,8},{14,12},{10,14},{6,10},{2,6},{1,3},{5,1},... | collective-permute-start | bytes 743432 | tf_op jit(solution)/shard_map/ppermute | solution.py:476
  53.3 12.7 %collective-permute-start.3 = (bf16[11,88,128]{2,1,0:T(8,128)(2,1)S(1)}, bf16[11,88,128]{2,1,0:T(8,128)(2,1)S(1)}, u32[]{:S(2)}, u32[]{:S(2)}) collective-permute-start(bf16[11,88,128]{2,1,0:T(8,128)(2,1)S(1)} %slice.8), channel_id=1, source_target_pairs={{0,4},{4,8},{8,12},{12,14},{14,10},{10,6},{6,2},{2,0},{1,5},{5,9},... | collective-permute-start | bytes 743432 | tf_op jit(solution)/shard_map/ppermute | solution.py:473
  56.7 5.0 %collective-permute-start.11 = (bf16[4,22,16,128]{3,2,1,0:T(8,128)(2,1)S(1)}, bf16[4,22,16,128]{3,2,1,0:T(8,128)(2,1)S(1)}, u32[]{:S(2)}, u32[]{:S(2)}) collective-permute-start(bf16[4,22,16,128]{3,2,1,0:T(8,128)(2,1)S(1)} %triangle.8.refs_6_.refs_0_), channel_id=1, source_target_pairs={{0,1},{1,0},{2,3},{3,2},{4,5},{5,4},{6,7},{7,6},{8,9},{9,8},{10,11... | collective-permute-start | bytes 1081352 | tf_op jit(solution)/shard_map/ppermute | solution.py:76
  64.3 13.4 %collective-permute-start.14 = (bf16[11,88,128]{2,1,0:T(8,128)(2,1)S(1)}, bf16[11,88,128]{2,1,0:T(8,128)(2,1)S(1)}, u32[]{:S(2)}, u32[]{:S(2)}) collective-permute-start(bf16[11,88,128]{2,1,0:T(8,128)(2,1)S(1)} %get-tuple-element.49.refs_4_), channel_id=1, source_target_pairs={{0,2},{4,0},{8,4},{12,8},{14,12},{10,14},{6,10},{2,6},{1,3},{5,1},... | collective-permute-start | bytes 743432 | tf_op jit(solution)/shard_map/ppermute | solution.py:476
  67.5 2.9 %collective-permute-start.13 = (bf16[2,22,16,128]{3,2,1,0:T(8,128)(2,1)S(1)}, bf16[2,22,16,128]{3,2,1,0:T(8,128)(2,1)S(1)}, u32[]{:S(2)}, u32[]{:S(2)}) collective-permute-start(bf16[2,22,16,128]{3,2,1,0:T(8,128)(2,1)S(1)} %triangle.9.refs_4_.refs_0_), channel_id=1, source_target_pairs={{0,1},{1,0},{2,3},{3,2},{4,5},{5,4},{6,7},{7,6},{8,9},{9,8},{10,11... | collective-permute-start | bytes 540680 | tf_op jit(solution)/shard_map/ppermute | solution.py:76
  67.8 9.9 %collective-permute-start.15 = (bf16[11,88,128]{2,1,0:T(8,128)(2,1)S(1)}, bf16[11,88,128]{2,1,0:T(8,128)(2,1)S(1)}, u32[]{:S(2)}, u32[]{:S(2)}) collective-permute-start(bf16[11,88,128]{2,1,0:T(8,128)(2,1)S(1)} %get-tuple-element.52), channel_id=1, source_target_pairs={{0,4},{4,8},{8,12},{12,14},{14,10},{10,6},{6,2},{2,0},{1,5},{5,9},... | collective-permute-start | bytes 743432 | tf_op jit(solution)/shard_map/ppermute | solution.py:473
  72.5 13.1 %collective-permute-start.19 = (bf16[11,88,128]{2,1,0:T(8,128)(2,1)S(1)}, bf16[11,88,128]{2,1,0:T(8,128)(2,1)S(1)}, u32[]{:S(2)}, u32[]{:S(2)}) collective-permute-start(bf16[11,88,128]{2,1,0:T(8,128)(2,1)S(1)} %get-tuple-element.60), channel_id=1, source_target_pairs={{0,4},{4,8},{8,12},{12,14},{14,10},{10,6},{6,2},{2,0},{1,5},{5,9},... | collective-permute-start | bytes 743432 | tf_op jit(solution)/shard_map/ppermute | solution.py:473
  75.7 9.9 %collective-permute-start.18 = (bf16[11,88,128]{2,1,0:T(8,128)(2,1)S(1)}, bf16[11,88,128]{2,1,0:T(8,128)(2,1)S(1)}, u32[]{:S(2)}, u32[]{:S(2)}) collective-permute-start(bf16[11,88,128]{2,1,0:T(8,128)(2,1)S(1)} %get-tuple-element.51.refs_4_), channel_id=1, source_target_pairs={{0,2},{4,0},{8,4},{12,8},{14,12},{10,14},{6,10},{2,6},{1,3},{5,1},... | collective-permute-start | bytes 743432 | tf_op jit(solution)/shard_map/ppermute | solution.py:476
  80.2 9.1 %collective-permute-start.17 = (bf16[11,88,128]{2,1,0:T(8,128)(2,1)S(1)}, bf16[11,88,128]{2,1,0:T(8,128)(2,1)S(1)}, u32[]{:S(2)}, u32[]{:S(2)}) collective-permute-start(bf16[11,88,128]{2,1,0:T(8,128)(2,1)S(1)} %get-tuple-element.59), channel_id=1, source_target_pairs={{0,4},{4,8},{8,12},{12,14},{14,10},{10,6},{6,2},{2,0},{1,5},{5,9},... | collective-permute-start | bytes 743432 | tf_op jit(solution)/shard_map/ppermute | solution.py:473
  83.5 7.5 %collective-permute-start.16 = (bf16[11,88,128]{2,1,0:T(8,128)(2,1)S(1)}, bf16[11,88,128]{2,1,0:T(8,128)(2,1)S(1)}, u32[]{:S(2)}, u32[]{:S(2)}) collective-permute-start(bf16[11,88,128]{2,1,0:T(8,128)(2,1)S(1)} %get-tuple-element.53.refs_4_), channel_id=1, source_target_pairs={{0,2},{4,0},{8,4},{12,8},{14,12},{10,14},{6,10},{2,6},{1,3},{5,1},... | collective-permute-start | bytes 743432 | tf_op jit(solution)/shard_map/ppermute | solution.py:476
  87.2 12.8 %collective-permute-start.21 = (bf16[11,88,128]{2,1,0:T(8,128)(2,1)S(1)}, bf16[11,88,128]{2,1,0:T(8,128)(2,1)S(1)}, u32[]{:S(2)}, u32[]{:S(2)}) collective-permute-start(bf16[11,88,128]{2,1,0:T(8,128)(2,1)S(1)} %get-tuple-element.64), channel_id=1, source_target_pairs={{0,4},{4,8},{8,12},{12,14},{14,10},{10,6},{6,2},{2,0},{1,5},{5,9},... | collective-permute-start | bytes 743432 | tf_op jit(solution)/shard_map/ppermute | solution.py:473
  89.3 10.7 %collective-permute-start.20 = (bf16[11,88,128]{2,1,0:T(8,128)(2,1)S(1)}, bf16[11,88,128]{2,1,0:T(8,128)(2,1)S(1)}, u32[]{:S(2)}, u32[]{:S(2)}) collective-permute-start(bf16[11,88,128]{2,1,0:T(8,128)(2,1)S(1)} %get-tuple-element.61.refs_6_), channel_id=1, source_target_pairs={{0,2},{4,0},{8,4},{12,8},{14,12},{10,14},{6,10},{2,6},{1,3},{5,1},... | collective-permute-start | bytes 743432 | tf_op jit(solution)/shard_map/ppermute | solution.py:476
  100.0 1.0 copy-start.13
  103.0 7.4 %collective-permute-start.23 = (bf16[11,88,128]{2,1,0:T(8,128)(2,1)S(1)}, bf16[11,88,128]{2,1,0:T(8,128)(2,1)S(1)}, u32[]{:S(2)}, u32[]{:S(2)}) collective-permute-start(bf16[11,88,128]{2,1,0:T(8,128)(2,1)S(1)} %get-tuple-element.68), channel_id=1, source_target_pairs={{0,4},{4,8},{8,12},{12,14},{14,10},{10,6},{6,2},{2,0},{1,5},{5,9},... | collective-permute-start | bytes 743432 | tf_op jit(solution)/shard_map/ppermute | solution.py:473
  104.8 8.8 %collective-permute-start.22 = (bf16[11,88,128]{2,1,0:T(8,128)(2,1)S(1)}, bf16[11,88,128]{2,1,0:T(8,128)(2,1)S(1)}, u32[]{:S(2)}, u32[]{:S(2)}) collective-permute-start(bf16[11,88,128]{2,1,0:T(8,128)(2,1)S(1)} %get-tuple-element.65.refs_4_), channel_id=1, source_target_pairs={{0,2},{4,0},{8,4},{12,8},{14,12},{10,14},{6,10},{2,6},{1,3},{5,1},... | collective-permute-start | bytes 743432 | tf_op jit(solution)/shard_map/ppermute | solution.py:476
  105.0 13.6 %collective-permute-start.27 = (bf16[11,88,128]{2,1,0:T(8,128)(2,1)S(1)}, bf16[11,88,128]{2,1,0:T(8,128)(2,1)S(1)}, u32[]{:S(2)}, u32[]{:S(2)}) collective-permute-start(bf16[11,88,128]{2,1,0:T(8,128)(2,1)S(1)} %get-tuple-element.62.refs_12_), channel_id=1, source_target_pairs={{0,2},{4,0},{8,4},{12,8},{14,12},{10,14},{6,10},{2,6},{1,3},{5,1},... | collective-permute-start | bytes 743432 | tf_op jit(solution)/shard_map/ppermute | solution.py:476
  105.6 12.5 %collective-permute-start.28 = (bf16[128,512]{1,0:T(8,128)(2,1)S(1)}, bf16[128,512]{1,0:T(8,128)(2,1)S(1)}, u32[]{:S(2)}, u32[]{:S(2)}) collective-permute-start(bf16[128,512]{1,0:T(8,128)(2,1)S(1)} %get-tuple-element.74), channel_id=1, source_target_pairs={{0,1},{1,0},{2,3},{3,2},{4,5},{5,4},{6,7},{7,6},{8,9},{9,8},{10,11... | collective-permute-start | bytes 393224 | tf_op jit(solution)/shard_map/ppermute | solution.py:76
  105.6 13.0 %collective-permute-start.25 = (bf16[11,88,128]{2,1,0:T(8,128)(2,1)S(1)}, bf16[11,88,128]{2,1,0:T(8,128)(2,1)S(1)}, u32[]{:S(2)}, u32[]{:S(2)}) collective-permute-start(bf16[11,88,128]{2,1,0:T(8,128)(2,1)S(1)} %get-tuple-element.70), channel_id=1, source_target_pairs={{0,4},{4,8},{8,12},{12,14},{14,10},{10,6},{6,2},{2,0},{1,5},{5,9},... | collective-permute-start | bytes 743432 | tf_op jit(solution)/shard_map/ppermute | solution.py:473
  116.0 6.3 %collective-permute-start.24 = (bf16[11,88,128]{2,1,0:T(8,128)(2,1)S(1)}, bf16[11,88,128]{2,1,0:T(8,128)(2,1)S(1)}, u32[]{:S(2)}, u32[]{:S(2)}) collective-permute-start(bf16[11,88,128]{2,1,0:T(8,128)(2,1)S(1)} %get-tuple-element.69), channel_id=1, source_target_pairs={{0,2},{4,0},{8,4},{12,8},{14,12},{10,14},{6,10},{2,6},{1,3},{5,1},... | collective-permute-start | bytes 743432 | tf_op jit(solution)/shard_map/ppermute | solution.py:476
  116.5 6.2 %collective-permute-start.26 = (bf16[11,88,128]{2,1,0:T(8,128)(2,1)S(1)}, bf16[11,88,128]{2,1,0:T(8,128)(2,1)S(1)}, u32[]{:S(2)}, u32[]{:S(2)}) collective-permute-start(bf16[11,88,128]{2,1,0:T(8,128)(2,1)S(1)} %get-tuple-element.71), channel_id=1, source_target_pairs={{0,4},{4,8},{8,12},{12,14},{14,10},{10,6},{6,2},{2,0},{1,5},{5,9},... | collective-permute-start | bytes 743432 | tf_op jit(solution)/shard_map/ppermute | solution.py:473
  118.2 6.7 %collective-permute-start.29 = (bf16[128,512]{1,0:T(8,128)(2,1)S(1)}, bf16[128,512]{1,0:T(8,128)(2,1)S(1)}, u32[]{:S(2)}, u32[]{:S(2)}) collective-permute-start(bf16[128,512]{1,0:T(8,128)(2,1)S(1)} %add_convert_fusion.3), channel_id=1, source_target_pairs={{0,2},{2,0},{4,6},{6,4},{8,10},{10,8},{12,14},{14,12},{1,3},{3,1},... | collective-permute-start | bytes 393224 | tf_op jit(solution)/shard_map/ppermute | solution.py:88
  124.8 15.3 %copy-start.2 = (bf16[22,88,128]{2,1,0:T(8,128)(2,1)S(1)}, bf16[22,88,128]{2,1,0:T(8,128)(2,1)}, u32[]{:S(2)}) copy-start(bf16[22,88,128]{2,1,0:T(8,128)(2,1)} %refs_0_.35) | copy-start | bytes 1486852
  124.8 15.3 %copy-start.12 = (f32[128]{0:T(128)S(1)}, f32[128]{0:T(128)}, u32[]{:S(2)}) copy-start(f32[128]{0:T(128)} %param.12) | copy-start | bytes 1540
  124.8 1.8 %collective-permute-start.32 = (bf16[128,256]{1,0:T(8,128)(2,1)S(1)}, bf16[128,256]{1,0:T(8,128)(2,1)S(1)}, u32[]{:S(2)}, u32[]{:S(2)}) collective-permute-start(bf16[128,256]{1,0:T(8,128)(2,1)S(1)} %get-tuple-element.75), channel_id=1, source_target_pairs={{0,1},{1,0},{2,3},{3,2},{4,5},{5,4},{6,7},{7,6},{8,9},{9,8},{10,11... | collective-permute-start | bytes 196616 | tf_op jit(solution)/shard_map/ppermute | solution.py:76
  124.9 6.0 %collective-permute-start.30 = (bf16[128,512]{1,0:T(8,128)(2,1)S(1)}, bf16[128,512]{1,0:T(8,128)(2,1)S(1)}, u32[]{:S(2)}, u32[]{:S(2)}) collective-permute-start(bf16[128,512]{1,0:T(8,128)(2,1)S(1)} %add_convert_fusion.2), channel_id=1, source_target_pairs={{0,4},{2,6},{4,0},{6,2},{8,12},{10,14},{12,8},{14,10},{1,5},{3,7},... | collective-permute-start | bytes 393224 | tf_op jit(solution)/shard_map/ppermute | solution.py:88
  126.6 6.4 %collective-permute-start.33 = (bf16[128,256]{1,0:T(8,128)(2,1)S(1)}, bf16[128,256]{1,0:T(8,128)(2,1)S(1)}, u32[]{:S(2)}, u32[]{:S(2)}) collective-permute-start(bf16[128,256]{1,0:T(8,128)(2,1)S(1)} %add_convert_fusion.6), channel_id=1, source_target_pairs={{0,2},{2,0},{4,6},{6,4},{8,10},{10,8},{12,14},{14,12},{1,3},{3,1},... | collective-permute-start | bytes 196616 | tf_op jit(solution)/shard_map/ppermute | solution.py:88
  130.9 8.9 %collective-permute-start.31 = (bf16[128,512]{1,0:T(8,128)(2,1)S(1)}, bf16[128,512]{1,0:T(8,128)(2,1)S(1)}, u32[]{:S(2)}, u32[]{:S(2)}) collective-permute-start(bf16[128,512]{1,0:T(8,128)(2,1)S(1)} %add_convert_fusion.1), channel_id=1, source_target_pairs={{0,8},{2,10},{4,12},{6,14},{8,0},{10,2},{12,4},{14,6},{1,9},{3,11}... | collective-permute-start | bytes 393224 | tf_op jit(solution)/shard_map/ppermute | solution.py:88
  133.0 6.8 %collective-permute-start.34 = (bf16[128,256]{1,0:T(8,128)(2,1)S(1)}, bf16[128,256]{1,0:T(8,128)(2,1)S(1)}, u32[]{:S(2)}, u32[]{:S(2)}) collective-permute-start(bf16[128,256]{1,0:T(8,128)(2,1)S(1)} %add_convert_fusion.5), channel_id=1, source_target_pairs={{0,4},{2,6},{4,0},{6,2},{8,12},{10,14},{12,8},{14,10},{1,5},{3,7},... | collective-permute-start | bytes 196616 | tf_op jit(solution)/shard_map/ppermute | solution.py:88
  139.9 6.2 %collective-permute-start.35 = (bf16[128,256]{1,0:T(8,128)(2,1)S(1)}, bf16[128,256]{1,0:T(8,128)(2,1)S(1)}, u32[]{:S(2)}, u32[]{:S(2)}) collective-permute-start(bf16[128,256]{1,0:T(8,128)(2,1)S(1)} %add_convert_fusion.4.refs_1_), channel_id=1, source_target_pairs={{0,8},{2,10},{4,12},{6,14},{8,0},{10,2},{12,4},{14,6},{1,9},{3,11}... | collective-permute-start | bytes 196616 | tf_op jit(solution)/shard_map/ppermute | solution.py:88

commit v6 on v5

--- a/solution.py
+++ b/solution.py
@@ -1,4 +1,5 @@
 import functools
+import math
 
 import jax
 import jax.numpy as jnp
@@ -90,33 +91,46 @@
     return x, other
 
 
-def whole_of(x):
-    return pl.BlockSpec(x.shape, lambda step: (0,) * x.ndim)
-
-
 def call(kernel, name, microseconds, args, specs, outs, scratch=(), after=()):
-    held = sum(a.size * a.dtype.itemsize for a, s in zip(args, specs) if s is not SMEM)
+    held = sum(a.size * a.dtype.itemsize for a, s in zip(args, specs) if s is VMEM)
     after = [x for x in after if x is not None]
-    streamed = any(s is not SMEM and s is not VMEM for s in specs)
     held += sum(int(o.size) * o.dtype.itemsize for o in outs)
-    held += sum(int(s.inner_aval.size) * 4 for s in scratch)
+    held += sum(math.prod(s.inner_aval.shape) * 4 for s in scratch)
 
     def body(*refs):
         kernel(*refs[: len(args)], *refs[len(args) + len(after) :])
 
     return pl.pallas_call(
         body,
-        grid=(1,) if streamed else (),
         out_shape=list(outs),
         in_specs=list(specs) + [ANY] * len(after),
         out_specs=[VMEM] * len(outs),
         scratch_shapes=list(scratch),
         compiler_params=pltpu.CompilerParams(vmem_limit_bytes=min(56 * MIB, held * 5 // 4 + 6 * MIB)),
         cost_estimate=pl.CostEstimate(
-            flops=int(microseconds * 1.1e9), bytes_accessed=MIB, transcendentals=0
+            flops=int(microseconds * 1e6), bytes_accessed=1024, transcendentals=0
         ),
         name=name,
     )(*args, *after)
+
+
+def tiles(half):
+    return [(k, min(16, half - k)) for k in range(0, half, 16)]
+
+
+def joined(terms):
+    chains = [terms[0::2], terms[1::2]]
+    sums = []
+    for chain in chains:
+        total = chain[0]
+        for term in chain[1:]:
+            total = total + term
+        sums.append(total.astype(f32))
+    return sums[0] + sums[1]
+
+
+def wide_row(ref, *at):
+    return jnp.broadcast_to(ref[at], (16, ref.shape[-1])).astype(bf16)
 
 
 def shape_of(dims, dtype):
@@ -140,7 +154,17 @@
     return lax.axis_index("row") * here
 
 
-def input_kernel(slot, lengths, pair, gain, bias, w, right, normed, mask):
+def input_kernel(slot, *refs):
+    given, (right, normed), held, (mask, sems) = refs[:5], refs[5:7], refs[7:12], refs[12:]
+    copies = [
+        pltpu.make_async_copy(source, target, sems.at[at])
+        for at, (source, target) in enumerate(zip(given, held))
+    ]
+    for copy in copies:
+        copy.start()
+    for copy in copies:
+        copy.wait()
+    lengths, pair, gain, bias, w = held
     here, half, hidden = pair.shape
     mask[...] = present_columns(lengths, slot, half)
 
@@ -173,7 +197,7 @@
         proj = dot(normed[i], w[:, : 2 * hidden], 1, 0)
         shown = mask[...] * present_row(lengths, slot, first_row(here) + i)
         gated = shown * jax.nn.sigmoid(proj[:, :hidden]) * proj[:, hidden:]
-        left[i] = gated.astype(bf16).astype(f32)
+        left[i] = gated.astype(bf16)
         gate = jax.nn.sigmoid(dot(normed[i], w[:, 4 * hidden :], 1, 0))
         grads = cotangent[i].astype(f32) * gate
         empty = jnp.zeros((padded - short, hidden), f32)
@@ -185,19 +209,26 @@
 
 
 def triangle_kernel(row_count, slot, halves, arrays, lengths, left, *refs):
-    rights, (out, right, partial, rows) = refs[:arrays], refs[arrays:]
+    rights, (out, partial, rows) = refs[:arrays], refs[arrays:]
     here, half, hidden = left.shape
     padded = out.shape[2]
-    short = right.shape[0]
+    short = here // 2
     for s, (array, first, place) in enumerate(halves):
-        right[...] = rights[array][pl.ds(first, short)].astype(f32)
         rows[...] = jnp.zeros_like(rows)
 
-        def body(j, carry):
-            held = right[j]
+        def body(j, carry, right=rights[array], first=first):
+            held = [right[first + j, pl.ds(k, size), :] for k, size in tiles(half)]
             for i in range(here):
-                product = (left[i] * held).reshape(half // 8, 8, hidden)
-                partial[pl.ds(8 * i, 8), :] = jnp.sum(product, axis=0)
+                products = [
+                    left[i, pl.ds(k, size), :] * held[at]
+                    for at, (k, size) in enumerate(tiles(half))
+                ]
+                rest = products.pop() if half % 16 else None
+                total = joined(products)
+                total = total[:8] + total[8:]
+                if rest is not None:
+                    total += rest.astype(f32)
+                partial[pl.ds(8 * i, 8), :] = total
             total = partial[pl.ds(0, here, stride=8), :]
             for sub in range(1, 8):
                 total += partial[pl.ds(sub, here, stride=8), :]
@@ -219,7 +250,6 @@
         [SMEM] + [VMEM] * (len(rights) + 1),
         [shape_of((count, here, padded, hidden), bf16)],
         [
-            pltpu.VMEM((here // 2, half, hidden), f32),
             pltpu.VMEM((here * 8, hidden), f32),
             pltpu.VMEM((here * padded, hidden), f32),
         ],
@@ -268,18 +298,23 @@
 
         def body(pair, carry, s=s, out=out):
             at = [jnp.minimum(2 * pair + x, short - 1) for x in range(2)]
-            totals = []
-            for j in at:
-                total = jnp.zeros((half, hidden), f32)
-                for more in range(carried):
-                    total += arrived[s + more * count][j].astype(f32)
-                totals.append(total)
-            for i in range(here):
-                held = left[i]
-                for x in range(2):
-                    totals[x] += wide[i, pl.ds(at[x], 1), :] * held
-            for x in range(2):
-                out[at[x]] = totals[x].astype(out.dtype)
+            totals = [[] for _ in at]
+            for j, total in zip(at, totals):
+                for k, size in tiles(half):
+                    start = jnp.zeros((size, hidden), f32)
+                    for more in range(carried):
+                        start += arrived[s + more * count][j, pl.ds(k, size), :].astype(f32)
+                    total.append(start)
+            for low in range(0, here, short):
+                chosen = range(low, min(low + short, here))
+                weights = [[wide_row(wide, i, pl.ds(j, 1)) for i in chosen] for j in at]
+                for t, (k, size) in enumerate(tiles(half)):
+                    held = [left[i, pl.ds(k, size), :] for i in chosen]
+                    for x in range(2):
+                        totals[x][t] += joined([w[:size] * h for w, h in zip(weights[x], held)])
+            for j, total in zip(at, totals):
+                for t, (k, size) in enumerate(tiles(half)):
+                    out[j, pl.ds(k, size), :] = total[t].astype(out.dtype)
             return carry
 
         def clear(j, carry, out=out):
@@ -311,23 +346,29 @@
 def left_gradient_kernel(halves, picks, arrays, carried, grads, *refs):
     count = len(picks)
     rights, refs = refs[:arrays], refs[arrays:]
-    before, (out, right, wide) = refs[:carried], refs[carried:]
+    before, (out, wide) = refs[:carried], refs[carried:]
     here, half, hidden = out.shape
     short = here // 2
     for s, pick in enumerate(picks):
-        array, first, _ = halves[pick]
-        right[s] = rights[array][pl.ds(first, short)].astype(f32)
         wide[s] = grads[pick].astype(f32)
 
-    def row(i, carry):
-        total = before[0][i] if carried else jnp.zeros((half, hidden), f32)
-        for s in range(count):
-            for j in range(short):
-                total += wide[s, i, pl.ds(j, 1), :] * right[s, j]
-        out[i] = total
+    def row(pair, carry):
+        rows = (2 * pair, 2 * pair + 1)
+        for s, pick in enumerate(picks):
+            array, first, _ = halves[pick]
+            weights = [[wide_row(wide, s, i, pl.ds(j, 1)) for j in range(short)] for i in rows]
+            for k, size in tiles(half):
+                held = [rights[array][first + j, pl.ds(k, size), :] for j in range(short)]
+                for i, weight in zip(rows, weights):
+                    total = joined([w[:size] * h for w, h in zip(weight, held)])
+                    if s:
+                        total += out[i, pl.ds(k, size), :]
+                    elif carried:
+                        total += before[0][i, pl.ds(k, size), :]
+                    out[i, pl.ds(k, size), :] = total
         return carry
 
-    lax.fori_loop(0, here, row, 0)
+    lax.fori_loop(0, here // 2, row, 0)
 
 
 def left_gradient(halves, picks, grads, rights, before, after):
@@ -340,10 +381,7 @@
         [grads, *rights, *before],
         [VMEM] * (1 + len(rights) + len(before)),
         [shape_of((here, half, hidden), f32)],
-        [
-            pltpu.VMEM((count, here // 2, half, hidden), f32),
-            pltpu.VMEM((count,) + grads.shape[1:], f32),
-        ],
+        [pltpu.VMEM((count,) + grads.shape[1:], f32)],
         after,
     )[0]
 
@@ -480,31 +518,41 @@
         "input_side",
         3.0,
         [chain_lengths, pair, in_gain, in_bias, w_in],
-        [SMEM] + [whole_of(x) for x in (pair, in_gain, in_bias, w_in)],
+        [pl.BlockSpec(memory_space=pltpu.HBM)] * 5,
         [shape_of(block, bf16)] * 2,
-        [mask],
+        [
+            pltpu.SMEM(chain_lengths.shape, jnp.int32),
+            pltpu.VMEM(block, bf16),
+            pltpu.VMEM(in_gain.shape, f32),
+            pltpu.VMEM(in_bias.shape, f32),
+            pltpu.VMEM(w_in.shape, bf16),
+            mask,
+            pltpu.SemaphoreType.DMA((5,)),
+        ],
     )
 
     hops = row_count // 2
     groups = [[right]]
     halves = [[(0, 0, (0, 0)), (0, short, (0, 1))]]
-    x = y = right
     for s in range(1, hops):
-        x, y = ahead(x), behind(y)
-        groups.append([x, y])
         halves.append(
             [(0, 0, (-s, 0)), (1, short, (s, 1)), (0, short, (-s, 1)), (1, 0, (s, 0))]
         )
-    groups.append([ahead(x[:short]), behind(y[short:])])
     halves.append([(0, 0, (-hops, 0)), (1, 0, (hops, 1))])
 
+    def gather(s, x, y):
+        if s == hops:
+            x, y = x[:short], y[short:]
+        groups.append([ahead(x), behind(y)])
+
+    gather(1, right, right)
     left, mine_out = call(
         functools.partial(left_kernel, slot),
         "left_side",
         4.0,
         [chain_lengths, normed, cotangent, w_in],
         [SMEM] + [VMEM] * 3,
-        [shape_of(block, f32), shape_of((row_count, here, padded, hidden), bf16)],
+        [shape_of(block, bf16), shape_of((row_count, here, padded, hidden), bf16)],
         [mask],
     )
     outs = jnp.concatenate([mine_out, swap_col(mine_out)], axis=0)
@@ -581,15 +629,17 @@
         last[:] = results[:1]
         return results
 
-    triangles(0)
-    for s in range(1, hops):
+    for s in range(hops):
         triangles(s)
-        normal(s - 1)
-        add_left(s - 1)
-    normal(hops - 1)
-    send(hops - 1, 2)
+        normal(s)
+        if s == hops - 1:
+            send(s, 2)
+            add_left(s, [0, 1])
+        else:
+            add_left(s)
+            x, y, _ = lax.optimization_barrier((*groups[s + 1], pieces[0]))
+            gather(s + 2, x, y)
     triangles(hops)
-    add_left(hops - 1, [0, 1])
     normal(hops)
     send(hops, 0)
     add_left(hops - 1, [2, 3])

time: 146 us -> 146 us (level); the launches traced: 147 us -> 145 us
  Pallas kernels: 67.7 us -> 58.8 us
  waiting for transfers between devices: 37.7 us -> 43 us
    pallas_call x30, Pallas kernels: 67.7 us -> 58.8 us  [call(): pl.pallas_call(body, out_shape=list(outs), in_specs=list(specs) + [ANY] *...]
    ppermute x11, waiting for transfers between devices: 2.23 us -> 8.64 us  [ahead(): return lax.ppermute(x, 'row', forward)]
    ppermute x11, waiting for transfers between devices: 24 us -> 18.6 us  [behind(): return lax.ppermute(x, 'row', backward)]
    ppermute x8, waiting for transfers between devices: 0.02 us -> 4.36 us  [swap_col(): return lax.ppermute(x, 'col', [(0, 1), (1, 0)])]
    ppermute x6, starting transfers between devices: 6.72 us -> 9.18 us  [sum_all(): other = lax.ppermute(x, 'row', [(r, r ^ step) for r in range(row_count)])]
    ppermute x11, starting transfers between devices: 15.6 us -> 13.3 us  [ahead(): return lax.ppermute(x, 'row', forward)]
    unnamed x29 -> x33, local copies, waits for them, and re-layouts: 5.55 us -> 6.79 us
  transfers between devices with their start and end apart: 36 -> 36, of which waited for: 12 -> 23; matrix products, arithmetic and copies ran while one was open for 0% -> 0% of each run, Pallas kernels for 43% -> 32%
where the time goes in v6:
time: 146 us; the launch traced here: 145 us
  Pallas kernels  58.8 us (40%)
  waiting for transfers between devices  43 us (29%)
  starting transfers between devices  34.8 us (24%)
  local copies, waits for them, and re-layouts  7.01 us (5%)
    pallas_call x30, Pallas kernels, call(): pl.pallas_call(body, out_shape=list(outs), in_specs=list(specs) + [ANY] *...  58.8 us
    ppermute x11, waiting for transfers between devices, behind(): return lax.ppermute(x, 'row', backward)  18.6 us
    ppermute x11, starting transfers between devices, ahead(): return lax.ppermute(x, 'row', forward)  13.3 us
    ppermute x6, waiting for transfers between devices, sum_all(): other = lax.ppermute(x, 'row', [(r, r ^ step) for r in range(row_count)])  11.3 us
    ppermute x11, starting transfers between devices, behind(): return lax.ppermute(x, 'row', backward)  11.3 us
    ppermute x6, starting transfers between devices, sum_all(): other = lax.ppermute(x, 'row', [(r, r ^ step) for r in range(row_count)])  9.18 us
    ppermute x11, waiting for transfers between devices, ahead(): return lax.ppermute(x, 'row', forward)  8.64 us
    unnamed x33, local copies, waits for them, and re-layouts  6.79 us
  transfers between devices with their start and end apart: 36, of which 23 were waited for; matrix products, arithmetic and copies ran while one was open for 0% of the time, Pallas kernels for 32%

profile of v6, /device:TPU:0, one launch (start us, length us, event | category | flops | bytes accessed | tf_op | source)
XLA Modules:
  0.0 144.8 jit_solution(15693124030511421434)
XLA Ops:
  1.6 1.0 copy-done.4
  4.5 1.5 %input_side.1 = (bf16[22,88,128]{2,1,0:T(8,128)(2,1)S(1)}, bf16[22,88,128]{2,1,0:T(8,128)(2,1)S(1)}) custom-call(s32[8]{0:T(128)S(1)} %copy-done.8, bf16[22,88,128]{2,1,0:T(8,128)(2,1)S(1)} %copy-done.4, f32[1,128]{1,0:T(1,128)S(1)} %bitcast.14, f32[1,128]{1,0:T(1,128)S(1)} %bitcast.16, bf16[128,640]{1,0:T(8,128)(2,1)S(1)} %copy-done), custom_call_target="tpu_custom_call" | custom-call | flops 3000000 | bytes 1024 | tf_op jit(solution)/shard_map/input_side/pallas_call | solution.py:103
  6.0 1.0 copy-done.2
  7.7 1.4 left_side.1
  9.7 2.6 %collective-permute-start.1 = (bf16[22,88,128]{2,1,0:T(8,128)(2,1)S(1)}, bf16[22,88,128]{2,1,0:T(8,128)(2,1)S(1)}, u32[]{:S(2)}, u32[]{:S(2)}) collective-permute-start(bf16[22,88,128]{2,1,0:T(8,128)(2,1)S(1)} %get-tuple-element.49.refs_2_.refs_1_), channel_id=1, source_target_pairs={{0,2},{4,0},{8,4},{12,8},{14,12},{10,14},{6,10},{2,6},{1,3},{5,1},... | collective-permute-start | bytes 1486856 | tf_op jit(solution)/shard_map/ppermute | solution.py:514
  12.4 2.8 %triangle.5.refs_0_.refs_6_ = bf16[2,22,16,128]{3,2,1,0:T(8,128)(2,1)S(1)} custom-call(s32[8]{0:T(128)S(1)} %copy-done.9, bf16[22,88,128]{2,1,0:T(8,128)(2,1)S(1)} %get-tuple-element.48.refs_1_.refs_3_, bf16[22,88,128]{2,1,0:T(8,128)(2,1)S(1)} %get-tuple-element.49.refs_2_.refs_1_, bf16[22,88,128]{2,1,0:T(8,128)(2,1)S(1)} %get-tuple-element.48.refs_1_.refs_3_), custom_call_target="tpu_custom_call" | custom-call | flops 1800000 | bytes 1024 | tf_op jit(solution)/shard_map/triangle/pallas_call | solution.py:103
  15.7 1.0 collective-permute-done.2.refs_1_
  17.3 1.1 left_gradient.6.refs_4_.refs_3_
  18.4 5.8 %collective-permute-done.1.refs_3_.refs_2_ = bf16[22,88,128]{2,1,0:T(8,128)(2,1)S(1)} collective-permute-done((bf16[22,88,128]{2,1,0:T(8,128)(2,1)S(1)}, bf16[22,88,128]{2,1,0:T(8,128)(2,1)S(1)}, u32[]{:S(2)}, u32[]{:S(2)}) %collective-permute-start.1) | collective-permute-done | bytes 495648 | tf_op jit(solution)/shard_map/ppermute | solution.py:514
  24.2 1.4 collective-permute-done.refs_2_.refs_1_
  26.0 1.7 %collective-permute-start.5 = (bf16[22,88,128]{2,1,0:T(8,128)(2,1)S(1)}, bf16[22,88,128]{2,1,0:T(8,128)(2,1)S(1)}, u32[]{:S(2)}, u32[]{:S(2)}) collective-permute-start(bf16[22,88,128]{2,1,0:T(8,128)(2,1)S(1)} %collective-permute-done.1.refs_3_.refs_2_), channel_id=1, source_target_pairs={{0,2},{4,0},{8,4},{12,8},{14,12},{10,14},{6,10},{2,6},{1,3},{5,1},... | collective-permute-start | bytes 1486856 | tf_op jit(solution)/shard_map/ppermute | solution.py:514
  27.6 3.1 %triangle.6.refs_0_.refs_6_ = bf16[4,22,16,128]{3,2,1,0:T(8,128)(2,1)S(1)} custom-call(s32[8]{0:T(128)S(1)} %copy-done.9, bf16[22,88,128]{2,1,0:T(8,128)(2,1)S(1)} %get-tuple-element.48.refs_1_.refs_3_, bf16[22,88,128]{2,1,0:T(8,128)(2,1)S(1)} %collective-permute-done.refs_2_.refs_1_, bf16[22,88,128]{2,1,0:T(8,128)(2,1)S(1)} %collective-permute-done.1.refs_3_.refs_2_, ...), custom_call_target="tpu_custom_call" | custom-call | flops 3600000 | bytes 1024 | tf_op jit(solution)/shard_map/triangle/pallas_call | solution.py:103
  30.9 1.7 %collective-permute-done.6.refs_1_ = bf16[4,22,16,128]{3,2,1,0:T(8,128)(2,1)S(1)} collective-permute-done((bf16[4,22,16,128]{3,2,1,0:T(8,128)(2,1)S(1)}, bf16[4,22,16,128]{3,2,1,0:T(8,128)(2,1)S(1)}, u32[]{:S(2)}, u32[]{:S(2)}) %collective-permute-start.6) | collective-permute-done | bytes 360480 | tf_op jit(solution)/shard_map/ppermute | solution.py:77
  32.5 1.0 triangle_norm.6
  33.5 2.3 %left_gradient.7.refs_4_.refs_3_ = f32[22,88,128]{2,1,0:T(8,128)S(1)} custom-call(bf16[4,22,16,128]{3,2,1,0:T(8,128)(2,1)S(1)} %get-tuple-element.54.refs_0_.refs_4_.refs_2_.refs_3_, bf16[22,88,128]{2,1,0:T(8,128)(2,1)S(1)} %collective-permute-done.refs_2_.refs_1_, bf16[22,88,128]{2,1,0:T(8,128)(2,1)S(1)} %collective-permute-done.1.refs_3_.refs_2_, ...), custom_call_target="tpu_custom_call" | custom-call | flops 3600000 | bytes 1024 | tf_op jit(solution)/shard_map/left_gradient/pallas_call | solution.py:103
  35.8 2.4 %collective-permute-done.4.refs_2_.refs_1_ = bf16[22,88,128]{2,1,0:T(8,128)(2,1)S(1)} collective-permute-done((bf16[22,88,128]{2,1,0:T(8,128)(2,1)S(1)}, bf16[22,88,128]{2,1,0:T(8,128)(2,1)S(1)}, u32[]{:S(2)}, u32[]{:S(2)}) %collective-permute-start.4) | collective-permute-done | bytes 495648 | tf_op jit(solution)/shard_map/ppermute | solution.py:511
  38.5 1.6 %collective-permute-start.7 = (bf16[22,88,128]{2,1,0:T(8,128)(2,1)S(1)}, bf16[22,88,128]{2,1,0:T(8,128)(2,1)S(1)}, u32[]{:S(2)}, u32[]{:S(2)}) collective-permute-start(bf16[22,88,128]{2,1,0:T(8,128)(2,1)S(1)} %collective-permute-done.4.refs_2_.refs_1_), channel_id=1, source_target_pairs={{0,4},{4,8},{8,12},{12,14},{14,10},{10,6},{6,2},{2,0},{1,5},{5,9},... | collective-permute-start | bytes 1486856 | tf_op jit(solution)/shard_map/ppermute | solution.py:511
  40.6 3.7 %triangle.7.refs_0_.refs_6_ = bf16[4,22,16,128]{3,2,1,0:T(8,128)(2,1)S(1)} custom-call(s32[8]{0:T(128)S(1)} %copy-done.9, bf16[22,88,128]{2,1,0:T(8,128)(2,1)S(1)} %get-tuple-element.48.refs_1_.refs_3_, bf16[22,88,128]{2,1,0:T(8,128)(2,1)S(1)} %collective-permute-done.4.refs_2_.refs_1_, bf16[22,88,128]{2,1,0:T(8,128)(2,1)S(1)} %collective-permute-done.5.refs_3_.refs_2_, ...), custom_call_target="tpu_custom_call" | custom-call | flops 3600000 | bytes 1024 | tf_op jit(solution)/shard_map/triangle/pallas_call | solution.py:103
  44.4 1.7 %collective-permute-done.9.refs_1_ = bf16[4,22,16,128]{3,2,1,0:T(8,128)(2,1)S(1)} collective-permute-done((bf16[4,22,16,128]{3,2,1,0:T(8,128)(2,1)S(1)}, bf16[4,22,16,128]{3,2,1,0:T(8,128)(2,1)S(1)}, u32[]{:S(2)}, u32[]{:S(2)}) %collective-permute-start.9) | collective-permute-done | bytes 360480 | tf_op jit(solution)/shard_map/ppermute | solution.py:77
  46.1 1.0 triangle_norm.7
  47.0 2.3 %left_gradient.8.refs_4_.refs_3_ = f32[22,88,128]{2,1,0:T(8,128)S(1)} custom-call(bf16[4,22,16,128]{3,2,1,0:T(8,128)(2,1)S(1)} %get-tuple-element.57.refs_0_.refs_4_.refs_2_.refs_3_, bf16[22,88,128]{2,1,0:T(8,128)(2,1)S(1)} %collective-permute-done.4.refs_2_.refs_1_, bf16[22,88,128]{2,1,0:T(8,128)(2,1)S(1)} %collective-permute-done.5.refs_3_.refs_2_, ...), custom_call_target="tpu_custom_call" | custom-call | flops 3600000 | bytes 1024 | tf_op jit(solution)/shard_map/left_gradient/pallas_call | solution.py:103
  50.2 1.1 collective-permute-done.8.refs_3_.refs_2_
  51.3 4.3 %triangle.8.refs_0_.refs_6_ = bf16[4,22,16,128]{3,2,1,0:T(8,128)(2,1)S(1)} custom-call(s32[8]{0:T(128)S(1)} %copy-done.9, bf16[22,88,128]{2,1,0:T(8,128)(2,1)S(1)} %get-tuple-element.48.refs_1_.refs_3_, bf16[22,88,128]{2,1,0:T(8,128)(2,1)S(1)} %collective-permute-done.7.refs_2_.refs_1_, bf16[22,88,128]{2,1,0:T(8,128)(2,1)S(1)} %collective-permute-done.8.refs_3_.refs_2_, ...), custom_call_target="tpu_custom_call" | custom-call | flops 3600000 | bytes 1024 | tf_op jit(solution)/shard_map/triangle/pallas_call | solution.py:103
  56.2 1.7 %collective-permute-start.10 = (bf16[11,88,128]{2,1,0:T(8,128)(2,1)S(1)}, bf16[11,88,128]{2,1,0:T(8,128)(2,1)S(1)}, u32[]{:S(2)}, u32[]{:S(2)}) collective-permute-start(bf16[11,88,128]{2,1,0:T(8,128)(2,1)S(1)} %slice.6), channel_id=1, source_target_pairs={{0,4},{4,8},{8,12},{12,14},{14,10},{10,6},{6,2},{2,0},{1,5},{5,9},... | collective-permute-start | bytes 743432 | tf_op jit(solution)/shard_map/ppermute | solution.py:511
  57.9 1.0 triangle_norm.8
  58.9 2.0 %scatter_hop.8 = (bf16[11,88,128]{2,1,0:T(8,128)(2,1)S(1)}, bf16[11,88,128]{2,1,0:T(8,128)(2,1)S(1)}) custom-call(s32[8]{0:T(128)S(1)} %copy-done.9, bf16[22,88,128]{2,1,0:T(8,128)(2,1)S(1)} %get-tuple-element.48.refs_1_.refs_3_, bf16[4,22,16,128]{3,2,1,0:T(8,128)(2,1)S(1)} %get-tuple-element.60.refs_2_.refs_3_.refs_4_.refs_0_, ...), custom_call_target="tpu_custom_call" | custom-call | flops 1400000 | bytes 1024 | tf_op jit(solution)/shard_map/scatter_hop/pallas_call | solution.py:103
  60.9 1.2 left_gradient.9.refs_4_.refs_3_
  62.1 2.2 %collective-permute-done.11.refs_3_.refs_2_ = bf16[11,88,128]{2,1,0:T(8,128)(2,1)S(1)} collective-permute-done((bf16[11,88,128]{2,1,0:T(8,128)(2,1)S(1)}, bf16[11,88,128]{2,1,0:T(8,128)(2,1)S(1)}, u32[]{:S(2)}, u32[]{:S(2)}) %collective-permute-start.11) | collective-permute-done | bytes 247840 | tf_op jit(solution)/shard_map/ppermute | solution.py:514
  64.3 2.3 %triangle.9.refs_0_.refs_6_ = bf16[2,22,16,128]{3,2,1,0:T(8,128)(2,1)S(1)} custom-call(s32[8]{0:T(128)S(1)} %copy-done.9, bf16[22,88,128]{2,1,0:T(8,128)(2,1)S(1)} %get-tuple-element.48.refs_1_.refs_3_, bf16[11,88,128]{2,1,0:T(8,128)(2,1)S(1)} %collective-permute-done.10.refs_2_.refs_1_, bf16[11,88,128]{2,1,0:T(8,128)(2,1)S(1)} %collective-permute-done.11.refs_3_.refs_2_, ...), custom_call_target="tpu_custom_call" | custom-call | flops 1800000 | bytes 1024 | tf_op jit(solution)/shard_map/triangle/pallas_call | solution.py:103
  66.7 2.2 %collective-permute-start.15 = (bf16[11,88,128]{2,1,0:T(8,128)(2,1)S(1)}, bf16[11,88,128]{2,1,0:T(8,128)(2,1)S(1)}, u32[]{:S(2)}, u32[]{:S(2)}) collective-permute-start(bf16[11,88,128]{2,1,0:T(8,128)(2,1)S(1)} %get-tuple-element.64), channel_id=1, source_target_pairs={{0,4},{4,8},{8,12},{12,14},{14,10},{10,6},{6,2},{2,0},{1,5},{5,9},... | collective-permute-start | bytes 743432 | tf_op jit(solution)/shard_map/ppermute | solution.py:511
  69.5 1.7 %scatter_hop.9 = (bf16[11,88,128]{2,1,0:T(8,128)(2,1)S(1)}, bf16[11,88,128]{2,1,0:T(8,128)(2,1)S(1)}) custom-call(s32[8]{0:T(128)S(1)} %copy-done.9, bf16[22,88,128]{2,1,0:T(8,128)(2,1)S(1)} %get-tuple-element.48.refs_1_.refs_3_, bf16[2,22,16,128]{3,2,1,0:T(8,128)(2,1)S(1)} %get-tuple-element.62.refs_2_.refs_3_.refs_4_.refs_0_, ...), custom_call_target="tpu_custom_call" | custom-call | flops 1400000 | bytes 1024 | tf_op jit(solution)/shard_map/scatter_hop/pallas_call | solution.py:103
  71.2 2.4 %collective-permute-start.19 = (bf16[11,88,128]{2,1,0:T(8,128)(2,1)S(1)}, bf16[11,88,128]{2,1,0:T(8,128)(2,1)S(1)}, u32[]{:S(2)}, u32[]{:S(2)}) collective-permute-start(bf16[11,88,128]{2,1,0:T(8,128)(2,1)S(1)} %get-tuple-element.72), channel_id=1, source_target_pairs={{0,4},{4,8},{8,12},{12,14},{14,10},{10,6},{6,2},{2,0},{1,5},{5,9},... | collective-permute-start | bytes 743432 | tf_op jit(solution)/shard_map/ppermute | solution.py:511
  73.6 1.2 left_gradient.10.refs_6_.refs_3_
  75.6 2.2 %collective-permute-done.14.refs_4_ = bf16[11,88,128]{2,1,0:T(8,128)(2,1)S(1)} collective-permute-done((bf16[11,88,128]{2,1,0:T(8,128)(2,1)S(1)}, bf16[11,88,128]{2,1,0:T(8,128)(2,1)S(1)}, u32[]{:S(2)}, u32[]{:S(2)}) %collective-permute-start.14) | collective-permute-done | bytes 247840 | tf_op jit(solution)/shard_map/ppermute | solution.py:514
  77.8 1.6 %scatter_hop.10 = (bf16[11,88,128]{2,1,0:T(8,128)(2,1)S(1)}, bf16[11,88,128]{2,1,0:T(8,128)(2,1)S(1)}) custom-call(s32[8]{0:T(128)S(1)} %copy-done.9, bf16[22,88,128]{2,1,0:T(8,128)(2,1)S(1)} %get-tuple-element.48.refs_1_.refs_3_, bf16[4,22,16,128]{3,2,1,0:T(8,128)(2,1)S(1)} %get-tuple-element.57.refs_0_.refs_4_.refs_2_.refs_3_, ...), custom_call_target="tpu_custom_call" | custom-call | flops 1400000 | bytes 1024 | tf_op jit(solution)/shard_map/scatter_hop/pallas_call | solution.py:103
  80.1 1.5 %collective-permute-start.16 = (bf16[11,88,128]{2,1,0:T(8,128)(2,1)S(1)}, bf16[11,88,128]{2,1,0:T(8,128)(2,1)S(1)}, u32[]{:S(2)}, u32[]{:S(2)}) collective-permute-start(bf16[11,88,128]{2,1,0:T(8,128)(2,1)S(1)} %get-tuple-element.65.refs_4_), channel_id=1, source_target_pairs={{0,2},{4,0},{8,4},{12,8},{14,12},{10,14},{6,10},{2,6},{1,3},{5,1},... | collective-permute-start | bytes 743432 | tf_op jit(solution)/shard_map/ppermute | solution.py:514
  81.5 1.2 left_gradient.11.refs_6_.refs_3_
  82.8 1.8 %scatter_hop.11 = (bf16[11,88,128]{2,1,0:T(8,128)(2,1)S(1)}, bf16[11,88,128]{2,1,0:T(8,128)(2,1)S(1)}) custom-call(s32[8]{0:T(128)S(1)} %copy-done.9, bf16[22,88,128]{2,1,0:T(8,128)(2,1)S(1)} %get-tuple-element.48.refs_1_.refs_3_, bf16[4,22,16,128]{3,2,1,0:T(8,128)(2,1)S(1)} %get-tuple-element.60.refs_2_.refs_3_.refs_4_.refs_0_, ...), custom_call_target="tpu_custom_call" | custom-call | flops 1400000 | bytes 1024 | tf_op jit(solution)/shard_map/scatter_hop/pallas_call | solution.py:103
  85.5 1.2 collective-permute-start.20
  86.7 1.1 collective-permute-done.16.refs_4_
  87.9 1.5 %scatter_hop.12 = (bf16[11,88,128]{2,1,0:T(8,128)(2,1)S(1)}, bf16[11,88,128]{2,1,0:T(8,128)(2,1)S(1)}) custom-call(s32[8]{0:T(128)S(1)} %copy-done.9, bf16[22,88,128]{2,1,0:T(8,128)(2,1)S(1)} %get-tuple-element.48.refs_1_.refs_3_, bf16[4,22,16,128]{3,2,1,0:T(8,128)(2,1)S(1)} %get-tuple-element.54.refs_0_.refs_4_.refs_2_.refs_3_, ...), custom_call_target="tpu_custom_call" | custom-call | flops 1400000 | bytes 1024 | tf_op jit(solution)/shard_map/scatter_hop/pallas_call | solution.py:103
  89.4 6.5 %output_side.1 = (bf16[22,88,128]{2,1,0:T(8,128)(2,1)}, f32[22,88,128]{2,1,0:T(8,128)S(1)}, bf16[128,512]{1,0:T(8,128)(2,1)S(1)}) custom-call(s32[8]{0:T(128)S(1)} %copy-done.10, bf16[22,88,128]{2,1,0:T(8,128)(2,1)S(1)} %get-tuple-element.47.refs_1_, bf16[22,88,128]{2,1,0:T(8,128)(2,1)S(1)} %copy-done.3, f32[22,88,128]{2,1,0:T(8,128)S(1)} %left_gradient.11.refs_6_.refs_3_, ...), custom_call_target="tpu_custom_call" | custom-call | flops 6000000 | bytes 1024 | tf_op jit(solution)/shard_map/output_side/pallas_call | solution.py:103
  96.0 1.0 copy-done.7
  97.0 1.7 %scatter_hop.13 = (bf16[11,88,128]{2,1,0:T(8,128)(2,1)S(1)}, bf16[11,88,128]{2,1,0:T(8,128)(2,1)S(1)}) custom-call(s32[8]{0:T(128)S(1)} %copy-done.10, bf16[22,88,128]{2,1,0:T(8,128)(2,1)S(1)} %get-tuple-element.48.refs_1_.refs_3_, bf16[4,22,16,128]{3,2,1,0:T(8,128)(2,1)S(1)} %get-tuple-element.57.refs_0_.refs_4_.refs_2_.refs_3_, ...), custom_call_target="tpu_custom_call" | custom-call | flops 1400000 | bytes 1024 | tf_op jit(solution)/shard_map/scatter_hop/pallas_call | solution.py:103
  98.7 1.5 %collective-permute-start.23 = (bf16[11,88,128]{2,1,0:T(8,128)(2,1)S(1)}, bf16[11,88,128]{2,1,0:T(8,128)(2,1)S(1)}, u32[]{:S(2)}, u32[]{:S(2)}) collective-permute-start(bf16[11,88,128]{2,1,0:T(8,128)(2,1)S(1)} %get-tuple-element.80), channel_id=1, source_target_pairs={{0,4},{4,8},{8,12},{12,14},{14,10},{10,6},{6,2},{2,0},{1,5},{5,9},... | collective-permute-start | bytes 743432 | tf_op jit(solution)/shard_map/ppermute | solution.py:511
  100.8 1.5 %collective-permute-start.27 = (bf16[11,88,128]{2,1,0:T(8,128)(2,1)S(1)}, bf16[11,88,128]{2,1,0:T(8,128)(2,1)S(1)}, u32[]{:S(2)}, u32[]{:S(2)}) collective-permute-start(bf16[11,88,128]{2,1,0:T(8,128)(2,1)S(1)} %get-tuple-element.74.refs_12_), channel_id=1, source_target_pairs={{0,2},{4,0},{8,4},{12,8},{14,12},{10,14},{6,10},{2,6},{1,3},{5,1},... | collective-permute-start | bytes 743432 | tf_op jit(solution)/shard_map/ppermute | solution.py:514
  102.9 1.9 %scatter_hop.14 = (f32[11,88,128]{2,1,0:T(8,128)S(1)}, f32[11,88,128]{2,1,0:T(8,128)S(1)}) custom-call(s32[8]{0:T(128)S(1)} %copy-done.10, bf16[22,88,128]{2,1,0:T(8,128)(2,1)S(1)} %get-tuple-element.48.refs_1_.refs_3_, bf16[2,22,16,128]{3,2,1,0:T(8,128)(2,1)S(1)} %get-tuple-element.51.refs_0_.refs_2_.refs_3_, ...), custom_call_target="tpu_custom_call" | custom-call | flops 1400000 | bytes 1024 | tf_op jit(solution)/shard_map/scatter_hop/pallas_call | solution.py:103
  104.8 2.5 %collective-permute-done.23.refs_5_ = bf16[11,88,128]{2,1,0:T(8,128)(2,1)S(1)} collective-permute-done((bf16[11,88,128]{2,1,0:T(8,128)(2,1)S(1)}, bf16[11,88,128]{2,1,0:T(8,128)(2,1)S(1)}, u32[]{:S(2)}, u32[]{:S(2)}) %collective-permute-start.23) | collective-permute-done | bytes 247840 | tf_op jit(solution)/shard_map/ppermute | solution.py:511
  107.2 1.5 %collective-permute-done.22.refs_4_ = bf16[11,88,128]{2,1,0:T(8,128)(2,1)S(1)} collective-permute-done((bf16[11,88,128]{2,1,0:T(8,128)(2,1)S(1)}, bf16[11,88,128]{2,1,0:T(8,128)(2,1)S(1)}, u32[]{:S(2)}, u32[]{:S(2)}) %collective-permute-start.22) | collective-permute-done | bytes 247840 | tf_op jit(solution)/shard_map/ppermute | solution.py:514
  108.7 1.4 scatter_hop.15
  110.2 1.4 collective-permute-start.24
  111.6 1.4 collective-permute-start.26
  113.9 3.2 %collective-permute-done.24.refs_5_ = bf16[11,88,128]{2,1,0:T(8,128)(2,1)S(1)} collective-permute-done((bf16[11,88,128]{2,1,0:T(8,128)(2,1)S(1)}, bf16[11,88,128]{2,1,0:T(8,128)(2,1)S(1)}, u32[]{:S(2)}, u32[]{:S(2)}) %collective-permute-start.24) | collective-permute-done | bytes 247840 | tf_op jit(solution)/shard_map/ppermute | solution.py:514
  117.8 2.0 %right_gradient.1 = (bf16[22,88,256]{2,1,0:T(8,128)(2,1)S(1)}, bf16[128,256]{1,0:T(8,128)(2,1)S(1)}) custom-call(s32[8]{0:T(128)S(1)} %copy-done.10, bf16[22,88,128]{2,1,0:T(8,128)(2,1)S(1)} %get-tuple-element.47.refs_1_, bf16[128,640]{1,0:T(8,128)(2,1)S(1)} %copy-done.1, f32[11,88,128]{2,1,0:T(8,128)S(1)} %get-tuple-element.78.refs_6_.refs_3_, ...), custom_call_target="tpu_custom_call" | custom-call | flops 3000000 | bytes 1024 | tf_op jit(solution)/shard_map/right_gradient/pallas_call | solution.py:103
  120.0 1.4 collective-permute-start.29
  121.4 1.2 collective-permute-start.33
  122.6 3.7 %collective-permute-done.29 = bf16[128,512]{1,0:T(8,128)(2,1)S(1)} collective-permute-done((bf16[128,512]{1,0:T(8,128)(2,1)S(1)}, bf16[128,512]{1,0:T(8,128)(2,1)S(1)}, u32[]{:S(2)}, u32[]{:S(2)}) %collective-permute-start.29) | collective-permute-done | bytes 131104 | tf_op jit(solution)/shard_map/ppermute | solution.py:89
  126.4 1.5 %collective-permute-start.30 = (bf16[128,512]{1,0:T(8,128)(2,1)S(1)}, bf16[128,512]{1,0:T(8,128)(2,1)S(1)}, u32[]{:S(2)}, u32[]{:S(2)}) collective-permute-start(bf16[128,512]{1,0:T(8,128)(2,1)S(1)} %add_convert_fusion.2), channel_id=1, source_target_pairs={{0,4},{2,6},{4,0},{6,2},{8,12},{10,14},{12,8},{14,10},{1,5},{3,7},... | collective-permute-start | bytes 393224 | tf_op jit(solution)/shard_map/ppermute | solution.py:89
  127.9 1.1 collective-permute-start.34
  129.0 3.0 %collective-permute-done.30 = bf16[128,512]{1,0:T(8,128)(2,1)S(1)} collective-permute-done((bf16[128,512]{1,0:T(8,128)(2,1)S(1)}, bf16[128,512]{1,0:T(8,128)(2,1)S(1)}, u32[]{:S(2)}, u32[]{:S(2)}) %collective-permute-start.30) | collective-permute-done | bytes 131104 | tf_op jit(solution)/shard_map/ppermute | solution.py:89
  132.0 3.0 %collective-permute-start.31 = (bf16[128,512]{1,0:T(8,128)(2,1)S(1)}, bf16[128,512]{1,0:T(8,128)(2,1)S(1)}, u32[]{:S(2)}, u32[]{:S(2)}) collective-permute-start(bf16[128,512]{1,0:T(8,128)(2,1)S(1)} %add_convert_fusion.1), channel_id=1, source_target_pairs={{0,8},{2,10},{4,12},{6,14},{8,0},{10,2},{12,4},{14,6},{1,9},{3,11}... | collective-permute-start | bytes 393224 | tf_op jit(solution)/shard_map/ppermute | solution.py:89
  135.0 1.0 collective-permute-start.35
  136.1 4.6 %collective-permute-done.31 = bf16[128,512]{1,0:T(8,128)(2,1)S(1)} collective-permute-done((bf16[128,512]{1,0:T(8,128)(2,1)S(1)}, bf16[128,512]{1,0:T(8,128)(2,1)S(1)}, u32[]{:S(2)}, u32[]{:S(2)}) %collective-permute-start.31) | collective-permute-done | bytes 131104 | tf_op jit(solution)/shard_map/ppermute | solution.py:89
  140.7 3.3 %pair_gradient.1 = bf16[22,88,128]{2,1,0:T(8,128)(2,1)} custom-call(bf16[22,88,128]{2,1,0:T(8,128)(2,1)S(1)} %copy-done.5, bf16[22,88,256]{2,1,0:T(8,128)(2,1)S(1)} %get-tuple-element.84.refs_1_, f32[22,88,128]{2,1,0:T(8,128)S(1)} %get-tuple-element.85.refs_2_, f32[1,128]{1,0:T(1,128)S(1)} %bitcast.15, bf16[128,640]{1,0:T(8,128)(2,1)S(1)} %copy-done.1), custom_call_target="tpu_custom_call" | custom-call | flops 3000000 | bytes 1024 | tf_op jit(solution)/shard_map/pair_gradient/pallas_call | solution.py:103
  (81 shorter events, 14.8 us)
Async XLA Ops:
  0.6 0.9 copy-start
  1.5 1.0 copy-start.4
  2.6 0.7 copy-start.8
  3.2 0.7 copy-start.13
  3.9 0.7 copy-start.15
  6.0 1.0 copy-start.2
  7.1 0.7 copy-start.9
  9.1 6.4 %collective-permute-start.3 = (bf16[8,22,16,128]{3,2,1,0:T(8,128)(2,1)S(1)}, bf16[8,22,16,128]{3,2,1,0:T(8,128)(2,1)S(1)}, u32[]{:S(2)}, u32[]{:S(2)}) collective-permute-start(bf16[8,22,16,128]{3,2,1,0:T(8,128)(2,1)S(1)} %get-tuple-element.50), channel_id=1, source_target_pairs={{0,1},{1,0},{2,3},{3,2},{4,5},{5,4},{6,7},{7,6},{8,9},{9,8},{10,11... | collective-permute-start | bytes 2162696 | tf_op jit(solution)/shard_map/ppermute | solution.py:77
  9.7 14.6 %collective-permute-start.1 = (bf16[22,88,128]{2,1,0:T(8,128)(2,1)S(1)}, bf16[22,88,128]{2,1,0:T(8,128)(2,1)S(1)}, u32[]{:S(2)}, u32[]{:S(2)}) collective-permute-start(bf16[22,88,128]{2,1,0:T(8,128)(2,1)S(1)} %get-tuple-element.49.refs_2_.refs_1_), channel_id=1, source_target_pairs={{0,2},{4,0},{8,4},{12,8},{14,12},{10,14},{6,10},{2,6},{1,3},{5,1},... | collective-permute-start | bytes 1486856 | tf_op jit(solution)/shard_map/ppermute | solution.py:514
  12.2 13.4 %collective-permute-start = (bf16[22,88,128]{2,1,0:T(8,128)(2,1)S(1)}, bf16[22,88,128]{2,1,0:T(8,128)(2,1)S(1)}, u32[]{:S(2)}, u32[]{:S(2)}) collective-permute-start(bf16[22,88,128]{2,1,0:T(8,128)(2,1)S(1)} %get-tuple-element.49.refs_2_.refs_1_), channel_id=1, source_target_pairs={{0,4},{4,8},{8,12},{12,14},{14,10},{10,6},{6,2},{2,0},{1,5},{5,9},... | collective-permute-start | bytes 1486856 | tf_op jit(solution)/shard_map/ppermute | solution.py:511
  15.2 1.5 %copy-start.6 = (bf16[128,128]{1,0:T(8,128)(2,1)S(1)}, bf16[128,128]{1,0:T(8,128)(2,1)}, u32[]{:S(2)}) copy-start(bf16[128,128]{1,0:T(8,128)(2,1)} %refs_5_.1) | copy-start | bytes 98308
  15.2 1.5 %copy-start.11 = (f32[128]{0:T(128)S(1)}, f32[128]{0:T(128)}, u32[]{:S(2)}) copy-start(f32[128]{0:T(128)} %param.15) | copy-start | bytes 1540
  15.2 1.5 %copy-start.12 = (f32[128]{0:T(128)S(1)}, f32[128]{0:T(128)}, u32[]{:S(2)}) copy-start(f32[128]{0:T(128)} %param.16) | copy-start | bytes 1540
  15.2 1.5 %collective-permute-start.2 = (bf16[2,22,16,128]{3,2,1,0:T(8,128)(2,1)S(1)}, bf16[2,22,16,128]{3,2,1,0:T(8,128)(2,1)S(1)}, u32[]{:S(2)}, u32[]{:S(2)}) collective-permute-start(bf16[2,22,16,128]{3,2,1,0:T(8,128)(2,1)S(1)} %triangle.5.refs_0_.refs_6_), channel_id=1, source_target_pairs={{0,1},{1,0},{2,3},{3,2},{4,5},{5,4},{6,7},{7,6},{8,9},{9,8},{10,11... | collective-permute-start | bytes 540680 | tf_op jit(solution)/shard_map/ppermute | solution.py:77
  25.6 12.6 %collective-permute-start.4 = (bf16[22,88,128]{2,1,0:T(8,128)(2,1)S(1)}, bf16[22,88,128]{2,1,0:T(8,128)(2,1)S(1)}, u32[]{:S(2)}, u32[]{:S(2)}) collective-permute-start(bf16[22,88,128]{2,1,0:T(8,128)(2,1)S(1)} %collective-permute-done.refs_2_.refs_1_), channel_id=1, source_target_pairs={{0,4},{4,8},{8,12},{12,14},{14,10},{10,6},{6,2},{2,0},{1,5},{5,9},... | collective-permute-start | bytes 1486856 | tf_op jit(solution)/shard_map/ppermute | solution.py:511
  26.0 12.6 %collective-permute-start.5 = (bf16[22,88,128]{2,1,0:T(8,128)(2,1)S(1)}, bf16[22,88,128]{2,1,0:T(8,128)(2,1)S(1)}, u32[]{:S(2)}, u32[]{:S(2)}) collective-permute-start(bf16[22,88,128]{2,1,0:T(8,128)(2,1)S(1)} %collective-permute-done.1.refs_3_.refs_2_), channel_id=1, source_target_pairs={{0,2},{4,0},{8,4},{12,8},{14,12},{10,14},{6,10},{2,6},{1,3},{5,1},... | collective-permute-start | bytes 1486856 | tf_op jit(solution)/shard_map/ppermute | solution.py:514
  30.8 1.7 %collective-permute-start.6 = (bf16[4,22,16,128]{3,2,1,0:T(8,128)(2,1)S(1)}, bf16[4,22,16,128]{3,2,1,0:T(8,128)(2,1)S(1)}, u32[]{:S(2)}, u32[]{:S(2)}) collective-permute-start(bf16[4,22,16,128]{3,2,1,0:T(8,128)(2,1)S(1)} %triangle.6.refs_0_.refs_6_), channel_id=1, source_target_pairs={{0,1},{1,0},{2,3},{3,2},{4,5},{5,4},{6,7},{7,6},{8,9},{9,8},{10,11... | collective-permute-start | bytes 1081352 | tf_op jit(solution)/shard_map/ppermute | solution.py:77
  38.5 11.7 %collective-permute-start.7 = (bf16[22,88,128]{2,1,0:T(8,128)(2,1)S(1)}, bf16[22,88,128]{2,1,0:T(8,128)(2,1)S(1)}, u32[]{:S(2)}, u32[]{:S(2)}) collective-permute-start(bf16[22,88,128]{2,1,0:T(8,128)(2,1)S(1)} %collective-permute-done.4.refs_2_.refs_1_), channel_id=1, source_target_pairs={{0,4},{4,8},{8,12},{12,14},{14,10},{10,6},{6,2},{2,0},{1,5},{5,9},... | collective-permute-start | bytes 1486856 | tf_op jit(solution)/shard_map/ppermute | solution.py:511
  40.1 11.2 %collective-permute-start.8 = (bf16[22,88,128]{2,1,0:T(8,128)(2,1)S(1)}, bf16[22,88,128]{2,1,0:T(8,128)(2,1)S(1)}, u32[]{:S(2)}, u32[]{:S(2)}) collective-permute-start(bf16[22,88,128]{2,1,0:T(8,128)(2,1)S(1)} %collective-permute-done.5.refs_3_.refs_2_), channel_id=1, source_target_pairs={{0,2},{4,0},{8,4},{12,8},{14,12},{10,14},{6,10},{2,6},{1,3},{5,1},... | collective-permute-start | bytes 1486856 | tf_op jit(solution)/shard_map/ppermute | solution.py:514
  44.3 1.7 %collective-permute-start.9 = (bf16[4,22,16,128]{3,2,1,0:T(8,128)(2,1)S(1)}, bf16[4,22,16,128]{3,2,1,0:T(8,128)(2,1)S(1)}, u32[]{:S(2)}, u32[]{:S(2)}) collective-permute-start(bf16[4,22,16,128]{3,2,1,0:T(8,128)(2,1)S(1)} %triangle.7.refs_0_.refs_6_), channel_id=1, source_target_pairs={{0,1},{1,0},{2,3},{3,2},{4,5},{5,4},{6,7},{7,6},{8,9},{9,8},{10,11... | collective-permute-start | bytes 1081352 | tf_op jit(solution)/shard_map/ppermute | solution.py:77
  55.7 2.2 %collective-permute-start.12 = (bf16[4,22,16,128]{3,2,1,0:T(8,128)(2,1)S(1)}, bf16[4,22,16,128]{3,2,1,0:T(8,128)(2,1)S(1)}, u32[]{:S(2)}, u32[]{:S(2)}) collective-permute-start(bf16[4,22,16,128]{3,2,1,0:T(8,128)(2,1)S(1)} %triangle.8.refs_0_.refs_6_), channel_id=1, source_target_pairs={{0,1},{1,0},{2,3},{3,2},{4,5},{5,4},{6,7},{7,6},{8,9},{9,8},{10,11... | collective-permute-start | bytes 1081352 | tf_op jit(solution)/shard_map/ppermute | solution.py:77
  55.8 8.4 %collective-permute-start.11 = (bf16[11,88,128]{2,1,0:T(8,128)(2,1)S(1)}, bf16[11,88,128]{2,1,0:T(8,128)(2,1)S(1)}, u32[]{:S(2)}, u32[]{:S(2)}) collective-permute-start(bf16[11,88,128]{2,1,0:T(8,128)(2,1)S(1)} %slice.7), channel_id=1, source_target_pairs={{0,2},{4,0},{8,4},{12,8},{14,12},{10,14},{6,10},{2,6},{1,3},{5,1},... | collective-permute-start | bytes 743432 | tf_op jit(solution)/shard_map/ppermute | solution.py:514
  56.2 8.1 %collective-permute-start.10 = (bf16[11,88,128]{2,1,0:T(8,128)(2,1)S(1)}, bf16[11,88,128]{2,1,0:T(8,128)(2,1)S(1)}, u32[]{:S(2)}, u32[]{:S(2)}) collective-permute-start(bf16[11,88,128]{2,1,0:T(8,128)(2,1)S(1)} %slice.6), channel_id=1, source_target_pairs={{0,4},{4,8},{8,12},{12,14},{14,10},{10,6},{6,2},{2,0},{1,5},{5,9},... | collective-permute-start | bytes 743432 | tf_op jit(solution)/shard_map/ppermute | solution.py:511
  66.6 2.3 %collective-permute-start.13 = (bf16[2,22,16,128]{3,2,1,0:T(8,128)(2,1)S(1)}, bf16[2,22,16,128]{3,2,1,0:T(8,128)(2,1)S(1)}, u32[]{:S(2)}, u32[]{:S(2)}) collective-permute-start(bf16[2,22,16,128]{3,2,1,0:T(8,128)(2,1)S(1)} %triangle.9.refs_0_.refs_6_), channel_id=1, source_target_pairs={{0,1},{1,0},{2,3},{3,2},{4,5},{5,4},{6,7},{7,6},{8,9},{9,8},{10,11... | collective-permute-start | bytes 540680 | tf_op jit(solution)/shard_map/ppermute | solution.py:77
  66.7 8.8 %collective-permute-start.15 = (bf16[11,88,128]{2,1,0:T(8,128)(2,1)S(1)}, bf16[11,88,128]{2,1,0:T(8,128)(2,1)S(1)}, u32[]{:S(2)}, u32[]{:S(2)}) collective-permute-start(bf16[11,88,128]{2,1,0:T(8,128)(2,1)S(1)} %get-tuple-element.64), channel_id=1, source_target_pairs={{0,4},{4,8},{8,12},{12,14},{14,10},{10,6},{6,2},{2,0},{1,5},{5,9},... | collective-permute-start | bytes 743432 | tf_op jit(solution)/shard_map/ppermute | solution.py:511
  68.9 8.8 %collective-permute-start.14 = (bf16[11,88,128]{2,1,0:T(8,128)(2,1)S(1)}, bf16[11,88,128]{2,1,0:T(8,128)(2,1)S(1)}, u32[]{:S(2)}, u32[]{:S(2)}) collective-permute-start(bf16[11,88,128]{2,1,0:T(8,128)(2,1)S(1)} %get-tuple-element.61.refs_4_), channel_id=1, source_target_pairs={{0,2},{4,0},{8,4},{12,8},{14,12},{10,14},{6,10},{2,6},{1,3},{5,1},... | collective-permute-start | bytes 743432 | tf_op jit(solution)/shard_map/ppermute | solution.py:514
  71.2 11.5 %collective-permute-start.19 = (bf16[11,88,128]{2,1,0:T(8,128)(2,1)S(1)}, bf16[11,88,128]{2,1,0:T(8,128)(2,1)S(1)}, u32[]{:S(2)}, u32[]{:S(2)}) collective-permute-start(bf16[11,88,128]{2,1,0:T(8,128)(2,1)S(1)} %get-tuple-element.72), channel_id=1, source_target_pairs={{0,4},{4,8},{8,12},{12,14},{14,10},{10,6},{6,2},{2,0},{1,5},{5,9},... | collective-permute-start | bytes 743432 | tf_op jit(solution)/shard_map/ppermute | solution.py:511
  73.5 9.2 %collective-permute-start.18 = (bf16[11,88,128]{2,1,0:T(8,128)(2,1)S(1)}, bf16[11,88,128]{2,1,0:T(8,128)(2,1)S(1)}, u32[]{:S(2)}, u32[]{:S(2)}) collective-permute-start(bf16[11,88,128]{2,1,0:T(8,128)(2,1)S(1)} %get-tuple-element.63.refs_4_), channel_id=1, source_target_pairs={{0,2},{4,0},{8,4},{12,8},{14,12},{10,14},{6,10},{2,6},{1,3},{5,1},... | collective-permute-start | bytes 743432 | tf_op jit(solution)/shard_map/ppermute | solution.py:514
  79.4 7.3 %collective-permute-start.17 = (bf16[11,88,128]{2,1,0:T(8,128)(2,1)S(1)}, bf16[11,88,128]{2,1,0:T(8,128)(2,1)S(1)}, u32[]{:S(2)}, u32[]{:S(2)}) collective-permute-start(bf16[11,88,128]{2,1,0:T(8,128)(2,1)S(1)} %get-tuple-element.71), channel_id=1, source_target_pairs={{0,4},{4,8},{8,12},{12,14},{14,10},{10,6},{6,2},{2,0},{1,5},{5,9},... | collective-permute-start | bytes 743432 | tf_op jit(solution)/shard_map/ppermute | solution.py:511
  80.1 7.8 %collective-permute-start.16 = (bf16[11,88,128]{2,1,0:T(8,128)(2,1)S(1)}, bf16[11,88,128]{2,1,0:T(8,128)(2,1)S(1)}, u32[]{:S(2)}, u32[]{:S(2)}) collective-permute-start(bf16[11,88,128]{2,1,0:T(8,128)(2,1)S(1)} %get-tuple-element.65.refs_4_), channel_id=1, source_target_pairs={{0,2},{4,0},{8,4},{12,8},{14,12},{10,14},{6,10},{2,6},{1,3},{5,1},... | collective-permute-start | bytes 743432 | tf_op jit(solution)/shard_map/ppermute | solution.py:514
  84.6 4.8 %copy-start.1 = (bf16[128,640]{1,0:T(8,128)(2,1)S(1)}, bf16[128,640]{1,0:T(8,128)(2,1)}, u32[]{:S(2)}) copy-start(bf16[128,640]{1,0:T(8,128)(2,1)} %refs_4_.5) | copy-start | bytes 491524
  84.6 4.8 %copy-start.3 = (bf16[22,88,128]{2,1,0:T(8,128)(2,1)S(1)}, bf16[22,88,128]{2,1,0:T(8,128)(2,1)}, u32[]{:S(2)}) copy-start(bf16[22,88,128]{2,1,0:T(8,128)(2,1)} %refs_2_.4) | copy-start | bytes 1486852
  84.6 4.8 %copy-start.10 = (s32[8]{0:T(128)S(1)}, s32[8]{0:T(128)}, u32[]{:S(2)}) copy-start(s32[8]{0:T(128)} %refs_0_.34) | copy-start | bytes 100
  84.7 11.3 %collective-permute-start.21 = (bf16[11,88,128]{2,1,0:T(8,128)(2,1)S(1)}, bf16[11,88,128]{2,1,0:T(8,128)(2,1)S(1)}, u32[]{:S(2)}, u32[]{:S(2)}) collective-permute-start(bf16[11,88,128]{2,1,0:T(8,128)(2,1)S(1)} %get-tuple-element.76), channel_id=1, source_target_pairs={{0,4},{4,8},{8,12},{12,14},{14,10},{10,6},{6,2},{2,0},{1,5},{5,9},... | collective-permute-start | bytes 743432 | tf_op jit(solution)/shard_map/ppermute | solution.py:511
  85.5 10.5 %collective-permute-start.20 = (bf16[11,88,128]{2,1,0:T(8,128)(2,1)S(1)}, bf16[11,88,128]{2,1,0:T(8,128)(2,1)S(1)}, u32[]{:S(2)}, u32[]{:S(2)}) collective-permute-start(bf16[11,88,128]{2,1,0:T(8,128)(2,1)S(1)} %get-tuple-element.73.refs_6_), channel_id=1, source_target_pairs={{0,2},{4,0},{8,4},{12,8},{14,12},{10,14},{6,10},{2,6},{1,3},{5,1},... | collective-permute-start | bytes 743432 | tf_op jit(solution)/shard_map/ppermute | solution.py:514
  96.0 1.0 copy-start.7
  98.7 8.5 %collective-permute-start.23 = (bf16[11,88,128]{2,1,0:T(8,128)(2,1)S(1)}, bf16[11,88,128]{2,1,0:T(8,128)(2,1)S(1)}, u32[]{:S(2)}, u32[]{:S(2)}) collective-permute-start(bf16[11,88,128]{2,1,0:T(8,128)(2,1)S(1)} %get-tuple-element.80), channel_id=1, source_target_pairs={{0,4},{4,8},{8,12},{12,14},{14,10},{10,6},{6,2},{2,0},{1,5},{5,9},... | collective-permute-start | bytes 743432 | tf_op jit(solution)/shard_map/ppermute | solution.py:511
  100.2 8.5 %collective-permute-start.22 = (bf16[11,88,128]{2,1,0:T(8,128)(2,1)S(1)}, bf16[11,88,128]{2,1,0:T(8,128)(2,1)S(1)}, u32[]{:S(2)}, u32[]{:S(2)}) collective-permute-start(bf16[11,88,128]{2,1,0:T(8,128)(2,1)S(1)} %get-tuple-element.77.refs_4_), channel_id=1, source_target_pairs={{0,2},{4,0},{8,4},{12,8},{14,12},{10,14},{6,10},{2,6},{1,3},{5,1},... | collective-permute-start | bytes 743432 | tf_op jit(solution)/shard_map/ppermute | solution.py:514
  100.8 13.1 %collective-permute-start.27 = (bf16[11,88,128]{2,1,0:T(8,128)(2,1)S(1)}, bf16[11,88,128]{2,1,0:T(8,128)(2,1)S(1)}, u32[]{:S(2)}, u32[]{:S(2)}) collective-permute-start(bf16[11,88,128]{2,1,0:T(8,128)(2,1)S(1)} %get-tuple-element.74.refs_12_), channel_id=1, source_target_pairs={{0,2},{4,0},{8,4},{12,8},{14,12},{10,14},{6,10},{2,6},{1,3},{5,1},... | collective-permute-start | bytes 743432 | tf_op jit(solution)/shard_map/ppermute | solution.py:514
  102.3 10.7 %collective-permute-start.25 = (bf16[11,88,128]{2,1,0:T(8,128)(2,1)S(1)}, bf16[11,88,128]{2,1,0:T(8,128)(2,1)S(1)}, u32[]{:S(2)}, u32[]{:S(2)}) collective-permute-start(bf16[11,88,128]{2,1,0:T(8,128)(2,1)S(1)} %get-tuple-element.82), channel_id=1, source_target_pairs={{0,4},{4,8},{8,12},{12,14},{14,10},{10,6},{6,2},{2,0},{1,5},{5,9},... | collective-permute-start | bytes 743432 | tf_op jit(solution)/shard_map/ppermute | solution.py:511
  110.2 7.0 %collective-permute-start.24 = (bf16[11,88,128]{2,1,0:T(8,128)(2,1)S(1)}, bf16[11,88,128]{2,1,0:T(8,128)(2,1)S(1)}, u32[]{:S(2)}, u32[]{:S(2)}) collective-permute-start(bf16[11,88,128]{2,1,0:T(8,128)(2,1)S(1)} %get-tuple-element.81), channel_id=1, source_target_pairs={{0,2},{4,0},{8,4},{12,8},{14,12},{10,14},{6,10},{2,6},{1,3},{5,1},... | collective-permute-start | bytes 743432 | tf_op jit(solution)/shard_map/ppermute | solution.py:514
  111.6 6.2 %collective-permute-start.26 = (bf16[11,88,128]{2,1,0:T(8,128)(2,1)S(1)}, bf16[11,88,128]{2,1,0:T(8,128)(2,1)S(1)}, u32[]{:S(2)}, u32[]{:S(2)}) collective-permute-start(bf16[11,88,128]{2,1,0:T(8,128)(2,1)S(1)} %get-tuple-element.83), channel_id=1, source_target_pairs={{0,4},{4,8},{8,12},{12,14},{14,10},{10,6},{6,2},{2,0},{1,5},{5,9},... | collective-permute-start | bytes 743432 | tf_op jit(solution)/shard_map/ppermute | solution.py:511
  113.0 6.9 %collective-permute-start.28 = (bf16[128,512]{1,0:T(8,128)(2,1)S(1)}, bf16[128,512]{1,0:T(8,128)(2,1)S(1)}, u32[]{:S(2)}, u32[]{:S(2)}) collective-permute-start(bf16[128,512]{1,0:T(8,128)(2,1)S(1)} %get-tuple-element.86), channel_id=1, source_target_pairs={{0,1},{1,0},{2,3},{3,2},{4,5},{5,4},{6,7},{7,6},{8,9},{9,8},{10,11... | collective-permute-start | bytes 393224 | tf_op jit(solution)/shard_map/ppermute | solution.py:77
  119.8 20.9 %copy-start.5 = (bf16[22,88,128]{2,1,0:T(8,128)(2,1)S(1)}, bf16[22,88,128]{2,1,0:T(8,128)(2,1)}, u32[]{:S(2)}) copy-start(bf16[22,88,128]{2,1,0:T(8,128)(2,1)} %refs_0_.35) | copy-start | bytes 1486852
  119.9 20.9 %copy-start.14 = (f32[128]{0:T(128)S(1)}, f32[128]{0:T(128)}, u32[]{:S(2)}) copy-start(f32[128]{0:T(128)} %param.12) | copy-start | bytes 1540
  119.9 1.5 %collective-permute-start.32 = (bf16[128,256]{1,0:T(8,128)(2,1)S(1)}, bf16[128,256]{1,0:T(8,128)(2,1)S(1)}, u32[]{:S(2)}, u32[]{:S(2)}) collective-permute-start(bf16[128,256]{1,0:T(8,128)(2,1)S(1)} %get-tuple-element.87), channel_id=1, source_target_pairs={{0,1},{1,0},{2,3},{3,2},{4,5},{5,4},{6,7},{7,6},{8,9},{9,8},{10,11... | collective-permute-start | bytes 196616 | tf_op jit(solution)/shard_map/ppermute | solution.py:77
  120.0 6.4 %collective-permute-start.29 = (bf16[128,512]{1,0:T(8,128)(2,1)S(1)}, bf16[128,512]{1,0:T(8,128)(2,1)S(1)}, u32[]{:S(2)}, u32[]{:S(2)}) collective-permute-start(bf16[128,512]{1,0:T(8,128)(2,1)S(1)} %add_convert_fusion.3), channel_id=1, source_target_pairs={{0,2},{2,0},{4,6},{6,4},{8,10},{10,8},{12,14},{14,12},{1,3},{3,1},... | collective-permute-start | bytes 393224 | tf_op jit(solution)/shard_map/ppermute | solution.py:89
  121.4 6.4 %collective-permute-start.33 = (bf16[128,256]{1,0:T(8,128)(2,1)S(1)}, bf16[128,256]{1,0:T(8,128)(2,1)S(1)}, u32[]{:S(2)}, u32[]{:S(2)}) collective-permute-start(bf16[128,256]{1,0:T(8,128)(2,1)S(1)} %add_convert_fusion.6), channel_id=1, source_target_pairs={{0,2},{2,0},{4,6},{6,4},{8,10},{10,8},{12,14},{14,12},{1,3},{3,1},... | collective-permute-start | bytes 196616 | tf_op jit(solution)/shard_map/ppermute | solution.py:89
  126.4 5.6 %collective-permute-start.30 = (bf16[128,512]{1,0:T(8,128)(2,1)S(1)}, bf16[128,512]{1,0:T(8,128)(2,1)S(1)}, u32[]{:S(2)}, u32[]{:S(2)}) collective-permute-start(bf16[128,512]{1,0:T(8,128)(2,1)S(1)} %add_convert_fusion.2), channel_id=1, source_target_pairs={{0,4},{2,6},{4,0},{6,2},{8,12},{10,14},{12,8},{14,10},{1,5},{3,7},... | collective-permute-start | bytes 393224 | tf_op jit(solution)/shard_map/ppermute | solution.py:89
  127.9 7.1 %collective-permute-start.34 = (bf16[128,256]{1,0:T(8,128)(2,1)S(1)}, bf16[128,256]{1,0:T(8,128)(2,1)S(1)}, u32[]{:S(2)}, u32[]{:S(2)}) collective-permute-start(bf16[128,256]{1,0:T(8,128)(2,1)S(1)} %add_convert_fusion.5), channel_id=1, source_target_pairs={{0,4},{2,6},{4,0},{6,2},{8,12},{10,14},{12,8},{14,10},{1,5},{3,7},... | collective-permute-start | bytes 196616 | tf_op jit(solution)/shard_map/ppermute | solution.py:89
  132.0 8.6 %collective-permute-start.31 = (bf16[128,512]{1,0:T(8,128)(2,1)S(1)}, bf16[128,512]{1,0:T(8,128)(2,1)S(1)}, u32[]{:S(2)}, u32[]{:S(2)}) collective-permute-start(bf16[128,512]{1,0:T(8,128)(2,1)S(1)} %add_convert_fusion.1), channel_id=1, source_target_pairs={{0,8},{2,10},{4,12},{6,14},{8,0},{10,2},{12,4},{14,6},{1,9},{3,11}... | collective-permute-start | bytes 393224 | tf_op jit(solution)/shard_map/ppermute | solution.py:89
  135.0 9.0 %collective-permute-start.35 = (bf16[128,256]{1,0:T(8,128)(2,1)S(1)}, bf16[128,256]{1,0:T(8,128)(2,1)S(1)}, u32[]{:S(2)}, u32[]{:S(2)}) collective-permute-start(bf16[128,256]{1,0:T(8,128)(2,1)S(1)} %add_convert_fusion.4.refs_1_), channel_id=1, source_target_pairs={{0,8},{2,10},{4,12},{6,14},{8,0},{10,2},{12,4},{14,6},{1,9},{3,11}... | collective-permute-start | bytes 196616 | tf_op jit(solution)/shard_map/ppermute | solution.py:89
